TPU v7x, 32 devices: a whole 2x2x4 slice. The times are simulated.
32 devices in a mesh: section: 2 (over core), tensor: 4 (over z), dp: 4 (over y, x).
Axes of the slice: x: 2, y: 2, z: 4, core: 2. Of those that a mesh axis runs over, the one named last changes fastest.
Arguments:
- inputs: bfloat16 [8192, 1024], P('dp'), may hold values from -6 to 6
- cotangent: bfloat16 [8192, 1024], P('dp'), may hold values from -6 to 6
- lengths: int32 [8], P('dp'), may hold values from 256 to 1024, as said below
- w_query: bfloat16 [2, 1024, 1024], P('section', None, 'tensor'), may hold values from -0.1875 to 0.1875
- w_latent: bfloat16 [2, 1024, 512], P('section'), may hold values from -0.1875 to 0.1875
- w_key: bfloat16 [2, 256, 1024], P('section', None, 'tensor'), may hold values from -0.375 to 0.375
- w_value: bfloat16 [2, 256, 1024], P('section', None, 'tensor'), may hold values from -0.375 to 0.375
- w_out: bfloat16 [2, 1024, 1024], P('section', 'tensor'), may hold values from -3 to 3
- gains: float32 [2, 2, 1024], P('section'), may hold values from 0.1 to 1.9
- w_gate: bfloat16 [2, 1024, 2816], P('section', None, 'tensor'), may hold values from -0.1875 to 0.1875
- w_up: bfloat16 [2, 1024, 2816], P('section', None, 'tensor'), may hold values from -0.25 to 0.25
- w_down: bfloat16 [2, 2816, 1024], P('section', 'tensor'), may hold values from -0.21875 to 0.21875
Outputs:
- layer_outputs: bfloat16 [2, 8192, 1024], P('section', 'dp')
- input_grads: bfloat16 [2, 8192, 1024], P('section', 'dp')
- grad_query: float32 [2, 1024, 1024], P('section', 'dp', 'tensor')
- grad_latent: float32 [2, 1024, 512], P('section', ('tensor', 'dp'))
- grad_key: float32 [2, 256, 1024], P('section', 'dp', 'tensor')
- grad_value: float32 [2, 256, 1024], P('section', 'dp', 'tensor')
- grad_out: float32 [2, 1024, 1024], P('section', 'tensor', 'dp')
- grad_gains: float32 [2, 2, 1024], P('section', None, ('tensor', 'dp'))
- grad_gate: float32 [2, 1024, 2816], P('section', 'dp', 'tensor')
- grad_up: float32 [2, 1024, 2816], P('section', 'dp', 'tensor')
- grad_down: float32 [2, 2816, 1024], P('section', 'tensor', 'dp')
Inputs may be any that keep to these rules, and one draw needn't show every extreme that they name: lengths[s] counts the live rows of sequence s, the rest of its bucket is padding; some sequence fills its bucket exactly.
All inputs are finite; a program needn't handle non-finite values.
Results may differ from a plain program's by a relative error of at most 0.025.
Values may be sent and summed in bfloat16 or wider, within the bound.
No kernel may reach another device: no remote copies, remote signals or barrier semaphores. Data moves between devices by JAX's collectives and lax.ppermute only.
A program may use at most 256 MiB of HBM per device.

v0:
```python
import jax
import jax.numpy as jnp
from jax import lax
from jax.sharding import PartitionSpec as P

HEADS = 16
HEAD_DIM = 64
KV_HEADS = 2
LATENT = 256
QBLOCK = 512


eps = 1e-06
masked_score = -1e30


def shifted(value, axis, steps):
    count = lax.axis_size(axis)
    initial, last = (max(0, -steps), min(count, count - steps))
    return lax.ppermute(value, axis, [(source, source + steps) for source in range(initial, last)])


def dot_plain(left, right):
    return jnp.dot(left, right, preferred_element_type=jnp.float32)


def dot_right_t(left, right):
    return lax.dot_general(
        left, right, (((1,), (1,)), ((), ())), preferred_element_type=jnp.float32
    )


def dot_left_t(left, right):
    return lax.dot_general(
        left, right, (((0,), (0,)), ((), ())), preferred_element_type=jnp.float32
    )


def inverse_rms(rows):
    return lax.rsqrt(jnp.mean(rows * rows, axis=-1, keepdims=True) + eps)


def share_rows(full):
    share = full.shape[0] // lax.axis_size("tensor")
    return lax.dynamic_slice_in_dim(full, lax.axis_index("tensor") * share, share, 0)


def norm_back(rows, gain, grad_norm):
    scale = inverse_rms(rows)
    weighted = grad_norm * gain
    inner = jnp.mean(weighted * rows, axis=-1, keepdims=True)
    grad_rows = scale * weighted - rows * scale * scale * scale * inner
    grad_gain = jnp.sum(grad_norm * rows * scale, axis=0)
    return (grad_rows, grad_gain)


def score_block(query_block, keys, start, length):
    scores = jnp.einsum(
        "qhd,khd->hqk", query_block, keys, preferred_element_type=jnp.float32
    ) * HEAD_DIM ** (-0.5)
    rows_here = query_block.shape[0]
    query_pos = start + lax.broadcasted_iota(jnp.int32, (rows_here, keys.shape[0]), 0)
    key_pos = lax.broadcasted_iota(jnp.int32, (rows_here, keys.shape[0]), 1)
    allowed = (key_pos <= query_pos) & (key_pos < length)
    return jnp.where(allowed[None], scores, masked_score)


def attention_forward(queries, keys, values, length):
    rows = queries.shape[0]
    outputs = []
    totals = []
    for first in range(0, rows, QBLOCK):
        end = first + QBLOCK
        scores = score_block(queries[first:end], keys[:end], first, length)
        peak = jnp.max(scores, axis=-1, keepdims=True)
        expo = jnp.exp(scores - peak)
        total = jnp.sum(expo, axis=-1, keepdims=True)
        probs = (expo / total).astype(jnp.bfloat16)
        mixed = jnp.einsum("hqk,khd->qhd", probs, values[:end], preferred_element_type=jnp.float32)
        outputs.append(mixed.astype(jnp.bfloat16))
        totals.append(peak + jnp.log(total))
    return (jnp.concatenate(outputs, axis=0), jnp.concatenate(totals, axis=1))


def attention_backward(queries, keys, values, totals, grad_out, length):
    rows = queries.shape[0]
    scale_factor = HEAD_DIM ** (-0.5)
    grad_query_parts = []
    grad_keys = jnp.zeros(keys.shape, jnp.float32)
    grad_values = jnp.zeros(values.shape, jnp.float32)
    for first in range(0, rows, QBLOCK):
        end = first + QBLOCK
        scores = score_block(queries[first:end], keys[:end], first, length)
        probs_full = jnp.exp(scores - totals[:, first:end, :])
        probs = probs_full.astype(jnp.bfloat16)
        grad_block = grad_out[first:end]
        grad_values = grad_values.at[:end].add(
            jnp.einsum("hqk,qhd->khd", probs, grad_block, preferred_element_type=jnp.float32)
        )
        grad_probs = jnp.einsum(
            "qhd,khd->hqk", grad_block, values[:end], preferred_element_type=jnp.float32
        )
        centre = jnp.sum(grad_probs * probs_full, axis=-1, keepdims=True)
        grad_scores = (probs_full * (grad_probs - centre)).astype(jnp.bfloat16)
        grad_query_parts.append(
            jnp.einsum("hqk,khd->qhd", grad_scores, keys[:end], preferred_element_type=jnp.float32)
            * scale_factor
        )
        grad_keys = grad_keys.at[:end].add(
            jnp.einsum(
                "hqk,qhd->khd", grad_scores, queries[first:end], preferred_element_type=jnp.float32
            )
            * scale_factor
        )
    return (jnp.concatenate(grad_query_parts, axis=0), grad_keys, grad_values)


def attend(layer_in, length, params):
    w_query, w_group, w_key, w_value, w_out, gains = params[:6]
    inputs32 = layer_in.astype(jnp.float32)
    normed = (inputs32 * inverse_rms(inputs32) * gains[0]).astype(jnp.bfloat16)
    rows = normed.shape[0]
    queries = dot_plain(normed, w_query).astype(jnp.bfloat16)
    latent = dot_plain(normed, w_group).astype(jnp.bfloat16)
    keys = dot_plain(latent, w_key).astype(jnp.bfloat16)
    values = dot_plain(latent, w_value).astype(jnp.bfloat16)
    split = (rows, -1, HEAD_DIM)
    mixed, totals = attention_forward(
        queries.reshape(split), keys.reshape(split), values.reshape(split), length
    )
    mixed = mixed.reshape(rows, -1)
    branch = lax.psum(dot_plain(mixed, w_out), "tensor")
    return (normed, queries, latent, keys, values, mixed, totals, inputs32 + branch)


def second_norm(residual, gains):
    normed2 = (residual * inverse_rms(residual) * gains[1]).astype(jnp.bfloat16)
    return (normed2, share_rows(residual))


def feed_forward(residual, normed2, length, params):
    w_gate, w_up, w_down = params[6:9]
    gate = dot_plain(normed2, w_gate)
    up = dot_plain(normed2, w_up)
    hidden = (jax.nn.silu(gate) * up).astype(jnp.bfloat16)
    branch = lax.psum(dot_plain(hidden, w_down), "tensor")
    live = (lax.broadcasted_iota(jnp.int32, (residual.shape[0], 1), 0) < length).astype(jnp.float32)
    return (live * (residual + branch)).astype(jnp.bfloat16)


def layer_backward(in_share, bundle, normed2, res_share, grad_out, length, params, group):
    w_query, w_group, w_key, w_value, w_out, gains, w_gate, w_up, w_down = params
    normed, queries, latent, keys, values, mixed, totals = bundle[:7]
    rows = normed2.shape[0]
    share = rows // lax.axis_size("tensor")
    first = lax.axis_index("tensor") * share
    live = (lax.broadcasted_iota(jnp.int32, (rows, 1), 0) < length).astype(jnp.float32)
    grad_res = live * grad_out.astype(jnp.float32)
    gate = dot_plain(normed2, w_gate)
    up = dot_plain(normed2, w_up)
    hidden = (jax.nn.silu(gate) * up).astype(jnp.bfloat16)
    grad_feed = grad_res.astype(jnp.bfloat16)
    grad_w_down = dot_left_t(hidden, grad_feed)
    grad_hidden = dot_right_t(grad_feed, w_down)
    sigma = jax.nn.sigmoid(gate)
    grad_gate = (grad_hidden * up * sigma * (1.0 + gate * (1.0 - sigma))).astype(jnp.bfloat16)
    grad_up = (grad_hidden * gate * sigma).astype(jnp.bfloat16)
    grad_w_gate = dot_left_t(normed2, grad_gate)
    grad_w_up = dot_left_t(normed2, grad_up)
    grad_norm2 = lax.psum_scatter(
        dot_right_t(grad_gate, w_gate) + dot_right_t(grad_up, w_up),
        "tensor",
        scatter_dimension=0,
        tiled=True,
    )
    grad_share, gain_second = norm_back(res_share, gains[1], grad_norm2)
    grad_share = grad_share + lax.dynamic_slice_in_dim(grad_res, first, share, 0)
    grad_branch = lax.all_gather(grad_share.astype(jnp.bfloat16), "tensor", axis=0, tiled=True)
    grad_w_out = dot_left_t(mixed, grad_branch)
    grad_mixed = dot_right_t(grad_branch, w_out).astype(jnp.bfloat16)
    split = (rows, -1, HEAD_DIM)
    grad_q, grad_k, grad_v = attention_backward(
        queries.reshape(split),
        keys.reshape(split),
        values.reshape(split),
        totals,
        grad_mixed.reshape(split),
        length,
    )
    grad_q = grad_q.reshape(rows, -1).astype(jnp.bfloat16)
    grad_k = grad_k.reshape(rows, -1).astype(jnp.bfloat16)
    grad_v = grad_v.reshape(rows, -1).astype(jnp.bfloat16)
    grad_w_query = dot_left_t(normed, grad_q)
    grad_w_key = dot_left_t(latent, grad_k)
    grad_w_value = dot_left_t(latent, grad_v)
    grad_group = (dot_right_t(grad_k, w_key) + dot_right_t(grad_v, w_value)).astype(jnp.bfloat16)
    grad_w_group = dot_left_t(normed, grad_group)
    width = normed.shape[1]
    grad_w_latent = jnp.zeros((width, KV_HEADS * LATENT), jnp.float32)
    grad_w_latent = lax.dynamic_update_slice_in_dim(grad_w_latent, grad_w_group, group * LATENT, 1)
    grad_norm1 = lax.psum_scatter(
        dot_right_t(grad_q, w_query) + dot_right_t(grad_group, w_group),
        "tensor",
        scatter_dimension=0,
        tiled=True,
    )
    grad_in_share, gain_first = norm_back(in_share, gains[0], grad_norm1)
    grad_in_share = grad_in_share + grad_share
    grad_in = lax.all_gather(grad_in_share.astype(jnp.bfloat16), "tensor", axis=0, tiled=True)
    weight_grads = (
        grad_w_query,
        grad_w_key,
        grad_w_value,
        grad_w_out,
        grad_w_gate,
        grad_w_up,
        grad_w_down,
    )
    latent_grads = (grad_w_latent, jnp.stack([gain_first, gain_second]))
    return (grad_in, weight_grads, latent_grads)


def shards(
    inputs,
    cotangent,
    lengths,
    w_query,
    w_latent,
    w_key,
    w_value,
    w_out,
    gains,
    w_gate,
    w_up,
    w_down,
):
    sections = lax.axis_size("section")
    section = lax.axis_index("section")
    micro = lengths.shape[0]
    bucket = inputs.shape[0] // micro
    width = inputs.shape[1]
    steps = micro + sections - 1
    heads_dev = w_query.shape[2] // HEAD_DIM
    group = lax.axis_index("tensor") * heads_dev // (HEADS // KV_HEADS)
    w_group = lax.dynamic_slice_in_dim(w_latent[0], group * LATENT, LATENT, 1)
    params = (
        w_query[0],
        w_group,
        w_key[0],
        w_value[0],
        w_out[0],
        gains[0],
        w_gate[0],
        w_up[0],
        w_down[0],
    )
    feed = inputs.reshape(micro, bucket, width)
    targets = cotangent.reshape(micro, bucket, width)
    saved = jnp.zeros((steps, bucket, width), jnp.bfloat16)
    results = jnp.zeros((steps, bucket, width), jnp.bfloat16)
    kept = ()

    def forward_step(step, carry):
        arriving, saved_in, outputs, stored = carry
        index = jnp.clip(step - section, 0, micro - 1)
        length = lax.dynamic_index_in_dim(lengths, index, 0, False)
        fresh = lax.dynamic_index_in_dim(feed, jnp.minimum(step, micro - 1), 0, False)
        layer_in = jnp.where(section == 0, fresh, arriving)
        bundle = attend(layer_in, length, params)
        normed2, res_share = second_norm(bundle[-1], gains[0])
        layer_out = feed_forward(bundle[-1], normed2, length, params)
        saved_in = lax.dynamic_update_index_in_dim(saved_in, layer_in, step, 0)
        outputs = lax.dynamic_update_index_in_dim(outputs, layer_out, step, 0)
        arriving = shifted(layer_out, "section", 1)
        return (arriving, saved_in, outputs, stored)

    start = (jnp.zeros((bucket, width), jnp.bfloat16), saved, results, kept)
    arriving, saved, results, kept = lax.fori_loop(0, steps, forward_step, start)
    full_shapes = tuple(
        (
            p.shape
            for p in (params[0], params[2], params[3], params[4], params[6], params[7], params[8])
        )
    )
    latent_shapes = ((width, KV_HEADS * LATENT), (2, width))
    weight_sum = tuple((jnp.zeros(s, jnp.float32) for s in full_shapes))
    latent_sum = tuple((jnp.zeros(s, jnp.float32) for s in latent_shapes))

    def backward_step(step, carry):
        arriving, sent, weight_acc, latent_acc = carry
        slot = micro - 1 - step + (sections - 1 - section)
        live = ((slot >= 0) & (slot < micro)).astype(jnp.float32)
        index = jnp.clip(slot, 0, micro - 1)
        length = lax.dynamic_index_in_dim(lengths, index, 0, False)
        layer_in = lax.dynamic_index_in_dim(saved, index + section, 0, False)
        target = lax.dynamic_index_in_dim(targets, index, 0, False)
        grad_out = jnp.where(section == sections - 1, target, arriving)
        bundle = attend(layer_in, length, params)
        normed2, res_share = second_norm(bundle[-1], gains[0])
        in_share = share_rows(layer_in).astype(jnp.float32)
        grad_in, weight_grads, latent_grads = layer_backward(
            in_share, bundle, normed2, res_share, grad_out, length, params, group
        )
        query_g, key_g, value_g, out_g, gate_g, up_g, down_g = tuple(
            (g * live for g in weight_grads)
        )
        latent_g, gain_g = tuple((g * live for g in latent_grads))
        weight_now = (query_g, key_g, value_g, out_g, gate_g, up_g, down_g)
        latent_now = (latent_g, gain_g)
        weight_acc = tuple((a + b for a, b in zip(weight_acc, weight_now)))
        latent_acc = tuple((a + b for a, b in zip(latent_acc, latent_now)))
        sent = lax.dynamic_update_index_in_dim(sent, grad_in, step, 0)
        arriving = shifted(grad_in, "section", -1)
        return (arriving, sent, weight_acc, latent_acc)

    start = (
        jnp.zeros((bucket, width), jnp.bfloat16),
        jnp.zeros((steps, bucket, width), jnp.bfloat16),
        weight_sum,
        latent_sum,
    )
    arriving, sent, weight_sum, latent_sum = lax.fori_loop(0, steps, backward_step, start)
    query_g, key_g, value_g, out_g, gate_g, up_g, down_g = weight_sum
    weight_total = (
        lax.psum_scatter(
            query_g.astype(jnp.bfloat16), "dp", scatter_dimension=0, tiled=True
        ).astype(jnp.float32),
        lax.psum_scatter(key_g.astype(jnp.bfloat16), "dp", scatter_dimension=0, tiled=True).astype(
            jnp.float32
        ),
        lax.psum_scatter(
            value_g.astype(jnp.bfloat16), "dp", scatter_dimension=0, tiled=True
        ).astype(jnp.float32),
        lax.psum_scatter(out_g.astype(jnp.bfloat16), "dp", scatter_dimension=1, tiled=True).astype(
            jnp.float32
        ),
        lax.psum_scatter(gate_g.astype(jnp.bfloat16), "dp", scatter_dimension=0, tiled=True).astype(
            jnp.float32
        ),
        lax.psum_scatter(up_g.astype(jnp.bfloat16), "dp", scatter_dimension=0, tiled=True).astype(
            jnp.float32
        ),
        lax.psum_scatter(down_g.astype(jnp.bfloat16), "dp", scatter_dimension=1, tiled=True).astype(
            jnp.float32
        ),
    )
    latent_g, gain_g = latent_sum
    latent_total = (
        lax.psum_scatter(latent_g, ("tensor", "dp"), scatter_dimension=0, tiled=True),
        lax.psum_scatter(gain_g, ("tensor", "dp"), scatter_dimension=1, tiled=True),
    )
    layer_outputs = lax.dynamic_slice_in_dim(results, section, micro, 0).reshape(
        1, micro * bucket, width
    )
    ordered = lax.dynamic_slice_in_dim(sent, sections - 1 - section, micro, 0)
    input_grads = jnp.flip(ordered, 0).reshape(1, micro * bucket, width)
    query_t, key_t, value_t, out_t, gate_t, up_t, down_t = weight_total
    latent_t, gain_t = latent_total
    return (
        layer_outputs,
        input_grads,
        query_t[None],
        latent_t[None],
        key_t[None],
        value_t[None],
        out_t[None],
        gain_t[None],
        gate_t[None],
        up_t[None],
        down_t[None],
    )


def solution(mesh):
    placed = (
        P("dp", None),
        P("dp", None),
        P("dp"),
        P("section", None, "tensor"),
        P("section", None, None),
        P("section", None, "tensor"),
        P("section", None, "tensor"),
        P("section", "tensor", None),
        P("section", None, None),
        P("section", None, "tensor"),
        P("section", None, "tensor"),
        P("section", "tensor", None),
    )
    return jax.shard_map(
        shards,
        mesh=mesh,
        in_specs=placed,
        out_specs=(
            P("section", "dp", None),
            P("section", "dp", None),
            P("section", "dp", "tensor"),
            P("section", ("tensor", "dp"), None),
            P("section", "dp", "tensor"),
            P("section", "dp", "tensor"),
            P("section", "tensor", "dp"),
            P("section", None, ("tensor", "dp")),
            P("section", "dp", "tensor"),
            P("section", "dp", "tensor"),
            P("section", "tensor", "dp"),
        ),
        check_vma=False,
    )
```

profile of v0, /device:TPU:1, one launch (start us, length us, event | category | flops | bytes accessed | tf_op | source)
XLA Modules:
  0.0 3016.0 jit_solution(5536058625639966148)
XLA Ops:
  22.7 1135.1 %while.77 = (s32[]{:T(128)}, bf16[1024,1024]{1,0:T(8,128)(2,1)}, bf16[3,1024,1024]{2,1,0:T(8,128)(2,1)}, bf16[3,1024,1024]{2,1,0:T(8,128)(2,1)}, s32[]{:T(128)},...) while((s32[]{:T(128)}, bf16[1024,1024]{1,0:T(8,128)(2,1)}, ...), condition=%wide.region_9.10_spmd, body=%wide.region_0.9_spmd.sunk | while | flops 7170039296 | bytes 210224288 | solution.py:278
  45.1 7.4 fusion.374
  52.5 4.9 fusion.375
  61.3 156.6 %all-reduce.6.cloned.1.call-done = f32[1024,1024]{1,0:T(8,128)} async-done(((f32[1024,1024]{1,0:T(8,128)}), f32[1024,1024]{1,0:T(8,128)}) %all-reduce.6.cloned.1.call-update) | async-done | bytes 4194320 | tf_op jit(solution)/shard_map/while/body/eval_jaxpr/psum | solution.py:132
  226.2 9.0 fusion.381
  235.8 153.5 %all-reduce.8.cloned.1.call-done = f32[1024,1024]{1,0:T(8,128)} async-done(((f32[1024,1024]{1,0:T(8,128)}), f32[1024,1024]{1,0:T(8,128)}) %all-reduce.8.cloned.1.call-update) | async-done | bytes 4194320 | tf_op jit(solution)/shard_map/while/body/eval_jaxpr/psum | solution.py:146
  389.3 6.2 bitcast_dynamic-update-slice_fusion.7
  396.8 5.0 collective-permute-done
  425.4 7.4 fusion.374
  441.7 153.7 %all-reduce.6.cloned.1.call-done = f32[1024,1024]{1,0:T(8,128)} async-done(((f32[1024,1024]{1,0:T(8,128)}), f32[1024,1024]{1,0:T(8,128)}) %all-reduce.6.cloned.1.call-update) | async-done | bytes 4194320 | tf_op jit(solution)/shard_map/while/body/eval_jaxpr/psum | solution.py:132
  603.5 9.0 fusion.381
  613.2 153.5 %all-reduce.8.cloned.1.call-done = f32[1024,1024]{1,0:T(8,128)} async-done(((f32[1024,1024]{1,0:T(8,128)}), f32[1024,1024]{1,0:T(8,128)}) %all-reduce.8.cloned.1.call-update) | async-done | bytes 4194320 | tf_op jit(solution)/shard_map/while/body/eval_jaxpr/psum | solution.py:146
  766.6 6.2 bitcast_dynamic-update-slice_fusion.7
  774.1 5.0 collective-permute-done
  802.8 7.4 fusion.374
  819.1 153.7 %all-reduce.6.cloned.1.call-done = f32[1024,1024]{1,0:T(8,128)} async-done(((f32[1024,1024]{1,0:T(8,128)}), f32[1024,1024]{1,0:T(8,128)}) %all-reduce.6.cloned.1.call-update) | async-done | bytes 4194320 | tf_op jit(solution)/shard_map/while/body/eval_jaxpr/psum | solution.py:132
  980.9 9.0 fusion.381
  990.6 153.5 %all-reduce.8.cloned.1.call-done = f32[1024,1024]{1,0:T(8,128)} async-done(((f32[1024,1024]{1,0:T(8,128)}), f32[1024,1024]{1,0:T(8,128)}) %all-reduce.8.cloned.1.call-update) | async-done | bytes 4194320 | tf_op jit(solution)/shard_map/while/body/eval_jaxpr/psum | solution.py:146
  1144.1 6.2 bitcast_dynamic-update-slice_fusion.7
  1151.5 5.0 collective-permute-done
  1162.9 1488.5 %while.78 = (s32[]{:T(128)}, bf16[1024,1024]{1,0:T(8,128)(2,1)}, bf16[3,1024,1024]{2,1,0:T(8,128)(2,1)}, f32[1024,256]{1,0:T(8,128)}, f32[256,256]{1,0:T(8,128)}...) while((s32[]{:T(128)}, bf16[1024,1024]{1,0:T(8,128)(2,1)}, ...), condition=%wide.region_28.29_spmd.clone, body=%wide.region_10.28_spmd.clone.sunk | while | flops 19995561984 | bytes 773144128 | solution.py:322
  1193.0 148.9 %all-reduce.10.cloned.1.call-done = f32[1024,1024]{1,0:T(8,128)} async-done(((f32[1024,1024]{1,0:T(8,128)}), f32[1024,1024]{1,0:T(8,128)}) %all-reduce.10.cloned.1.call-update) | async-done | bytes 4194320 | tf_op jit(solution)/shard_map/while/body/eval_jaxpr/psum | solution.py:132
  1364.4 74.5 %reduce-scatter.32.cloned.1.call-done = f32[256,1024]{1,0:T(8,128)} async-done(((f32[1024,1024]{1,0:T(8,128)}), f32[256,1024]{1,0:T(8,128)}) %reduce-scatter.32.cloned.1.call-update) | async-done | bytes 1048592 | tf_op jit(solution)/shard_map/while/body/eval_jaxpr/reduce_scatter | solution.py:170
  1446.1 44.9 %all-gather.3.cloned.1.call-done = bf16[1024,1024]{1,0:T(8,128)(2,1)} async-done(((bf16[256,1024]{1,0:T(8,128)(2,1)}), bf16[1024,1024]{1,0:T(8,128)(2,1)}) %all-gather.3.cloned.1.call-update) | async-done | bytes 2097168 | tf_op jit(solution)/shard_map/while/body/eval_jaxpr/all_gather | solution.py:178
  1517.7 73.9 %reduce-scatter.34.cloned.1.call-done = f32[256,1024]{1,0:T(8,128)} async-done(((f32[1024,1024]{1,0:T(8,128)}), f32[256,1024]{1,0:T(8,128)}) %reduce-scatter.34.cloned.1.call-update) | async-done | bytes 1048592 | tf_op jit(solution)/shard_map/while/body/eval_jaxpr/reduce_scatter | solution.py:201
  1596.1 5.4 select_add_fusion.8
  1610.9 31.5 %all-gather.5.cloned.1.call-done = bf16[1024,1024]{1,0:T(8,128)(2,1)} async-done(((bf16[256,1024]{1,0:T(8,128)(2,1)}), bf16[1024,1024]{1,0:T(8,128)(2,1)}) %all-gather.5.cloned.1.call-update) | async-done | bytes 2097168 | tf_op jit(solution)/shard_map/while/body/eval_jaxpr/all_gather | solution.py:209
  1688.2 148.6 %all-reduce.10.cloned.1.call-done = f32[1024,1024]{1,0:T(8,128)} async-done(((f32[1024,1024]{1,0:T(8,128)}), f32[1024,1024]{1,0:T(8,128)}) %all-reduce.10.cloned.1.call-update) | async-done | bytes 4194320 | tf_op jit(solution)/shard_map/while/body/eval_jaxpr/psum | solution.py:132
  1859.3 74.5 %reduce-scatter.32.cloned.1.call-done = f32[256,1024]{1,0:T(8,128)} async-done(((f32[1024,1024]{1,0:T(8,128)}), f32[256,1024]{1,0:T(8,128)}) %reduce-scatter.32.cloned.1.call-update) | async-done | bytes 1048592 | tf_op jit(solution)/shard_map/while/body/eval_jaxpr/reduce_scatter | solution.py:170
  1941.2 44.7 %all-gather.3.cloned.1.call-done = bf16[1024,1024]{1,0:T(8,128)(2,1)} async-done(((bf16[256,1024]{1,0:T(8,128)(2,1)}), bf16[1024,1024]{1,0:T(8,128)(2,1)}) %all-gather.3.cloned.1.call-update) | async-done | bytes 2097168 | tf_op jit(solution)/shard_map/while/body/eval_jaxpr/all_gather | solution.py:178
  2012.3 74.1 %reduce-scatter.34.cloned.1.call-done = f32[256,1024]{1,0:T(8,128)} async-done(((f32[1024,1024]{1,0:T(8,128)}), f32[256,1024]{1,0:T(8,128)}) %reduce-scatter.34.cloned.1.call-update) | async-done | bytes 1048592 | tf_op jit(solution)/shard_map/while/body/eval_jaxpr/reduce_scatter | solution.py:201
  2090.9 6.2 select_add_fusion.8
  2106.7 30.8 %all-gather.5.cloned.1.call-done = bf16[1024,1024]{1,0:T(8,128)(2,1)} async-done(((bf16[256,1024]{1,0:T(8,128)(2,1)}), bf16[1024,1024]{1,0:T(8,128)(2,1)}) %all-gather.5.cloned.1.call-update) | async-done | bytes 2097168 | tf_op jit(solution)/shard_map/while/body/eval_jaxpr/all_gather | solution.py:209
  2183.5 148.3 %all-reduce.10.cloned.1.call-done = f32[1024,1024]{1,0:T(8,128)} async-done(((f32[1024,1024]{1,0:T(8,128)}), f32[1024,1024]{1,0:T(8,128)}) %all-reduce.10.cloned.1.call-update) | async-done | bytes 4194320 | tf_op jit(solution)/shard_map/while/body/eval_jaxpr/psum | solution.py:132
  2354.3 74.5 %reduce-scatter.32.cloned.1.call-done = f32[256,1024]{1,0:T(8,128)} async-done(((f32[1024,1024]{1,0:T(8,128)}), f32[256,1024]{1,0:T(8,128)}) %reduce-scatter.32.cloned.1.call-update) | async-done | bytes 1048592 | tf_op jit(solution)/shard_map/while/body/eval_jaxpr/reduce_scatter | solution.py:170
  2435.9 44.9 %all-gather.3.cloned.1.call-done = bf16[1024,1024]{1,0:T(8,128)(2,1)} async-done(((bf16[256,1024]{1,0:T(8,128)(2,1)}), bf16[1024,1024]{1,0:T(8,128)(2,1)}) %all-gather.3.cloned.1.call-update) | async-done | bytes 2097168 | tf_op jit(solution)/shard_map/while/body/eval_jaxpr/all_gather | solution.py:178
  2507.3 74.1 %reduce-scatter.34.cloned.1.call-done = f32[256,1024]{1,0:T(8,128)} async-done(((f32[1024,1024]{1,0:T(8,128)}), f32[256,1024]{1,0:T(8,128)}) %reduce-scatter.34.cloned.1.call-update) | async-done | bytes 1048592 | tf_op jit(solution)/shard_map/while/body/eval_jaxpr/reduce_scatter | solution.py:201
  2585.9 6.2 select_add_fusion.8
  2601.7 30.8 %all-gather.5.cloned.1.call-done = bf16[1024,1024]{1,0:T(8,128)(2,1)} async-done(((bf16[256,1024]{1,0:T(8,128)(2,1)}), bf16[1024,1024]{1,0:T(8,128)(2,1)}) %all-gather.5.cloned.1.call-update) | async-done | bytes 2097168 | tf_op jit(solution)/shard_map/while/body/eval_jaxpr/all_gather | solution.py:209
  2684.1 34.3 %reduce-scatter.30.cloned.1.call-done = f32[64,2]{1,0:T(8,128)} async-done(((f32[1024,2]{1,0:T(8,128)}), f32[64,2]{1,0:T(8,128)}) %reduce-scatter.30.cloned.1.call-update) | async-done | bytes 528
  2719.8 32.1 %reduce-scatter.18.cloned.1.call-done = bf16[64,256]{1,0:T(8,128)(2,1)} async-done(((bf16[256,256]{1,0:T(8,128)(2,1)}), bf16[64,256]{1,0:T(8,128)(2,1)}) %reduce-scatter.18.cloned.1.call-update) | async-done | bytes 32784 | tf_op jit(solution)/shard_map/reduce_scatter | solution.py:328
  2753.3 25.7 reduce-scatter.20.cloned.1.call-done
  2780.4 27.3 reduce-scatter.14.cloned.1.call-done
  2809.4 26.6 reduce-scatter.22.cloned.1.call-done
  2837.5 31.9 %reduce-scatter.24.cloned.1.call-done = bf16[256,704]{0,1:T(8,128)(2,1)} async-done(((bf16[1024,704]{0,1:T(8,128)(2,1)}), bf16[256,704]{0,1:T(8,128)(2,1)}) %reduce-scatter.24.cloned.1.call-update) | async-done | bytes 360464 | tf_op jit(solution)/shard_map/reduce_scatter | solution.py:337
  2871.4 31.0 %reduce-scatter.26.cloned.1.call-done = bf16[256,704]{0,1:T(8,128)(2,1)} async-done(((bf16[1024,704]{0,1:T(8,128)(2,1)}), bf16[256,704]{0,1:T(8,128)(2,1)}) %reduce-scatter.26.cloned.1.call-update) | async-done | bytes 360464 | tf_op jit(solution)/shard_map/reduce_scatter | solution.py:340
  2904.3 31.3 %reduce-scatter.28.cloned.1.call-done = bf16[704,256]{1,0:T(8,128)(2,1)} async-done(((bf16[704,1024]{1,0:T(8,128)(2,1)}), bf16[704,256]{1,0:T(8,128)(2,1)}) %reduce-scatter.28.cloned.1.call-update) | async-done | bytes 360464 | tf_op jit(solution)/shard_map/reduce_scatter | solution.py:343
  2937.5 70.4 %reduce-scatter.16.cloned.1.call-done = f32[64,512]{1,0:T(8,128)} async-done(((f32[1024,512]{1,0:T(8,128)}), f32[64,512]{1,0:T(8,128)}) %reduce-scatter.16.cloned.1.call-update) | async-done | bytes 131088 | tf_op jit(solution)/shard_map/reduce_scatter | solution.py:349
  (903 shorter events, 532.1 us)
Async XLA Ops:
  22.7 195.3 %all-reduce.6.cloned.1.call-start = ((), (), s32[]{:S(2)}) async-start(), calls=%async_computation.20 | async-start | bytes 8388608 | tf_op jit(solution)/shard_map/while/body/eval_jaxpr/psum | solution.py:132
  61.3 328.0 %all-reduce.8.cloned.1.call-start = ((), (), s32[]{:S(2)}) async-start(), calls=%async_computation.21 | async-start | bytes 8388608 | tf_op jit(solution)/shard_map/while/body/eval_jaxpr/psum | solution.py:146
  395.5 6.3 collective-permute-start
  403.0 192.3 %all-reduce.6.cloned.1.call-start = ((), (), s32[]{:S(2)}) async-start(), calls=%async_computation.20 | async-start | bytes 8388608 | tf_op jit(solution)/shard_map/while/body/eval_jaxpr/psum | solution.py:132
  441.6 325.0 %all-reduce.8.cloned.1.call-start = ((), (), s32[]{:S(2)}) async-start(), calls=%async_computation.21 | async-start | bytes 8388608 | tf_op jit(solution)/shard_map/while/body/eval_jaxpr/psum | solution.py:146
  772.9 6.3 collective-permute-start
  780.4 192.3 %all-reduce.6.cloned.1.call-start = ((), (), s32[]{:S(2)}) async-start(), calls=%async_computation.20 | async-start | bytes 8388608 | tf_op jit(solution)/shard_map/while/body/eval_jaxpr/psum | solution.py:132
  819.0 325.0 %all-reduce.8.cloned.1.call-start = ((), (), s32[]{:S(2)}) async-start(), calls=%async_computation.21 | async-start | bytes 8388608 | tf_op jit(solution)/shard_map/while/body/eval_jaxpr/psum | solution.py:146
  1150.2 6.3 collective-permute-start
  1163.3 178.7 %all-reduce.10.cloned.1.call-start = ((), (), s32[]{:S(2)}) async-start(), calls=%async_computation.22 | async-start | bytes 8388608 | tf_op jit(solution)/shard_map/while/body/eval_jaxpr/psum | solution.py:132
  1188.2 250.7 %reduce-scatter.32.cloned.1.call-start = ((), (), s32[]{:S(2)}) async-start(), calls=%async_computation.23 | async-start | bytes 5242880 | tf_op jit(solution)/shard_map/while/body/eval_jaxpr/reduce_scatter | solution.py:170
  1362.9 76.0 %copy-start.64 = (f32[1,1024]{1,0:T(1,128)S(1)}, f32[1,1024]{1,0:T(1,128)}, u32[]{:S(2)}) copy-start(f32[1,1024]{1,0:T(1,128)} %get-tuple-element.1766) | copy-start | bytes 12292 | tf_op jit(solution)/shard_map/while
  1362.9 128.0 %all-gather.3.cloned.1.call-start = ((), (), s32[]{:S(2)}) async-start(), calls=%async_computation.24 | async-start | bytes 2621440 | tf_op jit(solution)/shard_map/while/body/eval_jaxpr/all_gather | solution.py:178
  1444.4 147.2 %reduce-scatter.34.cloned.1.call-start = ((), (), s32[]{:S(2)}) async-start(), calls=%async_computation.25 | async-start | bytes 5242880 | tf_op jit(solution)/shard_map/while/body/eval_jaxpr/reduce_scatter | solution.py:201
  1515.8 75.7 %copy-start.63 = (f32[1,1024]{1,0:T(1,128)S(1)}, f32[1,1024]{1,0:T(1,128)}, u32[]{:S(2)}) copy-start(f32[1,1024]{1,0:T(1,128)} %copy-done.62) | copy-start | bytes 12292 | tf_op jit(solution)/shard_map/while
  1515.9 126.5 %all-gather.5.cloned.1.call-start = ((), (), s32[]{:S(2)}) async-start(), calls=%async_computation.26 | async-start | bytes 2621440 | tf_op jit(solution)/shard_map/while/body/eval_jaxpr/all_gather | solution.py:209
  1606.8 38.3 %copy-start.46 = (f32[256,256]{1,0:T(8,128)S(1)}, f32[256,256]{1,0:T(8,128)}, u32[]{:S(2)}) copy-start(f32[256,256]{1,0:T(8,128)} %get-tuple-element.1885) | copy-start | bytes 786436 | tf_op jit(solution)/shard_map/while
  1610.9 37.7 %copy-start.45 = (f32[256,256]{1,0:T(8,128)}, f32[256,256]{1,0:T(8,128)S(1)}, u32[]{:S(2)}) copy-start(f32[256,256]{1,0:T(8,128)S(1)} %fusion.480) | copy-start | bytes 786436 | tf_op jit(solution)/shard_map/while
  1642.4 14.4 collective-permute-start.1
  1658.4 178.5 %all-reduce.10.cloned.1.call-start = ((), (), s32[]{:S(2)}) async-start(), calls=%async_computation.22 | async-start | bytes 8388608 | tf_op jit(solution)/shard_map/while/body/eval_jaxpr/psum | solution.py:132
  1683.3 250.5 %reduce-scatter.32.cloned.1.call-start = ((), (), s32[]{:S(2)}) async-start(), calls=%async_computation.23 | async-start | bytes 5242880 | tf_op jit(solution)/shard_map/while/body/eval_jaxpr/reduce_scatter | solution.py:170
  1857.8 76.0 %copy-start.64 = (f32[1,1024]{1,0:T(1,128)S(1)}, f32[1,1024]{1,0:T(1,128)}, u32[]{:S(2)}) copy-start(f32[1,1024]{1,0:T(1,128)} %get-tuple-element.1766) | copy-start | bytes 12292 | tf_op jit(solution)/shard_map/while
  1857.8 128.0 %all-gather.3.cloned.1.call-start = ((), (), s32[]{:S(2)}) async-start(), calls=%async_computation.24 | async-start | bytes 2621440 | tf_op jit(solution)/shard_map/while/body/eval_jaxpr/all_gather | solution.py:178
  1939.3 147.2 %reduce-scatter.34.cloned.1.call-start = ((), (), s32[]{:S(2)}) async-start(), calls=%async_computation.25 | async-start | bytes 5242880 | tf_op jit(solution)/shard_map/while/body/eval_jaxpr/reduce_scatter | solution.py:201
  2010.7 75.7 %copy-start.63 = (f32[1,1024]{1,0:T(1,128)S(1)}, f32[1,1024]{1,0:T(1,128)}, u32[]{:S(2)}) copy-start(f32[1,1024]{1,0:T(1,128)} %copy-done.62) | copy-start | bytes 12292 | tf_op jit(solution)/shard_map/while
  2010.8 126.7 %all-gather.5.cloned.1.call-start = ((), (), s32[]{:S(2)}) async-start(), calls=%async_computation.26 | async-start | bytes 2621440 | tf_op jit(solution)/shard_map/while/body/eval_jaxpr/all_gather | solution.py:209
  2102.5 37.7 %copy-start.46 = (f32[256,256]{1,0:T(8,128)S(1)}, f32[256,256]{1,0:T(8,128)}, u32[]{:S(2)}) copy-start(f32[256,256]{1,0:T(8,128)} %get-tuple-element.1885) | copy-start | bytes 786436 | tf_op jit(solution)/shard_map/while
  2137.5 14.5 collective-permute-start.1
  2153.6 178.3 %all-reduce.10.cloned.1.call-start = ((), (), s32[]{:S(2)}) async-start(), calls=%async_computation.22 | async-start | bytes 8388608 | tf_op jit(solution)/shard_map/while/body/eval_jaxpr/psum | solution.py:132
  2178.5 250.3 %reduce-scatter.32.cloned.1.call-start = ((), (), s32[]{:S(2)}) async-start(), calls=%async_computation.23 | async-start | bytes 5242880 | tf_op jit(solution)/shard_map/while/body/eval_jaxpr/reduce_scatter | solution.py:170
  2352.8 76.0 %copy-start.64 = (f32[1,1024]{1,0:T(1,128)S(1)}, f32[1,1024]{1,0:T(1,128)}, u32[]{:S(2)}) copy-start(f32[1,1024]{1,0:T(1,128)} %get-tuple-element.1766) | copy-start | bytes 12292 | tf_op jit(solution)/shard_map/while
  2352.8 128.0 %all-gather.3.cloned.1.call-start = ((), (), s32[]{:S(2)}) async-start(), calls=%async_computation.24 | async-start | bytes 2621440 | tf_op jit(solution)/shard_map/while/body/eval_jaxpr/all_gather | solution.py:178
  2434.3 147.2 %reduce-scatter.34.cloned.1.call-start = ((), (), s32[]{:S(2)}) async-start(), calls=%async_computation.25 | async-start | bytes 5242880 | tf_op jit(solution)/shard_map/while/body/eval_jaxpr/reduce_scatter | solution.py:201
  2505.7 75.7 %copy-start.63 = (f32[1,1024]{1,0:T(1,128)S(1)}, f32[1,1024]{1,0:T(1,128)}, u32[]{:S(2)}) copy-start(f32[1,1024]{1,0:T(1,128)} %copy-done.62) | copy-start | bytes 12292 | tf_op jit(solution)/shard_map/while
  2505.8 126.7 %all-gather.5.cloned.1.call-start = ((), (), s32[]{:S(2)}) async-start(), calls=%async_computation.26 | async-start | bytes 2621440 | tf_op jit(solution)/shard_map/while/body/eval_jaxpr/all_gather | solution.py:209
  2597.5 37.7 %copy-start.46 = (f32[256,256]{1,0:T(8,128)S(1)}, f32[256,256]{1,0:T(8,128)}, u32[]{:S(2)}) copy-start(f32[256,256]{1,0:T(8,128)} %get-tuple-element.1885) | copy-start | bytes 786436 | tf_op jit(solution)/shard_map/while
  2601.7 37.0 %copy-start.45 = (f32[256,256]{1,0:T(8,128)}, f32[256,256]{1,0:T(8,128)S(1)}, u32[]{:S(2)}) copy-start(f32[256,256]{1,0:T(8,128)S(1)} %fusion.480) | copy-start | bytes 786436 | tf_op jit(solution)/shard_map/while
  2632.5 14.3 collective-permute-start.1
  2651.4 67.1 %reduce-scatter.30.cloned.1.call-start = ((), (), s32[]{:S(2)}) async-start(), calls=%async_computation.19 | async-start | bytes 557056
  2653.3 98.7 %reduce-scatter.18.cloned.1.call-start = ((), (), s32[]{:S(2)}) async-start(), calls=%async_computation.13 | async-start | bytes 163840 | tf_op jit(solution)/shard_map/reduce_scatter | solution.py:328
  2654.9 124.1 %reduce-scatter.20.cloned.1.call-start = ((), (), s32[]{:S(2)}) async-start(), calls=%async_computation.14 | async-start | bytes 163840 | tf_op jit(solution)/shard_map/reduce_scatter | solution.py:331
  2656.6 151.1 %reduce-scatter.14.cloned.1.call-start = ((), (), s32[]{:S(2)}) async-start(), calls=%async_computation.11 | async-start | bytes 655360 | tf_op jit(solution)/shard_map/reduce_scatter | solution.py:325
  2658.8 177.1 %reduce-scatter.22.cloned.1.call-start = ((), (), s32[]{:S(2)}) async-start(), calls=%async_computation.15 | async-start | bytes 655360 | tf_op jit(solution)/shard_map/reduce_scatter | solution.py:334
  2659.8 209.7 %reduce-scatter.24.cloned.1.call-start = ((), (), s32[]{:S(2)}) async-start(), calls=%async_computation.16 | async-start | bytes 1802240 | tf_op jit(solution)/shard_map/reduce_scatter | solution.py:337
  2663.0 239.4 %reduce-scatter.26.cloned.1.call-start = ((), (), s32[]{:S(2)}) async-start(), calls=%async_computation.17 | async-start | bytes 1802240 | tf_op jit(solution)/shard_map/reduce_scatter | solution.py:340
  2666.2 269.4 %reduce-scatter.28.cloned.1.call-start = ((), (), s32[]{:S(2)}) async-start(), calls=%async_computation.18 | async-start | bytes 1802240 | tf_op jit(solution)/shard_map/reduce_scatter | solution.py:343
  2669.5 338.4 %reduce-scatter.16.cloned.1.call-start = ((), (), s32[]{:S(2)}) async-start(), calls=%async_computation.12 | async-start | bytes 2228224 | tf_op jit(solution)/shard_map/reduce_scatter | solution.py:349
  2679.4 328.5 %copy-start.1 = (bf16[1,1024,512]{2,1,0:T(8,128)(2,1)S(1)}, bf16[1,1024,512]{2,1,0:T(8,128)(2,1)}, u32[]{:S(2)}) copy-start(bf16[1,1024,512]{2,1,0:T(8,128)(2,1)} %param.32) | copy-start | bytes 3145732
  (233 other events, 1119.8 us)
Sparse Core Ops, SparseCore 0:
  61.4 156.5 all-reduce.5
  235.3 153.9 all-reduce.7
  441.7 153.5 all-reduce.5
  612.6 153.9 all-reduce.7
  819.1 153.5 all-reduce.5
  990.0 153.9 all-reduce.7
  1188.3 153.5 all-reduce.9
  1363.1 75.7 reduce-scatter.31
  1444.5 46.4 all-gather.2
  1516.0 75.4 reduce-scatter.33
  1596.1 46.1 all-gather.4
  1683.4 153.3 all-reduce.9
  1858.0 75.7 reduce-scatter.31
  1939.4 46.3 all-gather.2
  2010.9 75.4 reduce-scatter.33
  2091.0 46.4 all-gather.4
  2178.7 153.1 all-reduce.9
  2353.0 75.7 reduce-scatter.31
  2434.4 46.3 all-gather.2
  2505.9 75.4 reduce-scatter.33
  2586.0 46.4 all-gather.4
Sparse Core Ops, SparseCore 1:
  2654.7 63.7 reduce-scatter.29
  2721.3 30.6 reduce-scatter.17
  2755.1 23.8 reduce-scatter.19
  2782.7 25.0 reduce-scatter.13
  2811.1 24.7 reduce-scatter.21
  2839.2 30.3 reduce-scatter.23
  2872.3 30.0 reduce-scatter.25
  2905.5 30.1 reduce-scatter.27
  2938.3 69.5 reduce-scatter.15
where the time goes:
time: 3050 us; the launch traced here: 3020 us
  waiting for transfers between devices  2370 us (78%)
  matrix products  310 us (10%)
  other arithmetic  183 us (6%)
  local copies, waits for them, and re-layouts  113 us (4%)
    psum x6, waiting for transfers between devices, attend(): branch = lax.psum(dot_plain(mixed, w_out), 'tensor')  910 us
    psum x3, waiting for transfers between devices, feed_forward(): branch = lax.psum(dot_plain(hidden, w_down), 'tensor')  460 us
    reduce_scatter x3, waiting for transfers between devices, layer_backward(): lax.psum_scatter(dot_right_t(grad_gate, w_gate) + dot_right_t(grad_up, w_...  224 us
    reduce_scatter x3, waiting for transfers between devices, layer_backward(): lax.psum_scatter(dot_right_t(grad_q, w_query) + dot_right_t(grad_group, w...  222 us
    all_gather x3, waiting for transfers between devices, layer_backward(): lax.all_gather(grad_share.astype(jnp.bfloat16), 'tensor', axis=0, tiled=T...  134 us
    dot_general x42, matrix products, dot_plain(): return jnp.dot(left, right, preferred_element_type=jnp.float32)  94.3 us
    all_gather x3, waiting for transfers between devices, layer_backward(): lax.all_gather(grad_in_share.astype(jnp.bfloat16), 'tensor', axis=0, tile...  93 us
    reduce_scatter x1, waiting for transfers between devices, shards(): lax.psum_scatter(latent_g, ('tensor', 'dp'), scatter_dimension=0, tiled=T...  70.4 us
  transfers between devices with their start and end apart: 36, of which 33 were waited for; matrix products, arithmetic and copies ran while one was open for 4% of the time, Pallas kernels for 0%

commit v1 on v0

v1 whole, which is shorter than its diff:
```python
import functools

import jax
import jax.numpy as jnp
from jax import lax
from jax.experimental import pallas as pl
from jax.experimental.pallas import tpu as pltpu
from jax.sharding import PartitionSpec as P

HEAD_DIM = 64
eps = 1e-06
masked_score = -1e30
f32 = jnp.float32
bf16 = jnp.bfloat16


def dot_nn(left, right):
    return lax.dot_general(left, right, (((1,), (0,)), ((), ())), preferred_element_type=f32)


def dot_nt(left, right):
    return lax.dot_general(left, right, (((1,), (1,)), ((), ())), preferred_element_type=f32)


def dot_tn(left, right):
    return lax.dot_general(left, right, (((0,), (0,)), ((), ())), preferred_element_type=f32)


def core_swap(value):
    return lax.ppermute(value, "section", [(0, 1), (1, 0)])


def z_swap(value, step):
    count = lax.axis_size("tensor")
    return lax.ppermute(value, "tensor", [(i, i ^ step) for i in range(count)])


def plane_swap(value, bit):
    count = lax.axis_size("dp")
    return lax.ppermute(value, "dp", [(i, i ^ bit) for i in range(count)])


def tie(first, *others):
    return lax.optimization_barrier((first,) + others)[0]


def bits_of(count):
    return [1 << i for i in range(count.bit_length() - 1)]


def plane_gather(piece):
    count = lax.axis_size("dp")
    half = piece.shape[-2] // 2
    have = {0: (piece,)}
    for key in sorted(range(1, count), key=lambda k: (k.bit_count(), k)):
        bits = [b for b in bits_of(count) if key & b]
        if len(bits) == 1:
            have[key] = (plane_swap(piece, key),)
            continue
        parts = []
        for at, bit in enumerate((bits[-1], bits[0])):
            source = have[key ^ bit]
            part = source[at] if len(source) == 2 else lax.slice_in_dim(source[0], at * half, (at + 1) * half, axis=-2)
            parts.append(plane_swap(part, bit))
        have[key] = tuple(parts)
    return jnp.stack([jnp.concatenate(have[k], axis=-2) if len(have[k]) > 1 else have[k][0] for k in range(count)])


class Scatter:
    def __init__(self, keep, send):
        self.parts = [keep, core_swap(send)]

    def split(self):
        count = lax.axis_size("dp")
        order = bits_of(count)
        rows = self.parts[0].shape[2]
        self.halves = []
        for at, way in enumerate((order, order[::-1])):
            terms = [lax.slice_in_dim(p, at * (rows // 2), (at + 1) * (rows // 2), axis=2) for p in self.parts]
            terms = [
                t.reshape(t.shape[:1] + (2,) * len(order) + t.shape[2:]) for t in terms
            ]
            self.halves.append((terms, list(way), sorted(order, reverse=True)))

    def step(self):
        me = lax.axis_index("dp")
        after = []
        for terms, way, axes in self.halves:
            bit = way[0]
            axis = 1 + axes.index(bit)
            mine = (me // bit) % 2
            keep = sum(lax.dynamic_index_in_dim(t, mine, axis, False) for t in terms)
            send = sum(lax.dynamic_index_in_dim(t, 1 - mine, axis, False) for t in terms)
            after.append(([keep, plane_swap(send, bit)], way[1:], [a for a in axes if a != bit]))
        self.halves = after

    def leaves(self):
        return [t for terms, _, _ in self.halves for t in terms]

    def result(self):
        return jnp.concatenate([sum(terms) for terms, _, _ in self.halves], axis=1)


def by_plane(values, flip_of):
    count = values.shape[0]
    for bit in bits_of(count):
        order = [k ^ bit for k in range(count)]
        flipped = jnp.stack([values[k] for k in order])
        values = jnp.where((flip_of // bit) % 2 == 1, flipped, values)
    return values


def inverse_rms(rows):
    return lax.rsqrt(jnp.mean(rows * rows, axis=-1, keepdims=True) + eps)


def norm_back(rows, gain, grad_norm):
    scale = inverse_rms(rows)
    weighted = grad_norm * gain
    inner = jnp.mean(weighted * rows, axis=-1, keepdims=True)
    grad_rows = scale * weighted - rows * scale * scale * scale * inner
    grad_gain = jnp.sum(grad_norm * rows * scale, axis=0)
    return (grad_rows, grad_gain)


LENGTH, FIRST, CORE, MEMBER, RANK = range(5)


def kernel_call(kernel, info, arrays, grid, in_specs, out_specs, out_shape, scratch, name, flops, transcendentals=0):
    size = sum(a.size * a.dtype.itemsize for a in arrays)
    size += sum(o.size * o.dtype.itemsize for o in out_shape)
    return pl.pallas_call(
        kernel,
        grid_spec=pltpu.PrefetchScalarGridSpec(
            num_scalar_prefetch=1,
            grid=grid,
            in_specs=in_specs,
            out_specs=out_specs,
            scratch_shapes=scratch,
        ),
        out_shape=out_shape,
        compiler_params=pltpu.CompilerParams(
            dimension_semantics=("arbitrary",) * len(grid), vmem_limit_bytes=56 * 1024 * 1024
        ),
        cost_estimate=pl.CostEstimate(flops=flops, bytes_accessed=size, transcendentals=transcendentals),
        name=name,
    )(info, *arrays)


def whole(array):
    shape = array.shape
    return pl.BlockSpec(shape, lambda i, info: (0,) * len(shape))


def lead(array):
    shape = array.shape[1:]
    return pl.BlockSpec((1,) + shape, lambda i, info: (i,) + (0,) * len(shape))


def like(shape, dtype):
    return jax.ShapeDtypeStruct(shape, dtype)


def place_pack(info, step, own, near, other, pack):
    members, _, rows, cols = near.shape

    @pl.when(step == 0)
    def _():
        pack[...] = own[...]

    @pl.when(step > 0)
    def _():
        for key in range(members):
            for source, core in ((near, info[CORE]), (other, 1 - info[CORE])):
                at = (core * members + (info[MEMBER] ^ key)) * rows
                pack[pl.ds(pl.multiple_of(at, 16), rows), :] = source[key, 0]


def fill_bias(info, bias):
    keys, rows = bias.shape
    key_pos = lax.broadcasted_iota(jnp.int32, (keys, rows), 0)
    query_pos = lax.broadcasted_iota(jnp.int32, (keys, rows), 1) + info[FIRST]
    allowed = (key_pos <= query_pos) & (key_pos < info[LENGTH])
    bias[...] = jnp.where(allowed, 0.0, masked_score)


def attend_kernel(
    info, x, normed, lat0, lat1, lat2, lat3, own, near, other, gain, mixed_out, lse_out, lat_out, residual, normed2, bias, pack
):
    step = pl.program_id(0)
    rows, width = normed.shape
    latent = lat_out.shape[2]
    cols = pack.shape[1]

    @pl.when(step == 0)
    def _():
        fill_bias(info, bias)
        residual[...] = x[...].astype(f32)
        for key, piece in enumerate((lat0, lat1, lat2, lat3)):
            at = pl.multiple_of((info[RANK] ^ key) * rows, 16)
            for group in range(2):
                lat_out[group, pl.ds(at, rows), :] = piece[:, group * latent : (group + 1) * latent]

    place_pack(info, step, own, near, other, pack)
    w_query = pack[0:width]
    w_key = pack[width : width + latent]
    w_value = pack[width + latent : width + 2 * latent]
    w_out_t = pack[width + 2 * latent :]
    here = lat_out[step // 2]
    query = dot_nn(normed[...], w_query).astype(bf16) * bf16(HEAD_DIM**-0.5)
    keys = dot_nn(here, w_key).astype(bf16)
    values_t = dot_nn(here, w_value).astype(bf16).T
    lane_head = lax.broadcasted_iota(jnp.int32, (rows, cols), 1) // HEAD_DIM
    mixed_parts = []
    for head in range(cols // HEAD_DIM):
        query_here = jnp.where(lane_head == head, query, bf16(0))
        scores = dot_nt(keys, query_here) + bias[...]
        peak = jnp.max(scores, axis=0, keepdims=True)
        expo = jnp.exp(scores - peak)
        total = jnp.sum(expo, axis=0, keepdims=True)
        part = dot_nn(values_t[head * HEAD_DIM : (head + 1) * HEAD_DIM], expo.astype(bf16))
        mixed_parts.append(part * (1.0 / total))
        lse_out[0, head : head + 1, :] = peak + jnp.log(total)
    mixed = jnp.concatenate(mixed_parts, axis=0).T.astype(bf16)
    mixed_out[0] = mixed
    residual[...] += dot_nt(mixed, w_out_t)

    @pl.when(step == pl.num_programs(0) - 1)
    def _():
        full = residual[...]
        normed2[...] = (full * inverse_rms(full) * gain[...]).astype(bf16)


def attend_back_kernel(
    info, grad_branch, normed, lat, own, near, other, mixed_in, lse_in, grad_norm, grad_lat, keep, send, bias, pack
):
    step = pl.program_id(0)
    rows, width = normed.shape
    keys_count, latent = lat.shape[1:]
    cols = pack.shape[1]
    scale = HEAD_DIM**-0.5
    pieces = keep.shape[1]

    @pl.when(step == 0)
    def _():
        fill_bias(info, bias)
        grad_norm[...] = jnp.zeros_like(grad_norm)

    @pl.when(step % 2 == 0)
    def _():
        grad_lat[...] = jnp.zeros_like(grad_lat)

    place_pack(info, step, own, near, other, pack)
    w_query = pack[0:width]
    w_key = pack[width : width + latent]
    w_value = pack[width + latent : width + 2 * latent]
    w_out_t = pack[width + 2 * latent :]
    here = lat[0]
    query = dot_nn(normed[...], w_query).astype(bf16) * bf16(scale)
    keys = dot_nn(here, w_key).astype(bf16)
    keys_t = keys.T
    values = dot_nn(here, w_value).astype(bf16)
    mixed = mixed_in[0]
    grad_mixed = dot_nn(grad_branch[...], w_out_t).astype(bf16)
    centre = (grad_mixed.astype(f32) * mixed.astype(f32)).T
    lane_head = lax.broadcasted_iota(jnp.int32, (rows, cols), 1) // HEAD_DIM
    grad_keys = jnp.zeros((keys_count, cols), f32)
    grad_values = jnp.zeros((keys_count, cols), f32)
    grad_query_parts = []
    for head in range(cols // HEAD_DIM):
        mine = slice(head * HEAD_DIM, (head + 1) * HEAD_DIM)
        query_here = jnp.where(lane_head == head, query, bf16(0))
        grad_here = jnp.where(lane_head == head, grad_mixed, bf16(0))
        scores = dot_nt(keys, query_here) + bias[...]
        probs = jnp.exp(scores - lse_in[0, head : head + 1, :])
        grad_probs = dot_nt(values, grad_here)
        inner = jnp.sum(centre[mine], axis=0, keepdims=True)
        grad_scores = (probs * (grad_probs - inner)).astype(bf16)
        grad_values += dot_nn(probs.astype(bf16), grad_here)
        grad_keys += dot_nn(grad_scores, query_here)
        grad_query_parts.append(dot_nn(keys_t[mine], grad_scores) * scale)
    grad_keys = grad_keys.astype(bf16)
    grad_values = grad_values.astype(bf16)
    grad_query = jnp.concatenate(grad_query_parts, axis=0).T.astype(bf16)
    grad_norm[...] += dot_nt(grad_query, w_query)
    grad_lat[0] += dot_nt(grad_keys, w_key) + dot_nt(grad_values, w_value)
    halves = (
        (dot_tn(normed[...], grad_query), dot_tn(here, grad_keys)),
        (dot_tn(here, grad_values), dot_tn(grad_branch[...], mixed)),
    )
    for half, results in enumerate(halves):
        for out, wanted in ((keep, half), (send, 1 - half)):

            @pl.when(info[CORE] == wanted)
            def _(out=out, results=results):
                at = 0
                for result in results:
                    size = result.shape[0] // pieces
                    for piece in range(pieces):
                        out[0, piece, at : at + size, :] = result[piece * size : (piece + 1) * size].astype(bf16)
                    at += size


def attend_call(info, x, normed, lats, own, near, other, gain):
    rows, width = normed.shape
    members, others, _, cols = near.shape
    sets = others + 1
    latent = lats[0].shape[1] // 2
    keys = rows * 4
    heads = cols // HEAD_DIM
    piece = pl.BlockSpec((members, 1) + near.shape[2:], lambda i, info: (0, jnp.maximum(i - 1, 0), 0, 0))
    outs = [
        like((sets, rows, cols), bf16),
        like((sets, heads, rows), f32),
        like((2, keys, latent), bf16),
        like((rows, width), f32),
        like((rows, width), bf16),
    ]
    return kernel_call(
        attend_kernel,
        info,
        (x, normed, *lats, own, near, other, gain),
        (sets,),
        [whole(x), whole(normed)] + [whole(v) for v in lats] + [whole(own), piece, piece, whole(gain)],
        [lead(outs[0]), lead(outs[1])] + [whole(o) for o in outs[2:]],
        outs,
        [pltpu.VMEM((keys, rows), f32), pltpu.VMEM(own.shape, bf16)],
        "attend",
        2 * sets * rows * (2 * keys * cols * heads + width * cols * 2) + 4 * sets * keys * latent * cols,
        sets * heads * keys * rows,
    )


def attend_back_call(info, grad_branch, normed, lat, own, near, other, mixed, lse):
    rows, width = normed.shape
    members, others, piece_rows, cols = near.shape
    sets = others + 1
    keys, latent = lat.shape[1:]
    heads = cols // HEAD_DIM
    piece = pl.BlockSpec((members, 1) + near.shape[2:], lambda i, info: (0, jnp.maximum(i - 1, 0), 0, 0))
    group = pl.BlockSpec((1, keys, latent), lambda i, info: (i // 2, 0, 0))
    outs = [
        like((rows, width), f32),
        like((2, keys, latent), f32),
        like((sets, members, piece_rows, cols), bf16),
        like((sets, members, piece_rows, cols), bf16),
    ]
    return kernel_call(
        attend_back_kernel,
        info,
        (grad_branch, normed, lat, own, near, other, mixed, lse),
        (sets,),
        [whole(grad_branch), whole(normed), group, whole(own), piece, piece, lead(mixed), lead(lse)],
        [whole(outs[0]), group, lead(outs[2]), lead(outs[3])],
        outs,
        [pltpu.VMEM((keys, rows), f32), pltpu.VMEM(own.shape, bf16)],
        "attend_back",
        2 * sets * rows * (5 * keys * cols * heads + width * cols * 5) + 16 * sets * keys * latent * cols,
        sets * heads * keys * rows,
    )


def place_feed(info, step, own, near, other, weights):
    members, _, rows, _ = near.shape

    @pl.when(step == 0)
    def _():
        weights[...] = own[...]

    @pl.when(step > 0)
    def _():
        for key in range(members):
            for source, core in ((near, info[CORE]), (other, 1 - info[CORE])):
                at = (core * members + (info[MEMBER] ^ key)) * rows
                weights[:, pl.ds(pl.multiple_of(at, 16), rows), :] = source[key]


def feed_kernel(info, value, own, near, other, total_out, saved, weights, total):
    step = pl.program_id(0)
    place_feed(info, step, own, near, other, weights)
    gate = dot_nn(value[...], weights[0])
    up = dot_nn(value[...], weights[1])
    saved[0, 0] = gate.astype(bf16)
    saved[0, 1] = up.astype(bf16)
    hidden = (gate * jax.nn.sigmoid(gate) * up).astype(bf16)
    part = dot_nt(hidden, weights[2])

    @pl.when(step == 0)
    def _():
        total[...] = part

    @pl.when(step > 0)
    def _():
        total_out[...] = (total[...] + part).astype(total_out.dtype)


def feed_back_kernel(info, value, own, near, other, saved, total_out, rights, weights, total):
    step = pl.program_id(0)
    place_feed(info, step, own, near, other, weights)
    grad_hidden = dot_nn(value[...], weights[2])
    gate = saved[0, 0].astype(f32)
    up = saved[0, 1].astype(f32)
    sigma = jax.nn.sigmoid(gate)
    silu = gate * sigma
    grad_gate = (grad_hidden * up * sigma * (1.0 + gate * (1.0 - sigma))).astype(bf16)
    grad_up = (grad_hidden * silu).astype(bf16)
    rights[0, 0] = grad_gate
    rights[0, 1] = grad_up
    rights[0, 2] = (silu * up).astype(bf16)
    part = dot_nt(grad_gate, weights[0]) + dot_nt(grad_up, weights[1])

    @pl.when(step == 0)
    def _():
        total[...] = part

    @pl.when(step > 0)
    def _():
        total_out[...] = (total[...] + part).astype(total_out.dtype)


def feed_weights_kernel(info, normed2, far_normed2, grad, far_grad, rights, far_rights, keep, send, lefts):
    step = pl.program_id(0)
    rows = normed2.shape[0]
    pieces, size = keep.shape[2:4]

    @pl.when(step == 0)
    def _():
        for at, (near, far) in enumerate(((normed2, far_normed2), (grad, far_grad))):
            lefts[at, :, 0:rows] = near[...].T
            lefts[at, :, rows : 2 * rows] = far[...].T

    for kind in range(3):
        right = jnp.concatenate([rights[0, kind], far_rights[0, kind]], axis=0)
        for out, half in ((keep, info[CORE]), (send, 1 - info[CORE])):
            for piece in range(pieces):
                at = pl.multiple_of((2 * piece + half) * size, 16)
                left = lefts[kind // 2, pl.ds(at, size), :]
                out[0, kind, piece] = dot_nn(left, right).astype(bf16)


def feed_call(info, value, own, near, other, dtype):
    rows, width = value.shape
    cols = own.shape[2]
    outs = [like((rows, width), dtype), like((2, 2, rows, cols), bf16)]
    return kernel_call(
        feed_kernel,
        info,
        (value, own, near, other),
        (2,),
        [whole(value), whole(own), whole(near), whole(other)],
        [whole(outs[0]), lead(outs[1])],
        outs,
        [pltpu.VMEM(own.shape, bf16), pltpu.VMEM((rows, width), f32)],
        "feed",
        2 * 2 * 3 * rows * width * cols,
    )


def feed_back_call(info, value, own, near, other, saved, dtype):
    rows, width = value.shape
    cols = own.shape[2]
    outs = [like((rows, width), dtype), like((2, 3, rows, cols), bf16)]
    return kernel_call(
        feed_back_kernel,
        info,
        (value, own, near, other, saved),
        (2,),
        [whole(value), whole(own), whole(near), whole(other), lead(saved)],
        [whole(outs[0]), lead(outs[1])],
        outs,
        [pltpu.VMEM(own.shape, bf16), pltpu.VMEM((rows, width), f32)],
        "feed_back",
        2 * 2 * 3 * rows * width * cols,
    )


def feed_weights_call(info, values, rights, pieces):
    rows, width = values[0].shape
    cols = rights[0].shape[3]
    outs = [like((2, 3, pieces, width // pieces // 2, cols), bf16)] * 2
    return kernel_call(
        feed_weights_kernel,
        info,
        (*values, *rights),
        (2,),
        [whole(v) for v in values] + [lead(r) for r in rights],
        [lead(o) for o in outs],
        outs,
        [pltpu.VMEM((2, width, 2 * rows), bf16)],
        "feed_weights",
        2 * 2 * 3 * 2 * rows * width * cols,
    )


def shards(inputs, cotangent, lengths, w_query, w_latent, w_key, w_value, w_out, gains, w_gate, w_up, w_down):
    core = lax.axis_index("section")
    z = lax.axis_index("tensor")
    d = lax.axis_index("dp")
    planes = lax.axis_size("tensor")
    dp = lax.axis_size("dp")
    seqs = lengths.shape[0]
    bucket = inputs.shape[0] // seqs
    width = inputs.shape[1]
    layers = 2
    per_seq = planes // seqs * 2
    rows = bucket // per_seq
    rank = (z % (planes // seqs)) * 2 + core
    seq = z // (planes // seqs)
    first = rank * rows
    length = lax.dynamic_index_in_dim(lengths, seq, 0, False)
    info = jnp.stack([length, first, core, d, rank]).astype(jnp.int32)
    live = (lax.broadcasted_iota(jnp.int32, (rows, 1), 0) + first < length).astype(f32)
    row_at = seq * bucket + first
    own_in = lax.dynamic_slice_in_dim(inputs, row_at, rows, 0)
    own_target = lax.dynamic_slice_in_dim(cotangent, row_at, rows, 0)
    latent = w_latent.shape[2] // 2
    far_group = z // (planes // 2)

    pack_own = jnp.concatenate([w_query[0], w_key[0], w_value[0], w_out[0].T], axis=0)
    feed_own = jnp.stack([w_gate[0], w_up[0], w_down[0].T])

    def both(value):
        other = core_swap(value)
        return [jnp.where(core == layer, value, other) for layer in range(layers)]

    packs = both(pack_own)
    latents_w = both(w_latent[0])
    gains_all = both(gains[0])
    feeds = both(feed_own)
    pack_rows, cols = pack_own.shape
    hidden_cols = feed_own.shape[2]

    def gather_pack(own):
        lanes = own.reshape(2, dp, pack_rows // 2 // dp, cols)
        piece = lax.dynamic_slice(lanes, (core, d, 0, 0), (1, 1) + lanes.shape[2:])[0, 0]
        near = plane_gather(jnp.stack([z_swap(piece, step) for step in range(1, planes)]))
        return near, core_swap(near)

    def gather_feed(own):
        lanes = own.reshape(3, 2, dp, width // 2 // dp, hidden_cols)
        piece = lax.dynamic_slice(lanes, (0, core, d, 0, 0), (3, 1, 1) + lanes.shape[3:])[:, 0, 0]
        near = plane_gather(z_swap(piece, planes // 2))
        return near, core_swap(near)

    def by_group(value):
        return by_plane(value, far_group)

    def forward(layer, x, pack, feed_w):
        gain = gains_all[layer]
        x32 = x.astype(f32)
        normed = (x32 * inverse_rms(x32) * gain[0]).astype(bf16)
        own_lat = dot_nn(normed, latents_w[layer]).astype(bf16)
        own_lat = jnp.where(
            far_group == 1, jnp.concatenate([own_lat[:, latent:], own_lat[:, :latent]], axis=1), own_lat
        )
        far_lat = z_swap(own_lat, 1)
        lats = (own_lat, core_swap(own_lat), far_lat, core_swap(far_lat))
        mixed, lse, lat, residual, normed2 = attend_call(info, x, normed, lats, *pack, gain[1][None])
        far_normed2 = z_swap(normed2, 1)
        part, saved = feed_call(info, normed2, *feed_w, f32)
        far_part, far_saved = feed_call(info, far_normed2, *feed_w, bf16)
        feed = part + z_swap(far_part, 1).astype(f32)
        out = (live * (residual + feed)).astype(bf16)
        return out, (x, normed, lat, mixed, lse, residual, normed2, far_normed2, saved, far_saved)

    def gather_rows(layer, own):
        other = lax.ppermute(own, "section", [(1 - layer, layer)])
        chip = jnp.concatenate([own, other] if layer == 0 else [other, own], axis=0)
        found = [chip]
        for step in range(1, planes):
            pairs = [(layer * planes + i, layer * planes + (i ^ step)) for i in range(planes)]
            found.append(lax.ppermute(chip, ("section", "tensor"), pairs))
        return found

    def finish_rows(firsts, seconds):
        chosen = jnp.stack([jnp.where(core == 0, a, b) for a, b in zip(firsts, seconds)])
        return by_plane(chosen, z).reshape(planes * 2 * rows, width)

    def finish_core(firsts, seconds):
        mine = jnp.where(core == 0, firsts, seconds)
        other = core_swap(jnp.where(core == 0, seconds, firsts))
        return jnp.where(core == 0, jnp.stack([mine, other]), jnp.stack([other, mine]))

    def backward(layer, grad_out, stored, pack, feed_w, before):
        x, normed, lat, mixed, lse, residual, normed2, far_normed2, saved, far_saved = stored
        gain = gains_all[layer]
        grad_res = live * grad_out.astype(f32)
        grad_feed = grad_res.astype(bf16)
        far_feed = z_swap(grad_feed, 1)
        part, rights = feed_back_call(info, grad_feed, *feed_w, saved, f32)
        if before:
            far_feed = tie(far_feed, *before.pop(0)())
        far_part, far_rights = feed_back_call(info, far_feed, *feed_w, far_saved, bf16)
        back = z_swap(far_part, 1)
        keep, send = feed_weights_call(
            info, (normed2, far_normed2, grad_feed, far_feed), (rights, far_rights), dp
        )
        feed_shape = (6, dp) + keep.shape[3:]
        feed_sum = Scatter(keep.reshape(feed_shape), send.reshape(feed_shape))
        back = tie(back, keep)
        grad_norm2 = part + back.astype(f32)
        grad_residual, gain_second = norm_back(residual, gain[1], grad_norm2)
        grad_residual = grad_residual + grad_res
        grad_branch = grad_residual.astype(bf16)
        feed_sum.split()
        feed_sum.step()
        grad_branch = tie(grad_branch, *feed_sum.leaves()[::2])
        if before:
            grad_branch = tie(grad_branch, *before.pop(0)())

        grad_norm, grad_lat, keep, send = attend_back_call(
            info, grad_branch, normed, lat, *pack, mixed, lse
        )
        pack_sum = Scatter(keep, send)
        grad_lat = grad_lat.astype(bf16).reshape(2, per_seq // 2, 2, rows, latent)
        lat_sum = lax.dynamic_index_in_dim(grad_lat, core, 2, False) + core_swap(
            lax.dynamic_index_in_dim(grad_lat, 1 - core, 2, False)
        )
        near = rank // 2
        lat_own = lax.dynamic_index_in_dim(lat_sum, near, 1, False) + z_swap(
            lax.dynamic_index_in_dim(lat_sum, 1 - near, 1, False), 1
        )
        lat_own = by_group(lat_own)
        lat_own = jnp.concatenate([lat_own[0], lat_own[1]], axis=1)
        grad_norm = grad_norm + dot_nt(lat_own, latents_w[layer])
        grad_x, gain_first = norm_back(x.astype(f32), gain[0], grad_norm)
        grad_x = (grad_x + grad_residual).astype(bf16)

        lat_w = dot_tn(normed, lat_own).astype(bf16).reshape(planes, dp, width // planes // dp * 2, latent)
        gain_g = jnp.stack([gain_first, gain_second]).astype(bf16)
        gain_g = gain_g.reshape(2, planes, dp, -1).transpose(1, 2, 0, 3).reshape(planes, dp, 1, -1)
        gain_g = jnp.pad(gain_g, ((0, 0), (0, 0), (0, 31), (0, latent - gain_g.shape[3])))
        small = by_plane(jnp.concatenate([lat_w, gain_g], axis=2), z)
        half = small.shape[2] // 2
        small_keep = lax.dynamic_slice_in_dim(small, core * half, half, 2)
        small_send = lax.dynamic_slice_in_dim(small, (1 - core) * half, half, 2)
        small_sum = small_keep + core_swap(small_send)

        def feed_rest():
            while feed_sum.halves[0][1]:
                feed_sum.step()
            return feed_sum.leaves()

        def feed_far():
            sums = feed_sum.result()
            feed_sum.final = sums[:3] + z_swap(sums[3:], planes // 2)
            return [feed_sum.final]

        def pack_first():
            pack_sum.parts = [jnp.concatenate([sum(pack_sum.parts), small_sum], axis=2)]
            pack_sum.split()
            pack_sum.step()
            return pack_sum.leaves()

        def pack_rest():
            while pack_sum.halves[0][1]:
                pack_sum.step()
            return pack_sum.leaves()

        def pack_far():
            sums = pack_sum.result()
            pair = sums[0::2] + z_swap(sums[1::2], 1)
            pack_sum.final = pair[0] + z_swap(pair[1], 2)
            return [pack_sum.final]

        return grad_x, feed_sum, pack_sum, [feed_rest, pack_first, feed_far, pack_rest, pack_far]

    pack0 = (packs[0],) + gather_pack(packs[0])
    feed0 = (feeds[0],) + gather_feed(feeds[0])
    pack1 = (packs[1],) + gather_pack(packs[1])
    feed1 = (feeds[1],) + gather_feed(feeds[1])
    out0, stored0 = forward(0, own_in, pack0, feed0)
    out1, stored1 = forward(1, out0, pack1, feed1)
    outs0, outs1 = gather_rows(0, out0), gather_rows(1, out1)
    grad1, feed_sum1, pack_sum1, rest = backward(1, own_target, stored1, pack1, feed1, [])
    grads1 = gather_rows(1, grad1)
    grad0, feed_sum0, pack_sum0, last = backward(0, grad1, stored0, pack0, feed0, rest)
    grads0 = gather_rows(0, grad0)
    for step in rest + last:
        step()
    layer_outputs = finish_rows(outs0, outs1)
    input_grads = finish_rows(grads0, grads1)

    feed_total = finish_core(feed_sum0.final, feed_sum1.final).astype(f32)
    gate_t, up_t, down_t = jnp.moveaxis(feed_total, 0, 1).reshape(3, width // dp, hidden_cols)
    halves = finish_core(pack_sum0.final, pack_sum1.final).astype(f32)
    main = pack_rows // dp // 2
    query_t, key_t = halves[0, : width // dp], halves[0, width // dp : main]
    value_t, out_t = halves[1, : latent // dp], halves[1, latent // dp : main]
    small = halves[:, main:].reshape(-1, latent)
    lat_rows = width // planes // dp * 2
    lat_t = small[:lat_rows].reshape(lat_rows // 2, 2 * latent)
    gain_t = small[lat_rows, : 2 * width // planes // dp].reshape(2, -1)
    return (
        layer_outputs[None],
        input_grads[None],
        query_t[None],
        lat_t[None],
        key_t[None],
        value_t[None],
        out_t.T[None],
        gain_t[None],
        gate_t[None],
        up_t[None],
        down_t.T[None],
    )


def solution(mesh):
    placed = (
        P("dp", None),
        P("dp", None),
        P("dp"),
        P("section", None, "tensor"),
        P("section", None, None),
        P("section", None, "tensor"),
        P("section", None, "tensor"),
        P("section", "tensor", None),
        P("section", None, None),
        P("section", None, "tensor"),
        P("section", None, "tensor"),
        P("section", "tensor", None),
    )
    return jax.shard_map(
        shards,
        mesh=mesh,
        in_specs=placed,
        out_specs=(
            P("section", "dp", None),
            P("section", "dp", None),
            P("section", "dp", "tensor"),
            P("section", ("tensor", "dp"), None),
            P("section", "dp", "tensor"),
            P("section", "dp", "tensor"),
            P("section", "tensor", "dp"),
            P("section", None, ("tensor", "dp")),
            P("section", "dp", "tensor"),
            P("section", "dp", "tensor"),
            P("section", "tensor", "dp"),
        ),
        check_vma=False,
    )
```

time: 3050 us -> 839 us (0.28)
  waiting for transfers between devices: 2370 us -> 191 us
  matrix products: 310 us -> 12.5 us
  Pallas kernels: 0 us -> 189 us
  starting transfers between devices: 15.5 us -> 158 us
  other arithmetic: 183 us -> 122 us
  local copies, waits for them, and re-layouts: 113 us -> 153 us
    psum x9 -> x0, waiting for transfers between devices: 1370 us -> none  [the longest x6 910 us: attend(): branch = lax.psum(dot_plain(mixed, w_out), 'tensor')]
    reduce_scatter x14 -> x0, waiting for transfers between devices: 722 us -> none  [the longest x3 224 us: layer_backward(): lax.psum_scatter(dot_right_t(grad_gate, w_gate) + dot_right_t(grad_up, w_...]
    dot_general x132 -> x6, matrix products: 273 us -> 12.5 us  [the longest x2 6.62 us: dot_nt(): lax.dot_general(left, right, (((1,), (1,)), ((), ())), preferred_element_...]
    all_gather x6 -> x0, waiting for transfers between devices: 227 us -> none  [the longest x3 134 us: layer_backward(): lax.all_gather(grad_share.astype(jnp.bfloat16), 'tensor', axis=0, tiled=T...]
    pallas_call x0 -> x14, Pallas kernels: none -> 189 us  [kernel_call(): pl.pallas_call(kernel, grid_spec=pltpu.PrefetchScalarGridSpec(num_scalar_...]
    ppermute x6 -> x96, waiting for transfers between devices: 14.9 us -> 191 us  [the longest x26 77.4 us: z_swap(): return lax.ppermute(value, 'tensor', [(i, i ^ step) for i in range(count)])]
    ppermute x6 -> x96, starting transfers between devices: 11.9 us -> 158 us  [the longest x26 53.5 us: z_swap(): return lax.ppermute(value, 'tensor', [(i, i ^ step) for i in range(count)])]
    while x477 -> x0, local copies, waits for them, and re-layouts: 60.1 us -> none
  transfers between devices with their start and end apart: 36 -> 96, of which waited for: 33 -> 20; matrix products, arithmetic and copies ran while one was open for 4% -> 29% of each run, Pallas kernels for 0% -> 19%
where the time goes in v1:
time: 839 us; the launch traced here: 828 us
  waiting for transfers between devices  191 us (23%)
  Pallas kernels  189 us (23%)
  starting transfers between devices  158 us (19%)
  local copies, waits for them, and re-layouts  153 us (18%)
  other arithmetic  122 us (15%)
  matrix products  12.5 us (1%)
    pallas_call x14, Pallas kernels, kernel_call(): pl.pallas_call(kernel, grid_spec=pltpu.PrefetchScalarGridSpec(num_scalar_...  189 us
    ppermute x26, waiting for transfers between devices, z_swap(): return lax.ppermute(value, 'tensor', [(i, i ^ step) for i in range(count)])  77.4 us
    ppermute x12, waiting for transfers between devices, gather_rows(): found.append(lax.ppermute(chip, ('section', 'tensor'), pairs))  63.5 us
    ppermute x26, starting transfers between devices, z_swap(): return lax.ppermute(value, 'tensor', [(i, i ^ step) for i in range(count)])  53.5 us
    ppermute x32, waiting for transfers between devices, plane_swap(): return lax.ppermute(value, 'dp', [(i, i ^ bit) for i in range(count)])  46.9 us
    ppermute x22, starting transfers between devices, core_swap(): return lax.ppermute(value, 'section', [(0, 1), (1, 0)])  43.2 us
    unnamed x226, local copies, waits for them, and re-layouts  37.2 us
    slice x8, local copies, waits for them, and re-layouts, split(): lax.slice_in_dim(p, at * (rows // 2), (at + 1) * (rows // 2), axis=2)  34.4 us
  transfers between devices with their start and end apart: 96, of which 20 were waited for; matrix products, arithmetic and copies ran while one was open for 29% of the time, Pallas kernels for 19%

profile of v1, /device:TPU:1, one launch (start us, length us, event | category | flops | bytes accessed | tf_op | source)
XLA Modules:
  0.0 828.2 jit_solution(6517815940851617377)
XLA Ops:
  10.2 6.6 copy.105
  35.4 4.6 collective-permute-done.6
  41.0 5.2 collective-permute-done.8
  49.7 6.5 copy.106
  56.3 6.6 broadcast_select_fusion
  65.4 4.8 collective-permute-start.15
  73.5 19.8 %collective-permute-done.15 = bf16[3,128,704]{1,2,0:T(8,128)(2,1)S(1)} collective-permute-done((bf16[3,128,704]{1,2,0:T(8,128)(2,1)S(1)}, bf16[3,128,704]{1,2,0:T(8,128)(2,1)S(1)}, u32[]{:S(2)}, u32[]{:S(2)}) %collective-permute-start.15) | collective-permute-done | bytes 540704 | tf_op jit(solution)/shard_map/ppermute | solution.py:35
  100.8 4.7 collective-permute-done.16
  118.8 4.2 collective-permute-start.20
  131.3 4.0 collective-permute-done.31
  143.8 14.0 %collective-permute-done.36 = bf16[3,128,704]{1,2,0:T(8,128)(2,1)S(1)} collective-permute-done((bf16[3,128,704]{1,2,0:T(8,128)(2,1)S(1)}, bf16[3,128,704]{1,2,0:T(8,128)(2,1)S(1)}, u32[]{:S(2)}, u32[]{:S(2)}) %collective-permute-start.36) | collective-permute-done | bytes 540704 | tf_op jit(solution)/shard_map/ppermute | solution.py:35
  159.7 18.1 %attend.2 = (bf16[4,256,256]{2,1,0:T(8,128)(2,1)}, f32[4,4,256]{2,1,0:T(4,128)}, bf16[2,1024,256]{2,1,0:T(8,128)(2,1)}, f32[256,1024]{1,0:T(8,128)}, bf16[256,1024]{1,0:T(8,128)(2,1)}) custom-call(s32[5]{0:T(128)} %stack.216.info, bf16[256,1024]{1,0:T(8,128)(2,1)} %get-tuple-element.160.x, bf16[256,1024]{1,0:T(8,128)(2,1)} %copy-done.50, ...), custom_call_target="tpu_custom_call" | custom-call | flops 6442450944 | bytes 10506240 | tf_op jit(solution)/shard_map/attend/pallas_call | solution.py:132
  188.3 4.2 copy.114.other
  192.5 9.4 %feed.5 = (bf16[256,1024]{1,0:T(8,128)(2,1)}, bf16[2,2,256,704]{3,2,1,0:T(8,128)(2,1)}) custom-call(s32[5]{0:T(128)} %stack.216.info, bf16[256,1024]{1,0:T(8,128)(2,1)} %collective-permute-done.21.value.far_normed2, bf16[3,1024,704]{2,1,0:T(8,128)(2,1)} %copy-done, bf16[4,3,128,704]{3,2,1,0:T(8,128)(2,1)} %copy-done.1, bf16[4,3,128,704]{3,2,1,0:T(8,128)(2,1)} %copy.114.other), custom_call_target="tpu_custom_call" | custom-call | flops 2214592512 | bytes 11141120 | tf_op jit(solution)/shard_map/feed/pallas_call | solution.py:132
  208.1 9.6 %feed.4 = (f32[256,1024]{1,0:T(8,128)}, bf16[2,2,256,704]{3,2,1,0:T(8,128)(2,1)}) custom-call(s32[5]{0:T(128)} %stack.216.info, bf16[256,1024]{1,0:T(8,128)(2,1)} %get-tuple-element.54.value.normed2, bf16[3,1024,704]{2,1,0:T(8,128)(2,1)} %copy-done, bf16[4,3,128,704]{3,2,1,0:T(8,128)(2,1)} %copy-done.1, bf16[4,3,128,704]{3,2,1,0:T(8,128)(2,1)} %copy.114.other), custom_call_target="tpu_custom_call" | custom-call | flops 2214592512 | bytes 11665408 | tf_op jit(solution)/shard_map/feed/pallas_call | solution.py:132
  223.3 6.1 collective-permute-done.26.lat2
  230.9 4.2 copy.124.other
  236.0 17.8 %attend.3 = (bf16[4,256,256]{2,1,0:T(8,128)(2,1)}, f32[4,4,256]{2,1,0:T(4,128)}, bf16[2,1024,256]{2,1,0:T(8,128)(2,1)}, f32[256,1024]{1,0:T(8,128)}, bf16[256,1024]{1,0:T(8,128)(2,1)}) custom-call(s32[5]{0:T(128)} %stack.216.info, bf16[256,1024]{1,0:T(8,128)(2,1)} %copy-done.3, bf16[256,1024]{1,0:T(8,128)(2,1)} %copy-done.52, bf16[256,512]{1,0:T(8,128)(2,1)} %copy-done.86, ...), custom_call_target="tpu_custom_call" | custom-call | flops 6442450944 | bytes 10506240 | tf_op jit(solution)/shard_map/attend/pallas_call | solution.py:132
  255.2 9.5 %feed.6 = (f32[256,1024]{1,0:T(8,128)}, bf16[2,2,256,704]{3,2,1,0:T(8,128)(2,1)}) custom-call(s32[5]{0:T(128)} %stack.216.info, bf16[256,1024]{1,0:T(8,128)(2,1)} %get-tuple-element.58.value.normed2, bf16[3,1024,704]{2,1,0:T(8,128)(2,1)} %get-tuple-element.161.own, bf16[4,3,128,704]{3,2,1,0:T(8,128)(2,1)} %copy-done.2, bf16[4,3,128,704]{3,2,1,0:T(8,128)(2,1)} %copy.124.other), custom_call_target="tpu_custom_call" | custom-call | flops 2214592512 | bytes 11665408 | tf_op jit(solution)/shard_map/feed/pallas_call | solution.py:132
  267.9 9.3 %feed.7 = (bf16[256,1024]{1,0:T(8,128)(2,1)}, bf16[2,2,256,704]{3,2,1,0:T(8,128)(2,1)}) custom-call(s32[5]{0:T(128)} %stack.216.info, bf16[256,1024]{1,0:T(8,128)(2,1)} %copy-done.80, bf16[3,1024,704]{2,1,0:T(8,128)(2,1)} %get-tuple-element.161.own, bf16[4,3,128,704]{3,2,1,0:T(8,128)(2,1)} %copy-done.2, bf16[4,3,128,704]{3,2,1,0:T(8,128)(2,1)} %copy.124.other), custom_call_target="tpu_custom_call" | custom-call | flops 2214592512 | bytes 11141120 | tf_op jit(solution)/shard_map/feed/pallas_call | solution.py:132
  278.1 11.0 %feed_back.5 = (bf16[256,1024]{1,0:T(8,128)(2,1)}, bf16[2,3,256,704]{3,2,1,0:T(8,128)(2,1)}) custom-call(s32[5]{0:T(128)} %stack.216.info, bf16[256,1024]{1,0:T(8,128)(2,1)} %copy-done.79, bf16[3,1024,704]{2,1,0:T(8,128)(2,1)} %get-tuple-element.161.own, bf16[4,3,128,704]{3,2,1,0:T(8,128)(2,1)} %copy-done.2, bf16[4,3,128,704]{3,2,1,0:T(8,128)(2,1)} %copy.124.other, ...), custom_call_target="tpu_custom_call" | custom-call | flops 2214592512 | bytes 13303808 | tf_op jit(solution)/shard_map/feed_back/pallas_call | solution.py:132
  290.5 11.5 %feed_back.4 = (f32[256,1024]{1,0:T(8,128)}, bf16[2,3,256,704]{3,2,1,0:T(8,128)(2,1)}) custom-call(s32[5]{0:T(128)} %stack.216.info, bf16[256,1024]{1,0:T(8,128)(2,1)} %copy-done.54, bf16[3,1024,704]{2,1,0:T(8,128)(2,1)} %get-tuple-element.161.own, bf16[4,3,128,704]{3,2,1,0:T(8,128)(2,1)} %copy-done.2, bf16[4,3,128,704]{3,2,1,0:T(8,128)(2,1)} %copy.124.other, ...), custom_call_target="tpu_custom_call" | custom-call | flops 2214592512 | bytes 13828096 | tf_op jit(solution)/shard_map/feed_back/pallas_call | solution.py:132
  302.1 10.9 %feed_weights.2 = (bf16[2,3,4,128,704]{4,3,2,1,0:T(8,128)(2,1)}, bf16[2,3,4,128,704]{4,3,2,1,0:T(8,128)(2,1)}) custom-call(s32[5]{0:T(128)} %stack.216.info, bf16[256,1024]{1,0:T(8,128)(2,1)} %get-tuple-element.58.value.normed2, bf16[256,1024]{1,0:T(8,128)(2,1)} %copy-done.80, bf16[256,1024]{1,0:T(8,128)(2,1)} %copy-done.54, bf16[256,1024]{1,0:T(8,128)(2,1)} %copy-done.79, ...), custom_call_target="tpu_custom_call" | custom-call | flops 4429185024 | bytes 15073280 | tf_op jit(solution)/shard_map/feed_weights/pallas_call | solution.py:132
  317.1 24.3 %attend_back.2 = (f32[256,1024]{1,0:T(8,128)}, f32[2,1024,256]{2,1,0:T(8,128)}, bf16[4,4,320,256]{3,2,1,0:T(8,128)(2,1)}, bf16[4,4,320,256]{3,2,1,0:T(8,128)(2,1)}) custom-call(s32[5]{0:T(128)} %stack.216.info, bf16[256,1024]{1,0:T(8,128)(2,1)} %get-tuple-element.155.grad_branch, bf16[256,1024]{1,0:T(8,128)(2,1)} %copy-done.52, ...), custom_call_target="tpu_custom_call" | custom-call | flops 17716740096 | bytes 16269312 | tf_op jit(solution)/shard_map/attend_back/pallas_call | solution.py:132
  356.8 6.5 copy.129
  363.3 4.1 collective-permute-start.55
  382.1 4.1 collective-permute-start.47
  390.7 11.1 %feed_back.6 = (f32[256,1024]{1,0:T(8,128)}, bf16[2,3,256,704]{3,2,1,0:T(8,128)(2,1)}) custom-call(s32[5]{0:T(128)} %stack.216.info, bf16[256,1024]{1,0:T(8,128)(2,1)} %get-tuple-element.153.value.grad, bf16[3,1024,704]{2,1,0:T(8,128)(2,1)} %copy-done, bf16[4,3,128,704]{3,2,1,0:T(8,128)(2,1)} %copy-done.1, bf16[4,3,128,704]{3,2,1,0:T(8,128)(2,1)} %copy.114.other, ...), custom_call_target="tpu_custom_call" | custom-call | flops 2214592512 | bytes 13828096 | tf_op jit(solution)/shard_map/feed_back/pallas_call | solution.py:132
  410.7 26.0 %collective-permute-start.54 = (bf16[256,1024]{1,0:T(8,128)(2,1)}, bf16[256,1024]{1,0:T(8,128)(2,1)}, u32[]{:S(2)}, u32[]{:S(2)}) collective-permute-start(bf16[256,1024]{1,0:T(8,128)(2,1)} %get-tuple-element.153.value.grad), channel_id=1, source_target_pairs={{0,4},{4,0},{8,12},{12,8},{1,5},{5,1},{9,13},{13,9},{2,6},{6,2},{1... | collective-permute-start | bytes 1572872 | tf_op jit(solution)/shard_map/ppermute | solution.py:35
  437.8 8.0 fusion.70
  445.7 6.0 copy.133
  456.6 6.0 copy.161
  474.4 19.1 %collective-permute-done.56 = bf16[6,2,64,704]{3,2,1,0:T(8,128)(2,1)S(1)} collective-permute-done((bf16[6,2,64,704]{3,2,1,0:T(8,128)(2,1)S(1)}, bf16[6,2,64,704]{3,2,1,0:T(8,128)(2,1)S(1)}, u32[]{:S(2)}, u32[]{:S(2)}) %collective-permute-start.56) | collective-permute-done | bytes 1081376 | tf_op jit(solution)/shard_map/ppermute | solution.py:40
  498.8 7.3 collective-permute-done.59
  509.1 10.9 %feed_back.7 = (bf16[256,1024]{1,0:T(8,128)(2,1)}, bf16[2,3,256,704]{3,2,1,0:T(8,128)(2,1)}) custom-call(s32[5]{0:T(128)} %stack.216.info, bf16[256,1024]{1,0:T(8,128)(2,1)} %collective-permute-done.54.value.far_grad, bf16[3,1024,704]{2,1,0:T(8,128)(2,1)} %copy-done, bf16[4,3,128,704]{3,2,1,0:T(8,128)(2,1)} %copy-done.1, ...), custom_call_target="tpu_custom_call" | custom-call | flops 2214592512 | bytes 13303808 | tf_op jit(solution)/shard_map/feed_back/pallas_call | solution.py:132
  522.5 11.0 %feed_weights.3 = (bf16[2,3,4,128,704]{4,3,2,1,0:T(8,128)(2,1)}, bf16[2,3,4,128,704]{4,3,2,1,0:T(8,128)(2,1)}) custom-call(s32[5]{0:T(128)} %stack.216.info, bf16[256,1024]{1,0:T(8,128)(2,1)} %get-tuple-element.54.value.normed2, bf16[256,1024]{1,0:T(8,128)(2,1)} %collective-permute-done.21.value.far_normed2, ...), custom_call_target="tpu_custom_call" | custom-call | flops 4429185024 | bytes 15073280 | tf_op jit(solution)/shard_map/feed_weights/pallas_call | solution.py:132
  537.5 24.6 %attend_back.3 = (f32[256,1024]{1,0:T(8,128)}, f32[2,1024,256]{2,1,0:T(8,128)}, bf16[4,4,320,256]{3,2,1,0:T(8,128)(2,1)}, bf16[4,4,320,256]{3,2,1,0:T(8,128)(2,1)}) custom-call(s32[5]{0:T(128)} %stack.216.info, bf16[256,1024]{1,0:T(8,128)(2,1)} %get-tuple-element.86.grad_branch, bf16[256,1024]{1,0:T(8,128)(2,1)} %copy-done.50, ...), custom_call_target="tpu_custom_call" | custom-call | flops 17716740096 | bytes 16269312 | tf_op jit(solution)/shard_map/attend_back/pallas_call | solution.py:132
  571.4 6.8 collective-permute-done.84
  584.7 6.6 copy.143
  636.4 20.3 %collective-permute-done.72 = bf16[512,1024]{1,0:T(8,128)(2,1)} collective-permute-done((bf16[512,1024]{1,0:T(8,128)(2,1)}, bf16[512,1024]{1,0:T(8,128)(2,1)}, u32[]{:S(2)}, u32[]{:S(2)}) %collective-permute-start.72) | collective-permute-done | bytes 1048608 | tf_op jit(solution)/shard_map/ppermute | solution.py:572
  663.2 43.1 %collective-permute-done.74 = bf16[512,1024]{1,0:T(8,128)(2,1)S(1)} collective-permute-done((bf16[512,1024]{1,0:T(8,128)(2,1)}, bf16[512,1024]{1,0:T(8,128)(2,1)S(1)}, u32[]{:S(2)}, u32[]{:S(2)}) %collective-permute-start.74) | collective-permute-done | bytes 1048608 | tf_op jit(solution)/shard_map/ppermute | solution.py:572
  711.7 7.6 fusion.69
  719.3 5.9 copy.167
  730.1 5.9 copy.148
  745.6 4.7 collective-permute-done.81
  764.0 15.6 %collective-permute-start.87 = (bf16[400,256]{1,0:T(8,128)(2,1)}, bf16[400,256]{1,0:T(8,128)(2,1)S(1)}, u32[]{:S(2)}, u32[]{:S(2)}) collective-permute-start(bf16[400,256]{1,0:T(8,128)(2,1)} %get-tuple-element.208), channel_id=1, source_target_pairs={{0,16},{16,0},{1,17},{17,1},{2,18},{18,2},{3,19},{19,3},{4,20},{20... | collective-permute-start | bytes 614408 | tf_op jit(solution)/shard_map/ppermute | solution.py:30
  787.0 6.6 maximum_select_fusion.3
  793.8 17.2 %collective-permute-done.93 = bf16[3,128,704]{1,2,0:T(8,128)(2,1)} collective-permute-done((bf16[3,128,704]{1,2,0:T(8,128)(2,1)}, bf16[3,128,704]{1,2,0:T(8,128)(2,1)}, u32[]{:S(2)}, u32[]{:S(2)}) %collective-permute-start.93) | collective-permute-done | bytes 540704 | tf_op jit(solution)/shard_map/ppermute | solution.py:35
  (591 shorter events, 313.1 us)
Async XLA Ops:
  16.7 33.0 %collective-permute-start.14 = (bf16[3,1024,704]{1,2,0:T(8,128)(2,1)}, bf16[3,1024,704]{1,2,0:T(8,128)(2,1)}, u32[]{:S(2)}, u32[]{:S(2)}) collective-permute-start(bf16[3,1024,704]{1,2,0:T(8,128)(2,1)} %copy.105), channel_id=1, source_target_pairs={{0,16},{16,0},{1,17},{17,1},{2,18},{18,2},{3,19},{19,3},{4,20},{20... | collective-permute-start | bytes 12976136 | tf_op jit(solution)/shard_map/ppermute | solution.py:30
  21.6 48.5 %collective-permute-start = (f32[2,1024]{1,0:T(2,128)S(1)}, f32[2,1024]{1,0:T(2,128)S(1)}, u32[]{:S(2)}, u32[]{:S(2)}) collective-permute-start(f32[2,1024]{1,0:T(2,128)S(1)} %bitcast.410), channel_id=1, source_target_pairs={{0,16},{16,0},{1,17},{17,1},{2,18},{18,2},{3,19},{19,3},{4,20},{20... | collective-permute-start | bytes 24584 | tf_op jit(solution)/shard_map/ppermute | solution.py:30
  40.0 58.8 %collective-permute-start.1 = (bf16[1024,512]{1,0:T(8,128)(2,1)}, bf16[1024,512]{1,0:T(8,128)(2,1)}, u32[]{:S(2)}, u32[]{:S(2)}) collective-permute-start(bf16[1024,512]{1,0:T(8,128)(2,1)} %bitcast.7), channel_id=1, source_target_pairs={{0,16},{16,0},{1,17},{17,1},{2,18},{18,2},{3,19},{19,3},{4,20},{20... | collective-permute-start | bytes 3145736 | tf_op jit(solution)/shard_map/ppermute | solution.py:30
  47.3 23.5 %collective-permute-start.9 = (bf16[3,320,256]{2,1,0:T(8,128)(2,1)}, bf16[3,320,256]{2,1,0:T(8,128)(2,1)}, u32[]{:S(2)}, u32[]{:S(2)}) collective-permute-start(bf16[3,320,256]{2,1,0:T(8,128)(2,1)} %get-tuple-element.218), channel_id=1, source_target_pairs={{0,1},{1,0},{2,3},{3,2},{4,5},{5,4},{6,7},{7,6},{8,9},{9,8},{10,11... | collective-permute-start | bytes 1474568 | tf_op jit(solution)/shard_map/ppermute | solution.py:40
  48.5 23.5 %collective-permute-start.10 = (bf16[3,320,256]{2,1,0:T(8,128)(2,1)}, bf16[3,320,256]{2,1,0:T(8,128)(2,1)}, u32[]{:S(2)}, u32[]{:S(2)}) collective-permute-start(bf16[3,320,256]{2,1,0:T(8,128)(2,1)} %get-tuple-element.218), channel_id=1, source_target_pairs={{0,2},{1,3},{2,0},{3,1},{4,6},{5,7},{6,4},{7,5},{8,10},{9,11},{10,... | collective-permute-start | bytes 1474568 | tf_op jit(solution)/shard_map/ppermute | solution.py:40
  65.4 28.0 %collective-permute-start.15 = (bf16[3,128,704]{1,2,0:T(8,128)(2,1)S(1)}, bf16[3,128,704]{1,2,0:T(8,128)(2,1)S(1)}, u32[]{:S(2)}, u32[]{:S(2)}) collective-permute-start(bf16[3,128,704]{1,2,0:T(8,128)(2,1)S(1)} %bitcast.388), channel_id=1, source_target_pairs={{0,8},{4,12},{8,0},{12,4},{1,9},{5,13},{9,1},{13,5},{2,10},{6,14},... | collective-permute-start | bytes 1622024 | tf_op jit(solution)/shard_map/ppermute | solution.py:35
  96.6 61.8 %collective-permute-start.13 = (bf16[4,3,320,256]{3,2,1,0:T(8,128)(2,1)}, bf16[4,3,320,256]{3,2,1,0:T(8,128)(2,1)}, u32[]{:S(2)}, u32[]{:S(2)}) collective-permute-start(bf16[4,3,320,256]{3,2,1,0:T(8,128)(2,1)} %pad_maximum_fusion.3.near), channel_id=1, source_target_pairs={{0,16},{16,0},{1,17},{17,1},{2,18},{18,2},{3,19},{19,3},{4,20},{20... | collective-permute-start | bytes 5898248 | tf_op jit(solution)/shard_map/ppermute | solution.py:30
  118.8 69.5 %collective-permute-start.20 = (bf16[4,3,128,704]{2,3,1,0:T(8,128)(2,1)}, bf16[4,3,128,704]{2,3,1,0:T(8,128)(2,1)}, u32[]{:S(2)}, u32[]{:S(2)}) collective-permute-start(bf16[4,3,128,704]{2,3,1,0:T(8,128)(2,1)} %copy.113), channel_id=1, source_target_pairs={{0,16},{16,0},{1,17},{17,1},{2,18},{18,2},{3,19},{19,3},{4,20},{20... | collective-permute-start | bytes 6488072 | tf_op jit(solution)/shard_map/ppermute | solution.py:30
  131.2 26.6 %collective-permute-start.36 = (bf16[3,128,704]{1,2,0:T(8,128)(2,1)S(1)}, bf16[3,128,704]{1,2,0:T(8,128)(2,1)S(1)}, u32[]{:S(2)}, u32[]{:S(2)}) collective-permute-start(bf16[3,128,704]{1,2,0:T(8,128)(2,1)S(1)} %bitcast.387), channel_id=1, source_target_pairs={{0,8},{4,12},{8,0},{12,4},{1,9},{5,13},{9,1},{13,5},{2,10},{6,14},... | collective-permute-start | bytes 1622024 | tf_op jit(solution)/shard_map/ppermute | solution.py:35
  142.3 35.5 %collective-permute-start.33 = (bf16[3,160,256]{2,1,0:T(8,128)(2,1)S(1)}, bf16[3,160,256]{2,1,0:T(8,128)(2,1)S(1)}, u32[]{:S(2)}, u32[]{:S(2)}) collective-permute-start(bf16[3,160,256]{2,1,0:T(8,128)(2,1)S(1)} %slice.318), channel_id=1, source_target_pairs={{0,2},{1,3},{2,0},{3,1},{4,6},{5,7},{6,4},{7,5},{8,10},{9,11},{10,... | collective-permute-start | bytes 737288 | tf_op jit(solution)/shard_map/ppermute | solution.py:40
  143.6 34.9 %collective-permute-start.34 = (bf16[3,160,256]{2,1,0:T(8,128)(2,1)S(1)}, bf16[3,160,256]{2,1,0:T(8,128)(2,1)S(1)}, u32[]{:S(2)}, u32[]{:S(2)}) collective-permute-start(bf16[3,160,256]{2,1,0:T(8,128)(2,1)S(1)} %slice.319), channel_id=1, source_target_pairs={{0,1},{1,0},{2,3},{3,2},{4,5},{5,4},{6,7},{7,6},{8,9},{9,8},{10,11... | collective-permute-start | bytes 737288 | tf_op jit(solution)/shard_map/ppermute | solution.py:40
  179.8 23.8 %collective-permute-start.39 = (bf16[3,64,704]{2,1,0:T(8,128)(2,1)S(1)}, bf16[3,64,704]{2,1,0:T(8,128)(2,1)}, u32[]{:S(2)}, u32[]{:S(2)}) collective-permute-start(bf16[3,64,704]{2,1,0:T(8,128)(2,1)S(1)} %slice.321), channel_id=1, source_target_pairs={{0,2},{1,3},{2,0},{3,1},{4,6},{5,7},{6,4},{7,5},{8,10},{9,11},{10,... | collective-permute-start | bytes 811016 | tf_op jit(solution)/shard_map/ppermute | solution.py:40
  184.5 50.6 %collective-permute-start.35 = (bf16[4,3,320,256]{3,2,1,0:T(8,128)(2,1)}, bf16[4,3,320,256]{3,2,1,0:T(8,128)(2,1)}, u32[]{:S(2)}, u32[]{:S(2)}) collective-permute-start(bf16[4,3,320,256]{3,2,1,0:T(8,128)(2,1)} %pad_maximum_fusion.4.near), channel_id=1, source_target_pairs={{0,16},{16,0},{1,17},{17,1},{2,18},{18,2},{3,19},{19,3},{4,20},{20... | collective-permute-start | bytes 5898248 | tf_op jit(solution)/shard_map/ppermute | solution.py:30
  235.1 42.2 %collective-permute-start.50 = (bf16[256,1024]{1,0:T(8,128)(2,1)S(1)}, bf16[256,1024]{1,0:T(8,128)(2,1)S(1)}, u32[]{:S(2)}, u32[]{:S(2)}) collective-permute-start(bf16[256,1024]{1,0:T(8,128)(2,1)S(1)} %get-tuple-element.237.value.grad), channel_id=1, source_target_pairs={{0,4},{4,0},{8,12},{12,8},{1,5},{5,1},{9,13},{13,9},{2,6},{6,2},{1... | collective-permute-start | bytes 1572872 | tf_op jit(solution)/shard_map/ppermute | solution.py:35
  289.0 24.0 %collective-permute-start.51 = (bf16[256,1024]{1,0:T(8,128)(2,1)}, bf16[256,1024]{1,0:T(8,128)(2,1)S(1)}, u32[]{:S(2)}, u32[]{:S(2)}) collective-permute-start(bf16[256,1024]{1,0:T(8,128)(2,1)} %get-tuple-element.64), channel_id=1, source_target_pairs={{0,4},{4,0},{8,12},{12,8},{1,5},{5,1},{9,13},{13,9},{2,6},{6,2},{1... | collective-permute-start | bytes 1572872 | tf_op jit(solution)/shard_map/ppermute | solution.py:35
  353.5 28.6 %collective-permute-start.24 = (bf16[512,1024]{1,0:T(8,128)(2,1)}, bf16[512,1024]{1,0:T(8,128)(2,1)}, u32[]{:S(2)}, u32[]{:S(2)}) collective-permute-start(bf16[512,1024]{1,0:T(8,128)(2,1)} %pad_maximum_fusion.8), channel_id=1, source_target_pairs={{0,4},{4,0},{8,12},{12,8},{1,5},{5,1},{9,13},{13,9},{2,6},{6,2},{1... | collective-permute-start | bytes 3145736 | tf_op jit(solution)/shard_map/ppermute | solution.py:572
  355.2 53.3 %collective-permute-start.46 = (bf16[512,1024]{1,0:T(8,128)(2,1)}, bf16[512,1024]{1,0:T(8,128)(2,1)}, u32[]{:S(2)}, u32[]{:S(2)}) collective-permute-start(bf16[512,1024]{1,0:T(8,128)(2,1)} %pad_maximum_fusion.8), channel_id=1, source_target_pairs={{0,12},{4,8},{8,4},{12,0},{1,13},{5,9},{9,5},{13,1},{2,14},{6,10},... | collective-permute-start | bytes 3145736 | tf_op jit(solution)/shard_map/ppermute | solution.py:572
  363.3 74.4 %collective-permute-start.55 = (bf16[6,4,128,704]{2,3,1,0:T(8,128)(2,1)}, bf16[6,4,128,704]{2,3,1,0:T(8,128)(2,1)}, u32[]{:S(2)}, u32[]{:S(2)}) collective-permute-start(bf16[6,4,128,704]{2,3,1,0:T(8,128)(2,1)} %copy.129), channel_id=1, source_target_pairs={{0,16},{16,0},{1,17},{17,1},{2,18},{18,2},{3,19},{19,3},{4,20},{20... | collective-permute-start | bytes 12976136 | tf_op jit(solution)/shard_map/ppermute | solution.py:30
  368.6 36.9 %collective-permute-start.45 = (bf16[512,1024]{1,0:T(8,128)(2,1)}, bf16[512,1024]{1,0:T(8,128)(2,1)}, u32[]{:S(2)}, u32[]{:S(2)}) collective-permute-start(bf16[512,1024]{1,0:T(8,128)(2,1)} %pad_maximum_fusion.9), channel_id=1, source_target_pairs={{16,20},{20,16},{24,28},{28,24},{17,21},{21,17},{25,29},{29,25},{1... | collective-permute-start | bytes 3145736 | tf_op jit(solution)/shard_map/ppermute | solution.py:572
  382.1 28.6 %collective-permute-start.47 = (bf16[512,1024]{1,0:T(8,128)(2,1)}, bf16[512,1024]{1,0:T(8,128)(2,1)S(1)}, u32[]{:S(2)}, u32[]{:S(2)}) collective-permute-start(bf16[512,1024]{1,0:T(8,128)(2,1)} %pad_maximum_fusion.9), channel_id=1, source_target_pairs={{16,28},{20,24},{24,20},{28,16},{17,29},{21,25},{25,21},{29,17},{1... | collective-permute-start | bytes 3145736 | tf_op jit(solution)/shard_map/ppermute | solution.py:572
  402.9 66.4 %collective-permute-start.61 = (bf16[4,4,320,256]{3,2,1,0:T(8,128)(2,1)}, bf16[4,4,320,256]{3,2,1,0:T(8,128)(2,1)}, u32[]{:S(2)}, u32[]{:S(2)}) collective-permute-start(bf16[4,4,320,256]{3,2,1,0:T(8,128)(2,1)} %get-tuple-element.85), channel_id=1, source_target_pairs={{0,16},{16,0},{1,17},{17,1},{2,18},{18,2},{3,19},{19,3},{4,20},{20... | collective-permute-start | bytes 7864328 | tf_op jit(solution)/shard_map/ppermute | solution.py:30
  405.5 59.7 %collective-permute-start.48 = (bf16[512,1024]{1,0:T(8,128)(2,1)}, bf16[512,1024]{1,0:T(8,128)(2,1)}, u32[]{:S(2)}, u32[]{:S(2)}) collective-permute-start(bf16[512,1024]{1,0:T(8,128)(2,1)} %pad_maximum_fusion.8), channel_id=1, source_target_pairs={{0,8},{4,12},{8,0},{12,4},{1,9},{5,13},{9,1},{13,5},{2,10},{6,14},... | collective-permute-start | bytes 3145736 | tf_op jit(solution)/shard_map/ppermute | solution.py:572
  408.4 58.3 %collective-permute-start.49 = (bf16[512,1024]{1,0:T(8,128)(2,1)}, bf16[512,1024]{1,0:T(8,128)(2,1)}, u32[]{:S(2)}, u32[]{:S(2)}) collective-permute-start(bf16[512,1024]{1,0:T(8,128)(2,1)} %pad_maximum_fusion.9), channel_id=1, source_target_pairs={{16,24},{20,28},{24,16},{28,20},{17,25},{21,29},{25,17},{29,21},{1... | collective-permute-start | bytes 3145736 | tf_op jit(solution)/shard_map/ppermute | solution.py:572
  410.7 98.4 %collective-permute-start.54 = (bf16[256,1024]{1,0:T(8,128)(2,1)}, bf16[256,1024]{1,0:T(8,128)(2,1)}, u32[]{:S(2)}, u32[]{:S(2)}) collective-permute-start(bf16[256,1024]{1,0:T(8,128)(2,1)} %get-tuple-element.153.value.grad), channel_id=1, source_target_pairs={{0,4},{4,0},{8,12},{12,8},{1,5},{5,1},{9,13},{13,9},{2,6},{6,2},{1... | collective-permute-start | bytes 1572872 | tf_op jit(solution)/shard_map/ppermute | solution.py:35
  465.1 28.4 %collective-permute-start.56 = (bf16[6,2,64,704]{3,2,1,0:T(8,128)(2,1)S(1)}, bf16[6,2,64,704]{3,2,1,0:T(8,128)(2,1)S(1)}, u32[]{:S(2)}, u32[]{:S(2)}) collective-permute-start(bf16[6,2,64,704]{3,2,1,0:T(8,128)(2,1)S(1)} %get-tuple-element.172), channel_id=1, source_target_pairs={{0,1},{1,0},{2,3},{3,2},{4,5},{5,4},{6,7},{7,6},{8,9},{9,8},{10,11... | collective-permute-start | bytes 3244040 | tf_op jit(solution)/shard_map/ppermute | solution.py:40
  474.2 31.9 %collective-permute-start.59 = (bf16[6,64,704]{2,1,0:T(8,128)(2,1)S(1)}, bf16[6,64,704]{2,1,0:T(8,128)(2,1)S(1)}, u32[]{:S(2)}, u32[]{:S(2)}) collective-permute-start(bf16[6,64,704]{2,1,0:T(8,128)(2,1)S(1)} %fusion.38), channel_id=1, source_target_pairs={{0,1},{1,0},{2,3},{3,2},{4,5},{5,4},{6,7},{7,6},{8,9},{9,8},{10,11... | collective-permute-start | bytes 1622024 | tf_op jit(solution)/shard_map/ppermute | solution.py:40
  495.4 24.6 %collective-permute-start.62 = (bf16[4,2,200,256]{3,2,1,0:T(8,128)(2,1)}, bf16[4,2,200,256]{3,2,1,0:T(8,128)(2,1)}, u32[]{:S(2)}, u32[]{:S(2)}) collective-permute-start(bf16[4,2,200,256]{3,2,1,0:T(8,128)(2,1)} %dynamic-slice_bitcast_fusion.3), channel_id=1, source_target_pairs={{0,1},{1,0},{2,3},{3,2},{4,5},{5,4},{6,7},{7,6},{8,9},{9,8},{10,11... | collective-permute-start | bytes 2457608 | tf_op jit(solution)/shard_map/ppermute | solution.py:40
  497.4 40.2 %collective-permute-start.64 = (bf16[4,2,200,256]{3,2,1,0:T(8,128)(2,1)}, bf16[4,2,200,256]{3,2,1,0:T(8,128)(2,1)}, u32[]{:S(2)}, u32[]{:S(2)}) collective-permute-start(bf16[4,2,200,256]{3,2,1,0:T(8,128)(2,1)} %dynamic-slice_bitcast_fusion.2), channel_id=1, source_target_pairs={{0,2},{1,3},{2,0},{3,1},{4,6},{5,7},{6,4},{7,5},{8,10},{9,11},{10,... | collective-permute-start | bytes 2457608 | tf_op jit(solution)/shard_map/ppermute | solution.py:40
  522.0 46.6 %collective-permute-start.83 = (bf16[4,200,256]{2,1,0:T(8,128)(2,1)}, bf16[4,200,256]{2,1,0:T(8,128)(2,1)S(1)}, u32[]{:S(2)}, u32[]{:S(2)}) collective-permute-start(bf16[4,200,256]{2,1,0:T(8,128)(2,1)} %bitcast_add_fusion.14), channel_id=1, source_target_pairs={{0,2},{1,3},{2,0},{3,1},{4,6},{5,7},{6,4},{7,5},{8,10},{9,11},{10,... | collective-permute-start | bytes 1228808 | tf_op jit(solution)/shard_map/ppermute | solution.py:40
  569.8 23.3 %collective-permute-start.66 = (bf16[2,256,256]{2,1,0:T(8,128)(2,1)S(1)}, bf16[2,256,256]{2,1,0:T(8,128)(2,1)}, u32[]{:S(2)}, u32[]{:S(2)}) collective-permute-start(bf16[2,256,256]{2,1,0:T(8,128)(2,1)S(1)} %dynamic-slice_bitcast_fusion.6), channel_id=1, source_target_pairs={{0,4},{4,0},{8,12},{12,8},{1,5},{5,1},{9,13},{13,9},{2,6},{6,2},{1... | collective-permute-start | bytes 786440 | tf_op jit(solution)/shard_map/ppermute | solution.py:35
  581.1 23.3 %collective-permute-start.85 = (bf16[2,400,256]{2,1,0:T(8,128)(2,1)}, bf16[2,400,256]{2,1,0:T(8,128)(2,1)}, u32[]{:S(2)}, u32[]{:S(2)}) collective-permute-start(bf16[2,400,256]{2,1,0:T(8,128)(2,1)} %slice.289), channel_id=1, source_target_pairs={{0,4},{4,0},{8,12},{12,8},{1,5},{5,1},{9,13},{13,9},{2,6},{6,2},{1... | collective-permute-start | bytes 1228808 | tf_op jit(solution)/shard_map/ppermute | solution.py:35
  583.6 27.4 %collective-permute-start.94 = (bf16[3,128,704]{1,2,0:T(8,128)(2,1)}, bf16[3,128,704]{1,2,0:T(8,128)(2,1)}, u32[]{:S(2)}, u32[]{:S(2)}) collective-permute-start(bf16[3,128,704]{1,2,0:T(8,128)(2,1)} %copy.151), channel_id=1, source_target_pairs={{0,8},{4,12},{8,0},{12,4},{1,9},{5,13},{9,1},{13,5},{2,10},{6,14},... | collective-permute-start | bytes 1622024 | tf_op jit(solution)/shard_map/ppermute | solution.py:35
  591.3 120.4 %collective-permute-start.88 = (bf16[6,4,128,704]{2,3,1,0:T(8,128)(2,1)}, bf16[6,4,128,704]{2,3,1,0:T(8,128)(2,1)}, u32[]{:S(2)}, u32[]{:S(2)}) collective-permute-start(bf16[6,4,128,704]{2,3,1,0:T(8,128)(2,1)} %copy.143), channel_id=1, source_target_pairs={{0,16},{16,0},{1,17},{17,1},{2,18},{18,2},{3,19},{19,3},{4,20},{20... | collective-permute-start | bytes 12976136 | tf_op jit(solution)/shard_map/ppermute | solution.py:30
  593.2 27.6 %collective-permute-start.75 = (bf16[4,4,320,256]{3,2,1,0:T(8,128)(2,1)}, bf16[4,4,320,256]{3,2,1,0:T(8,128)(2,1)}, u32[]{:S(2)}, u32[]{:S(2)}) collective-permute-start(bf16[4,4,320,256]{3,2,1,0:T(8,128)(2,1)} %get-tuple-element.93), channel_id=1, source_target_pairs={{0,16},{16,0},{1,17},{17,1},{2,18},{18,2},{3,19},{19,3},{4,20},{20... | collective-permute-start | bytes 7864328 | tf_op jit(solution)/shard_map/ppermute | solution.py:30
  614.4 42.3 %collective-permute-start.72 = (bf16[512,1024]{1,0:T(8,128)(2,1)}, bf16[512,1024]{1,0:T(8,128)(2,1)}, u32[]{:S(2)}, u32[]{:S(2)}) collective-permute-start(bf16[512,1024]{1,0:T(8,128)(2,1)} %pad_maximum_fusion.11), channel_id=1, source_target_pairs={{16,28},{20,24},{24,20},{28,16},{17,29},{21,25},{25,21},{29,17},{1... | collective-permute-start | bytes 3145736 | tf_op jit(solution)/shard_map/ppermute | solution.py:572
  619.1 38.8 %collective-permute-start.68 = (bf16[512,1024]{1,0:T(8,128)(2,1)}, bf16[512,1024]{1,0:T(8,128)(2,1)}, u32[]{:S(2)}, u32[]{:S(2)}) collective-permute-start(bf16[512,1024]{1,0:T(8,128)(2,1)} %pad_maximum_fusion.10), channel_id=1, source_target_pairs={{0,4},{4,0},{8,12},{12,8},{1,5},{5,1},{9,13},{13,9},{2,6},{6,2},{1... | collective-permute-start | bytes 3145736 | tf_op jit(solution)/shard_map/ppermute | solution.py:572
  620.8 38.2 %collective-permute-start.71 = (bf16[512,1024]{1,0:T(8,128)(2,1)}, bf16[512,1024]{1,0:T(8,128)(2,1)}, u32[]{:S(2)}, u32[]{:S(2)}) collective-permute-start(bf16[512,1024]{1,0:T(8,128)(2,1)} %pad_maximum_fusion.10), channel_id=1, source_target_pairs={{0,12},{4,8},{8,4},{12,0},{1,13},{5,9},{9,5},{13,1},{2,14},{6,10},... | collective-permute-start | bytes 3145736 | tf_op jit(solution)/shard_map/ppermute | solution.py:572
  633.4 72.9 %collective-permute-start.74 = (bf16[512,1024]{1,0:T(8,128)(2,1)}, bf16[512,1024]{1,0:T(8,128)(2,1)S(1)}, u32[]{:S(2)}, u32[]{:S(2)}) collective-permute-start(bf16[512,1024]{1,0:T(8,128)(2,1)} %pad_maximum_fusion.11), channel_id=1, source_target_pairs={{16,24},{20,28},{24,16},{28,20},{17,25},{21,29},{25,17},{29,21},{1... | collective-permute-start | bytes 3145736 | tf_op jit(solution)/shard_map/ppermute | solution.py:572
  656.8 49.5 %collective-permute-start.73 = (bf16[512,1024]{1,0:T(8,128)(2,1)}, bf16[512,1024]{1,0:T(8,128)(2,1)S(1)}, u32[]{:S(2)}, u32[]{:S(2)}) collective-permute-start(bf16[512,1024]{1,0:T(8,128)(2,1)} %pad_maximum_fusion.10), channel_id=1, source_target_pairs={{0,8},{4,12},{8,0},{12,4},{1,9},{5,13},{9,1},{13,5},{2,10},{6,14},... | collective-permute-start | bytes 3145736 | tf_op jit(solution)/shard_map/ppermute | solution.py:572
  658.0 49.5 %collective-permute-start.76 = (bf16[4,2,200,256]{3,2,1,0:T(8,128)(2,1)S(1)}, bf16[4,2,200,256]{3,2,1,0:T(8,128)(2,1)S(1)}, u32[]{:S(2)}, u32[]{:S(2)}) collective-permute-start(bf16[4,2,200,256]{3,2,1,0:T(8,128)(2,1)S(1)} %dynamic-slice_bitcast_fusion.1), channel_id=1, source_target_pairs={{0,1},{1,0},{2,3},{3,2},{4,5},{5,4},{6,7},{7,6},{8,9},{9,8},{10,11... | collective-permute-start | bytes 2457608 | tf_op jit(solution)/shard_map/ppermute | solution.py:40
  659.0 50.3 %collective-permute-start.79 = (bf16[4,2,200,256]{3,2,1,0:T(8,128)(2,1)S(1)}, bf16[4,2,200,256]{3,2,1,0:T(8,128)(2,1)S(1)}, u32[]{:S(2)}, u32[]{:S(2)}) collective-permute-start(bf16[4,2,200,256]{3,2,1,0:T(8,128)(2,1)S(1)} %dynamic-slice_bitcast_fusion), channel_id=1, source_target_pairs={{0,2},{1,3},{2,0},{3,1},{4,6},{5,7},{6,4},{7,5},{8,10},{9,11},{10,... | collective-permute-start | bytes 2457608 | tf_op jit(solution)/shard_map/ppermute | solution.py:40
  706.3 55.9 %collective-permute-start.86 = (bf16[400,256]{1,0:T(8,128)(2,1)}, bf16[400,256]{1,0:T(8,128)(2,1)}, u32[]{:S(2)}, u32[]{:S(2)}) collective-permute-start(bf16[400,256]{1,0:T(8,128)(2,1)} %slice_bitcast_fusion.1), channel_id=1, source_target_pairs={{0,8},{4,12},{8,0},{12,4},{1,9},{5,13},{9,1},{13,5},{2,10},{6,14},... | collective-permute-start | bytes 614408 | tf_op jit(solution)/shard_map/ppermute | solution.py:35
  708.3 31.0 %collective-permute-start.77 = (bf16[4,200,256]{2,1,0:T(8,128)(2,1)}, bf16[4,200,256]{2,1,0:T(8,128)(2,1)}, u32[]{:S(2)}, u32[]{:S(2)}) collective-permute-start(bf16[4,200,256]{2,1,0:T(8,128)(2,1)} %bitcast_add_fusion.18), channel_id=1, source_target_pairs={{0,2},{1,3},{2,0},{3,1},{4,6},{5,7},{6,4},{7,5},{8,10},{9,11},{10,... | collective-permute-start | bytes 1228808 | tf_op jit(solution)/shard_map/ppermute | solution.py:40
  710.2 30.3 %collective-permute-start.80 = (bf16[4,200,256]{2,1,0:T(8,128)(2,1)}, bf16[4,200,256]{2,1,0:T(8,128)(2,1)}, u32[]{:S(2)}, u32[]{:S(2)}) collective-permute-start(bf16[4,200,256]{2,1,0:T(8,128)(2,1)} %bitcast_add_fusion.16), channel_id=1, source_target_pairs={{0,1},{1,0},{2,3},{3,2},{4,5},{5,4},{6,7},{7,6},{8,9},{9,8},{10,11... | collective-permute-start | bytes 1228808 | tf_op jit(solution)/shard_map/ppermute | solution.py:40
  752.8 26.7 %collective-permute-start.90 = (bf16[6,64,704]{2,1,0:T(8,128)(2,1)S(1)}, bf16[6,64,704]{2,1,0:T(8,128)(2,1)S(1)}, u32[]{:S(2)}, u32[]{:S(2)}) collective-permute-start(bf16[6,64,704]{2,1,0:T(8,128)(2,1)S(1)} %fusion.37), channel_id=1, source_target_pairs={{0,2},{1,3},{2,0},{3,1},{4,6},{5,7},{6,4},{7,5},{8,10},{9,11},{10,... | collective-permute-start | bytes 1622024 | tf_op jit(solution)/shard_map/ppermute | solution.py:40
  757.4 23.4 %collective-permute-start.92 = (bf16[6,64,704]{2,1,0:T(8,128)(2,1)S(1)}, bf16[6,64,704]{2,1,0:T(8,128)(2,1)S(1)}, u32[]{:S(2)}, u32[]{:S(2)}) collective-permute-start(bf16[6,64,704]{2,1,0:T(8,128)(2,1)S(1)} %fusion.36), channel_id=1, source_target_pairs={{0,1},{1,0},{2,3},{3,2},{4,5},{5,4},{6,7},{7,6},{8,9},{9,8},{10,11... | collective-permute-start | bytes 1622024 | tf_op jit(solution)/shard_map/ppermute | solution.py:40
  764.0 29.7 %collective-permute-start.87 = (bf16[400,256]{1,0:T(8,128)(2,1)}, bf16[400,256]{1,0:T(8,128)(2,1)S(1)}, u32[]{:S(2)}, u32[]{:S(2)}) collective-permute-start(bf16[400,256]{1,0:T(8,128)(2,1)} %get-tuple-element.208), channel_id=1, source_target_pairs={{0,16},{16,0},{1,17},{17,1},{2,18},{18,2},{3,19},{19,3},{4,20},{20... | collective-permute-start | bytes 614408 | tf_op jit(solution)/shard_map/ppermute | solution.py:30
  785.4 25.7 %collective-permute-start.93 = (bf16[3,128,704]{1,2,0:T(8,128)(2,1)}, bf16[3,128,704]{1,2,0:T(8,128)(2,1)}, u32[]{:S(2)}, u32[]{:S(2)}) collective-permute-start(bf16[3,128,704]{1,2,0:T(8,128)(2,1)} %copy.149), channel_id=1, source_target_pairs={{0,8},{4,12},{8,0},{12,4},{1,9},{5,13},{9,1},{13,5},{2,10},{6,14},... | collective-permute-start | bytes 1622024 | tf_op jit(solution)/shard_map/ppermute | solution.py:35
  (156 other events, 1867.2 us)

commit v2 on v1

v2 whole, which is shorter than its diff:
```python
import functools

import jax
import jax.numpy as jnp
from jax import lax
from jax.experimental import pallas as pl
from jax.experimental.pallas import tpu as pltpu
from jax.sharding import PartitionSpec as P

HEAD_DIM = 64
eps = 1e-06
masked_score = -1e30
f32 = jnp.float32
bf16 = jnp.bfloat16


def dot_nn(left, right):
    return lax.dot_general(left, right, (((1,), (0,)), ((), ())), preferred_element_type=f32)


def dot_nt(left, right):
    return lax.dot_general(left, right, (((1,), (1,)), ((), ())), preferred_element_type=f32)


def dot_tn(left, right):
    return lax.dot_general(left, right, (((0,), (0,)), ((), ())), preferred_element_type=f32)


def core_swap(value):
    return lax.ppermute(value, "section", [(0, 1), (1, 0)])


def z_swap(value, step):
    count = lax.axis_size("tensor")
    return lax.ppermute(value, "tensor", [(i, i ^ step) for i in range(count)])


def tie(first, *others):
    return lax.optimization_barrier((first,) + others)[0]


def bits_of(count):
    return [1 << i for i in range(count.bit_length() - 1)]


def plane_gather(piece):
    count = lax.axis_size("dp")
    return lax.all_to_all(jnp.broadcast_to(piece[None], (count,) + piece.shape), "dp", 0, 0)


def plane_sum(parts):
    return jnp.sum(lax.all_to_all(parts, "dp", 0, 0).astype(f32), axis=0).astype(bf16)


def by_plane(values, flip_of):
    count = values.shape[0]
    for bit in bits_of(count):
        order = [k ^ bit for k in range(count)]
        flipped = jnp.stack([values[k] for k in order])
        values = jnp.where((flip_of // bit) % 2 == 1, flipped, values)
    return values


def inverse_rms(rows):
    return lax.rsqrt(jnp.mean(rows * rows, axis=-1, keepdims=True) + eps)


def norm_back(rows, gain, grad_norm):
    scale = inverse_rms(rows)
    weighted = grad_norm * gain
    inner = jnp.mean(weighted * rows, axis=-1, keepdims=True)
    grad_rows = scale * weighted - rows * scale * scale * scale * inner
    grad_gain = jnp.sum(grad_norm * rows * scale, axis=0)
    return (grad_rows, grad_gain)


LENGTH, FIRST, CORE, MEMBER, RANK, PLANE = range(6)


def kernel_call(kernel, info, arrays, grid, in_specs, out_specs, out_shape, scratch, name, flops, transcendentals=0):
    size = sum(a.size * a.dtype.itemsize for a in arrays)
    size += sum(o.size * o.dtype.itemsize for o in out_shape)
    return pl.pallas_call(
        kernel,
        grid_spec=pltpu.PrefetchScalarGridSpec(
            num_scalar_prefetch=1,
            grid=grid,
            in_specs=in_specs,
            out_specs=out_specs,
            scratch_shapes=scratch,
        ),
        out_shape=out_shape,
        compiler_params=pltpu.CompilerParams(
            dimension_semantics=("arbitrary",) * len(grid), vmem_limit_bytes=56 * 1024 * 1024
        ),
        cost_estimate=pl.CostEstimate(flops=flops, bytes_accessed=size, transcendentals=transcendentals),
        name=name,
    )(info, *arrays)


def whole(array):
    shape = array.shape
    return pl.BlockSpec(shape, lambda i, info: (0,) * len(shape))


def lead(array):
    shape = array.shape[1:]
    return pl.BlockSpec((1,) + shape, lambda i, info: (i,) + (0,) * len(shape))


def like(shape, dtype):
    return jax.ShapeDtypeStruct(shape, dtype)


class PackCopies:
    def __init__(self, info, layer, parts, held, sems):
        self.info, self.layer, self.parts, self.held, self.sems = info, layer, parts, held, sems

    def own(self, slot, there):
        for at, (part, target) in enumerate(zip(self.parts, self.held)):
            source = part[1] if there else part[0]
            rows = source.shape[0]
            yield pltpu.make_async_copy(source, target.at[slot, pl.ds(0, rows)], self.sems.at[slot, at])

    def pieces(self, slot, step):
        at = 0
        for (_, _, near, other, begin, rows), held in zip(self.parts, self.held):
            members = near.shape[0]
            source_at = pl.multiple_of(begin + (step - 1) * rows, 16)
            for key in range(members):
                for source, core in ((near, self.info[CORE]), (other, 1 - self.info[CORE])):
                    target = pl.multiple_of((core * members + key) * rows, 16)
                    yield pltpu.make_async_copy(
                        source.at[key, pl.ds(source_at, rows)],
                        held.at[slot, pl.ds(target, rows)],
                        self.sems.at[slot, at],
                    )
                    at += 1

    def each(self, step, act):
        slot = step % 2

        def run(copies):
            for copy in copies:
                act(copy)

        there = self.info[CORE] != self.layer
        pl.when((step == 0) & there)(lambda: run(self.own(slot, True)))
        pl.when((step == 0) & jnp.logical_not(there))(lambda: run(self.own(slot, False)))
        pl.when(step > 0)(lambda: run(self.pieces(slot, step)))

    def start(self, step):
        self.each(step, lambda copy: copy.start())

    def turn(self, step, first, last):
        @pl.when(step == first)
        def _():
            self.start(step)

        @pl.when(step < last)
        def _():
            self.start(step + 1)

        self.each(step, lambda copy: copy.wait())
        return [held.at[step % 2] for held in self.held]


def pack_refs(spec, refs):
    return [tuple(refs[4 * at : 4 * at + 4]) + part for at, part in enumerate(spec)]


def fill_bias(info, bias):
    keys, rows = bias.shape
    key_pos = lax.broadcasted_iota(jnp.int32, (keys, rows), 0)
    query_pos = lax.broadcasted_iota(jnp.int32, (keys, rows), 1) + info[FIRST]
    allowed = (key_pos <= query_pos) & (key_pos < info[LENGTH])
    bias[...] = jnp.where(allowed, 0.0, masked_score)


def head_parts(heads, width, latent):
    at = (0, width, width + latent, width + 2 * latent)
    return [heads[lo:hi] for lo, hi in zip(at[:-1], at[1:])]


def attend_sets(keys, values_t, query, bias, heads):
    lane_head = lax.broadcasted_iota(jnp.int32, query.shape, 1) // HEAD_DIM
    mixed, sums = [], []
    for head in range(heads):
        query_here = jnp.where(lane_head == head, query, bf16(0))
        scores = dot_nt(keys, query_here) + bias
        peak = jnp.max(scores, axis=0, keepdims=True)
        expo = jnp.exp(scores - peak)
        total = jnp.sum(expo, axis=0, keepdims=True)
        part = dot_nn(values_t[head * HEAD_DIM : (head + 1) * HEAD_DIM], expo.astype(bf16))
        mixed.append(part * (1.0 / total))
        sums.append(peak + jnp.log(total))
    return jnp.concatenate(mixed, axis=0), jnp.concatenate(sums, axis=0)


def attend_first_kernel(
    info, x, lat_here, lat_there, heads_here, heads_there, gain_here, gain_there, out, normed, query_all, keys_all, values_t_all
):
    keys_count, width = x.shape
    latent = lat_here.shape[1]
    cols = heads_here.shape[1]
    heads = cols // HEAD_DIM
    rows = keys_count // out.shape[0]
    here = info[2] == 0
    gain = jnp.where(here, gain_here[0:1], gain_there[0:1])
    pack = jnp.where(here, heads_here[...], heads_there[...])
    w_latent = jnp.where(here, lat_here[...], lat_there[...])
    for block in range(keys_count // rows):
        here = slice(block * rows, (block + 1) * rows)
        value = x[here].astype(f32)
        normed[here] = (value * inverse_rms(value) * gain).astype(bf16)
    w_query, w_key, w_value = head_parts(pack, width, latent)
    query_all[...] = dot_nn(normed[...], w_query).astype(bf16) * bf16(HEAD_DIM**-0.5)
    lat = dot_nn(normed[...], w_latent).astype(bf16)
    keys_all[...] = dot_nn(lat, w_key).astype(bf16)
    values_t_all[...] = dot_nn(lat, w_value).astype(bf16).T
    for block in range(keys_count // rows):
        first = block * rows
        end = first + rows
        key_pos = lax.broadcasted_iota(jnp.int32, (end, rows), 0)
        query_pos = lax.broadcasted_iota(jnp.int32, (end, rows), 1) + first
        bias = jnp.where((key_pos <= query_pos) & (key_pos < info[0]), 0.0, masked_score)
        mixed, sums = attend_sets(keys_all[0:end], values_t_all[:, 0:end], query_all[first:end], bias, heads)
        high = sums.astype(bf16)
        low = (sums - high.astype(f32)).astype(bf16)
        at = info[1] ^ block
        out[at, 0:rows, :] = mixed.T.astype(bf16)
        out[at, rows:, :] = jnp.concatenate([high, low, jnp.zeros((16 - 2 * heads, rows), bf16)], axis=0)


def attend_out_kernel(
    spec, layer, info, x, m0, m1, m2, m3, gain, o0, o1, o2, o3, mixed_out, lse_out, residual, normed2, sets, outs, sems
):
    step = pl.program_id(0)
    rows, width = x.shape
    heads = lse_out.shape[1]
    copies = PackCopies(info, layer, pack_refs(spec, (o0, o1, o2, o3)), [outs], sems)
    w_out = copies.turn(step, 0, pl.num_programs(0) - 1)[0]

    @pl.when(step == 0)
    def _():
        residual[...] = x[...].astype(f32)
        for key, piece in enumerate((m0, m1, m2, m3)):
            sets[key ^ info[RANK] ^ info[PLANE]] = piece[...]

    mixed = sets[step, 0:rows, :]
    tail = sets[step, rows:, :].astype(f32)
    mixed_out[0] = mixed
    lse_out[0] = tail[0:heads] + tail[heads : 2 * heads]
    residual[...] += dot_nn(mixed, w_out[0 : mixed.shape[1]])

    @pl.when(step == pl.num_programs(0) - 1)
    def _():
        full = residual[...]
        normed2[...] = (full * inverse_rms(full) * gain[...]).astype(bf16)


def attend_kernel(
    spec, layer, info, x, normed, lat0, lat1, lat2, lat3, gain, h0, h1, h2, h3, o0, o1, o2, o3,
    mixed_out, lse_out, lat_out, residual, normed2, bias, heads_held, outs_held, sems,
):
    step = pl.program_id(0)
    rows, width = normed.shape
    latent = lat_out.shape[2]
    heads = lse_out.shape[1]
    parts = pack_refs(spec, (h0, h1, h2, h3, o0, o1, o2, o3))
    copies = PackCopies(info, layer, parts, [heads_held, outs_held], sems)
    w_heads, w_out = copies.turn(step, 0, pl.num_programs(0) - 1)

    @pl.when(step == 0)
    def _():
        fill_bias(info, bias)
        residual[...] = x[...].astype(f32)
        for key, piece in enumerate((lat0, lat1, lat2, lat3)):
            at = pl.multiple_of((info[RANK] ^ key) * rows, 16)
            for group in range(2):
                lat_out[group, pl.ds(at, rows), :] = piece[:, group * latent : (group + 1) * latent]

    w_query, w_key, w_value = head_parts(w_heads, width, latent)
    lat = lat_out[step // 2]
    query = dot_nn(normed[...], w_query).astype(bf16) * bf16(HEAD_DIM**-0.5)
    keys = dot_nn(lat, w_key).astype(bf16)
    values_t = dot_nn(lat, w_value).astype(bf16).T
    mixed, sums = attend_sets(keys, values_t, query, bias[...], heads)
    lse_out[0] = sums
    mixed = mixed.T.astype(bf16)
    mixed_out[0] = mixed
    residual[...] += dot_nn(mixed, w_out[0 : mixed.shape[1]])

    @pl.when(step == pl.num_programs(0) - 1)
    def _():
        full = residual[...]
        normed2[...] = (full * inverse_rms(full) * gain[...]).astype(bf16)


def attend_back_kernel(
    first_set, spec, layer, info, grad_branch, normed, lat, mixed_in, lse_in, h0, h1, h2, h3, o0, o1, o2, o3,
    grad_norm, grad_lat, keep, send, bias, heads_held, outs_held, sems, lat_sum,
):
    step = pl.program_id(0)
    rows, width = normed.shape
    keys_count, latent = grad_lat.shape
    cols = heads_held.shape[2]
    scale = HEAD_DIM**-0.5
    members = keep.shape[0]
    parts = pack_refs(spec, (h0, h1, h2, h3, o0, o1, o2, o3))
    copies = PackCopies(info, layer, parts, [heads_held, outs_held], sems)
    w_heads, w_out = copies.turn(step + first_set, first_set, first_set + pl.num_programs(0) - 1)

    @pl.when(step == 0)
    def _():
        fill_bias(info, bias)
        grad_norm[...] = jnp.zeros_like(grad_norm)
        lat_sum[...] = jnp.zeros_like(lat_sum)

    w_query, w_key, w_value = head_parts(w_heads, width, latent)
    here = lat[0]
    query = dot_nn(normed[...], w_query).astype(bf16) * bf16(scale)
    keys = dot_nn(here, w_key).astype(bf16)
    keys_t = keys.T
    values = dot_nn(here, w_value).astype(bf16)
    mixed = mixed_in[0]
    grad_mixed = dot_nt(grad_branch[...], w_out[0:cols]).astype(bf16)
    centre = (grad_mixed.astype(f32) * mixed.astype(f32)).T
    lane_head = lax.broadcasted_iota(jnp.int32, (rows, cols), 1) // HEAD_DIM
    grad_keys = jnp.zeros((keys_count, cols), f32)
    grad_values = jnp.zeros((keys_count, cols), f32)
    grad_query_parts = []
    for head in range(cols // HEAD_DIM):
        mine = slice(head * HEAD_DIM, (head + 1) * HEAD_DIM)
        query_here = jnp.where(lane_head == head, query, bf16(0))
        grad_here = jnp.where(lane_head == head, grad_mixed, bf16(0))
        scores = dot_nt(keys, query_here) + bias[...]
        probs = jnp.exp(scores - lse_in[0, head : head + 1, :])
        grad_probs = dot_nt(values, grad_here)
        inner = jnp.sum(centre[mine], axis=0, keepdims=True)
        grad_scores = (probs * (grad_probs - inner)).astype(bf16)
        grad_values += dot_nn(probs.astype(bf16), grad_here)
        grad_keys += dot_nn(grad_scores, query_here)
        grad_query_parts.append(dot_nn(keys_t[mine], grad_scores) * scale)
    grad_keys = grad_keys.astype(bf16)
    grad_values = grad_values.astype(bf16)
    grad_query = jnp.concatenate(grad_query_parts, axis=0).T.astype(bf16)
    grad_norm[...] += dot_nt(grad_query, w_query)
    lat_sum[...] += dot_nt(grad_keys, w_key) + dot_nt(grad_values, w_value)
    halves = (
        (dot_tn(normed[...], grad_query), dot_tn(here, grad_keys)),
        (dot_tn(here, grad_values), dot_tn(grad_branch[...], mixed)),
    )
    for half, results in enumerate(halves):
        for out, wanted in ((keep, half), (send, 1 - half)):

            @pl.when(info[CORE] == wanted)
            def _(out=out, results=results):
                at = 0
                for result in results:
                    size = result.shape[0] // members
                    for member in range(members):
                        out[member, 0, at : at + size, :] = result[member * size : (member + 1) * size].astype(bf16)
                    at += size

    @pl.when(step == pl.num_programs(0) - 1)
    def _():
        grad_lat[...] = lat_sum[...].astype(bf16)


def attend_first_call(info, x, lat_here, lat_there, heads_here, heads_there, gain_here, gain_there, keys, blocks):
    width = x.shape[1]
    latent = lat_here.shape[1] // 2
    cols = heads_here.shape[1]
    outs = [like((blocks, keys // blocks + 16, cols), bf16)]
    arrays = (x, lat_here, lat_there, heads_here, heads_there, gain_here, gain_there)
    group = pl.BlockSpec((width, latent), lambda i, info: (0, info[3]))
    return kernel_call(
        attend_first_kernel,
        info,
        arrays,
        (1,),
        [pl.BlockSpec((keys, width), lambda i, info: (info[2], 0)), group, group] + [whole(v) for v in arrays[3:]],
        [whole(o) for o in outs],
        outs,
        [pltpu.VMEM((keys, width), bf16)] + [pltpu.VMEM((keys, cols), bf16)] * 2 + [pltpu.VMEM((cols, keys), bf16)],
        "attend_first",
        2 * keys * width * (cols + latent) + 4 * keys * latent * cols + 4 * keys * keys * cols * 3,
        keys * keys * 3,
    )[0]


def pack_in(*parts):
    arrays = sum((tuple(part[0:4]) for part in parts), ())
    spec = tuple(tuple(part[4:]) for part in parts)
    members = parts[0][2].shape[0]
    scratch = [pltpu.VMEM((2, 2 * members * part[5], part[0].shape[1]), bf16) for part in parts]
    scratch.append(pltpu.SemaphoreType.DMA((2, 2 * members * len(parts))))
    return arrays, spec, [pl.BlockSpec(memory_space=pl.ANY)] * len(arrays), scratch


def attend_out_call(info, layer, x, messages, outs_w, gain):
    rows, width = x.shape
    arrays, spec, specs, scratch = pack_in(outs_w)
    sets = 4
    cols = messages[0].shape[1]
    heads = cols // HEAD_DIM
    outs = [
        like((sets, rows, cols), bf16),
        like((sets, heads, rows), f32),
        like((rows, width), f32),
        like((rows, width), bf16),
    ]
    return kernel_call(
        functools.partial(attend_out_kernel, spec, layer),
        info,
        (x, *messages, gain) + arrays,
        (sets,),
        [whole(x)] + [whole(m) for m in messages] + [whole(gain)] + specs,
        [lead(outs[0]), lead(outs[1]), whole(outs[2]), whole(outs[3])],
        outs,
        [pltpu.VMEM((sets,) + messages[0].shape, bf16)] + scratch,
        "attend_out",
        2 * sets * rows * width * cols,
    )


def attend_call(info, layer, x, normed, lats, pack, gain):
    rows, width = normed.shape
    arrays, spec, specs, scratch = pack_in(*pack)
    sets = 4
    cols = arrays[0].shape[1]
    latent = lats[0].shape[1] // 2
    keys = rows * len(lats)
    heads = cols // HEAD_DIM
    outs = [
        like((sets, rows, cols), bf16),
        like((sets, heads, rows), f32),
        like((2, keys, latent), bf16),
        like((rows, width), f32),
        like((rows, width), bf16),
    ]
    return kernel_call(
        functools.partial(attend_kernel, spec, layer),
        info,
        (x, normed, *lats, gain) + arrays,
        (sets,),
        [whole(x), whole(normed)] + [whole(v) for v in lats] + [whole(gain)] + specs,
        [lead(outs[0]), lead(outs[1])] + [whole(o) for o in outs[2:]],
        outs,
        [pltpu.VMEM((keys, rows), f32)] + scratch,
        "attend",
        2 * sets * rows * (2 * keys * cols * heads + width * cols * 2) + 4 * sets * keys * latent * cols,
        sets * heads * keys * rows,
    )


def attend_back_call(first_set, info, layer, grad_branch, normed, lat, pack, mixed, lse, members):
    rows, width = normed.shape
    arrays, spec, specs, scratch = pack_in(*pack)
    cols = arrays[0].shape[1]
    piece_rows = (arrays[0].shape[0] + width) // members // 2
    sets = 2
    keys, latent = lat.shape[1:]
    heads = cols // HEAD_DIM
    group = pl.BlockSpec((1, keys, latent), lambda i, info: (first_set // 2, 0, 0))
    outs = [
        like((rows, width), f32),
        like((keys, latent), bf16),
        like((members, sets, piece_rows, cols), bf16),
        like((members, sets, piece_rows, cols), bf16),
    ]
    summed = pl.BlockSpec((members, 1, piece_rows, cols), lambda i, info: (0, i, 0, 0))
    mine = [pl.BlockSpec((1,) + v.shape[1:], lambda i, info: (i + first_set, 0, 0)) for v in (mixed, lse)]
    return kernel_call(
        functools.partial(attend_back_kernel, first_set, spec, layer),
        info,
        (grad_branch, normed, lat, mixed, lse) + arrays,
        (sets,),
        [whole(grad_branch), whole(normed), group] + mine + specs,
        [whole(outs[0]), whole(outs[1]), summed, summed],
        outs,
        [pltpu.VMEM((keys, rows), f32)] + scratch + [pltpu.VMEM((keys, latent), f32)],
        "attend_back",
        2 * sets * rows * (5 * keys * cols * heads + width * cols * 5) + 16 * sets * keys * latent * cols,
        sets * heads * keys * rows,
    )


def feed_shards(spec, layer, info, refs, weights, sems, use):
    here, there, pieces = refs[0:3], refs[3:6], refs[6:12]
    hidden = here[0].shape[0]

    def run(act, far):
        if not far:
            for wanted, sources in ((True, here), (False, there)):

                @pl.when((info[CORE] == layer) == wanted)
                def _(sources=sources):
                    for kind, source in enumerate(sources):
                        act(pltpu.make_async_copy(source, weights.at[0, kind, pl.ds(0, hidden)], sems.at[kind]))

            return
        at = 3
        for kind, (begin, rows) in enumerate(spec):
            members = pieces[2 * kind].shape[0]
            for key in range(members):
                for source, core in ((pieces[2 * kind], info[CORE]), (pieces[2 * kind + 1], 1 - info[CORE])):
                    target = pl.multiple_of((core * members + key) * rows, 16)
                    act(
                        pltpu.make_async_copy(
                            source.at[key, pl.ds(begin, rows)], weights.at[1, kind, pl.ds(target, rows)], sems.at[at]
                        )
                    )
                    at += 1

    run(lambda copy: copy.start(), False)
    run(lambda copy: copy.start(), True)
    run(lambda copy: copy.wait(), False)
    use(0, [weights[0, kind, 0:hidden] for kind in range(3)])
    run(lambda copy: copy.wait(), True)
    use(1, [weights[1, kind, 0:hidden] for kind in range(3)])


def feed_kernel(spec, layer, info, value, *refs):
    total_out, saved, weights, sems, total = refs[12:]

    def use(shard, held):
        gate = dot_nt(value[...], held[0])
        up = dot_nt(value[...], held[1])
        saved[shard, 0] = gate.astype(bf16)
        saved[shard, 1] = up.astype(bf16)
        hidden = (gate * jax.nn.sigmoid(gate) * up).astype(bf16)
        part = dot_nn(hidden, held[2])
        if shard == 0:
            total[...] = part
        else:
            total_out[...] = (total[...] + part).astype(total_out.dtype)

    feed_shards(spec, layer, info, refs[0:12], weights, sems, use)


def feed_back_kernel(spec, layer, info, value, saved, *refs):
    total_out, keep, send, weights, sems, total = refs[12:]

    width = saved.shape[3]

    def use(shard, held):
        grad_hidden = dot_nt(value[...], held[2])
        gate = saved[shard, 0].astype(f32)
        up = saved[shard, 1].astype(f32)
        sigma = jax.nn.sigmoid(gate)
        silu = gate * sigma
        grad_gate = (grad_hidden * up * sigma * (1.0 + gate * (1.0 - sigma))).astype(bf16)
        grad_up = (grad_hidden * silu).astype(bf16)
        hidden = (silu * up).astype(bf16)
        mine = info[CORE] == layer if shard == 0 else info[CORE] != layer
        for out, wanted in ((keep, mine), (send, jnp.logical_not(mine))):

            @pl.when(wanted)
            def _(out=out):
                out[0, :, 0:width] = grad_gate
                out[1, :, 0:width] = grad_up
                out[2, :, 0:width] = hidden

        part = dot_nn(grad_gate, held[0]) + dot_nn(grad_up, held[1])
        if shard == 0:
            total[...] = part
        else:
            total_out[...] = (total[...] + part).astype(total_out.dtype)

    feed_shards(spec, layer, info, refs[0:12], weights, sems, use)


def feed_weights_kernel(hidden, info, *refs):
    lefts, rights, out, turned = refs[0:8], refs[8:12], refs[12], refs[13]
    kind = pl.program_id(0)
    rows = lefts[0].shape[0]
    members, _, size, lanes = out.shape

    @pl.when(kind == 0)
    def _():
        for at in range(2):
            for block in range(4):
                turned[at, :, block * rows : (block + 1) * rows] = lefts[4 * at + block][...].T

    right = jnp.concatenate([r[0] for r in rights], axis=0)
    left = turned[kind // 2]
    for first in range(0, hidden, 256):
        end = min(first + 256, hidden)
        result = dot_nn(left, right[:, first:end]).astype(bf16)
        for member in range(members):
            out[member, 0, :, first:end] = result[member * size : (member + 1) * size]
    out[:, :, :, hidden:] = jnp.zeros((members, 1, size, lanes - hidden), bf16)


def whole_lanes(count):
    return -(-count // 128) * 128


def feed_in(feed_w):
    here, there, pieces = feed_w
    arrays = (*here, *there, *sum((part[0:2] for part in pieces), ()))
    spec = tuple(part[2:4] for part in pieces)
    members, _, width = pieces[0][0].shape
    scratch = [
        pltpu.VMEM((2, 3, 2 * members * pieces[0][3], width), bf16),
        pltpu.SemaphoreType.DMA((3 + 6 * members,)),
    ]
    return arrays, spec, [pl.BlockSpec(memory_space=pl.ANY)] * len(arrays), scratch


def feed_call(info, layer, value, feed_w, dtype):
    rows, width = value.shape
    arrays, spec, specs, scratch = feed_in(feed_w)
    hidden = arrays[0].shape[0]
    outs = [like((rows, width), dtype), like((2, 2, rows, hidden), bf16)]
    return kernel_call(
        functools.partial(feed_kernel, spec, layer),
        info,
        (value,) + arrays,
        (1,),
        [whole(value)] + specs,
        [whole(o) for o in outs],
        outs,
        scratch + [pltpu.VMEM((rows, width), f32)],
        "feed",
        2 * 2 * 3 * rows * width * hidden,
    )


def feed_back_call(info, layer, value, saved, feed_w, dtype):
    rows, width = value.shape
    arrays, spec, specs, scratch = feed_in(feed_w)
    hidden = arrays[0].shape[0]
    outs = [like((rows, width), dtype)] + [like((3, rows, whole_lanes(hidden)), bf16)] * 2
    return kernel_call(
        functools.partial(feed_back_kernel, spec, layer),
        info,
        (value, saved) + arrays,
        (1,),
        [whole(value), whole(saved)] + specs,
        [whole(o) for o in outs],
        outs,
        scratch + [pltpu.VMEM((rows, width), f32)],
        "feed_back",
        2 * 2 * 3 * rows * width * hidden,
    )


def feed_weights_call(info, lefts, rights, members, hidden):
    rows, width = lefts[0].shape
    kinds, _, lanes = rights[0].shape
    shape = (members, kinds, width // members, lanes)
    outs = [like(shape, bf16)]
    return kernel_call(
        functools.partial(feed_weights_kernel, hidden),
        info,
        (*lefts, *rights),
        (kinds,),
        [whole(v) for v in lefts] + [lead(r) for r in rights],
        [pl.BlockSpec((members, 1) + shape[2:], lambda i, info: (0, i, 0, 0))],
        outs,
        [pltpu.VMEM((2, width, 4 * rows), bf16)],
        "feed_weights",
        2 * kinds * 4 * rows * width * hidden,
    )[0]


def shards(inputs, cotangent, lengths, w_query, w_latent, w_key, w_value, w_out, gains, w_gate, w_up, w_down):
    core = lax.axis_index("section")
    z = lax.axis_index("tensor")
    d = lax.axis_index("dp")
    planes = lax.axis_size("tensor")
    dp = lax.axis_size("dp")
    seqs = lengths.shape[0]
    bucket = inputs.shape[0] // seqs
    width = inputs.shape[1]
    layers = 2
    per_seq = planes // seqs * 2
    rows = bucket // per_seq
    rank = (z % (planes // seqs)) * 2 + core
    seq = z // (planes // seqs)
    first = rank * rows
    length = lax.dynamic_index_in_dim(lengths, seq, 0, False)
    info = jnp.stack([length, first, core, d, rank, z]).astype(jnp.int32)
    live = (lax.broadcasted_iota(jnp.int32, (rows, 1), 0) + first < length).astype(f32)
    row_at = seq * bucket + first
    own_in = lax.dynamic_slice_in_dim(inputs, row_at, rows, 0)
    own_target = lax.dynamic_slice_in_dim(cotangent, row_at, rows, 0)
    latent = w_latent.shape[2] // 2
    far_group = z // (planes // 2)

    cols = w_query.shape[2]
    hidden_cols = w_gate.shape[2]
    heads_here = jnp.concatenate([w_query[0], w_key[0], w_value[0]], axis=0)
    heads_there = core_swap(heads_here)
    lat_here = w_latent[0]
    lat_there = core_swap(lat_here)
    gain_here = gains[0]
    gain_there = core_swap(gain_here)
    out_here = w_out[0]
    feed_here = [w_gate[0].T, w_up[0].T, w_down[0]]
    head_rows, out_rows, feed_rows = heads_here.shape[0], out_here.shape[0], hidden_cols

    def piece_rows(count):
        return -(-count // (2 * dp * 16)) * 16

    def piece_of(value, side):
        rows_each = piece_rows(value.shape[0])
        value = jnp.pad(value, ((0, rows_each * 2 * dp - value.shape[0]), (0, 0)))
        return lax.dynamic_slice_in_dim(value, (side * dp + d) * rows_each, rows_each, 0)

    def feed_and_out(side):
        return jnp.concatenate([piece_of(v, side) for v in [out_here] + feed_here], axis=0)

    def layers_of(mine, received):
        return [jnp.where(core == layer, mine, received) for layer in range(layers)]

    main_pieces = layers_of(feed_and_out(core), core_swap(feed_and_out(1 - core)))
    head_pieces = layers_of(piece_of(heads_here, core), core_swap(piece_of(heads_here, 1 - core)))
    head_piece, out_piece, feed_piece = piece_rows(head_rows), piece_rows(out_rows), piece_rows(feed_rows)
    over = [z_swap(main_pieces[0][:out_piece], step) for step in range(1, lax.axis_size("tensor"))]
    feed_far = z_swap(main_pieces[0][out_piece:], planes // 2)
    out_there = core_swap(tie(out_here, feed_far))
    feed_there = [core_swap(tie(v, feed_far)) for v in feed_here]
    latents_w = [jnp.where(core == layer, lat_here, lat_there) for layer in range(layers)]
    gains_all = [jnp.where(core == layer, gain_here, gain_there) for layer in range(layers)]

    def over_planes(piece):
        return [z_swap(piece, step) for step in range(1, planes)]

    def gather_near(parts, *before):
        return plane_gather(jnp.concatenate([tie(v, *before) for v in parts], axis=0))

    def gather(parts, before=(), after=()):
        near = gather_near(parts, *before)
        return near, core_swap(tie(near, *after))

    def gather_slow(parts, before=()):
        return lax.all_gather(jnp.concatenate([tie(v, *before) for v in parts], axis=0), "dp", axis=0, tiled=False)

    def by_group(value):
        return by_plane(value, far_group)

    def normalise(x, gain):
        x = x.astype(f32)
        return (x * inverse_rms(x) * gain).astype(bf16)

    def first_attention(*after):
        scalars = jnp.stack([lax.dynamic_index_in_dim(lengths, core, 0, False), z, core, far_group]).astype(jnp.int32)
        out = attend_first_call(
            scalars, inputs, lat_here, lat_there, tie(heads_here, *after), heads_there, gain_here, gain_there, bucket, per_seq
        )
        messages = []
        for way in range(per_seq):
            pairs = []
            for side in range(2):
                for plane in range(planes):
                    to = plane ^ way
                    target = (to % 2) * planes + side * (planes // seqs) + to // 2
                    pairs.append((side * planes + plane, target))
            messages.append(lax.ppermute(out[way], ("section", "tensor"), pairs))
        return out, messages

    def first_latents(*after):
        all_rows = tie(lax.dynamic_slice_in_dim(inputs, seq * bucket, bucket, 0), *after)
        lat = dot_nn(normalise(all_rows, gains_all[0][0]), latents_w[0]).astype(bf16)
        return by_group(jnp.stack([lat[:, :latent], lat[:, latent:]]))

    def attention(layer, x, pack):
        gain = gains_all[layer]
        normed = normalise(x, gain[0])
        own_lat = dot_nn(normed, latents_w[layer]).astype(bf16)
        own_lat = jnp.where(
            far_group == 1, jnp.concatenate([own_lat[:, latent:], own_lat[:, :latent]], axis=1), own_lat
        )
        far_lat = z_swap(own_lat, 1)
        lats = (own_lat, core_swap(own_lat), far_lat, core_swap(far_lat))
        mixed, lse, lat, residual, normed2 = attend_call(info, layer, x, normed, lats, pack, gain[1][None])
        return normed, lat, mixed, lse, residual, normed2

    def feed_own(layer, normed2, feed_w):
        far_normed2 = z_swap(normed2, 1)
        part, saved = feed_call(info, layer, normed2, feed_w, f32)
        return part, saved, tie(far_normed2, part)

    def feed_rest(layer, residual, part, far_normed2, feed_w):
        far_part, far_saved = feed_call(info, layer, far_normed2, feed_w, bf16)
        feed = part + z_swap(far_part, 1).astype(f32)
        return (live * (residual + feed)).astype(bf16), far_saved

    def finish_core(firsts, seconds):
        mine = jnp.where(core == 0, firsts, seconds)
        other = core_swap(jnp.where(core == 0, seconds, firsts))
        return jnp.where(core == 0, jnp.stack([mine, other]), jnp.stack([other, mine]))

    def backward(layer, grad_out, x, normed, lat, mixed, lse, residual, feed_kept, pack, feed_w, hooks):
        normed2, far_normed2, saved, far_saved = feed_kept
        gain = gains_all[layer]
        grad_res = live * grad_out.astype(f32)
        grad_feed = grad_res.astype(bf16)
        far_feed = z_swap(grad_feed, 1)
        part, *rights = feed_back_call(info, layer, grad_feed, saved, feed_w, f32)
        far_part, *far_rights = feed_back_call(info, layer, far_feed, far_saved, feed_w, bf16)
        back = z_swap(far_part, 1)
        lefts = [normed2, far_normed2, core_swap(normed2), core_swap(far_normed2)]
        lefts += [grad_feed, far_feed, core_swap(grad_feed), core_swap(far_feed)]
        rights = [rights[0], far_rights[0], core_swap(rights[1]), core_swap(far_rights[1])]
        feed_grads = feed_weights_call(info, lefts, rights, dp, hidden_cols)
        back = tie(back, feed_grads, *hooks[0]())
        grad_norm2 = part + back.astype(f32)
        grad_residual, gain_second = norm_back(residual, gain[1], grad_norm2)
        grad_residual = grad_residual + grad_res
        grad_branch = grad_residual.astype(bf16)

        feed_parts = lax.all_to_all(feed_grads, "dp", 0, 0)
        grad_norms = []
        lat_parts = []
        pack_parts_here = []
        for first_set in (2, 0):
            if first_set == 0:
                grad_branch = tie(grad_branch, grad_norms[0], *hooks[1](grad_branch))
            grad_norm, grad_lat, pack_keep, pack_send = attend_back_call(
                first_set, info, layer, grad_branch, normed, lat, pack, mixed, lse, dp
            )
            grad_norms.append(grad_norm)
            pack_parts_here.append((pack_keep, core_swap(pack_send)))
            grad_lat = grad_lat.reshape(per_seq // 2, 2, rows, latent)
            total = lax.dynamic_index_in_dim(grad_lat, core, 1, False) + core_swap(
                lax.dynamic_index_in_dim(grad_lat, 1 - core, 1, False)
            )
            near = rank // 2
            total = lax.dynamic_index_in_dim(total, near, 0, False) + z_swap(
                lax.dynamic_index_in_dim(total, 1 - near, 0, False), 1
            )
            lat_parts.append(total)
        if layer == 0:
            lat_parts[1] = tie(lat_parts[1], *hooks[2]())
        else:
            lat_parts[1] = tie(lat_parts[1], feed_parts)
        lat_own = by_group(jnp.stack(lat_parts[::-1]))
        lat_own = jnp.concatenate([lat_own[0], lat_own[1]], axis=1)
        grad_norm = grad_norms[0] + grad_norms[1] + dot_nt(lat_own, latents_w[layer])
        grad_x, gain_first = norm_back(x.astype(f32), gain[0], grad_norm)
        grad_x = (grad_x + grad_residual).astype(bf16)

        lat_w = dot_tn(normed, lat_own).astype(bf16).reshape(planes, dp, width // planes // dp * 2, latent)
        gain_g = jnp.stack([gain_first, gain_second]).astype(bf16)
        gain_g = gain_g.reshape(2, planes, dp, -1).transpose(1, 2, 0, 3).reshape(planes, dp, 1, -1)
        gain_g = jnp.pad(gain_g, ((0, 0), (0, 0), (0, 31), (0, latent - gain_g.shape[3])))
        small = jnp.swapaxes(by_plane(jnp.concatenate([lat_w, gain_g], axis=2), z), 0, 1)
        half = small.shape[2] // 2
        small_keep = lax.dynamic_slice_in_dim(small, core * half, half, 2)
        small_send = lax.dynamic_slice_in_dim(small, (1 - core) * half, half, 2)
        small_parts = (small_keep, core_swap(small_send))

        feed_sums = jnp.sum(tie(feed_parts, grad_x).astype(f32), axis=0).astype(bf16)
        pack_total = jnp.concatenate([a + b for a, b in pack_parts_here[::-1]], axis=1)
        small_total = small_parts[0] + small_parts[1]
        if layer == 0:
            pack_total = tie(pack_total, grad_x)
            small_total = tie(small_total, grad_x)
        pack_parts = lax.all_to_all(jnp.concatenate([pack_total, small_total], axis=2), "dp", 0, 0)

        def finish_feed():
            pairs = [((1 - layer) * planes + i, layer * planes + (i ^ (planes // 2))) for i in range(planes)]
            return feed_sums.astype(f32) + lax.ppermute(feed_sums, ("section", "tensor"), pairs).astype(f32)

        def finish_pack(*after):
            parts = tie(pack_parts, *after)
            sums = jnp.sum(parts.astype(f32), axis=0).astype(bf16)
            sums = sums[0::2] + z_swap(sums[1::2], 1)
            return sums[0] + z_swap(sums[1], 2)

        return grad_x, finish_feed, finish_pack

    first_out, messages = first_attention(feed_far)
    main0 = gather(over + [feed_far], (), messages)
    outs0 = (out_here, out_there) + main0 + (0, out_piece)
    at = (planes - 1) * out_piece
    feed0 = (feed_here, feed_there, [main0 + (at + k * feed_piece, feed_piece) for k in range(3)])
    lat0 = first_latents()
    mixed0, lse0, residual0, normed2_0 = attend_out_call(info, 0, tie(own_in, lat0), messages, outs0, gains_all[0][1][None])
    near_heads1 = gather_slow(over_planes(head_pieces[1]), (first_out,))
    part0, saved0, far_normed2 = feed_own(0, normed2_0, feed0)
    far_normed2 = tie(far_normed2, near_heads1)
    main_piece = tie(main_pieces[1], *messages)
    far_main = over_planes(main_piece[:out_piece]) + [z_swap(main_piece[out_piece:], planes // 2)]
    near1 = gather_near(far_main, part0)
    out0, far_saved0 = feed_rest(0, residual0, part0, far_normed2, feed0)
    kept0 = [normed2_0, far_normed2, saved0, far_saved0]
    main1 = near1, core_swap(tie(near1, out0))
    heads1 = (heads_here, heads_there, near_heads1, core_swap(near_heads1), 0, head_piece)
    outs1 = (out_here, out_there) + main1 + (0, out_piece)
    feed1 = (feed_here, feed_there, [main1 + (at + k * feed_piece, feed_piece) for k in range(3)])

    normed1, lat1, mixed1, lse1, residual1, normed2_1 = attention(1, out0, (heads1, outs1))
    part1, saved1, far_normed2 = feed_own(1, normed2_1, feed1)
    out1, far_saved1 = feed_rest(1, residual1, part1, far_normed2, feed1)
    kept1 = [normed2_1, far_normed2, saved1, far_saved1]
    far_heads = over_planes(head_pieces[0])
    near_heads0 = gather_slow(far_heads, (normed2_1,))
    heads0 = (heads_here, heads_there, near_heads0, core_swap(tie(near_heads0, out1)), 0, head_piece)

    def gather_rows(own):
        return lax.all_gather(own, "tensor", axis=0, tiled=False)

    def finish_rows(firsts, seconds):
        mine = jnp.where(core == 0, firsts, seconds)
        other = core_swap(jnp.where(core == 0, seconds, firsts))
        both = jnp.where(core == 0, jnp.stack([mine, other], axis=1), jnp.stack([other, mine], axis=1))
        return both.reshape(planes * 2 * rows, width)

    rows_out = [gather_rows(out0), gather_rows(out1)]
    grad1, finish_feed1, finish_pack1 = backward(
        1, own_target, out0, normed1, lat1, mixed1, lse1, residual1, kept1, (heads1, outs1), feed1,
        [lambda: (rows_out[0],), lambda token: ()],
    )
    normed0 = normalise(own_in, gains_all[0][0])
    later = {}

    def during_attention(token):
        later["feed"] = finish_feed1()
        return (later["feed"],)

    def after_attention():
        later["pack"] = finish_pack1()
        later["grad"] = gather_rows(grad1)
        return (later["pack"], later["grad"])

    grad0, finish_feed0, finish_pack0 = backward(
        0, grad1, own_in, normed0, lat0, mixed0, lse0, residual0, kept0, (heads0, outs0), feed0,
        [lambda: (rows_out[1],), during_attention, after_attention],
    )
    rows_grad0 = gather_rows(grad0)
    layer_outputs = finish_rows(*rows_out)
    input_grads = finish_rows(rows_grad0, later["grad"])

    feed_final0 = finish_feed0()
    feed_total = jnp.where(core == 0, feed_final0, later["feed"])
    gate_t, up_t, down_t = feed_total[:, :, :hidden_cols]
    halves = finish_core(finish_pack0(feed_final0), later["pack"]).astype(f32)
    main = (head_rows + width) // dp // 2
    query_t, key_t = halves[0, : width // dp], halves[0, width // dp : main]
    value_t, out_t = halves[1, : latent // dp], halves[1, latent // dp : main]
    small = halves[:, main:].reshape(-1, latent)
    lat_rows = width // planes // dp * 2
    lat_t = small[:lat_rows].reshape(lat_rows // 2, 2 * latent)
    gain_t = small[lat_rows, : 2 * width // planes // dp].reshape(2, -1)
    return (
        layer_outputs[None],
        input_grads[None],
        query_t[None],
        lat_t[None],
        key_t[None],
        value_t[None],
        out_t.T[None],
        gain_t[None],
        gate_t[None],
        up_t[None],
        down_t.T[None],
    )


def solution(mesh):
    placed = (
        P("dp", None),
        P("dp", None),
        P("dp"),
        P("section", None, "tensor"),
        P("section", None, None),
        P("section", None, "tensor"),
        P("section", None, "tensor"),
        P("section", "tensor", None),
        P("section", None, None),
        P("section", None, "tensor"),
        P("section", None, "tensor"),
        P("section", "tensor", None),
    )
    return jax.shard_map(
        shards,
        mesh=mesh,
        in_specs=placed,
        out_specs=(
            P("section", "dp", None),
            P("section", "dp", None),
            P("section", "dp", "tensor"),
            P("section", ("tensor", "dp"), None),
            P("section", "dp", "tensor"),
            P("section", "dp", "tensor"),
            P("section", "tensor", "dp"),
            P("section", None, ("tensor", "dp")),
            P("section", "dp", "tensor"),
            P("section", "dp", "tensor"),
            P("section", "tensor", "dp"),
        ),
        check_vma=False,
    )
```

time: 839 us -> 689 us (0.82)
  local copies, waits for them, and re-layouts: 153 us -> 54.5 us
  starting transfers between devices: 158 us -> 123 us
  other arithmetic: 122 us -> 87.2 us
  between operations: 3.1 us -> 15.8 us
    ppermute x48 -> x6, waiting for transfers between devices: 110 us -> 27.2 us  [the longest x2 18.2 us: finish_feed(): lax.ppermute(feed_sums, ('section', 'tensor'), pairs).astype(f32)]
    ppermute x48 -> x6, starting transfers between devices: 61.2 us -> 17.7 us  [the longest x2 9.24 us: finish_feed(): lax.ppermute(feed_sums, ('section', 'tensor'), pairs).astype(f32)]
    slice x24 -> x9, local copies, waits for them, and re-layouts: 43 us -> 5.09 us  [the longest x2 2.13 us: finish_pack(): sums = sums[0::2] + z_swap(sums[1::2], 1)]
    ppermute x26 -> x31, waiting for transfers between devices: 77.4 us -> 114 us  [z_swap(): return lax.ppermute(value, 'tensor', [(i, i ^ step) for i in range(count)])]
    all_to_all x0 -> x6, waiting for transfers between devices: none -> 29.4 us  [the longest x2 16.5 us: backward(): feed_parts = lax.all_to_all(feed_grads, 'dp', 0, 0)]
    add x31 -> x15, other arithmetic: 41.2 us -> 14.2 us  [the longest x4 10.5 us: backward(): a + b]
    ppermute x11 -> x0, local copies, waits for them, and re-layouts: 25.5 us -> none  [the longest x3 14.9 us: core_swap(): return lax.ppermute(value, 'section', [(0, 1), (1, 0)])]
    all_to_all x0 -> x6, starting transfers between devices: none -> 25.4 us  [the longest x2 10 us: backward(): feed_parts = lax.all_to_all(feed_grads, 'dp', 0, 0)]
  transfers between devices with their start and end apart: 96 -> 89, of which waited for: 20 -> 30; matrix products, arithmetic and copies ran while one was open for 29% -> 20% of each run, Pallas kernels for 19% -> 29%
where the time goes in v2:
time: 689 us; the launch traced here: 678 us
  Pallas kernels  197 us (29%)
  waiting for transfers between devices  187 us (27%)
  starting transfers between devices  123 us (18%)
  other arithmetic  87.2 us (13%)
  local copies, waits for them, and re-layouts  54.5 us (8%)
  between operations  15.8 us (2%)
  matrix products  13.1 us (2%)
    pallas_call x17, Pallas kernels, kernel_call(): pl.pallas_call(kernel, grid_spec=pltpu.PrefetchScalarGridSpec(num_scalar_...  197 us
    ppermute x31, waiting for transfers between devices, z_swap(): return lax.ppermute(value, 'tensor', [(i, i ^ step) for i in range(count)])  114 us
    ppermute x31, starting transfers between devices, z_swap(): return lax.ppermute(value, 'tensor', [(i, i ^ step) for i in range(count)])  39.6 us
    ppermute x40, starting transfers between devices, core_swap(): return lax.ppermute(value, 'section', [(0, 1), (1, 0)])  38.6 us
    ppermute x2, waiting for transfers between devices, finish_feed(): lax.ppermute(feed_sums, ('section', 'tensor'), pairs).astype(f32)  18.2 us
    all_to_all x2, waiting for transfers between devices, backward(): feed_parts = lax.all_to_all(feed_grads, 'dp', 0, 0)  16.5 us
    unnamed x128, local copies, waits for them, and re-layouts  16.3 us
  transfers between devices with their start and end apart: 89, of which 30 were waited for; matrix products, arithmetic and copies ran while one was open for 20% of the time, Pallas kernels for 29%

profile of v2, /device:TPU:1, one launch (start us, length us, event | category | flops | bytes accessed | tf_op | source)
XLA Modules:
  0.0 677.6 jit_solution(1662487206580768944)
XLA Ops:
  21.2 10.2 %collective-permute-done.10 = bf16[32,1024]{1,0:T(8,128)(2,1)S(1)} collective-permute-done((bf16[32,1024]{1,0:T(8,128)(2,1)S(1)}, bf16[32,1024]{1,0:T(8,128)(2,1)S(1)}, u32[]{:S(2)}, u32[]{:S(2)}) %collective-permute-start.10) | collective-permute-done | bytes 65568 | tf_op jit(solution)/shard_map/ppermute | solution.py:35
  31.4 16.5 %collective-permute-done.11 = bf16[32,1024]{1,0:T(8,128)(2,1)S(1)} collective-permute-done((bf16[32,1024]{1,0:T(8,128)(2,1)S(1)}, bf16[32,1024]{1,0:T(8,128)(2,1)S(1)}, u32[]{:S(2)}, u32[]{:S(2)}) %collective-permute-start.11) | collective-permute-done | bytes 65568 | tf_op jit(solution)/shard_map/ppermute | solution.py:35
  50.0 3.8 all-to-all-start
  60.5 13.5 %attend_first.1 = bf16[4,272,256]{2,1,0:T(8,128)(2,1)} custom-call(s32[4]{0:T(128)} %pad_add_fusion.info, bf16[2048,1024]{1,0:T(8,128)(2,1)} %x.11, bf16[1024,512]{1,0:T(8,128)(2,1)} %bitcast.214, bf16[1024,512]{1,0:T(8,128)(2,1)} %collective-permute-done.1.lat_there, bf16[1536,256]{1,0:T(8,128)(2,1)} %pad_maximum_fusion.3.heads_here.h0, ...), custom_call_target="tpu_custom_call" | custom-call | flops 4563402752 | bytes 8437760 | tf_op jit(solution)/shard_map/attend_first/pallas_call | solution.py:83
  75.1 5.0 collective-permute-start.5
  89.0 4.4 collective-permute-done.8.m3
  125.1 6.9 %attend_out.1 = (bf16[4,256,256]{2,1,0:T(8,128)(2,1)}, f32[4,4,256]{2,1,0:T(4,128)}, f32[256,1024]{1,0:T(8,128)}, bf16[256,1024]{1,0:T(8,128)(2,1)}) custom-call(s32[6]{0:T(128)} %stack.143.info, bf16[256,1024]{1,0:T(8,128)(2,1)} %get-tuple-element.90.x, bf16[272,256]{1,0:T(8,128)(2,1)} %copy-done.45, bf16[272,256]{1,0:T(8,128)(2,1)} %copy-done.46, ...), custom_call_target="tpu_custom_call" | custom-call | flops 536870912 | bytes 10539008 | tf_op jit(solution)/shard_map/attend_out/pallas_call | solution.py:83
  135.5 8.2 %feed.4 = (f32[256,1024]{1,0:T(8,128)}, bf16[2,2,256,704]{3,2,1,0:T(8,128)(2,1)}) custom-call(s32[6]{0:T(128)} %stack.143.info, bf16[256,1024]{1,0:T(8,128)(2,1)} %get-tuple-element.95.value.refs_0_, bf16[704,1024]{1,0:T(8,128)(2,1)} %bitcast.203, bf16[704,1024]{1,0:T(8,128)(2,1)} %bitcast.193, bf16[704,1024]{1,0:T(8,128)(2,1)} %bitcast.182, ...), custom_call_target="tpu_custom_call" | custom-call | flops 2214592512 | bytes 30539776 | tf_op jit(solution)/shard_map/feed/pallas_call | solution.py:83
  143.7 7.4 %collective-permute-done.28 = bf16[32,1024]{1,0:T(8,128)(2,1)S(1)} collective-permute-done((bf16[32,1024]{1,0:T(8,128)(2,1)S(1)}, bf16[32,1024]{1,0:T(8,128)(2,1)S(1)}, u32[]{:S(2)}, u32[]{:S(2)}) %collective-permute-start.28) | collective-permute-done | bytes 65568 | tf_op jit(solution)/shard_map/ppermute | solution.py:35
  159.9 11.6 %collective-permute-done.17.value.refs_1_ = bf16[256,1024]{1,0:T(8,128)(2,1)} collective-permute-done((bf16[256,1024]{1,0:T(8,128)(2,1)}, bf16[256,1024]{1,0:T(8,128)(2,1)}, u32[]{:S(2)}, u32[]{:S(2)}) %collective-permute-start.17) | collective-permute-done | bytes 524320 | tf_op jit(solution)/shard_map/ppermute | solution.py:35
  171.4 8.0 %feed.5 = (bf16[256,1024]{1,0:T(8,128)(2,1)}, bf16[2,2,256,704]{3,2,1,0:T(8,128)(2,1)}) custom-call(s32[6]{0:T(128)} %stack.143.info, bf16[256,1024]{1,0:T(8,128)(2,1)} %collective-permute-done.17.value.refs_1_, bf16[704,1024]{1,0:T(8,128)(2,1)} %bitcast.204, bf16[704,1024]{1,0:T(8,128)(2,1)} %bitcast.194, bf16[704,1024]{1,0:T(8,128)(2,1)} %bitcast.183, ...), custom_call_target="tpu_custom_call" | custom-call | flops 2214592512 | bytes 30015488 | tf_op jit(solution)/shard_map/feed/pallas_call | solution.py:83
  181.6 9.9 %collective-permute-done.22 = bf16[256,1024]{1,0:T(8,128)(2,1)S(1)} collective-permute-done((bf16[256,1024]{1,0:T(8,128)(2,1)}, bf16[256,1024]{1,0:T(8,128)(2,1)S(1)}, u32[]{:S(2)}, u32[]{:S(2)}) %collective-permute-start.22) | collective-permute-done | bytes 524320 | tf_op jit(solution)/shard_map/ppermute | solution.py:35
  203.8 4.2 collective-permute-done.24.lat2
  211.7 18.5 %attend.1 = (bf16[4,256,256]{2,1,0:T(8,128)(2,1)}, f32[4,4,256]{2,1,0:T(4,128)}, bf16[2,1024,256]{2,1,0:T(8,128)(2,1)}, f32[256,1024]{1,0:T(8,128)}, bf16[256,1024]{1,0:T(8,128)(2,1)}) custom-call(s32[6]{0:T(128)} %stack.143.info, bf16[256,1024]{1,0:T(8,128)(2,1)} %get-tuple-element.219.x, bf16[256,1024]{1,0:T(8,128)(2,1)} %copy-done.27, ...), custom_call_target="tpu_custom_call" | custom-call | flops 6442450944 | bytes 16535552 | tf_op jit(solution)/shard_map/attend/pallas_call | solution.py:83
  231.8 8.0 %feed.6 = (f32[256,1024]{1,0:T(8,128)}, bf16[2,2,256,704]{3,2,1,0:T(8,128)(2,1)}) custom-call(s32[6]{0:T(128)} %stack.143.info, bf16[256,1024]{1,0:T(8,128)(2,1)} %get-tuple-element.113.value.refs_0_, bf16[704,1024]{1,0:T(8,128)(2,1)} %bitcast.205, bf16[704,1024]{1,0:T(8,128)(2,1)} %bitcast.195, bf16[704,1024]{1,0:T(8,128)(2,1)} %bitcast.184, ...), custom_call_target="tpu_custom_call" | custom-call | flops 2214592512 | bytes 30539776 | tf_op jit(solution)/shard_map/feed/pallas_call | solution.py:83
  239.8 10.8 %feed_back.4 = (f32[256,1024]{1,0:T(8,128)}, bf16[3,256,768]{2,1,0:T(8,128)(2,1)}, bf16[3,256,768]{2,1,0:T(8,128)(2,1)}) custom-call(s32[6]{0:T(128)} %stack.143.info, bf16[256,1024]{1,0:T(8,128)(2,1)} %get-tuple-element.277.value.refs_4_, bf16[2,2,256,704]{3,2,1,0:T(8,128)(2,1)} %get-tuple-element.117.saved, bf16[704,1024]{1,0:T(8,128)(2,1)} %bitcast.206, ...), custom_call_target="tpu_custom_call" | custom-call | flops 2214592512 | bytes 32899072 | tf_op jit(solution)/shard_map/feed_back/pallas_call | solution.py:83
  251.6 5.1 collective-permute-done.32.value.refs_1_
  257.5 7.9 %feed.7 = (bf16[256,1024]{1,0:T(8,128)(2,1)}, bf16[2,2,256,704]{3,2,1,0:T(8,128)(2,1)}) custom-call(s32[6]{0:T(128)} %stack.143.info, bf16[256,1024]{1,0:T(8,128)(2,1)} %copy-done.40, bf16[704,1024]{1,0:T(8,128)(2,1)} %bitcast.207, bf16[704,1024]{1,0:T(8,128)(2,1)} %bitcast.197, bf16[704,1024]{1,0:T(8,128)(2,1)} %bitcast.186, ...), custom_call_target="tpu_custom_call" | custom-call | flops 2214592512 | bytes 30015488 | tf_op jit(solution)/shard_map/feed/pallas_call | solution.py:83
  268.8 10.6 %feed_back.5 = (bf16[256,1024]{1,0:T(8,128)(2,1)}, bf16[3,256,768]{2,1,0:T(8,128)(2,1)}, bf16[3,256,768]{2,1,0:T(8,128)(2,1)}) custom-call(s32[6]{0:T(128)} %stack.143.info, bf16[256,1024]{1,0:T(8,128)(2,1)} %copy-done.37, bf16[2,2,256,704]{3,2,1,0:T(8,128)(2,1)} %get-tuple-element.119.saved, bf16[704,1024]{1,0:T(8,128)(2,1)} %bitcast.208, ...), custom_call_target="tpu_custom_call" | custom-call | flops 2214592512 | bytes 32374784 | tf_op jit(solution)/shard_map/feed_back/pallas_call | solution.py:83
  299.2 11.4 %feed_weights.2 = bf16[4,3,256,768]{3,2,1,0:T(8,128)(2,1)} custom-call(s32[6]{0:T(128)} %stack.143.info, bf16[256,1024]{1,0:T(8,128)(2,1)} %get-tuple-element.113.value.refs_0_, bf16[256,1024]{1,0:T(8,128)(2,1)} %copy-done.40, bf16[256,1024]{1,0:T(8,128)(2,1)} %collective-permute-done.37.refs_2_, bf16[256,1024]{1,0:T(8,128)(2,1)} %collective-permute-done.38.refs_3_, ...), custom_call_target="tpu_custom_call" | custom-call | flops 4429185024 | bytes 13631488 | tf_op jit(solution)/shard_map/feed_weights/pallas_call | solution.py:83
  310.6 5.1 all-to-all-start.2
  316.8 3.8 collective-permute-done.33
  323.6 15.0 %attend_back.4 = (f32[256,1024]{1,0:T(8,128)}, bf16[1024,256]{1,0:T(8,128)(2,1)}, bf16[4,2,320,256]{3,2,1,0:T(8,128)(2,1)}, bf16[4,2,320,256]{3,2,1,0:T(8,128)(2,1)}) custom-call(s32[6]{0:T(128)} %stack.143.info, bf16[256,1024]{1,0:T(8,128)(2,1)} %get-tuple-element.130.grad_branch, bf16[256,1024]{1,0:T(8,128)(2,1)} %copy-done.27, ...), custom_call_target="tpu_custom_call" | custom-call | flops 8858370048 | bytes 18104320 | tf_op jit(solution)/shard_map/attend_back/pallas_call | solution.py:83
  341.0 15.1 %attend_back.5 = (f32[256,1024]{1,0:T(8,128)}, bf16[1024,256]{1,0:T(8,128)(2,1)}, bf16[4,2,320,256]{3,2,1,0:T(8,128)(2,1)}, bf16[4,2,320,256]{3,2,1,0:T(8,128)(2,1)}) custom-call(s32[6]{0:T(128)} %stack.143.info, bf16[256,1024]{1,0:T(8,128)(2,1)} %get-tuple-element.130.grad_branch, bf16[256,1024]{1,0:T(8,128)(2,1)} %copy-done.27, ...), custom_call_target="tpu_custom_call" | custom-call | flops 8858370048 | bytes 18104320 | tf_op jit(solution)/shard_map/attend_back/pallas_call | solution.py:83
  366.3 8.5 %all-to-all-done.2 = bf16[4,3,256,768]{3,2,1,0:T(8,128)(2,1)} async-done(((bf16[4,3,256,768]{3,2,1,0:T(8,128)(2,1)}), bf16[4,3,256,768]{3,2,1,0:T(8,128)(2,1)}, u32[]{:S(2)}, u32[]{:S(2)}) %all-to-all-start.2) | async-done | bytes 4718624 | tf_op jit(solution)/shard_map/all_to_all | solution.py:817
  380.7 10.9 %feed_back.6 = (f32[256,1024]{1,0:T(8,128)}, bf16[3,256,768]{2,1,0:T(8,128)(2,1)}, bf16[3,256,768]{2,1,0:T(8,128)(2,1)}) custom-call(s32[6]{0:T(128)} %stack.143.info, bf16[256,1024]{1,0:T(8,128)(2,1)} %get-tuple-element.214.value.refs_4_, bf16[2,2,256,704]{3,2,1,0:T(8,128)(2,1)} %get-tuple-element.135.saved, bf16[704,1024]{1,0:T(8,128)(2,1)} %bitcast.209, ...), custom_call_target="tpu_custom_call" | custom-call | flops 2214592512 | bytes 32899072 | tf_op jit(solution)/shard_map/feed_back/pallas_call | solution.py:83
  396.7 17.2 %collective-permute-done.47.value.refs_5_ = bf16[256,1024]{1,0:T(8,128)(2,1)S(1)} collective-permute-done((bf16[256,1024]{1,0:T(8,128)(2,1)}, bf16[256,1024]{1,0:T(8,128)(2,1)S(1)}, u32[]{:S(2)}, u32[]{:S(2)}) %collective-permute-start.47) | collective-permute-done | bytes 524320 | tf_op jit(solution)/shard_map/ppermute | solution.py:35
  414.8 10.8 %feed_back.7 = (bf16[256,1024]{1,0:T(8,128)(2,1)}, bf16[3,256,768]{2,1,0:T(8,128)(2,1)}, bf16[3,256,768]{2,1,0:T(8,128)(2,1)}) custom-call(s32[6]{0:T(128)} %stack.143.info, bf16[256,1024]{1,0:T(8,128)(2,1)} %copy-done.38, bf16[2,2,256,704]{3,2,1,0:T(8,128)(2,1)} %get-tuple-element.137.saved, bf16[704,1024]{1,0:T(8,128)(2,1)} %bitcast.210, ...), custom_call_target="tpu_custom_call" | custom-call | flops 2214592512 | bytes 32374784 | tf_op jit(solution)/shard_map/feed_back/pallas_call | solution.py:83
  442.8 11.5 %feed_weights.3 = bf16[4,3,256,768]{3,2,1,0:T(8,128)(2,1)} custom-call(s32[6]{0:T(128)} %stack.143.info, bf16[256,1024]{1,0:T(8,128)(2,1)} %get-tuple-element.95.value.refs_0_, bf16[256,1024]{1,0:T(8,128)(2,1)} %collective-permute-done.17.value.refs_1_, bf16[256,1024]{1,0:T(8,128)(2,1)} %collective-permute-done.49.refs_2_, ...), custom_call_target="tpu_custom_call" | custom-call | flops 4429185024 | bytes 13631488 | tf_op jit(solution)/shard_map/feed_weights/pallas_call | solution.py:83
  454.3 4.0 collective-permute-done.48
  463.1 15.1 %attend_back.6 = (f32[256,1024]{1,0:T(8,128)}, bf16[1024,256]{1,0:T(8,128)(2,1)}, bf16[4,2,320,256]{3,2,1,0:T(8,128)(2,1)}, bf16[4,2,320,256]{3,2,1,0:T(8,128)(2,1)}) custom-call(s32[6]{0:T(128)} %stack.143.info, bf16[256,1024]{1,0:T(8,128)(2,1)} %get-tuple-element.152.grad_branch, bf16[256,1024]{1,0:T(8,128)(2,1)} %fusion.18.normed, ...), custom_call_target="tpu_custom_call" | custom-call | flops 8858370048 | bytes 18104320 | tf_op jit(solution)/shard_map/attend_back/pallas_call | solution.py:83
  479.2 4.4 collective-permute-start.60
  483.6 15.2 %attend_back.7 = (f32[256,1024]{1,0:T(8,128)}, bf16[1024,256]{1,0:T(8,128)(2,1)}, bf16[4,2,320,256]{3,2,1,0:T(8,128)(2,1)}, bf16[4,2,320,256]{3,2,1,0:T(8,128)(2,1)}) custom-call(s32[6]{0:T(128)} %stack.143.info, bf16[256,1024]{1,0:T(8,128)(2,1)} %get-tuple-element.152.grad_branch, bf16[256,1024]{1,0:T(8,128)(2,1)} %fusion.18.normed, ...), custom_call_target="tpu_custom_call" | custom-call | flops 8858370048 | bytes 18104320 | tf_op jit(solution)/shard_map/attend_back/pallas_call | solution.py:83
  502.9 5.0 all-to-all-start.5
  514.4 7.0 %collective-permute-done.67 = bf16[2,400,256]{2,1,0:T(8,128)(2,1)S(1)} collective-permute-done((bf16[2,400,256]{2,1,0:T(8,128)(2,1)S(1)}, bf16[2,400,256]{2,1,0:T(8,128)(2,1)S(1)}, u32[]{:S(2)}, u32[]{:S(2)}) %collective-permute-start.67) | collective-permute-done | bytes 409632 | tf_op jit(solution)/shard_map/ppermute | solution.py:35
  521.5 3.8 collective-permute-start.68
  541.1 4.6 collective-permute-start.72
  552.6 7.9 %all-to-all-done.5 = bf16[4,3,256,768]{3,2,1,0:T(8,128)(2,1)} async-done(((bf16[4,3,256,768]{3,2,1,0:T(8,128)(2,1)}), bf16[4,3,256,768]{3,2,1,0:T(8,128)(2,1)}, u32[]{:S(2)}, u32[]{:S(2)}) %all-to-all-start.5) | async-done | bytes 4718624 | tf_op jit(solution)/shard_map/all_to_all | solution.py:817
  560.5 4.0 all-to-all-start.4
  564.5 4.5 select_bitcast_fusion.1
  570.3 4.5 reduce_sum.181
  576.1 4.5 reduce_sum.188
  580.6 8.0 %collective-permute-start.73 = (bf16[3,256,768]{2,1,0:T(8,128)(2,1)}, bf16[3,256,768]{2,1,0:T(8,128)(2,1)}, u32[]{:S(2)}, u32[]{:S(2)}) collective-permute-start(bf16[3,256,768]{2,1,0:T(8,128)(2,1)} %reduce_sum.188), channel_id=1, source_target_pairs={{16,8},{20,12},{24,0},{28,4},{17,9},{21,13},{25,1},{29,5},{18,10},... | collective-permute-start | bytes 3538952 | tf_op jit(solution)/shard_map/ppermute | solution.py:868
  588.6 12.9 %all-to-all-done.4 = bf16[4,4,400,256]{3,2,1,0:T(8,128)(2,1)S(1)} async-done(((bf16[4,4,400,256]{3,2,1,0:T(8,128)(2,1)}), bf16[4,4,400,256]{3,2,1,0:T(8,128)(2,1)S(1)}, u32[]{:S(2)}, u32[]{:S(2)}) %all-to-all-start.4) | async-done | bytes 3276832 | tf_op jit(solution)/shard_map/all_to_all | solution.py:864
  605.6 4.3 maximum_select_fusion
  612.3 12.7 %all-gather.23.cloned.1.call-done = bf16[1024,1024]{1,0:T(8,128)(2,1)} async-done(((bf16[256,1024]{1,0:T(8,128)(2,1)}), bf16[1024,1024]{1,0:T(8,128)(2,1)}) %all-gather.23.cloned.1.call-update) | async-done | bytes 2097168 | tf_op jit(solution)/shard_map/all_gather | solution.py:907
  625.1 4.0 select_bitcast_fusion
  630.3 18.2 %collective-permute-done.59 = bf16[3,256,768]{2,1,0:T(8,128)(2,1)} collective-permute-done((bf16[3,256,768]{2,1,0:T(8,128)(2,1)}, bf16[3,256,768]{2,1,0:T(8,128)(2,1)}, u32[]{:S(2)}, u32[]{:S(2)}) %collective-permute-start.59) | collective-permute-done | bytes 1179680 | tf_op jit(solution)/shard_map/ppermute | solution.py:868
  (420 shorter events, 237.5 us)
Async XLA Ops:
  14.1 33.8 %collective-permute-start.3 = (bf16[288,1024]{1,0:T(8,128)(2,1)S(1)}, bf16[288,1024]{1,0:T(8,128)(2,1)S(1)}, u32[]{:S(2)}, u32[]{:S(2)}) collective-permute-start(bf16[288,1024]{1,0:T(8,128)(2,1)S(1)} %slice.210), channel_id=1, source_target_pairs={{0,8},{4,12},{8,0},{12,4},{1,9},{5,13},{9,1},{13,5},{2,10},{6,14},... | collective-permute-start | bytes 1769480 | tf_op jit(solution)/shard_map/ppermute | solution.py:35
  19.0 28.9 %collective-permute-start.11 = (bf16[32,1024]{1,0:T(8,128)(2,1)S(1)}, bf16[32,1024]{1,0:T(8,128)(2,1)S(1)}, u32[]{:S(2)}, u32[]{:S(2)}) collective-permute-start(bf16[32,1024]{1,0:T(8,128)(2,1)S(1)} %slice.216), channel_id=1, source_target_pairs={{0,8},{4,12},{8,0},{12,4},{1,9},{5,13},{9,1},{13,5},{2,10},{6,14},... | collective-permute-start | bytes 196616 | tf_op jit(solution)/shard_map/ppermute | solution.py:35
  19.0 28.9 %collective-permute-start.12 = (bf16[32,1024]{1,0:T(8,128)(2,1)S(1)}, bf16[32,1024]{1,0:T(8,128)(2,1)S(1)}, u32[]{:S(2)}, u32[]{:S(2)}) collective-permute-start(bf16[32,1024]{1,0:T(8,128)(2,1)S(1)} %slice.216), channel_id=1, source_target_pairs={{0,12},{4,8},{8,4},{12,0},{1,13},{5,9},{9,5},{13,1},{2,14},{6,10},... | collective-permute-start | bytes 196616 | tf_op jit(solution)/shard_map/ppermute | solution.py:35
  50.0 43.3 %all-to-all-start = ((bf16[4,384,1024]{2,1,0:T(8,128)(2,1)}), bf16[4,384,1024]{2,1,0:T(8,128)(2,1)S(1)}, u32[]{:S(2)}, u32[]{:S(2)}) async-start(bf16[4,384,1024]{2,1,0:T(8,128)(2,1)} %broadcast_in_dim.8), calls=%async_computation | async-start | bytes 6291456 | tf_op jit(solution)/shard_map/all_to_all | solution.py:48
  53.9 117.5 %all-gather.13.cloned.1.call-start = ((), (), s32[]{:S(2)}) async-start(), calls=%async_computation.6 | async-start | bytes 1474560 | tf_op jit(solution)/shard_map/all_gather | solution.py:741
  93.4 31.6 %collective-permute-start.13 = (bf16[4,384,1024]{2,1,0:T(8,128)(2,1)S(1)}, bf16[4,384,1024]{2,1,0:T(8,128)(2,1)}, u32[]{:S(2)}, u32[]{:S(2)}) collective-permute-start(bf16[4,384,1024]{2,1,0:T(8,128)(2,1)S(1)} %all-to-all-done.o2.refs_6_.refs_8_.refs_10_), channel_id=1, source_target_pairs={{0,16},{16,0},{1,17},{17,1},{2,18},{18,2},{3,19},{19,3},{4,20},{20... | collective-permute-start | bytes 9437192 | tf_op jit(solution)/shard_map/ppermute | solution.py:30
  106.4 25.6 %collective-permute-start.14 = (bf16[704,1024]{1,0:T(8,128)(2,1)}, bf16[704,1024]{1,0:T(8,128)(2,1)}, u32[]{:S(2)}, u32[]{:S(2)}) collective-permute-start(bf16[704,1024]{1,0:T(8,128)(2,1)} %bitcast.202), channel_id=1, source_target_pairs={{0,16},{16,0},{1,17},{17,1},{2,18},{18,2},{3,19},{19,3},{4,20},{20... | collective-permute-start | bytes 4325384 | tf_op jit(solution)/shard_map/ppermute | solution.py:30
  107.4 25.9 %collective-permute-start.15 = (bf16[704,1024]{1,0:T(8,128)(2,1)}, bf16[704,1024]{1,0:T(8,128)(2,1)}, u32[]{:S(2)}, u32[]{:S(2)}) collective-permute-start(bf16[704,1024]{1,0:T(8,128)(2,1)} %bitcast.192), channel_id=1, source_target_pairs={{0,16},{16,0},{1,17},{17,1},{2,18},{18,2},{3,19},{19,3},{4,20},{20... | collective-permute-start | bytes 4325384 | tf_op jit(solution)/shard_map/ppermute | solution.py:30
  107.5 28.0 %collective-permute-start.16 = (bf16[704,1024]{1,0:T(8,128)(2,1)}, bf16[704,1024]{1,0:T(8,128)(2,1)}, u32[]{:S(2)}, u32[]{:S(2)}) collective-permute-start(bf16[704,1024]{1,0:T(8,128)(2,1)} %bitcast.181), channel_id=1, source_target_pairs={{0,16},{16,0},{1,17},{17,1},{2,18},{18,2},{3,19},{19,3},{4,20},{20... | collective-permute-start | bytes 4325384 | tf_op jit(solution)/shard_map/ppermute | solution.py:30
  118.0 33.2 %collective-permute-start.30 = (bf16[288,1024]{1,0:T(8,128)(2,1)}, bf16[288,1024]{1,0:T(8,128)(2,1)}, u32[]{:S(2)}, u32[]{:S(2)}) collective-permute-start(bf16[288,1024]{1,0:T(8,128)(2,1)} %slice.175), channel_id=1, source_target_pairs={{0,8},{4,12},{8,0},{12,4},{1,9},{5,13},{9,1},{13,5},{2,10},{6,14},... | collective-permute-start | bytes 1769480 | tf_op jit(solution)/shard_map/ppermute | solution.py:35
  124.9 18.8 %collective-permute-start.27 = (bf16[32,1024]{1,0:T(8,128)(2,1)S(1)}, bf16[32,1024]{1,0:T(8,128)(2,1)S(1)}, u32[]{:S(2)}, u32[]{:S(2)}) collective-permute-start(bf16[32,1024]{1,0:T(8,128)(2,1)S(1)} %slice.174), channel_id=1, source_target_pairs={{0,4},{4,0},{8,12},{12,8},{1,5},{5,1},{9,13},{13,9},{2,6},{6,2},{1... | collective-permute-start | bytes 196616 | tf_op jit(solution)/shard_map/ppermute | solution.py:35
  132.0 19.1 %collective-permute-start.28 = (bf16[32,1024]{1,0:T(8,128)(2,1)S(1)}, bf16[32,1024]{1,0:T(8,128)(2,1)S(1)}, u32[]{:S(2)}, u32[]{:S(2)}) collective-permute-start(bf16[32,1024]{1,0:T(8,128)(2,1)S(1)} %slice.174), channel_id=1, source_target_pairs={{0,8},{4,12},{8,0},{12,4},{1,9},{5,13},{9,1},{13,5},{2,10},{6,14},... | collective-permute-start | bytes 196616 | tf_op jit(solution)/shard_map/ppermute | solution.py:35
  133.3 17.8 %collective-permute-start.29 = (bf16[32,1024]{1,0:T(8,128)(2,1)S(1)}, bf16[32,1024]{1,0:T(8,128)(2,1)S(1)}, u32[]{:S(2)}, u32[]{:S(2)}) collective-permute-start(bf16[32,1024]{1,0:T(8,128)(2,1)S(1)} %slice.174), channel_id=1, source_target_pairs={{0,12},{4,8},{8,4},{12,0},{1,13},{5,9},{9,5},{13,1},{2,14},{6,10},... | collective-permute-start | bytes 196616 | tf_op jit(solution)/shard_map/ppermute | solution.py:35
  154.3 39.9 %all-to-all-start.1 = ((bf16[4,384,1024]{2,1,0:T(8,128)(2,1)}), bf16[4,384,1024]{2,1,0:T(8,128)(2,1)S(1)}, u32[]{:S(2)}, u32[]{:S(2)}) async-start(bf16[4,384,1024]{2,1,0:T(8,128)(2,1)} %broadcast_in_dim.9), calls=%async_computation.1 | async-start | bytes 6291456 | tf_op jit(solution)/shard_map/all_to_all | solution.py:48
  158.2 157.8 %all-gather.15.cloned.1.call-start = ((), (), s32[]{:S(2)}) async-start(), calls=%async_computation.7 | async-start | bytes 2621440 | tf_op jit(solution)/shard_map/all_gather | solution.py:907
  194.3 16.7 %collective-permute-start.31 = (bf16[4,384,1024]{2,1,0:T(8,128)(2,1)S(1)}, bf16[4,384,1024]{2,1,0:T(8,128)(2,1)}, u32[]{:S(2)}, u32[]{:S(2)}) collective-permute-start(bf16[4,384,1024]{2,1,0:T(8,128)(2,1)S(1)} %all-to-all-done.1.o2.refs_6_.refs_8_.refs_10_), channel_id=1, source_target_pairs={{0,16},{16,0},{1,17},{17,1},{2,18},{18,2},{3,19},{19,3},{4,20},{20... | collective-permute-start | bytes 9437192 | tf_op jit(solution)/shard_map/ppermute | solution.py:30
  202.2 226.0 %all-gather.19.cloned.1.call-start = ((), (), s32[]{:S(2)}) async-start(), calls=%async_computation.9 | async-start | bytes 1474560 | tf_op jit(solution)/shard_map/all_gather | solution.py:741
  230.2 26.5 %collective-permute-start.32 = (bf16[256,1024]{1,0:T(8,128)(2,1)}, bf16[256,1024]{1,0:T(8,128)(2,1)S(1)}, u32[]{:S(2)}, u32[]{:S(2)}) collective-permute-start(bf16[256,1024]{1,0:T(8,128)(2,1)} %get-tuple-element.113.value.refs_0_), channel_id=1, source_target_pairs={{0,4},{4,0},{8,12},{12,8},{1,5},{5,1},{9,13},{13,9},{2,6},{6,2},{1... | collective-permute-start | bytes 1572872 | tf_op jit(solution)/shard_map/ppermute | solution.py:35
  231.7 36.3 %collective-permute-start.35 = (bf16[256,1024]{1,0:T(8,128)(2,1)S(1)}, bf16[256,1024]{1,0:T(8,128)(2,1)S(1)}, u32[]{:S(2)}, u32[]{:S(2)}) collective-permute-start(bf16[256,1024]{1,0:T(8,128)(2,1)S(1)} %copy-done.25), channel_id=1, source_target_pairs={{0,4},{4,0},{8,12},{12,8},{1,5},{5,1},{9,13},{13,9},{2,6},{6,2},{1... | collective-permute-start | bytes 1572872 | tf_op jit(solution)/shard_map/ppermute | solution.py:35
  250.6 48.5 %collective-permute-start.41 = (bf16[3,256,768]{2,1,0:T(8,128)(2,1)}, bf16[3,256,768]{2,1,0:T(8,128)(2,1)}, u32[]{:S(2)}, u32[]{:S(2)}) collective-permute-start(bf16[3,256,768]{2,1,0:T(8,128)(2,1)} %get-tuple-element.123), channel_id=1, source_target_pairs={{0,16},{16,0},{1,17},{17,1},{2,18},{18,2},{3,19},{19,3},{4,20},{20... | collective-permute-start | bytes 3538952 | tf_op jit(solution)/shard_map/ppermute | solution.py:30
  279.4 19.7 %collective-permute-start.42 = (bf16[3,256,768]{2,1,0:T(8,128)(2,1)}, bf16[3,256,768]{2,1,0:T(8,128)(2,1)}, u32[]{:S(2)}, u32[]{:S(2)}) collective-permute-start(bf16[3,256,768]{2,1,0:T(8,128)(2,1)} %get-tuple-element.124), channel_id=1, source_target_pairs={{0,16},{16,0},{1,17},{17,1},{2,18},{18,2},{3,19},{19,3},{4,20},{20... | collective-permute-start | bytes 3538952 | tf_op jit(solution)/shard_map/ppermute | solution.py:30
  296.0 20.0 %collective-permute-start.36 = (bf16[256,1024]{1,0:T(8,128)(2,1)}, bf16[256,1024]{1,0:T(8,128)(2,1)S(1)}, u32[]{:S(2)}, u32[]{:S(2)}) collective-permute-start(bf16[256,1024]{1,0:T(8,128)(2,1)} %get-tuple-element.120), channel_id=1, source_target_pairs={{0,4},{4,0},{8,12},{12,8},{1,5},{5,1},{9,13},{13,9},{2,6},{6,2},{1... | collective-permute-start | bytes 1572872 | tf_op jit(solution)/shard_map/ppermute | solution.py:35
  298.1 127.6 %collective-permute-start.49 = (bf16[256,1024]{1,0:T(8,128)(2,1)}, bf16[256,1024]{1,0:T(8,128)(2,1)}, u32[]{:S(2)}, u32[]{:S(2)}) collective-permute-start(bf16[256,1024]{1,0:T(8,128)(2,1)} %get-tuple-element.95.value.refs_0_), channel_id=1, source_target_pairs={{0,16},{16,0},{1,17},{17,1},{2,18},{18,2},{3,19},{19,3},{4,20},{20... | collective-permute-start | bytes 1572872 | tf_op jit(solution)/shard_map/ppermute | solution.py:30
  298.9 21.7 %collective-permute-start.33 = (bf16[256,1024]{1,0:T(8,128)(2,1)}, bf16[256,1024]{1,0:T(8,128)(2,1)}, u32[]{:S(2)}, u32[]{:S(2)}) collective-permute-start(bf16[256,1024]{1,0:T(8,128)(2,1)} %get-tuple-element.116), channel_id=1, source_target_pairs={{0,4},{4,0},{8,12},{12,8},{1,5},{5,1},{9,13},{13,9},{2,6},{6,2},{1... | collective-permute-start | bytes 1572872 | tf_op jit(solution)/shard_map/ppermute | solution.py:35
  310.6 64.3 %all-to-all-start.2 = ((bf16[4,3,256,768]{3,2,1,0:T(8,128)(2,1)}), bf16[4,3,256,768]{3,2,1,0:T(8,128)(2,1)}, u32[]{:S(2)}, u32[]{:S(2)}) async-start(bf16[4,3,256,768]{3,2,1,0:T(8,128)(2,1)} %feed_weights.2), calls=%async_computation.2 | async-start | bytes 9437184 | tf_op jit(solution)/shard_map/all_to_all | solution.py:817
  315.6 138.6 %all-gather.17.cloned.1.call-start = ((), (), s32[]{:S(2)}) async-start(), calls=%async_computation.8 | async-start | bytes 2621440 | tf_op jit(solution)/shard_map/all_gather | solution.py:907
  339.6 18.8 %collective-permute-start.43 = (bf16[2,256,256]{2,1,0:T(8,128)(2,1)S(1)}, bf16[2,256,256]{2,1,0:T(8,128)(2,1)S(1)}, u32[]{:S(2)}, u32[]{:S(2)}) collective-permute-start(bf16[2,256,256]{2,1,0:T(8,128)(2,1)S(1)} %dynamic-slice_bitcast_fusion.5), channel_id=1, source_target_pairs={{0,16},{16,0},{1,17},{17,1},{2,18},{18,2},{3,19},{19,3},{4,20},{20... | collective-permute-start | bytes 786440 | tf_op jit(solution)/shard_map/ppermute | solution.py:30
  357.2 69.3 %collective-permute-start.64 = (bf16[4,2,320,256]{3,2,1,0:T(8,128)(2,1)}, bf16[4,2,320,256]{3,2,1,0:T(8,128)(2,1)}, u32[]{:S(2)}, u32[]{:S(2)}) collective-permute-start(bf16[4,2,320,256]{3,2,1,0:T(8,128)(2,1)} %get-tuple-element.157), channel_id=1, source_target_pairs={{0,16},{16,0},{1,17},{17,1},{2,18},{18,2},{3,19},{19,3},{4,20},{20... | collective-permute-start | bytes 3932168 | tf_op jit(solution)/shard_map/ppermute | solution.py:30
  357.7 69.9 %collective-permute-start.65 = (bf16[4,2,320,256]{3,2,1,0:T(8,128)(2,1)}, bf16[4,2,320,256]{3,2,1,0:T(8,128)(2,1)}, u32[]{:S(2)}, u32[]{:S(2)}) collective-permute-start(bf16[4,2,320,256]{3,2,1,0:T(8,128)(2,1)} %get-tuple-element.159), channel_id=1, source_target_pairs={{0,16},{16,0},{1,17},{17,1},{2,18},{18,2},{3,19},{19,3},{4,20},{20... | collective-permute-start | bytes 3932168 | tf_op jit(solution)/shard_map/ppermute | solution.py:30
  357.9 172.3 %all-gather.21.cloned.1.call-start = ((), (), s32[]{:S(2)}) async-start(), calls=%async_computation.10 | async-start | bytes 2621440 | tf_op jit(solution)/shard_map/all_gather | solution.py:907
  379.5 34.5 %collective-permute-start.47 = (bf16[256,1024]{1,0:T(8,128)(2,1)}, bf16[256,1024]{1,0:T(8,128)(2,1)S(1)}, u32[]{:S(2)}, u32[]{:S(2)}) collective-permute-start(bf16[256,1024]{1,0:T(8,128)(2,1)} %get-tuple-element.214.value.refs_4_), channel_id=1, source_target_pairs={{0,4},{4,0},{8,12},{12,8},{1,5},{5,1},{9,13},{13,9},{2,6},{6,2},{1... | collective-permute-start | bytes 1572872 | tf_op jit(solution)/shard_map/ppermute | solution.py:35
  391.6 51.2 %collective-permute-start.53 = (bf16[3,256,768]{2,1,0:T(8,128)(2,1)}, bf16[3,256,768]{2,1,0:T(8,128)(2,1)}, u32[]{:S(2)}, u32[]{:S(2)}) collective-permute-start(bf16[3,256,768]{2,1,0:T(8,128)(2,1)} %get-tuple-element.141), channel_id=1, source_target_pairs={{0,16},{16,0},{1,17},{17,1},{2,18},{18,2},{3,19},{19,3},{4,20},{20... | collective-permute-start | bytes 3538952 | tf_op jit(solution)/shard_map/ppermute | solution.py:30
  425.6 17.1 %collective-permute-start.54 = (bf16[3,256,768]{2,1,0:T(8,128)(2,1)}, bf16[3,256,768]{2,1,0:T(8,128)(2,1)}, u32[]{:S(2)}, u32[]{:S(2)}) collective-permute-start(bf16[3,256,768]{2,1,0:T(8,128)(2,1)} %get-tuple-element.142), channel_id=1, source_target_pairs={{0,16},{16,0},{1,17},{17,1},{2,18},{18,2},{3,19},{19,3},{4,20},{20... | collective-permute-start | bytes 3538952 | tf_op jit(solution)/shard_map/ppermute | solution.py:30
  434.4 23.9 %collective-permute-start.48 = (bf16[256,1024]{1,0:T(8,128)(2,1)}, bf16[256,1024]{1,0:T(8,128)(2,1)}, u32[]{:S(2)}, u32[]{:S(2)}) collective-permute-start(bf16[256,1024]{1,0:T(8,128)(2,1)} %get-tuple-element.138), channel_id=1, source_target_pairs={{0,4},{4,0},{8,12},{12,8},{1,5},{5,1},{9,13},{13,9},{2,6},{6,2},{1... | collective-permute-start | bytes 1572872 | tf_op jit(solution)/shard_map/ppermute | solution.py:35
  438.5 64.4 %all-to-all-start.3 = ((bf16[4,4,400,256]{3,2,1,0:T(8,128)(2,1)}), bf16[4,4,400,256]{3,2,1,0:T(8,128)(2,1)S(1)}, u32[]{:S(2)}, u32[]{:S(2)}) async-start(bf16[4,4,400,256]{3,2,1,0:T(8,128)(2,1)} %pad_maximum_fusion), calls=%async_computation.3 | async-start | bytes 6553600 | tf_op jit(solution)/shard_map/all_to_all | solution.py:864
  442.3 20.8 %collective-permute-start.58 = (bf16[4,576,256]{2,1,0:T(8,128)(2,1)}, bf16[4,576,256]{2,1,0:T(8,128)(2,1)}, u32[]{:S(2)}, u32[]{:S(2)}) collective-permute-start(bf16[4,576,256]{2,1,0:T(8,128)(2,1)} %bitcast.259), channel_id=1, source_target_pairs={{0,16},{16,0},{1,17},{17,1},{2,18},{18,2},{3,19},{19,3},{4,20},{20... | collective-permute-start | bytes 3538952 | tf_op jit(solution)/shard_map/ppermute | solution.py:30
  479.2 22.0 %collective-permute-start.60 = (bf16[2,256,256]{2,1,0:T(8,128)(2,1)S(1)}, bf16[2,256,256]{2,1,0:T(8,128)(2,1)}, u32[]{:S(2)}, u32[]{:S(2)}) collective-permute-start(bf16[2,256,256]{2,1,0:T(8,128)(2,1)S(1)} %dynamic-slice_bitcast_fusion.3), channel_id=1, source_target_pairs={{0,16},{16,0},{1,17},{17,1},{2,18},{18,2},{3,19},{19,3},{4,20},{20... | collective-permute-start | bytes 786440 | tf_op jit(solution)/shard_map/ppermute | solution.py:30
  500.6 24.7 %collective-permute-start.70 = (bf16[4,2,320,256]{3,2,1,0:T(8,128)(2,1)}, bf16[4,2,320,256]{3,2,1,0:T(8,128)(2,1)}, u32[]{:S(2)}, u32[]{:S(2)}) collective-permute-start(bf16[4,2,320,256]{3,2,1,0:T(8,128)(2,1)} %get-tuple-element.162), channel_id=1, source_target_pairs={{0,16},{16,0},{1,17},{17,1},{2,18},{18,2},{3,19},{19,3},{4,20},{20... | collective-permute-start | bytes 3932168 | tf_op jit(solution)/shard_map/ppermute | solution.py:30
  501.0 26.1 %collective-permute-start.71 = (bf16[4,2,320,256]{3,2,1,0:T(8,128)(2,1)}, bf16[4,2,320,256]{3,2,1,0:T(8,128)(2,1)}, u32[]{:S(2)}, u32[]{:S(2)}) collective-permute-start(bf16[4,2,320,256]{3,2,1,0:T(8,128)(2,1)} %get-tuple-element.164), channel_id=1, source_target_pairs={{0,16},{16,0},{1,17},{17,1},{2,18},{18,2},{3,19},{19,3},{4,20},{20... | collective-permute-start | bytes 3932168 | tf_op jit(solution)/shard_map/ppermute | solution.py:30
  502.9 57.6 %all-to-all-start.5 = ((bf16[4,3,256,768]{3,2,1,0:T(8,128)(2,1)}), bf16[4,3,256,768]{3,2,1,0:T(8,128)(2,1)}, u32[]{:S(2)}, u32[]{:S(2)}) async-start(bf16[4,3,256,768]{3,2,1,0:T(8,128)(2,1)} %feed_weights.3), calls=%async_computation.5 | async-start | bytes 9437184 | tf_op jit(solution)/shard_map/all_to_all | solution.py:817
  507.9 117.2 %all-gather.23.cloned.1.call-start = ((), (), s32[]{:S(2)}) async-start(), calls=%async_computation.11 | async-start | bytes 2621440 | tf_op jit(solution)/shard_map/all_gather | solution.py:907
  560.5 41.0 %all-to-all-start.4 = ((bf16[4,4,400,256]{3,2,1,0:T(8,128)(2,1)}), bf16[4,4,400,256]{3,2,1,0:T(8,128)(2,1)S(1)}, u32[]{:S(2)}, u32[]{:S(2)}) async-start(bf16[4,4,400,256]{3,2,1,0:T(8,128)(2,1)} %pad_maximum_fusion.1), calls=%async_computation.4 | async-start | bytes 6553600 | tf_op jit(solution)/shard_map/all_to_all | solution.py:864
  569.0 36.6 %collective-permute-start.34 = (bf16[4,256,1024]{2,1,0:T(8,128)(2,1)}, bf16[4,256,1024]{2,1,0:T(8,128)(2,1)}, u32[]{:S(2)}, u32[]{:S(2)}) collective-permute-start(bf16[4,256,1024]{2,1,0:T(8,128)(2,1)} %get-tuple-element.223), channel_id=1, source_target_pairs={{0,16},{16,0},{1,17},{17,1},{2,18},{18,2},{3,19},{19,3},{4,20},{20... | collective-permute-start | bytes 6291464 | tf_op jit(solution)/shard_map/ppermute | solution.py:30
  574.8 73.6 %collective-permute-start.59 = (bf16[3,256,768]{2,1,0:T(8,128)(2,1)}, bf16[3,256,768]{2,1,0:T(8,128)(2,1)}, u32[]{:S(2)}, u32[]{:S(2)}) collective-permute-start(bf16[3,256,768]{2,1,0:T(8,128)(2,1)} %reduce_sum.181), channel_id=1, source_target_pairs={{0,24},{4,28},{8,16},{12,20},{1,25},{5,29},{9,17},{13,21},{2,26},{... | collective-permute-start | bytes 3538952 | tf_op jit(solution)/shard_map/ppermute | solution.py:868
  580.6 67.9 %collective-permute-start.73 = (bf16[3,256,768]{2,1,0:T(8,128)(2,1)}, bf16[3,256,768]{2,1,0:T(8,128)(2,1)}, u32[]{:S(2)}, u32[]{:S(2)}) collective-permute-start(bf16[3,256,768]{2,1,0:T(8,128)(2,1)} %reduce_sum.188), channel_id=1, source_target_pairs={{16,8},{20,12},{24,0},{28,4},{17,9},{21,13},{25,1},{29,5},{18,10},... | collective-permute-start | bytes 3538952 | tf_op jit(solution)/shard_map/ppermute | solution.py:868
  604.2 26.0 %collective-permute-start.74 = (bf16[2,400,256]{2,1,0:T(8,128)(2,1)S(1)}, bf16[2,400,256]{2,1,0:T(8,128)(2,1)S(1)}, u32[]{:S(2)}, u32[]{:S(2)}) collective-permute-start(bf16[2,400,256]{2,1,0:T(8,128)(2,1)S(1)} %slice.197), channel_id=1, source_target_pairs={{0,4},{4,0},{8,12},{12,8},{1,5},{5,1},{9,13},{13,9},{2,6},{6,2},{1... | collective-permute-start | bytes 1228808 | tf_op jit(solution)/shard_map/ppermute | solution.py:35
  629.1 36.0 %collective-permute-start.69 = (bf16[4,256,1024]{2,1,0:T(8,128)(2,1)}, bf16[4,256,1024]{2,1,0:T(8,128)(2,1)}, u32[]{:S(2)}, u32[]{:S(2)}) collective-permute-start(bf16[4,256,1024]{2,1,0:T(8,128)(2,1)} %get-tuple-element.221), channel_id=1, source_target_pairs={{0,16},{16,0},{1,17},{17,1},{2,18},{18,2},{3,19},{19,3},{4,20},{20... | collective-permute-start | bytes 6291464 | tf_op jit(solution)/shard_map/ppermute | solution.py:30
  630.3 23.4 %collective-permute-start.75 = (bf16[400,256]{1,0:T(8,128)(2,1)S(1)}, bf16[400,256]{1,0:T(8,128)(2,1)S(1)}, u32[]{:S(2)}, u32[]{:S(2)}) collective-permute-start(bf16[400,256]{1,0:T(8,128)(2,1)S(1)} %slice_bitcast_fusion.4), channel_id=1, source_target_pairs={{0,8},{4,12},{8,0},{12,4},{1,9},{5,13},{9,1},{13,5},{2,10},{6,14},... | collective-permute-start | bytes 614408 | tf_op jit(solution)/shard_map/ppermute | solution.py:35
  (103 other events, 843.6 us)
Sparse Core Ops, SparseCore 0:
  121.4 26.5 all-gather.12
  202.3 52.4 all-gather.14
  298.2 59.5 all-gather.18
  359.1 53.2 all-gather.16
  434.3 48.3 all-gather.20
  548.7 76.3 all-gather.22

commit v3 on v2

--- a/solution.py
+++ b/solution.py
@@ -91,7 +91,7 @@
         ),
         out_shape=out_shape,
         compiler_params=pltpu.CompilerParams(
-            dimension_semantics=("arbitrary",) * len(grid), vmem_limit_bytes=56 * 1024 * 1024
+            dimension_semantics=("arbitrary",) * len(grid), vmem_limit_bytes=52 * 1024 * 1024
         ),
         cost_estimate=pl.CostEstimate(flops=flops, bytes_accessed=size, transcendentals=transcendentals),
         name=name,
@@ -720,8 +720,11 @@
     main_pieces = layers_of(feed_and_out(core), core_swap(feed_and_out(1 - core)))
     head_pieces = layers_of(piece_of(heads_here, core), core_swap(piece_of(heads_here, 1 - core)))
     head_piece, out_piece, feed_piece = piece_rows(head_rows), piece_rows(out_rows), piece_rows(feed_rows)
-    over = [z_swap(main_pieces[0][:out_piece], step) for step in range(1, lax.axis_size("tensor"))]
-    feed_far = z_swap(main_pieces[0][out_piece:], planes // 2)
+    out_pieces = jnp.concatenate([piece[:out_piece] for piece in main_pieces], axis=0)
+    feed_far = z_swap(jnp.concatenate([out_pieces, main_pieces[0][out_piece:]], axis=0), planes // 2)
+    out_far = [z_swap(out_pieces, 1), feed_far[: 2 * out_piece], z_swap(out_pieces, 3)]
+    out_far = [[v[layer * out_piece : (layer + 1) * out_piece] for v in out_far] for layer in range(layers)]
+    feed_far = feed_far[2 * out_piece :]
     out_there = core_swap(tie(out_here, feed_far))
     feed_there = [core_swap(tie(v, feed_far)) for v in feed_here]
     latents_w = [jnp.where(core == layer, lat_here, lat_there) for layer in range(layers)]
@@ -807,6 +810,7 @@
         lefts = [normed2, far_normed2, core_swap(normed2), core_swap(far_normed2)]
         lefts += [grad_feed, far_feed, core_swap(grad_feed), core_swap(far_feed)]
         rights = [rights[0], far_rights[0], core_swap(rights[1]), core_swap(far_rights[1])]
+        lefts[0] = tie(lefts[0], *hooks[3]())
         feed_grads = feed_weights_call(info, lefts, rights, dp, hidden_cols)
         back = tie(back, feed_grads, *hooks[0]())
         grad_norm2 = part + back.astype(f32)
@@ -835,10 +839,7 @@
                 lax.dynamic_index_in_dim(total, 1 - near, 0, False), 1
             )
             lat_parts.append(total)
-        if layer == 0:
-            lat_parts[1] = tie(lat_parts[1], *hooks[2]())
-        else:
-            lat_parts[1] = tie(lat_parts[1], feed_parts)
+        lat_parts[1] = tie(lat_parts[1], feed_parts, *hooks[2]())
         lat_own = by_group(jnp.stack(lat_parts[::-1]))
         lat_own = jnp.concatenate([lat_own[0], lat_own[1]], axis=1)
         grad_norm = grad_norms[0] + grad_norms[1] + dot_nt(lat_own, latents_w[layer])
@@ -856,11 +857,10 @@
         small_parts = (small_keep, core_swap(small_send))
 
         feed_sums = jnp.sum(tie(feed_parts, grad_x).astype(f32), axis=0).astype(bf16)
+        if layer == 0:
+            pack_parts_here = [(a, tie(b, grad_x)) for a, b in pack_parts_here]
         pack_total = jnp.concatenate([a + b for a, b in pack_parts_here[::-1]], axis=1)
         small_total = small_parts[0] + small_parts[1]
-        if layer == 0:
-            pack_total = tie(pack_total, grad_x)
-            small_total = tie(small_total, grad_x)
         pack_parts = lax.all_to_all(jnp.concatenate([pack_total, small_total], axis=2), "dp", 0, 0)
 
         def finish_feed():
@@ -873,21 +873,20 @@
             sums = sums[0::2] + z_swap(sums[1::2], 1)
             return sums[0] + z_swap(sums[1], 2)
 
-        return grad_x, finish_feed, finish_pack
-
-    first_out, messages = first_attention(feed_far)
-    main0 = gather(over + [feed_far], (), messages)
+        return grad_x, pack_parts, finish_feed, finish_pack
+
+    lat0 = first_latents()
+    first_out, messages = first_attention(feed_far, lat0)
+    main0 = gather(out_far[0] + [feed_far], (), messages)
     outs0 = (out_here, out_there) + main0 + (0, out_piece)
     at = (planes - 1) * out_piece
     feed0 = (feed_here, feed_there, [main0 + (at + k * feed_piece, feed_piece) for k in range(3)])
-    lat0 = first_latents()
-    mixed0, lse0, residual0, normed2_0 = attend_out_call(info, 0, tie(own_in, lat0), messages, outs0, gains_all[0][1][None])
+    mixed0, lse0, residual0, normed2_0 = attend_out_call(info, 0, own_in, messages, outs0, gains_all[0][1][None])
     near_heads1 = gather_slow(over_planes(head_pieces[1]), (first_out,))
     part0, saved0, far_normed2 = feed_own(0, normed2_0, feed0)
     far_normed2 = tie(far_normed2, near_heads1)
-    main_piece = tie(main_pieces[1], *messages)
-    far_main = over_planes(main_piece[:out_piece]) + [z_swap(main_piece[out_piece:], planes // 2)]
-    near1 = gather_near(far_main, part0)
+    feed_far1 = z_swap(tie(main_pieces[1][out_piece:], *messages), planes // 2)
+    near1 = gather_near(out_far[1] + [feed_far1], part0)
     out0, far_saved0 = feed_rest(0, residual0, part0, far_normed2, feed0)
     kept0 = [normed2_0, far_normed2, saved0, far_saved0]
     main1 = near1, core_swap(tie(near1, out0))
@@ -899,10 +898,6 @@
     part1, saved1, far_normed2 = feed_own(1, normed2_1, feed1)
     out1, far_saved1 = feed_rest(1, residual1, part1, far_normed2, feed1)
     kept1 = [normed2_1, far_normed2, saved1, far_saved1]
-    far_heads = over_planes(head_pieces[0])
-    near_heads0 = gather_slow(far_heads, (normed2_1,))
-    heads0 = (heads_here, heads_there, near_heads0, core_swap(tie(near_heads0, out1)), 0, head_piece)
-
     def gather_rows(own):
         return lax.all_gather(own, "tensor", axis=0, tiled=False)
 
@@ -913,9 +908,11 @@
         return both.reshape(planes * 2 * rows, width)
 
     rows_out = [gather_rows(out0), gather_rows(out1)]
-    grad1, finish_feed1, finish_pack1 = backward(
+    near_heads0 = gather_slow(over_planes(head_pieces[0]), (out0,))
+    heads0 = (heads_here, heads_there, near_heads0, core_swap(tie(near_heads0, out1)), 0, head_piece)
+    grad1, pack_parts1, finish_feed1, finish_pack1 = backward(
         1, own_target, out0, normed1, lat1, mixed1, lse1, residual1, kept1, (heads1, outs1), feed1,
-        [lambda: (rows_out[0],), lambda token: ()],
+        [lambda: (rows_out[0],), lambda token: (), lambda: (rows_out[1],), lambda: ()],
     )
     normed0 = normalise(own_in, gains_all[0][0])
     later = {}
@@ -929,9 +926,9 @@
         later["grad"] = gather_rows(grad1)
         return (later["pack"], later["grad"])
 
-    grad0, finish_feed0, finish_pack0 = backward(
+    grad0, _, finish_feed0, finish_pack0 = backward(
         0, grad1, own_in, normed0, lat0, mixed0, lse0, residual0, kept0, (heads0, outs0), feed0,
-        [lambda: (rows_out[1],), during_attention, after_attention],
+        [lambda: (), during_attention, after_attention, lambda: (pack_parts1,)],
     )
     rows_grad0 = gather_rows(grad0)
     layer_outputs = finish_rows(*rows_out)

time: 689 us -> 671 us (0.974)
  waiting for transfers between devices: 187 us -> 236 us
  starting transfers between devices: 123 us -> 95.4 us
  Pallas kernels: 197 us -> 183 us
  local copies, waits for them, and re-layouts: 54.5 us -> 43.6 us
  other arithmetic: 87.2 us -> 77.8 us
    ppermute x31 -> x27, waiting for transfers between devices: 114 us -> 142 us  [z_swap(): return lax.ppermute(value, 'tensor', [(i, i ^ step) for i in range(count)])]
    ppermute x40, starting transfers between devices: 38.6 us -> 21.6 us  [core_swap(): return lax.ppermute(value, 'section', [(0, 1), (1, 0)])]
    all_to_all x2, waiting for transfers between devices: 16.5 us -> 0.01 us  [backward(): feed_parts = lax.all_to_all(feed_grads, 'dp', 0, 0)]
    all_gather x2, waiting for transfers between devices: 0.01 us -> 15.1 us  [gather_slow(): lax.all_gather(jnp.concatenate([tie(v, *before) for v in parts], axis=0),...]
    pallas_call x17, Pallas kernels: 197 us -> 183 us  [kernel_call(): pl.pallas_call(kernel, grid_spec=pltpu.PrefetchScalarGridSpec(num_scalar_...]
    ppermute x31 -> x27, starting transfers between devices: 39.6 us -> 25.3 us  [z_swap(): return lax.ppermute(value, 'tensor', [(i, i ^ step) for i in range(count)])]
    all_gather x4, waiting for transfers between devices: 12.8 us -> 24.6 us  [gather_rows(): return lax.all_gather(own, 'tensor', axis=0, tiled=False)]
    ppermute x40, waiting for transfers between devices: 3.72 us -> 14.3 us  [core_swap(): return lax.ppermute(value, 'section', [(0, 1), (1, 0)])]
  transfers between devices with their start and end apart: 89 -> 85, of which waited for: 30 -> 35; matrix products, arithmetic and copies ran while one was open for 20% -> 17% of each run, Pallas kernels for 29% -> 27%
where the time goes in v3:
time: 671 us; the launch traced here: 665 us
  waiting for transfers between devices  236 us (35%)
  Pallas kernels  183 us (27%)
  starting transfers between devices  95.4 us (14%)
  other arithmetic  77.8 us (12%)
  local copies, waits for them, and re-layouts  43.6 us (6%)
  between operations  15.8 us (2%)
  matrix products  13.6 us (2%)
    pallas_call x17, Pallas kernels, kernel_call(): pl.pallas_call(kernel, grid_spec=pltpu.PrefetchScalarGridSpec(num_scalar_...  183 us
    ppermute x27, waiting for transfers between devices, z_swap(): return lax.ppermute(value, 'tensor', [(i, i ^ step) for i in range(count)])  142 us
    ppermute x27, starting transfers between devices, z_swap(): return lax.ppermute(value, 'tensor', [(i, i ^ step) for i in range(count)])  25.3 us
    all_gather x4, waiting for transfers between devices, gather_rows(): return lax.all_gather(own, 'tensor', axis=0, tiled=False)  24.6 us
    ppermute x40, starting transfers between devices, core_swap(): return lax.ppermute(value, 'section', [(0, 1), (1, 0)])  21.6 us
    all_gather x2, waiting for transfers between devices, gather_slow(): lax.all_gather(jnp.concatenate([tie(v, *before) for v in parts], axis=0),...  15.1 us
    unnamed x108, local copies, waits for them, and re-layouts  14.4 us
    all_to_all x2, waiting for transfers between devices, backward(): lax.all_to_all(jnp.concatenate([pack_total, small_total], axis=2), 'dp',...  14.4 us
  transfers between devices with their start and end apart: 85, of which 35 were waited for; matrix products, arithmetic and copies ran while one was open for 17% of the time, Pallas kernels for 27%

profile of v3, /device:TPU:1, one launch (start us, length us, event | category | flops | bytes accessed | tf_op | source)
XLA Modules:
  0.0 665.0 jit_solution(2627195334953603386)
XLA Ops:
  24.6 16.2 %collective-permute-done.10 = bf16[64,1024]{1,0:T(8,128)(2,1)S(1)} collective-permute-done((bf16[64,1024]{1,0:T(8,128)(2,1)S(1)}, bf16[64,1024]{1,0:T(8,128)(2,1)S(1)}, u32[]{:S(2)}, u32[]{:S(2)}) %collective-permute-start.10) | collective-permute-done | bytes 131104 | tf_op jit(solution)/shard_map/ppermute | solution.py:35
  41.9 4.6 collective-permute-done.11
  46.6 10.7 %collective-permute-done.2 = bf16[352,1024]{1,0:T(8,128)(2,1)S(1)} collective-permute-done((bf16[352,1024]{1,0:T(8,128)(2,1)S(1)}, bf16[352,1024]{1,0:T(8,128)(2,1)S(1)}, u32[]{:S(2)}, u32[]{:S(2)}) %collective-permute-start.2) | collective-permute-done | bytes 720928 | tf_op jit(solution)/shard_map/ppermute | solution.py:35
  59.5 4.6 all-to-all-start
  70.0 12.3 %attend_first.1 = bf16[4,272,256]{2,1,0:T(8,128)(2,1)S(1)} custom-call(s32[4]{0:T(128)S(1)} %pad_add_fusion.info, bf16[2048,1024]{1,0:T(8,128)(2,1)} %x.11, bf16[1024,512]{1,0:T(8,128)(2,1)} %bitcast.7.lat_here, bf16[1024,512]{1,0:T(8,128)(2,1)} %collective-permute-done.lat_there, bf16[1536,256]{1,0:T(8,128)(2,1)S(1)} %pad_maximum_fusion.2.heads_here.h0, ...), custom_call_target="tpu_custom_call" | custom-call | flops 4563402752 | bytes 8437760 | tf_op jit(solution)/shard_map/attend_first/pallas_call | solution.py:83
  82.4 7.6 %collective-permute-start.5 = (bf16[272,256]{1,0:T(8,128)(2,1)S(1)}, bf16[272,256]{1,0:T(8,128)(2,1)S(1)}, u32[]{:S(2)}, u32[]{:S(2)}) collective-permute-start(bf16[272,256]{1,0:T(8,128)(2,1)S(1)} %get-tuple-element.264), channel_id=1, source_target_pairs={{0,0},{4,16},{8,4},{12,20},{16,8},{20,24},{24,12},{28,28},{1,1},{5... | collective-permute-start | bytes 417800 | tf_op jit(solution)/shard_map/ppermute | solution.py:766
  98.0 5.2 collective-permute-done.8.m3
  104.8 4.6 collective-permute-done.17
  118.3 5.1 collective-permute-done.19
  124.1 4.7 collective-permute-done.20
  137.0 6.2 attend_out.1
  143.2 6.6 feed.4
  149.9 11.8 %collective-permute-done.26 = bf16[288,1024]{1,0:T(8,128)(2,1)} collective-permute-done((bf16[288,1024]{1,0:T(8,128)(2,1)}, bf16[288,1024]{1,0:T(8,128)(2,1)}, u32[]{:S(2)}, u32[]{:S(2)}) %collective-permute-start.26) | collective-permute-done | bytes 589856 | tf_op jit(solution)/shard_map/ppermute | solution.py:35
  164.9 4.7 all-to-all-start.1
  169.7 13.0 %collective-permute-done.16.value.refs_1_ = bf16[256,1024]{1,0:T(8,128)(2,1)S(1)} collective-permute-done((bf16[256,1024]{1,0:T(8,128)(2,1)S(1)}, bf16[256,1024]{1,0:T(8,128)(2,1)S(1)}, u32[]{:S(2)}, u32[]{:S(2)}) %collective-permute-start.16) | collective-permute-done | bytes 524320 | tf_op jit(solution)/shard_map/ppermute | solution.py:35
  182.7 6.7 %feed.5 = (bf16[256,1024]{1,0:T(8,128)(2,1)S(1)}, bf16[2,2,256,704]{3,2,1,0:T(8,128)(2,1)}) custom-call(s32[6]{0:T(128)S(1)} %stack.143.info, bf16[256,1024]{1,0:T(8,128)(2,1)S(1)} %collective-permute-done.16.value.refs_1_, bf16[704,1024]{1,0:T(8,128)(2,1)} %bitcast.218, bf16[704,1024]{1,0:T(8,128)(2,1)} %bitcast.208, bf16[704,1024]{1,0:T(8,128)(2,1)} %bitcast.196, ...), custom_call_target="tpu_custom_call" | custom-call | flops 2214592512 | bytes 30015488 | tf_op jit(solution)/shard_map/feed/pallas_call | solution.py:83
  190.5 11.4 %collective-permute-done.21 = bf16[256,1024]{1,0:T(8,128)(2,1)S(1)} collective-permute-done((bf16[256,1024]{1,0:T(8,128)(2,1)S(1)}, bf16[256,1024]{1,0:T(8,128)(2,1)S(1)}, u32[]{:S(2)}, u32[]{:S(2)}) %collective-permute-start.21) | collective-permute-done | bytes 524320 | tf_op jit(solution)/shard_map/ppermute | solution.py:35
  209.9 6.1 collective-permute-done.23.lat2
  218.9 17.7 %attend.1 = (bf16[4,256,256]{2,1,0:T(8,128)(2,1)S(1)}, f32[4,4,256]{2,1,0:T(4,128)S(1)}, bf16[2,1024,256]{2,1,0:T(8,128)(2,1)}, f32[256,1024]{1,0:T(8,128)}, bf16[256,1024]{1,0:T(8,128)(2,1)}) custom-call(s32[6]{0:T(128)S(1)} %stack.143.info, bf16[256,1024]{1,0:T(8,128)(2,1)} %copy-done.19, bf16[256,1024]{1,0:T(8,128)(2,1)} %copy-done.2, ...), custom_call_target="tpu_custom_call" | custom-call | flops 6442450944 | bytes 16535552 | tf_op jit(solution)/shard_map/attend/pallas_call | solution.py:83
  239.9 6.5 feed.6
  246.5 9.8 %feed_back.4 = (f32[256,1024]{1,0:T(8,128)S(1)}, bf16[3,256,768]{2,1,0:T(8,128)(2,1)}, bf16[3,256,768]{2,1,0:T(8,128)(2,1)}) custom-call(s32[6]{0:T(128)S(1)} %stack.143.info, bf16[256,1024]{1,0:T(8,128)(2,1)S(1)} %get-tuple-element.283.value.refs_4_, bf16[2,2,256,704]{3,2,1,0:T(8,128)(2,1)} %get-tuple-element.116.saved, bf16[704,1024]{1,0:T(8,128)(2,1)} %bitcast.220, ...), custom_call_target="tpu_custom_call" | custom-call | flops 2214592512 | bytes 32899072 | tf_op jit(solution)/shard_map/feed_back/pallas_call | solution.py:83
  257.2 13.7 %collective-permute-done.28.value.refs_1_ = bf16[256,1024]{1,0:T(8,128)(2,1)S(1)} collective-permute-done((bf16[256,1024]{1,0:T(8,128)(2,1)}, bf16[256,1024]{1,0:T(8,128)(2,1)S(1)}, u32[]{:S(2)}, u32[]{:S(2)}) %collective-permute-start.28) | collective-permute-done | bytes 524320 | tf_op jit(solution)/shard_map/ppermute | solution.py:35
  271.0 6.7 %feed.7 = (bf16[256,1024]{1,0:T(8,128)(2,1)}, bf16[2,2,256,704]{3,2,1,0:T(8,128)(2,1)}) custom-call(s32[6]{0:T(128)S(1)} %stack.143.info, bf16[256,1024]{1,0:T(8,128)(2,1)S(1)} %collective-permute-done.28.value.refs_1_, bf16[704,1024]{1,0:T(8,128)(2,1)} %bitcast.221, bf16[704,1024]{1,0:T(8,128)(2,1)} %bitcast.211, bf16[704,1024]{1,0:T(8,128)(2,1)} %bitcast.199, ...), custom_call_target="tpu_custom_call" | custom-call | flops 2214592512 | bytes 30015488 | tf_op jit(solution)/shard_map/feed/pallas_call | solution.py:83
  277.7 4.5 collective-permute-done.31.value.refs_5_
  282.2 10.4 %feed_back.5 = (bf16[256,1024]{1,0:T(8,128)(2,1)}, bf16[3,256,768]{2,1,0:T(8,128)(2,1)}, bf16[3,256,768]{2,1,0:T(8,128)(2,1)}) custom-call(s32[6]{0:T(128)S(1)} %stack.143.info, bf16[256,1024]{1,0:T(8,128)(2,1)S(1)} %collective-permute-done.31.value.refs_5_, bf16[2,2,256,704]{3,2,1,0:T(8,128)(2,1)} %get-tuple-element.118.saved, bf16[704,1024]{1,0:T(8,128)(2,1)} %bitcast.222, ...), custom_call_target="tpu_custom_call" | custom-call | flops 2214592512 | bytes 32374784 | tf_op jit(solution)/shard_map/feed_back/pallas_call | solution.py:83
  300.2 10.7 %feed_weights.2 = bf16[4,3,256,768]{3,2,1,0:T(8,128)(2,1)} custom-call(s32[6]{0:T(128)S(1)} %stack.143.info, bf16[256,1024]{1,0:T(8,128)(2,1)S(1)} %copy-done.12, bf16[256,1024]{1,0:T(8,128)(2,1)S(1)} %collective-permute-done.28.value.refs_1_, bf16[256,1024]{1,0:T(8,128)(2,1)S(1)} %collective-permute-done.33.refs_2_, bf16[256,1024]{1,0:T(8,128)(2,1)} %copy-done.51, ...), custom_call_target="tpu_custom_call" | custom-call | flops 4429185024 | bytes 13631488 | tf_op jit(solution)/shard_map/feed_weights/pallas_call | solution.py:83
  311.0 5.0 all-to-all-start.2
  326.4 14.9 %attend_back.4 = (f32[256,1024]{1,0:T(8,128)}, bf16[1024,256]{1,0:T(8,128)(2,1)S(1)}, bf16[4,2,320,256]{3,2,1,0:T(8,128)(2,1)}, bf16[4,2,320,256]{3,2,1,0:T(8,128)(2,1)}) custom-call(s32[6]{0:T(128)S(1)} %stack.143.info, bf16[256,1024]{1,0:T(8,128)(2,1)S(1)} %copy-done.10, bf16[256,1024]{1,0:T(8,128)(2,1)S(1)} %copy-done.3, ...), custom_call_target="tpu_custom_call" | custom-call | flops 8858370048 | bytes 18104320 | tf_op jit(solution)/shard_map/attend_back/pallas_call | solution.py:83
  342.6 14.4 %attend_back.5 = (f32[256,1024]{1,0:T(8,128)}, bf16[1024,256]{1,0:T(8,128)(2,1)S(1)}, bf16[4,2,320,256]{3,2,1,0:T(8,128)(2,1)}, bf16[4,2,320,256]{3,2,1,0:T(8,128)(2,1)}) custom-call(s32[6]{0:T(128)S(1)} %stack.143.info, bf16[256,1024]{1,0:T(8,128)(2,1)S(1)} %copy-done.10, bf16[256,1024]{1,0:T(8,128)(2,1)S(1)} %copy-done.3, ...), custom_call_target="tpu_custom_call" | custom-call | flops 8858370048 | bytes 18104320 | tf_op jit(solution)/shard_map/attend_back/pallas_call | solution.py:83
  361.1 10.6 %collective-permute-done.40 = bf16[256,256]{1,0:T(8,128)(2,1)S(1)} collective-permute-done((bf16[256,256]{1,0:T(8,128)(2,1)S(1)}, bf16[256,256]{1,0:T(8,128)(2,1)S(1)}, u32[]{:S(2)}, u32[]{:S(2)}) %collective-permute-start.40) | collective-permute-done | bytes 131104 | tf_op jit(solution)/shard_map/ppermute | solution.py:35
  390.0 4.8 all-to-all-start.3
  401.4 4.3 collective-permute-done.56
  408.2 9.5 %feed_back.6 = (f32[256,1024]{1,0:T(8,128)S(1)}, bf16[3,256,768]{2,1,0:T(8,128)(2,1)}, bf16[3,256,768]{2,1,0:T(8,128)(2,1)}) custom-call(s32[6]{0:T(128)S(1)} %stack.143.info, bf16[256,1024]{1,0:T(8,128)(2,1)S(1)} %get-tuple-element.214.value.refs_4_, bf16[2,2,256,704]{3,2,1,0:T(8,128)(2,1)} %get-tuple-element.134.saved, bf16[704,1024]{1,0:T(8,128)(2,1)} %bitcast.223, ...), custom_call_target="tpu_custom_call" | custom-call | flops 2214592512 | bytes 32899072 | tf_op jit(solution)/shard_map/feed_back/pallas_call | solution.py:83
  417.9 10.3 %feed_back.7 = (bf16[256,1024]{1,0:T(8,128)(2,1)}, bf16[3,256,768]{2,1,0:T(8,128)(2,1)}, bf16[3,256,768]{2,1,0:T(8,128)(2,1)}) custom-call(s32[6]{0:T(128)S(1)} %stack.143.info, bf16[256,1024]{1,0:T(8,128)(2,1)S(1)} %collective-permute-done.43.value.refs_5_, bf16[2,2,256,704]{3,2,1,0:T(8,128)(2,1)} %get-tuple-element.136.saved, bf16[704,1024]{1,0:T(8,128)(2,1)} %bitcast.224, ...), custom_call_target="tpu_custom_call" | custom-call | flops 2214592512 | bytes 32374784 | tf_op jit(solution)/shard_map/feed_back/pallas_call | solution.py:83
  434.3 15.1 %all-gather.19.cloned.1.call-done = bf16[2304,256]{1,0:T(8,128)(2,1)} async-done(((bf16[576,256]{1,0:T(8,128)(2,1)}), bf16[2304,256]{1,0:T(8,128)(2,1)}) %all-gather.19.cloned.1.call-update) | async-done | bytes 1179664 | tf_op jit(solution)/shard_map/all_gather | solution.py:744
  452.3 10.8 %feed_weights.3 = bf16[4,3,256,768]{3,2,1,0:T(8,128)(2,1)} custom-call(s32[6]{0:T(128)S(1)} %stack.143.info, bf16[256,1024]{1,0:T(8,128)(2,1)S(1)} %get-tuple-element.142.value.refs_0_, bf16[256,1024]{1,0:T(8,128)(2,1)S(1)} %copy-done.9, bf16[256,1024]{1,0:T(8,128)(2,1)S(1)} %copy-done.16, bf16[256,1024]{1,0:T(8,128)(2,1)} %copy-done.48, ...), custom_call_target="tpu_custom_call" | custom-call | flops 4429185024 | bytes 13631488 | tf_op jit(solution)/shard_map/feed_weights/pallas_call | solution.py:83
  463.1 5.1 all-to-all-start.4
  472.6 14.5 %attend_back.6 = (f32[256,1024]{1,0:T(8,128)}, bf16[1024,256]{1,0:T(8,128)(2,1)S(1)}, bf16[4,2,320,256]{3,2,1,0:T(8,128)(2,1)}, bf16[4,2,320,256]{3,2,1,0:T(8,128)(2,1)}) custom-call(s32[6]{0:T(128)S(1)} %stack.143.info, bf16[256,1024]{1,0:T(8,128)(2,1)S(1)} %get-tuple-element.156.grad_branch, bf16[256,1024]{1,0:T(8,128)(2,1)S(1)} %fusion.18.normed, ...), custom_call_target="tpu_custom_call" | custom-call | flops 8858370048 | bytes 18104320 | tf_op jit(solution)/shard_map/attend_back/pallas_call | solution.py:83
  492.4 14.8 %attend_back.7 = (f32[256,1024]{1,0:T(8,128)}, bf16[1024,256]{1,0:T(8,128)(2,1)S(1)}, bf16[4,2,320,256]{3,2,1,0:T(8,128)(2,1)}, bf16[4,2,320,256]{3,2,1,0:T(8,128)(2,1)}) custom-call(s32[6]{0:T(128)S(1)} %stack.143.info, bf16[256,1024]{1,0:T(8,128)(2,1)S(1)} %get-tuple-element.156.grad_branch, bf16[256,1024]{1,0:T(8,128)(2,1)S(1)} %fusion.18.normed, ...), custom_call_target="tpu_custom_call" | custom-call | flops 8858370048 | bytes 18104320 | tf_op jit(solution)/shard_map/attend_back/pallas_call | solution.py:83
  517.8 8.4 %collective-permute-done.64 = bf16[400,256]{1,0:T(8,128)(2,1)S(1)} collective-permute-done((bf16[400,256]{1,0:T(8,128)(2,1)S(1)}, bf16[400,256]{1,0:T(8,128)(2,1)S(1)}, u32[]{:S(2)}, u32[]{:S(2)}) %collective-permute-start.64) | collective-permute-done | bytes 204832 | tf_op jit(solution)/shard_map/ppermute | solution.py:35
  545.9 4.5 select_bitcast_fusion.1
  551.1 4.5 reduce_sum.183
  556.8 4.5 reduce_sum.188
  561.3 7.3 %collective-permute-start.69 = (bf16[3,256,768]{2,1,0:T(8,128)(2,1)}, bf16[3,256,768]{2,1,0:T(8,128)(2,1)}, u32[]{:S(2)}, u32[]{:S(2)}) collective-permute-start(bf16[3,256,768]{2,1,0:T(8,128)(2,1)} %reduce_sum.188), channel_id=1, source_target_pairs={{16,8},{20,12},{24,0},{28,4},{17,9},{21,13},{25,1},{29,5},{18,10},... | collective-permute-start | bytes 3538952 | tf_op jit(solution)/shard_map/ppermute | solution.py:868
  568.6 14.4 %all-to-all-done.5 = bf16[4,4,400,256]{3,2,1,0:T(8,128)(2,1)S(1)} async-done(((bf16[4,4,400,256]{3,2,1,0:T(8,128)(2,1)}), bf16[4,4,400,256]{3,2,1,0:T(8,128)(2,1)S(1)}, u32[]{:S(2)}, u32[]{:S(2)}) %all-to-all-start.5) | async-done | bytes 3276832 | tf_op jit(solution)/shard_map/all_to_all | solution.py:864
  585.7 4.4 maximum_select_fusion
  592.5 24.5 %all-gather.23.cloned.1.call-done = bf16[1024,1024]{1,0:T(8,128)(2,1)} async-done(((bf16[256,1024]{1,0:T(8,128)(2,1)}), bf16[1024,1024]{1,0:T(8,128)(2,1)}) %all-gather.23.cloned.1.call-update) | async-done | bytes 2097168 | tf_op jit(solution)/shard_map/all_gather | solution.py:902
  622.3 14.0 %collective-permute-done.58 = bf16[3,256,768]{2,1,0:T(8,128)(2,1)} collective-permute-done((bf16[3,256,768]{2,1,0:T(8,128)(2,1)}, bf16[3,256,768]{2,1,0:T(8,128)(2,1)}, u32[]{:S(2)}, u32[]{:S(2)}) %collective-permute-start.58) | collective-permute-done | bytes 1179680 | tf_op jit(solution)/shard_map/ppermute | solution.py:868
  (397 shorter events, 206.3 us)
Async XLA Ops:
  11.8 53.5 %collective-permute-start.3 = (f32[2,1024]{1,0:T(2,128)S(1)}, f32[2,1024]{1,0:T(2,128)S(1)}, u32[]{:S(2)}, u32[]{:S(2)}) collective-permute-start(f32[2,1024]{1,0:T(2,128)S(1)} %bitcast.193), channel_id=1, source_target_pairs={{0,16},{16,0},{1,17},{17,1},{2,18},{18,2},{3,19},{19,3},{4,20},{20... | collective-permute-start | bytes 24584 | tf_op jit(solution)/shard_map/ppermute | solution.py:30
  12.2 53.0 %collective-permute-start = (bf16[1024,512]{1,0:T(8,128)(2,1)}, bf16[1024,512]{1,0:T(8,128)(2,1)}, u32[]{:S(2)}, u32[]{:S(2)}) collective-permute-start(bf16[1024,512]{1,0:T(8,128)(2,1)} %bitcast.7.lat_here), channel_id=1, source_target_pairs={{0,16},{16,0},{1,17},{17,1},{2,18},{18,2},{3,19},{19,3},{4,20},{20... | collective-permute-start | bytes 3145736 | tf_op jit(solution)/shard_map/ppermute | solution.py:30
  13.4 56.6 %collective-permute-start.4 = (bf16[1536,256]{1,0:T(8,128)(2,1)S(1)}, bf16[1536,256]{1,0:T(8,128)(2,1)}, u32[]{:S(2)}, u32[]{:S(2)}) collective-permute-start(bf16[1536,256]{1,0:T(8,128)(2,1)S(1)} %pad_maximum_fusion.2.heads_here.h0), channel_id=1, source_target_pairs={{0,16},{16,0},{1,17},{17,1},{2,18},{18,2},{3,19},{19,3},{4,20},{20... | collective-permute-start | bytes 2359304 | tf_op jit(solution)/shard_map/ppermute | solution.py:30
  19.2 38.1 %collective-permute-start.2 = (bf16[352,1024]{1,0:T(8,128)(2,1)S(1)}, bf16[352,1024]{1,0:T(8,128)(2,1)S(1)}, u32[]{:S(2)}, u32[]{:S(2)}) collective-permute-start(bf16[352,1024]{1,0:T(8,128)(2,1)S(1)} %pad_maximum_fusion.5), channel_id=1, source_target_pairs={{0,8},{4,12},{8,0},{12,4},{1,9},{5,13},{9,1},{13,5},{2,10},{6,14},... | collective-permute-start | bytes 2162696 | tf_op jit(solution)/shard_map/ppermute | solution.py:35
  22.8 18.1 %collective-permute-start.10 = (bf16[64,1024]{1,0:T(8,128)(2,1)S(1)}, bf16[64,1024]{1,0:T(8,128)(2,1)S(1)}, u32[]{:S(2)}, u32[]{:S(2)}) collective-permute-start(bf16[64,1024]{1,0:T(8,128)(2,1)S(1)} %pad_maximum_fusion.16), channel_id=1, source_target_pairs={{0,4},{4,0},{8,12},{12,8},{1,5},{5,1},{9,13},{13,9},{2,6},{6,2},{1... | collective-permute-start | bytes 393224 | tf_op jit(solution)/shard_map/ppermute | solution.py:35
  59.5 43.6 %all-to-all-start = ((bf16[4,384,1024]{2,1,0:T(8,128)(2,1)}), bf16[4,384,1024]{2,1,0:T(8,128)(2,1)}, u32[]{:S(2)}, u32[]{:S(2)}) async-start(bf16[4,384,1024]{2,1,0:T(8,128)(2,1)} %broadcast_in_dim.8), calls=%async_computation | async-start | bytes 6291456 | tf_op jit(solution)/shard_map/all_to_all | solution.py:48
  64.2 118.6 %all-gather.13.cloned.1.call-start = ((), (), s32[]{:S(2)}) async-start(), calls=%async_computation.6 | async-start | bytes 1474560 | tf_op jit(solution)/shard_map/all_gather | solution.py:744
  103.1 33.8 %collective-permute-start.12 = (bf16[4,384,1024]{2,1,0:T(8,128)(2,1)}, bf16[4,384,1024]{2,1,0:T(8,128)(2,1)}, u32[]{:S(2)}, u32[]{:S(2)}) collective-permute-start(bf16[4,384,1024]{2,1,0:T(8,128)(2,1)} %all-to-all-done.o2.refs_6_.refs_8_.refs_10_), channel_id=1, source_target_pairs={{0,16},{16,0},{1,17},{17,1},{2,18},{18,2},{3,19},{19,3},{4,20},{20... | collective-permute-start | bytes 9437192 | tf_op jit(solution)/shard_map/ppermute | solution.py:30
  104.3 38.9 %collective-permute-start.13 = (bf16[704,1024]{1,0:T(8,128)(2,1)}, bf16[704,1024]{1,0:T(8,128)(2,1)}, u32[]{:S(2)}, u32[]{:S(2)}) collective-permute-start(bf16[704,1024]{1,0:T(8,128)(2,1)} %bitcast.216), channel_id=1, source_target_pairs={{0,16},{16,0},{1,17},{17,1},{2,18},{18,2},{3,19},{19,3},{4,20},{20... | collective-permute-start | bytes 4325384 | tf_op jit(solution)/shard_map/ppermute | solution.py:30
  104.3 38.9 %collective-permute-start.14 = (bf16[704,1024]{1,0:T(8,128)(2,1)}, bf16[704,1024]{1,0:T(8,128)(2,1)}, u32[]{:S(2)}, u32[]{:S(2)}) collective-permute-start(bf16[704,1024]{1,0:T(8,128)(2,1)} %bitcast.206), channel_id=1, source_target_pairs={{0,16},{16,0},{1,17},{17,1},{2,18},{18,2},{3,19},{19,3},{4,20},{20... | collective-permute-start | bytes 4325384 | tf_op jit(solution)/shard_map/ppermute | solution.py:30
  104.8 38.4 %collective-permute-start.15 = (bf16[704,1024]{1,0:T(8,128)(2,1)S(1)}, bf16[704,1024]{1,0:T(8,128)(2,1)}, u32[]{:S(2)}, u32[]{:S(2)}) collective-permute-start(bf16[704,1024]{1,0:T(8,128)(2,1)S(1)} %bitcast.204), channel_id=1, source_target_pairs={{0,16},{16,0},{1,17},{17,1},{2,18},{18,2},{3,19},{19,3},{4,20},{20... | collective-permute-start | bytes 4325384 | tf_op jit(solution)/shard_map/ppermute | solution.py:30
  132.6 29.1 %collective-permute-start.26 = (bf16[288,1024]{1,0:T(8,128)(2,1)}, bf16[288,1024]{1,0:T(8,128)(2,1)}, u32[]{:S(2)}, u32[]{:S(2)}) collective-permute-start(bf16[288,1024]{1,0:T(8,128)(2,1)} %slice.258), channel_id=1, source_target_pairs={{0,8},{4,12},{8,0},{12,4},{1,9},{5,13},{9,1},{13,5},{2,10},{6,14},... | collective-permute-start | bytes 1769480 | tf_op jit(solution)/shard_map/ppermute | solution.py:35
  164.9 40.4 %all-to-all-start.1 = ((bf16[4,384,1024]{2,1,0:T(8,128)(2,1)}), bf16[4,384,1024]{2,1,0:T(8,128)(2,1)}, u32[]{:S(2)}, u32[]{:S(2)}) async-start(bf16[4,384,1024]{2,1,0:T(8,128)(2,1)} %broadcast_in_dim.9), calls=%async_computation.1 | async-start | bytes 6291456 | tf_op jit(solution)/shard_map/all_to_all | solution.py:48
  169.6 146.5 %all-gather.15.cloned.1.call-start = ((), (), s32[]{:S(2)}) async-start(), calls=%async_computation.7 | async-start | bytes 2621440 | tf_op jit(solution)/shard_map/all_gather | solution.py:902
  237.4 33.5 %collective-permute-start.28 = (bf16[256,1024]{1,0:T(8,128)(2,1)}, bf16[256,1024]{1,0:T(8,128)(2,1)S(1)}, u32[]{:S(2)}, u32[]{:S(2)}) collective-permute-start(bf16[256,1024]{1,0:T(8,128)(2,1)} %get-tuple-element.112.value.refs_0_), channel_id=1, source_target_pairs={{0,4},{4,0},{8,12},{12,8},{1,5},{5,1},{9,13},{13,9},{2,6},{6,2},{1... | collective-permute-start | bytes 1572872 | tf_op jit(solution)/shard_map/ppermute | solution.py:35
  237.4 44.8 %collective-permute-start.31 = (bf16[256,1024]{1,0:T(8,128)(2,1)S(1)}, bf16[256,1024]{1,0:T(8,128)(2,1)S(1)}, u32[]{:S(2)}, u32[]{:S(2)}) collective-permute-start(bf16[256,1024]{1,0:T(8,128)(2,1)S(1)} %get-tuple-element.283.value.refs_4_), channel_id=1, source_target_pairs={{0,4},{4,0},{8,12},{12,8},{1,5},{5,1},{9,13},{13,9},{2,6},{6,2},{1... | collective-permute-start | bytes 1572872 | tf_op jit(solution)/shard_map/ppermute | solution.py:35
  256.2 42.4 %collective-permute-start.37 = (bf16[3,256,768]{2,1,0:T(8,128)(2,1)}, bf16[3,256,768]{2,1,0:T(8,128)(2,1)S(1)}, u32[]{:S(2)}, u32[]{:S(2)}) collective-permute-start(bf16[3,256,768]{2,1,0:T(8,128)(2,1)} %get-tuple-element.122), channel_id=1, source_target_pairs={{0,16},{16,0},{1,17},{17,1},{2,18},{18,2},{3,19},{19,3},{4,20},{20... | collective-permute-start | bytes 3538952 | tf_op jit(solution)/shard_map/ppermute | solution.py:30
  297.1 18.9 %collective-permute-start.32 = (bf16[256,1024]{1,0:T(8,128)(2,1)}, bf16[256,1024]{1,0:T(8,128)(2,1)S(1)}, u32[]{:S(2)}, u32[]{:S(2)}) collective-permute-start(bf16[256,1024]{1,0:T(8,128)(2,1)} %get-tuple-element.119), channel_id=1, source_target_pairs={{0,4},{4,0},{8,12},{12,8},{1,5},{5,1},{9,13},{13,9},{2,6},{6,2},{1... | collective-permute-start | bytes 1572872 | tf_op jit(solution)/shard_map/ppermute | solution.py:35
  297.9 23.9 %collective-permute-start.29 = (bf16[256,1024]{1,0:T(8,128)(2,1)}, bf16[256,1024]{1,0:T(8,128)(2,1)}, u32[]{:S(2)}, u32[]{:S(2)}) collective-permute-start(bf16[256,1024]{1,0:T(8,128)(2,1)} %get-tuple-element.115), channel_id=1, source_target_pairs={{0,4},{4,0},{8,12},{12,8},{1,5},{5,1},{9,13},{13,9},{2,6},{6,2},{1... | collective-permute-start | bytes 1572872 | tf_op jit(solution)/shard_map/ppermute | solution.py:35
  311.0 64.9 %all-to-all-start.2 = ((bf16[4,3,256,768]{3,2,1,0:T(8,128)(2,1)}), bf16[4,3,256,768]{3,2,1,0:T(8,128)(2,1)}, u32[]{:S(2)}, u32[]{:S(2)}) async-start(bf16[4,3,256,768]{3,2,1,0:T(8,128)(2,1)} %feed_weights.2), calls=%async_computation.2 | async-start | bytes 9437184 | tf_op jit(solution)/shard_map/all_to_all | solution.py:821
  315.9 59.9 %all-gather.17.cloned.1.call-start = ((), (), s32[]{:S(2)}) async-start(), calls=%async_computation.8 | async-start | bytes 2621440 | tf_op jit(solution)/shard_map/all_gather | solution.py:902
  341.3 16.5 %collective-permute-start.39 = (bf16[2,256,256]{2,1,0:T(8,128)(2,1)S(1)}, bf16[2,256,256]{2,1,0:T(8,128)(2,1)S(1)}, u32[]{:S(2)}, u32[]{:S(2)}) collective-permute-start(bf16[2,256,256]{2,1,0:T(8,128)(2,1)S(1)} %dynamic-slice_bitcast_fusion.5), channel_id=1, source_target_pairs={{0,16},{16,0},{1,17},{17,1},{2,18},{18,2},{3,19},{19,3},{4,20},{20... | collective-permute-start | bytes 786440 | tf_op jit(solution)/shard_map/ppermute | solution.py:30
  357.0 26.0 %collective-permute-start.45 = (bf16[4,2,320,256]{3,2,1,0:T(8,128)(2,1)}, bf16[4,2,320,256]{3,2,1,0:T(8,128)(2,1)}, u32[]{:S(2)}, u32[]{:S(2)}) collective-permute-start(bf16[4,2,320,256]{3,2,1,0:T(8,128)(2,1)} %get-tuple-element.139), channel_id=1, source_target_pairs={{0,16},{16,0},{1,17},{17,1},{2,18},{18,2},{3,19},{19,3},{4,20},{20... | collective-permute-start | bytes 3932168 | tf_op jit(solution)/shard_map/ppermute | solution.py:30
  357.1 28.1 %collective-permute-start.46 = (bf16[4,2,320,256]{3,2,1,0:T(8,128)(2,1)}, bf16[4,2,320,256]{3,2,1,0:T(8,128)(2,1)}, u32[]{:S(2)}, u32[]{:S(2)}) collective-permute-start(bf16[4,2,320,256]{3,2,1,0:T(8,128)(2,1)} %get-tuple-element.141), channel_id=1, source_target_pairs={{0,16},{16,0},{1,17},{17,1},{2,18},{18,2},{3,19},{19,3},{4,20},{20... | collective-permute-start | bytes 3932168 | tf_op jit(solution)/shard_map/ppermute | solution.py:30
  390.0 59.5 %all-to-all-start.3 = ((bf16[4,4,400,256]{3,2,1,0:T(8,128)(2,1)}), bf16[4,4,400,256]{3,2,1,0:T(8,128)(2,1)}, u32[]{:S(2)}, u32[]{:S(2)}) async-start(bf16[4,4,400,256]{3,2,1,0:T(8,128)(2,1)} %pad_maximum_fusion), calls=%async_computation.3 | async-start | bytes 6553600 | tf_op jit(solution)/shard_map/all_to_all | solution.py:864
  394.8 54.6 %all-gather.19.cloned.1.call-start = ((), (), s32[]{:S(2)}) async-start(), calls=%async_computation.9 | async-start | bytes 1474560 | tf_op jit(solution)/shard_map/all_gather | solution.py:744
  401.1 16.8 %collective-permute-start.43 = (bf16[256,1024]{1,0:T(8,128)(2,1)S(1)}, bf16[256,1024]{1,0:T(8,128)(2,1)S(1)}, u32[]{:S(2)}, u32[]{:S(2)}) collective-permute-start(bf16[256,1024]{1,0:T(8,128)(2,1)S(1)} %get-tuple-element.214.value.refs_4_), channel_id=1, source_target_pairs={{0,4},{4,0},{8,12},{12,8},{1,5},{5,1},{9,13},{13,9},{2,6},{6,2},{1... | collective-permute-start | bytes 1572872 | tf_op jit(solution)/shard_map/ppermute | solution.py:35
  406.5 119.7 %all-gather.21.cloned.1.call-start = ((), (), s32[]{:S(2)}) async-start(), calls=%async_computation.10 | async-start | bytes 2621440 | tf_op jit(solution)/shard_map/all_gather | solution.py:902
  406.6 22.6 %collective-permute-start.48 = (bf16[256,1024]{1,0:T(8,128)(2,1)S(1)}, bf16[256,1024]{1,0:T(8,128)(2,1)S(1)}, u32[]{:S(2)}, u32[]{:S(2)}) collective-permute-start(bf16[256,1024]{1,0:T(8,128)(2,1)S(1)} %get-tuple-element.142.value.refs_0_), channel_id=1, source_target_pairs={{0,16},{16,0},{1,17},{17,1},{2,18},{18,2},{3,19},{19,3},{4,20},{20... | collective-permute-start | bytes 1572872 | tf_op jit(solution)/shard_map/ppermute | solution.py:30
  417.7 32.4 %collective-permute-start.52 = (bf16[3,256,768]{2,1,0:T(8,128)(2,1)}, bf16[3,256,768]{2,1,0:T(8,128)(2,1)}, u32[]{:S(2)}, u32[]{:S(2)}) collective-permute-start(bf16[3,256,768]{2,1,0:T(8,128)(2,1)} %get-tuple-element.145), channel_id=1, source_target_pairs={{0,16},{16,0},{1,17},{17,1},{2,18},{18,2},{3,19},{19,3},{4,20},{20... | collective-permute-start | bytes 3538952 | tf_op jit(solution)/shard_map/ppermute | solution.py:30
  428.2 22.0 %collective-permute-start.53 = (bf16[3,256,768]{2,1,0:T(8,128)(2,1)}, bf16[3,256,768]{2,1,0:T(8,128)(2,1)}, u32[]{:S(2)}, u32[]{:S(2)}) collective-permute-start(bf16[3,256,768]{2,1,0:T(8,128)(2,1)} %get-tuple-element.146), channel_id=1, source_target_pairs={{0,16},{16,0},{1,17},{17,1},{2,18},{18,2},{3,19},{19,3},{4,20},{20... | collective-permute-start | bytes 3538952 | tf_op jit(solution)/shard_map/ppermute | solution.py:30
  428.8 20.6 %collective-permute-start.50 = (bf16[256,1024]{1,0:T(8,128)(2,1)S(1)}, bf16[256,1024]{1,0:T(8,128)(2,1)}, u32[]{:S(2)}, u32[]{:S(2)}) collective-permute-start(bf16[256,1024]{1,0:T(8,128)(2,1)S(1)} %get-tuple-element.214.value.refs_4_), channel_id=1, source_target_pairs={{0,16},{16,0},{1,17},{17,1},{2,18},{18,2},{3,19},{19,3},{4,20},{20... | collective-permute-start | bytes 1572872 | tf_op jit(solution)/shard_map/ppermute | solution.py:30
  430.0 20.2 %collective-permute-start.51 = (bf16[256,1024]{1,0:T(8,128)(2,1)S(1)}, bf16[256,1024]{1,0:T(8,128)(2,1)}, u32[]{:S(2)}, u32[]{:S(2)}) collective-permute-start(bf16[256,1024]{1,0:T(8,128)(2,1)S(1)} %collective-permute-done.43.value.refs_5_), channel_id=1, source_target_pairs={{0,16},{16,0},{1,17},{17,1},{2,18},{18,2},{3,19},{19,3},{4,20},{20... | collective-permute-start | bytes 1572872 | tf_op jit(solution)/shard_map/ppermute | solution.py:30
  432.6 35.9 %collective-permute-start.44 = (bf16[256,1024]{1,0:T(8,128)(2,1)}, bf16[256,1024]{1,0:T(8,128)(2,1)}, u32[]{:S(2)}, u32[]{:S(2)}) collective-permute-start(bf16[256,1024]{1,0:T(8,128)(2,1)} %get-tuple-element.137), channel_id=1, source_target_pairs={{0,4},{4,0},{8,12},{12,8},{1,5},{5,1},{9,13},{13,9},{2,6},{6,2},{1... | collective-permute-start | bytes 1572872 | tf_op jit(solution)/shard_map/ppermute | solution.py:35
  449.4 23.1 %collective-permute-start.57 = (bf16[4,576,256]{2,1,0:T(8,128)(2,1)}, bf16[4,576,256]{2,1,0:T(8,128)(2,1)}, u32[]{:S(2)}, u32[]{:S(2)}) collective-permute-start(bf16[4,576,256]{2,1,0:T(8,128)(2,1)} %bitcast.257), channel_id=1, source_target_pairs={{0,16},{16,0},{1,17},{17,1},{2,18},{18,2},{3,19},{19,3},{4,20},{20... | collective-permute-start | bytes 3538952 | tf_op jit(solution)/shard_map/ppermute | solution.py:30
  463.1 63.2 %all-to-all-start.4 = ((bf16[4,3,256,768]{3,2,1,0:T(8,128)(2,1)}), bf16[4,3,256,768]{3,2,1,0:T(8,128)(2,1)}, u32[]{:S(2)}, u32[]{:S(2)}) async-start(bf16[4,3,256,768]{3,2,1,0:T(8,128)(2,1)} %feed_weights.3), calls=%async_computation.4 | async-start | bytes 9437184 | tf_op jit(solution)/shard_map/all_to_all | solution.py:821
  468.2 148.8 %all-gather.23.cloned.1.call-start = ((), (), s32[]{:S(2)}) async-start(), calls=%async_computation.11 | async-start | bytes 2621440 | tf_op jit(solution)/shard_map/all_gather | solution.py:902
  487.8 20.9 %collective-permute-start.59 = (bf16[2,256,256]{2,1,0:T(8,128)(2,1)}, bf16[2,256,256]{2,1,0:T(8,128)(2,1)}, u32[]{:S(2)}, u32[]{:S(2)}) collective-permute-start(bf16[2,256,256]{2,1,0:T(8,128)(2,1)} %dynamic-slice_bitcast_fusion.3), channel_id=1, source_target_pairs={{0,16},{16,0},{1,17},{17,1},{2,18},{18,2},{3,19},{19,3},{4,20},{20... | collective-permute-start | bytes 786440 | tf_op jit(solution)/shard_map/ppermute | solution.py:30
  491.2 23.8 %collective-permute-start.63 = (bf16[2,400,256]{2,1,0:T(8,128)(2,1)}, bf16[2,400,256]{2,1,0:T(8,128)(2,1)S(1)}, u32[]{:S(2)}, u32[]{:S(2)}) collective-permute-start(bf16[2,400,256]{2,1,0:T(8,128)(2,1)} %slice.214), channel_id=1, source_target_pairs={{0,4},{4,0},{8,12},{12,8},{1,5},{5,1},{9,13},{13,9},{2,6},{6,2},{1... | collective-permute-start | bytes 1228808 | tf_op jit(solution)/shard_map/ppermute | solution.py:35
  508.1 28.2 %collective-permute-start.66 = (bf16[4,2,320,256]{3,2,1,0:T(8,128)(2,1)}, bf16[4,2,320,256]{3,2,1,0:T(8,128)(2,1)}, u32[]{:S(2)}, u32[]{:S(2)}) collective-permute-start(bf16[4,2,320,256]{3,2,1,0:T(8,128)(2,1)} %get-tuple-element.162), channel_id=1, source_target_pairs={{0,16},{16,0},{1,17},{17,1},{2,18},{18,2},{3,19},{19,3},{4,20},{20... | collective-permute-start | bytes 3932168 | tf_op jit(solution)/shard_map/ppermute | solution.py:30
  508.2 28.1 %collective-permute-start.67 = (bf16[4,2,320,256]{3,2,1,0:T(8,128)(2,1)}, bf16[4,2,320,256]{3,2,1,0:T(8,128)(2,1)}, u32[]{:S(2)}, u32[]{:S(2)}) collective-permute-start(bf16[4,2,320,256]{3,2,1,0:T(8,128)(2,1)} %get-tuple-element.165), channel_id=1, source_target_pairs={{0,16},{16,0},{1,17},{17,1},{2,18},{18,2},{3,19},{19,3},{4,20},{20... | collective-permute-start | bytes 3932168 | tf_op jit(solution)/shard_map/ppermute | solution.py:30
  542.1 40.8 %all-to-all-start.5 = ((bf16[4,4,400,256]{3,2,1,0:T(8,128)(2,1)}), bf16[4,4,400,256]{3,2,1,0:T(8,128)(2,1)S(1)}, u32[]{:S(2)}, u32[]{:S(2)}) async-start(bf16[4,4,400,256]{3,2,1,0:T(8,128)(2,1)} %pad_maximum_fusion.1), calls=%async_computation.5 | async-start | bytes 6553600 | tf_op jit(solution)/shard_map/all_to_all | solution.py:864
  550.4 35.3 %collective-permute-start.30 = (bf16[4,256,1024]{2,1,0:T(8,128)(2,1)}, bf16[4,256,1024]{2,1,0:T(8,128)(2,1)}, u32[]{:S(2)}, u32[]{:S(2)}) collective-permute-start(bf16[4,256,1024]{2,1,0:T(8,128)(2,1)} %get-tuple-element.223), channel_id=1, source_target_pairs={{0,16},{16,0},{1,17},{17,1},{2,18},{18,2},{3,19},{19,3},{4,20},{20... | collective-permute-start | bytes 6291464 | tf_op jit(solution)/shard_map/ppermute | solution.py:30
  555.5 80.8 %collective-permute-start.58 = (bf16[3,256,768]{2,1,0:T(8,128)(2,1)}, bf16[3,256,768]{2,1,0:T(8,128)(2,1)}, u32[]{:S(2)}, u32[]{:S(2)}) collective-permute-start(bf16[3,256,768]{2,1,0:T(8,128)(2,1)} %reduce_sum.183), channel_id=1, source_target_pairs={{0,24},{4,28},{8,16},{12,20},{1,25},{5,29},{9,17},{13,21},{2,26},{... | collective-permute-start | bytes 3538952 | tf_op jit(solution)/shard_map/ppermute | solution.py:868
  561.3 75.0 %collective-permute-start.69 = (bf16[3,256,768]{2,1,0:T(8,128)(2,1)}, bf16[3,256,768]{2,1,0:T(8,128)(2,1)}, u32[]{:S(2)}, u32[]{:S(2)}) collective-permute-start(bf16[3,256,768]{2,1,0:T(8,128)(2,1)} %reduce_sum.188), channel_id=1, source_target_pairs={{16,8},{20,12},{24,0},{28,4},{17,9},{21,13},{25,1},{29,5},{18,10},... | collective-permute-start | bytes 3538952 | tf_op jit(solution)/shard_map/ppermute | solution.py:868
  585.6 36.5 %collective-permute-start.70 = (bf16[2,400,256]{2,1,0:T(8,128)(2,1)S(1)}, bf16[2,400,256]{2,1,0:T(8,128)(2,1)S(1)}, u32[]{:S(2)}, u32[]{:S(2)}) collective-permute-start(bf16[2,400,256]{2,1,0:T(8,128)(2,1)S(1)} %slice.226), channel_id=1, source_target_pairs={{0,4},{4,0},{8,12},{12,8},{1,5},{5,1},{9,13},{13,9},{2,6},{6,2},{1... | collective-permute-start | bytes 1228808 | tf_op jit(solution)/shard_map/ppermute | solution.py:35
  621.0 31.6 %collective-permute-start.65 = (bf16[4,256,1024]{2,1,0:T(8,128)(2,1)}, bf16[4,256,1024]{2,1,0:T(8,128)(2,1)}, u32[]{:S(2)}, u32[]{:S(2)}) collective-permute-start(bf16[4,256,1024]{2,1,0:T(8,128)(2,1)} %get-tuple-element.221), channel_id=1, source_target_pairs={{0,16},{16,0},{1,17},{17,1},{2,18},{18,2},{3,19},{19,3},{4,20},{20... | collective-permute-start | bytes 6291464 | tf_op jit(solution)/shard_map/ppermute | solution.py:30
  622.2 19.0 %collective-permute-start.71 = (bf16[400,256]{1,0:T(8,128)(2,1)S(1)}, bf16[400,256]{1,0:T(8,128)(2,1)S(1)}, u32[]{:S(2)}, u32[]{:S(2)}) collective-permute-start(bf16[400,256]{1,0:T(8,128)(2,1)S(1)} %slice_bitcast_fusion.4), channel_id=1, source_target_pairs={{0,8},{4,12},{8,0},{12,4},{1,9},{5,13},{9,1},{13,5},{2,10},{6,14},... | collective-permute-start | bytes 614408 | tf_op jit(solution)/shard_map/ppermute | solution.py:35
  (89 other events, 764.4 us)
Sparse Core Ops, SparseCore 0:
  135.2 27.0 all-gather.12
  217.9 59.1 all-gather.14
  325.4 48.7 all-gather.16
  406.6 42.6 all-gather.18
  451.4 45.9 all-gather.20
  536.4 80.6 all-gather.22

commit v4 on v3

--- a/solution.py
+++ b/solution.py
@@ -667,6 +667,41 @@
     )[0]
 
 
+def rows_kernel(info, first, first_other, second, second_other, out, held, sems):
+    planes, rows, _ = first.shape
+    for core, sources in ((0, (first, first_other)), (1, (second_other, second))):
+
+        @pl.when(info[CORE] == core)
+        def _(sources=sources):
+            copies = [pltpu.make_async_copy(v, held.at[:, at], sems.at[0, at]) for at, v in enumerate(sources)]
+            for copy in copies:
+                copy.start()
+            for copy in copies:
+                copy.wait()
+
+    whole_copy = pltpu.make_async_copy(held, out, sems.at[1, 0])
+    whole_copy.start()
+    whole_copy.wait()
+
+
+def rows_call(info, *arrays):
+    planes, rows, width = arrays[0].shape
+    shape = (planes, 2, rows, width)
+    out = kernel_call(
+        rows_kernel,
+        info,
+        arrays,
+        (1,),
+        [pl.BlockSpec(memory_space=pl.ANY)] * 4,
+        [pl.BlockSpec(memory_space=pl.ANY)],
+        [like(shape, bf16)],
+        [pltpu.VMEM(shape, bf16), pltpu.SemaphoreType.DMA((2, 2))],
+        "rows",
+        0,
+    )[0]
+    return out.reshape(planes * 2 * rows, width)
+
+
 def shards(inputs, cotangent, lengths, w_query, w_latent, w_key, w_value, w_out, gains, w_gate, w_up, w_down):
     core = lax.axis_index("section")
     z = lax.axis_index("tensor")
@@ -720,11 +755,8 @@
     main_pieces = layers_of(feed_and_out(core), core_swap(feed_and_out(1 - core)))
     head_pieces = layers_of(piece_of(heads_here, core), core_swap(piece_of(heads_here, 1 - core)))
     head_piece, out_piece, feed_piece = piece_rows(head_rows), piece_rows(out_rows), piece_rows(feed_rows)
-    out_pieces = jnp.concatenate([piece[:out_piece] for piece in main_pieces], axis=0)
-    feed_far = z_swap(jnp.concatenate([out_pieces, main_pieces[0][out_piece:]], axis=0), planes // 2)
-    out_far = [z_swap(out_pieces, 1), feed_far[: 2 * out_piece], z_swap(out_pieces, 3)]
-    out_far = [[v[layer * out_piece : (layer + 1) * out_piece] for v in out_far] for layer in range(layers)]
-    feed_far = feed_far[2 * out_piece :]
+    out_far = [z_swap(main_pieces[0][:out_piece], step) for step in range(1, planes)]
+    feed_far = z_swap(main_pieces[0][out_piece:], planes // 2)
     out_there = core_swap(tie(out_here, feed_far))
     feed_there = [core_swap(tie(v, feed_far)) for v in feed_here]
     latents_w = [jnp.where(core == layer, lat_here, lat_there) for layer in range(layers)]
@@ -839,7 +871,11 @@
                 lax.dynamic_index_in_dim(total, 1 - near, 0, False), 1
             )
             lat_parts.append(total)
-        lat_parts[1] = tie(lat_parts[1], feed_parts, *hooks[2]())
+        if layer == 0:
+            feed_sums = jnp.sum(feed_parts.astype(f32), axis=0).astype(bf16)
+            lat_parts[1] = tie(lat_parts[1], feed_sums, *hooks[2]())
+        else:
+            lat_parts[1] = tie(lat_parts[1], feed_parts, *hooks[2]())
         lat_own = by_group(jnp.stack(lat_parts[::-1]))
         lat_own = jnp.concatenate([lat_own[0], lat_own[1]], axis=1)
         grad_norm = grad_norms[0] + grad_norms[1] + dot_nt(lat_own, latents_w[layer])
@@ -856,7 +892,8 @@
         small_send = lax.dynamic_slice_in_dim(small, (1 - core) * half, half, 2)
         small_parts = (small_keep, core_swap(small_send))
 
-        feed_sums = jnp.sum(tie(feed_parts, grad_x).astype(f32), axis=0).astype(bf16)
+        if layer == 1:
+            feed_sums = jnp.sum(tie(feed_parts, grad_x).astype(f32), axis=0).astype(bf16)
         if layer == 0:
             pack_parts_here = [(a, tie(b, grad_x)) for a, b in pack_parts_here]
         pack_total = jnp.concatenate([a + b for a, b in pack_parts_here[::-1]], axis=1)
@@ -865,7 +902,8 @@
 
         def finish_feed():
             pairs = [((1 - layer) * planes + i, layer * planes + (i ^ (planes // 2))) for i in range(planes)]
-            return feed_sums.astype(f32) + lax.ppermute(feed_sums, ("section", "tensor"), pairs).astype(f32)
+            far = lax.ppermute(feed_sums, ("section", "tensor"), pairs)
+            return feed_sums.astype(f32) + far.astype(f32), far
 
         def finish_pack(*after):
             parts = tie(pack_parts, *after)
@@ -877,7 +915,7 @@
 
     lat0 = first_latents()
     first_out, messages = first_attention(feed_far, lat0)
-    main0 = gather(out_far[0] + [feed_far], (), messages)
+    main0 = gather(out_far + [feed_far], (), messages)
     outs0 = (out_here, out_there) + main0 + (0, out_piece)
     at = (planes - 1) * out_piece
     feed0 = (feed_here, feed_there, [main0 + (at + k * feed_piece, feed_piece) for k in range(3)])
@@ -885,8 +923,9 @@
     near_heads1 = gather_slow(over_planes(head_pieces[1]), (first_out,))
     part0, saved0, far_normed2 = feed_own(0, normed2_0, feed0)
     far_normed2 = tie(far_normed2, near_heads1)
-    feed_far1 = z_swap(tie(main_pieces[1][out_piece:], *messages), planes // 2)
-    near1 = gather_near(out_far[1] + [feed_far1], part0)
+    main_piece = tie(main_pieces[1], *messages)
+    far_main = over_planes(main_piece[:out_piece]) + [z_swap(main_piece[out_piece:], planes // 2)]
+    near1 = gather_near(far_main, part0)
     out0, far_saved0 = feed_rest(0, residual0, part0, far_normed2, feed0)
     kept0 = [normed2_0, far_normed2, saved0, far_saved0]
     main1 = near1, core_swap(tie(near1, out0))
@@ -901,14 +940,11 @@
     def gather_rows(own):
         return lax.all_gather(own, "tensor", axis=0, tiled=False)
 
-    def finish_rows(firsts, seconds):
-        mine = jnp.where(core == 0, firsts, seconds)
-        other = core_swap(jnp.where(core == 0, seconds, firsts))
-        both = jnp.where(core == 0, jnp.stack([mine, other], axis=1), jnp.stack([other, mine], axis=1))
-        return both.reshape(planes * 2 * rows, width)
+    def to_core(layer, found):
+        return found, lax.ppermute(found, "section", [(1 - layer, layer)])
 
     rows_out = [gather_rows(out0), gather_rows(out1)]
-    near_heads0 = gather_slow(over_planes(head_pieces[0]), (out0,))
+    near_heads0 = gather_slow(over_planes(tie(head_pieces[0], normed2_1)), (part1,))
     heads0 = (heads_here, heads_there, near_heads0, core_swap(tie(near_heads0, out1)), 0, head_piece)
     grad1, pack_parts1, finish_feed1, finish_pack1 = backward(
         1, own_target, out0, normed1, lat1, mixed1, lse1, residual1, kept1, (heads1, outs1), feed1,
@@ -917,9 +953,12 @@
     normed0 = normalise(own_in, gains_all[0][0])
     later = {}
 
+    def before_weights():
+        later["feed"], far = finish_feed1()
+        return (pack_parts1, far)
+
     def during_attention(token):
-        later["feed"] = finish_feed1()
-        return (later["feed"],)
+        return ()
 
     def after_attention():
         later["pack"] = finish_pack1()
@@ -928,16 +967,16 @@
 
     grad0, _, finish_feed0, finish_pack0 = backward(
         0, grad1, own_in, normed0, lat0, mixed0, lse0, residual0, kept0, (heads0, outs0), feed0,
-        [lambda: (), during_attention, after_attention, lambda: (pack_parts1,)],
+        [lambda: (), during_attention, after_attention, before_weights],
     )
     rows_grad0 = gather_rows(grad0)
-    layer_outputs = finish_rows(*rows_out)
-    input_grads = finish_rows(rows_grad0, later["grad"])
-
-    feed_final0 = finish_feed0()
+    layer_outputs = rows_call(info, *to_core(0, rows_out[0]), *to_core(1, rows_out[1]))
+    input_grads = rows_call(info, *to_core(0, rows_grad0), *to_core(1, later["grad"]))
+
+    feed_final0, feed_far0 = finish_feed0()
     feed_total = jnp.where(core == 0, feed_final0, later["feed"])
     gate_t, up_t, down_t = feed_total[:, :, :hidden_cols]
-    halves = finish_core(finish_pack0(feed_final0), later["pack"]).astype(f32)
+    halves = finish_core(finish_pack0(), later["pack"]).astype(f32)
     main = (head_rows + width) // dp // 2
     query_t, key_t = halves[0, : width // dp], halves[0, width // dp : main]
     value_t, out_t = halves[1, : latent // dp], halves[1, latent // dp : main]

time: 671 us -> 649 us (0.967)
  waiting for transfers between devices: 236 us -> 209 us
  starting transfers between devices: 95.4 us -> 118 us
  other arithmetic: 77.8 us -> 60.2 us
  local copies, waits for them, and re-layouts: 43.6 us -> 33.2 us
  Pallas kernels: 183 us -> 193 us
    all_gather x4, waiting for transfers between devices: 24.6 us -> 8.81 us  [gather_rows(): return lax.all_gather(own, 'tensor', axis=0, tiled=False)]
    all_to_all x2, waiting for transfers between devices: 14.4 us -> 27.3 us  [backward(): lax.all_to_all(jnp.concatenate([pack_total, small_total], axis=2), 'dp',...]
    pallas_call x17 -> x19, Pallas kernels: 183 us -> 193 us  [kernel_call(): pl.pallas_call(kernel, grid_spec=pltpu.PrefetchScalarGridSpec(num_scalar_...]
    all_gather x2, waiting for transfers between devices: 15.1 us -> 5.23 us  [gather_slow(): lax.all_gather(jnp.concatenate([tie(v, *before) for v in parts], axis=0),...]
    ppermute x2 -> x6, waiting for transfers between devices: 14.1 us -> 4.28 us  [the longest x2 4.27 us: finish_feed(): far = lax.ppermute(feed_sums, ('section', 'tensor'), pairs)]
    ppermute x27 -> x31, starting transfers between devices: 25.3 us -> 34.5 us  [z_swap(): return lax.ppermute(value, 'tensor', [(i, i ^ step) for i in range(count)])]
    another operation x2 -> x0, other arithmetic: 8.47 us -> none  [finish_rows(): jnp.stack([mine, other], axis=1)]
    ppermute x2 -> x6, starting transfers between devices: 8.54 us -> 16.6 us  [the longest x4 10.8 us: to_core(): return (found, lax.ppermute(found, 'section', [(1 - layer, layer)]))]
  transfers between devices with their start and end apart: 85 -> 91, of which waited for: 35 -> 35; matrix products, arithmetic and copies ran while one was open for 17% -> 15% of each run, Pallas kernels for 27% -> 29%
where the time goes in v4:
time: 649 us; the launch traced here: 643 us
  waiting for transfers between devices  209 us (32%)
  Pallas kernels  193 us (30%)
  starting transfers between devices  118 us (18%)
  other arithmetic  60.2 us (9%)
  local copies, waits for them, and re-layouts  33.2 us (5%)
  between operations  15.8 us (2%)
  matrix products  14.3 us (2%)
    pallas_call x19, Pallas kernels, kernel_call(): pl.pallas_call(kernel, grid_spec=pltpu.PrefetchScalarGridSpec(num_scalar_...  193 us
    ppermute x31, waiting for transfers between devices, z_swap(): return lax.ppermute(value, 'tensor', [(i, i ^ step) for i in range(count)])  141 us
    ppermute x31, starting transfers between devices, z_swap(): return lax.ppermute(value, 'tensor', [(i, i ^ step) for i in range(count)])  34.5 us
    ppermute x38, starting transfers between devices, core_swap(): return lax.ppermute(value, 'section', [(0, 1), (1, 0)])  29.3 us
    all_to_all x2, waiting for transfers between devices, backward(): lax.all_to_all(jnp.concatenate([pack_total, small_total], axis=2), 'dp',...  27.3 us
  transfers between devices with their start and end apart: 91, of which 35 were waited for; matrix products, arithmetic and copies ran while one was open for 15% of the time, Pallas kernels for 29%

profile of v4, /device:TPU:1, one launch (start us, length us, event | category | flops | bytes accessed | tf_op | source)
XLA Modules:
  0.0 643.0 jit_solution(1751148380746836289)
XLA Ops:
  26.4 7.4 %collective-permute-done.10 = bf16[32,1024]{1,0:T(8,128)(2,1)S(1)} collective-permute-done((bf16[32,1024]{1,0:T(8,128)(2,1)S(1)}, bf16[32,1024]{1,0:T(8,128)(2,1)S(1)}, u32[]{:S(2)}, u32[]{:S(2)}) %collective-permute-start.10) | collective-permute-done | bytes 65568 | tf_op jit(solution)/shard_map/ppermute | solution.py:35
  35.8 14.5 %collective-permute-done.11 = bf16[32,1024]{1,0:T(8,128)(2,1)S(1)} collective-permute-done((bf16[32,1024]{1,0:T(8,128)(2,1)S(1)}, bf16[32,1024]{1,0:T(8,128)(2,1)S(1)}, u32[]{:S(2)}, u32[]{:S(2)}) %collective-permute-start.11) | collective-permute-done | bytes 65568 | tf_op jit(solution)/shard_map/ppermute | solution.py:35
  53.8 4.6 all-to-all-start
  64.5 12.3 %attend_first.1 = bf16[4,272,256]{2,1,0:T(8,128)(2,1)S(1)} custom-call(s32[4]{0:T(128)S(1)} %pad_add_fusion.info, bf16[2048,1024]{1,0:T(8,128)(2,1)} %x.11, bf16[1024,512]{1,0:T(8,128)(2,1)} %bitcast.7.lat_here, bf16[1024,512]{1,0:T(8,128)(2,1)} %collective-permute-done.lat_there, bf16[1536,256]{1,0:T(8,128)(2,1)S(1)} %pad_maximum_fusion.2.heads_here.h0, ...), custom_call_target="tpu_custom_call" | custom-call | flops 4563402752 | bytes 8437760 | tf_op jit(solution)/shard_map/attend_first/pallas_call | solution.py:83
  76.9 4.9 collective-permute-start.5
  89.8 5.2 collective-permute-done.8.m3
  96.7 4.5 collective-permute-done.18
  104.9 5.2 collective-permute-done.20
  131.3 6.2 attend_out.1
  139.7 6.5 %feed.4 = (f32[256,1024]{1,0:T(8,128)S(1)}, bf16[2,2,256,704]{3,2,1,0:T(8,128)(2,1)}) custom-call(s32[6]{0:T(128)S(1)} %stack.115.info, bf16[256,1024]{1,0:T(8,128)(2,1)S(1)} %get-tuple-element.142.value.refs_0_, bf16[704,1024]{1,0:T(8,128)(2,1)} %bitcast.211, bf16[704,1024]{1,0:T(8,128)(2,1)} %bitcast.201, bf16[704,1024]{1,0:T(8,128)(2,1)} %bitcast.189, ...), custom_call_target="tpu_custom_call" | custom-call | flops 2214592512 | bytes 30539776 | tf_op jit(solution)/shard_map/feed/pallas_call | solution.py:83
  146.2 10.6 %collective-permute-done.29 = bf16[32,1024]{1,0:T(8,128)(2,1)S(1)} collective-permute-done((bf16[32,1024]{1,0:T(8,128)(2,1)S(1)}, bf16[32,1024]{1,0:T(8,128)(2,1)S(1)}, u32[]{:S(2)}, u32[]{:S(2)}) %collective-permute-start.29) | collective-permute-done | bytes 65568 | tf_op jit(solution)/shard_map/ppermute | solution.py:35
  160.1 4.6 all-to-all-start.1
  166.5 11.7 %collective-permute-done.17.value.refs_1_ = bf16[256,1024]{1,0:T(8,128)(2,1)S(1)} collective-permute-done((bf16[256,1024]{1,0:T(8,128)(2,1)S(1)}, bf16[256,1024]{1,0:T(8,128)(2,1)S(1)}, u32[]{:S(2)}, u32[]{:S(2)}) %collective-permute-start.17) | collective-permute-done | bytes 524320 | tf_op jit(solution)/shard_map/ppermute | solution.py:35
  178.2 6.5 %feed.5 = (bf16[256,1024]{1,0:T(8,128)(2,1)S(1)}, bf16[2,2,256,704]{3,2,1,0:T(8,128)(2,1)}) custom-call(s32[6]{0:T(128)S(1)} %stack.115.info, bf16[256,1024]{1,0:T(8,128)(2,1)S(1)} %collective-permute-done.17.value.refs_1_, bf16[704,1024]{1,0:T(8,128)(2,1)} %bitcast.212, bf16[704,1024]{1,0:T(8,128)(2,1)} %bitcast.202, bf16[704,1024]{1,0:T(8,128)(2,1)} %bitcast.190, ...), custom_call_target="tpu_custom_call" | custom-call | flops 2214592512 | bytes 30015488 | tf_op jit(solution)/shard_map/feed/pallas_call | solution.py:83
  186.8 10.3 %collective-permute-done.22 = bf16[256,1024]{1,0:T(8,128)(2,1)S(1)} collective-permute-done((bf16[256,1024]{1,0:T(8,128)(2,1)S(1)}, bf16[256,1024]{1,0:T(8,128)(2,1)S(1)}, u32[]{:S(2)}, u32[]{:S(2)}) %collective-permute-start.22) | collective-permute-done | bytes 524320 | tf_op jit(solution)/shard_map/ppermute | solution.py:35
  207.0 4.7 collective-permute-done.25.lat2
  214.3 17.7 %attend.1 = (bf16[4,256,256]{2,1,0:T(8,128)(2,1)S(1)}, f32[4,4,256]{2,1,0:T(4,128)S(1)}, bf16[2,1024,256]{2,1,0:T(8,128)(2,1)}, f32[256,1024]{1,0:T(8,128)}, bf16[256,1024]{1,0:T(8,128)(2,1)}) custom-call(s32[6]{0:T(128)S(1)} %stack.115.info, bf16[256,1024]{1,0:T(8,128)(2,1)} %copy-done.17, bf16[256,1024]{1,0:T(8,128)(2,1)} %copy-done.2, ...), custom_call_target="tpu_custom_call" | custom-call | flops 6442450944 | bytes 16535552 | tf_op jit(solution)/shard_map/attend/pallas_call | solution.py:83
  235.4 6.5 %feed.6 = (f32[256,1024]{1,0:T(8,128)S(1)}, bf16[2,2,256,704]{3,2,1,0:T(8,128)(2,1)}) custom-call(s32[6]{0:T(128)S(1)} %stack.115.info, bf16[256,1024]{1,0:T(8,128)(2,1)S(1)} %copy-done.11, bf16[704,1024]{1,0:T(8,128)(2,1)} %bitcast.213, bf16[704,1024]{1,0:T(8,128)(2,1)} %bitcast.203, bf16[704,1024]{1,0:T(8,128)(2,1)} %bitcast.191, ...), custom_call_target="tpu_custom_call" | custom-call | flops 2214592512 | bytes 30539776 | tf_op jit(solution)/shard_map/feed/pallas_call | solution.py:83
  241.9 10.0 %feed_back.4 = (f32[256,1024]{1,0:T(8,128)S(1)}, bf16[3,256,768]{2,1,0:T(8,128)(2,1)}, bf16[3,256,768]{2,1,0:T(8,128)(2,1)}) custom-call(s32[6]{0:T(128)S(1)} %stack.115.info, bf16[256,1024]{1,0:T(8,128)(2,1)S(1)} %get-tuple-element.271.value.refs_4_, bf16[2,2,256,704]{3,2,1,0:T(8,128)(2,1)} %get-tuple-element.115.saved, bf16[704,1024]{1,0:T(8,128)(2,1)} %bitcast.214, ...), custom_call_target="tpu_custom_call" | custom-call | flops 2214592512 | bytes 32899072 | tf_op jit(solution)/shard_map/feed_back/pallas_call | solution.py:83
  252.9 14.6 %collective-permute-done.33.value.refs_1_ = bf16[256,1024]{1,0:T(8,128)(2,1)S(1)} collective-permute-done((bf16[256,1024]{1,0:T(8,128)(2,1)}, bf16[256,1024]{1,0:T(8,128)(2,1)S(1)}, u32[]{:S(2)}, u32[]{:S(2)}) %collective-permute-start.33) | collective-permute-done | bytes 524320 | tf_op jit(solution)/shard_map/ppermute | solution.py:35
  267.4 6.7 %feed.7 = (bf16[256,1024]{1,0:T(8,128)(2,1)}, bf16[2,2,256,704]{3,2,1,0:T(8,128)(2,1)}) custom-call(s32[6]{0:T(128)S(1)} %stack.115.info, bf16[256,1024]{1,0:T(8,128)(2,1)S(1)} %collective-permute-done.33.value.refs_1_, bf16[704,1024]{1,0:T(8,128)(2,1)} %bitcast.215, bf16[704,1024]{1,0:T(8,128)(2,1)} %bitcast.205, bf16[704,1024]{1,0:T(8,128)(2,1)} %bitcast.193, ...), custom_call_target="tpu_custom_call" | custom-call | flops 2214592512 | bytes 30015488 | tf_op jit(solution)/shard_map/feed/pallas_call | solution.py:83
  274.1 4.5 collective-permute-done.36.value.refs_5_
  278.7 10.4 %feed_back.5 = (bf16[256,1024]{1,0:T(8,128)(2,1)}, bf16[3,256,768]{2,1,0:T(8,128)(2,1)}, bf16[3,256,768]{2,1,0:T(8,128)(2,1)}) custom-call(s32[6]{0:T(128)S(1)} %stack.115.info, bf16[256,1024]{1,0:T(8,128)(2,1)S(1)} %collective-permute-done.36.value.refs_5_, bf16[2,2,256,704]{3,2,1,0:T(8,128)(2,1)} %get-tuple-element.117.saved, bf16[704,1024]{1,0:T(8,128)(2,1)} %bitcast.216, ...), custom_call_target="tpu_custom_call" | custom-call | flops 2214592512 | bytes 32374784 | tf_op jit(solution)/shard_map/feed_back/pallas_call | solution.py:83
  296.8 10.8 %feed_weights.2 = bf16[4,3,256,768]{3,2,1,0:T(8,128)(2,1)} custom-call(s32[6]{0:T(128)S(1)} %stack.115.info, bf16[256,1024]{1,0:T(8,128)(2,1)S(1)} %copy-done.12, bf16[256,1024]{1,0:T(8,128)(2,1)S(1)} %collective-permute-done.33.value.refs_1_, bf16[256,1024]{1,0:T(8,128)(2,1)S(1)} %collective-permute-done.38.refs_2_, bf16[256,1024]{1,0:T(8,128)(2,1)} %copy-done.49, ...), custom_call_target="tpu_custom_call" | custom-call | flops 4429185024 | bytes 13631488 | tf_op jit(solution)/shard_map/feed_weights/pallas_call | solution.py:83
  307.6 4.9 all-to-all-start.2
  322.9 14.7 %attend_back.4 = (f32[256,1024]{1,0:T(8,128)}, bf16[1024,256]{1,0:T(8,128)(2,1)S(1)}, bf16[4,2,320,256]{3,2,1,0:T(8,128)(2,1)}, bf16[4,2,320,256]{3,2,1,0:T(8,128)(2,1)}) custom-call(s32[6]{0:T(128)S(1)} %stack.115.info, bf16[256,1024]{1,0:T(8,128)(2,1)S(1)} %copy-done.10, bf16[256,1024]{1,0:T(8,128)(2,1)S(1)} %copy-done.3, ...), custom_call_target="tpu_custom_call" | custom-call | flops 8858370048 | bytes 18104320 | tf_op jit(solution)/shard_map/attend_back/pallas_call | solution.py:83
  338.9 14.5 %attend_back.5 = (f32[256,1024]{1,0:T(8,128)}, bf16[1024,256]{1,0:T(8,128)(2,1)S(1)}, bf16[4,2,320,256]{3,2,1,0:T(8,128)(2,1)}, bf16[4,2,320,256]{3,2,1,0:T(8,128)(2,1)}) custom-call(s32[6]{0:T(128)S(1)} %stack.115.info, bf16[256,1024]{1,0:T(8,128)(2,1)S(1)} %copy-done.10, bf16[256,1024]{1,0:T(8,128)(2,1)S(1)} %copy-done.3, ...), custom_call_target="tpu_custom_call" | custom-call | flops 8858370048 | bytes 18104320 | tf_op jit(solution)/shard_map/attend_back/pallas_call | solution.py:83
  356.0 12.4 %collective-permute-done.45 = bf16[256,256]{1,0:T(8,128)(2,1)S(1)} collective-permute-done((bf16[256,256]{1,0:T(8,128)(2,1)S(1)}, bf16[256,256]{1,0:T(8,128)(2,1)S(1)}, u32[]{:S(2)}, u32[]{:S(2)}) %collective-permute-start.45) | collective-permute-done | bytes 131104 | tf_op jit(solution)/shard_map/ppermute | solution.py:35
  387.4 4.8 all-to-all-start.3
  398.9 4.3 collective-permute-done.62
  405.7 4.5 reduce_sum.182
  411.5 9.8 %feed_back.6 = (f32[256,1024]{1,0:T(8,128)S(1)}, bf16[3,256,768]{2,1,0:T(8,128)(2,1)}, bf16[3,256,768]{2,1,0:T(8,128)(2,1)}) custom-call(s32[6]{0:T(128)S(1)} %stack.115.info, bf16[256,1024]{1,0:T(8,128)(2,1)S(1)} %get-tuple-element.212.value.refs_4_, bf16[2,2,256,704]{3,2,1,0:T(8,128)(2,1)} %get-tuple-element.133.saved, bf16[704,1024]{1,0:T(8,128)(2,1)} %bitcast.217, ...), custom_call_target="tpu_custom_call" | custom-call | flops 2214592512 | bytes 32899072 | tf_op jit(solution)/shard_map/feed_back/pallas_call | solution.py:83
  421.3 4.8 collective-permute-start.58
  426.1 10.3 %feed_back.7 = (bf16[256,1024]{1,0:T(8,128)(2,1)}, bf16[3,256,768]{2,1,0:T(8,128)(2,1)}, bf16[3,256,768]{2,1,0:T(8,128)(2,1)}) custom-call(s32[6]{0:T(128)S(1)} %stack.115.info, bf16[256,1024]{1,0:T(8,128)(2,1)S(1)} %collective-permute-done.48.value.refs_5_, bf16[2,2,256,704]{3,2,1,0:T(8,128)(2,1)} %get-tuple-element.135.saved, bf16[704,1024]{1,0:T(8,128)(2,1)} %bitcast.218, ...), custom_call_target="tpu_custom_call" | custom-call | flops 2214592512 | bytes 32374784 | tf_op jit(solution)/shard_map/feed_back/pallas_call | solution.py:83
  441.6 5.2 all-gather.19.cloned.1.call-done
  448.6 11.0 %feed_weights.3 = bf16[4,3,256,768]{3,2,1,0:T(8,128)(2,1)} custom-call(s32[6]{0:T(128)S(1)} %stack.115.info, bf16[256,1024]{1,0:T(8,128)(2,1)S(1)} %get-tuple-element.142.value.refs_0_, bf16[256,1024]{1,0:T(8,128)(2,1)S(1)} %copy-done.9, bf16[256,1024]{1,0:T(8,128)(2,1)} %collective-permute-done.54.refs_2_, ...), custom_call_target="tpu_custom_call" | custom-call | flops 4429185024 | bytes 13631488 | tf_op jit(solution)/shard_map/feed_weights/pallas_call | solution.py:83
  459.6 5.1 all-to-all-start.4
  469.1 14.6 %attend_back.6 = (f32[256,1024]{1,0:T(8,128)}, bf16[1024,256]{1,0:T(8,128)(2,1)S(1)}, bf16[4,2,320,256]{3,2,1,0:T(8,128)(2,1)}, bf16[4,2,320,256]{3,2,1,0:T(8,128)(2,1)}) custom-call(s32[6]{0:T(128)S(1)} %stack.115.info, bf16[256,1024]{1,0:T(8,128)(2,1)S(1)} %get-tuple-element.156.grad_branch, bf16[256,1024]{1,0:T(8,128)(2,1)S(1)} %fusion.18.normed, ...), custom_call_target="tpu_custom_call" | custom-call | flops 8858370048 | bytes 18104320 | tf_op jit(solution)/shard_map/attend_back/pallas_call | solution.py:83
  488.9 14.7 %attend_back.7 = (f32[256,1024]{1,0:T(8,128)}, bf16[1024,256]{1,0:T(8,128)(2,1)S(1)}, bf16[4,2,320,256]{3,2,1,0:T(8,128)(2,1)}, bf16[4,2,320,256]{3,2,1,0:T(8,128)(2,1)}) custom-call(s32[6]{0:T(128)S(1)} %stack.115.info, bf16[256,1024]{1,0:T(8,128)(2,1)S(1)} %get-tuple-element.156.grad_branch, bf16[256,1024]{1,0:T(8,128)(2,1)S(1)} %fusion.18.normed, ...), custom_call_target="tpu_custom_call" | custom-call | flops 8858370048 | bytes 18104320 | tf_op jit(solution)/shard_map/attend_back/pallas_call | solution.py:83
  514.2 8.5 %collective-permute-done.69 = bf16[400,256]{1,0:T(8,128)(2,1)S(1)} collective-permute-done((bf16[400,256]{1,0:T(8,128)(2,1)S(1)}, bf16[400,256]{1,0:T(8,128)(2,1)S(1)}, u32[]{:S(2)}, u32[]{:S(2)}) %collective-permute-start.69) | collective-permute-done | bytes 204832 | tf_op jit(solution)/shard_map/ppermute | solution.py:35
  522.7 4.4 reduce_sum.184
  551.9 4.5 collective-permute-start.78
  556.5 27.3 %all-to-all-done.5 = bf16[4,4,400,256]{3,2,1,0:T(8,128)(2,1)S(1)} async-done(((bf16[4,4,400,256]{3,2,1,0:T(8,128)(2,1)}), bf16[4,4,400,256]{3,2,1,0:T(8,128)(2,1)S(1)}, u32[]{:S(2)}, u32[]{:S(2)}) %all-to-all-start.5) | async-done | bytes 3276832 | tf_op jit(solution)/shard_map/all_to_all | solution.py:901
  586.5 4.8 rows.2
  592.8 8.8 %all-gather.23.cloned.1.call-done = bf16[1024,1024]{1,0:T(8,128)(2,1)} async-done(((bf16[256,1024]{1,0:T(8,128)(2,1)}), bf16[1024,1024]{1,0:T(8,128)(2,1)}) %all-gather.23.cloned.1.call-update) | async-done | bytes 2097168 | tf_op jit(solution)/shard_map/all_gather | solution.py:941
  605.7 6.1 collective-permute-done.75
  614.7 8.6 %collective-permute-done.76 = bf16[400,256]{1,0:T(8,128)(2,1)S(1)} collective-permute-done((bf16[400,256]{1,0:T(8,128)(2,1)S(1)}, bf16[400,256]{1,0:T(8,128)(2,1)S(1)}, u32[]{:S(2)}, u32[]{:S(2)}) %collective-permute-start.76) | collective-permute-done | bytes 204832 | tf_op jit(solution)/shard_map/ppermute | solution.py:35
  631.1 4.8 rows.3
  (395 shorter events, 212.8 us)
Async XLA Ops:
  11.0 48.8 %collective-permute-start = (bf16[1024,512]{1,0:T(8,128)(2,1)}, bf16[1024,512]{1,0:T(8,128)(2,1)}, u32[]{:S(2)}, u32[]{:S(2)}) collective-permute-start(bf16[1024,512]{1,0:T(8,128)(2,1)} %bitcast.7.lat_here), channel_id=1, source_target_pairs={{0,16},{16,0},{1,17},{17,1},{2,18},{18,2},{3,19},{19,3},{4,20},{20... | collective-permute-start | bytes 3145736 | tf_op jit(solution)/shard_map/ppermute | solution.py:30
  16.4 35.3 %collective-permute-start.2 = (bf16[288,1024]{1,0:T(8,128)(2,1)}, bf16[288,1024]{1,0:T(8,128)(2,1)S(1)}, u32[]{:S(2)}, u32[]{:S(2)}) collective-permute-start(bf16[288,1024]{1,0:T(8,128)(2,1)} %slice.207), channel_id=1, source_target_pairs={{0,8},{4,12},{8,0},{12,4},{1,9},{5,13},{9,1},{13,5},{2,10},{6,14},... | collective-permute-start | bytes 1769480 | tf_op jit(solution)/shard_map/ppermute | solution.py:35
  23.1 27.2 %collective-permute-start.11 = (bf16[32,1024]{1,0:T(8,128)(2,1)S(1)}, bf16[32,1024]{1,0:T(8,128)(2,1)S(1)}, u32[]{:S(2)}, u32[]{:S(2)}) collective-permute-start(bf16[32,1024]{1,0:T(8,128)(2,1)S(1)} %slice.216), channel_id=1, source_target_pairs={{0,8},{4,12},{8,0},{12,4},{1,9},{5,13},{9,1},{13,5},{2,10},{6,14},... | collective-permute-start | bytes 196616 | tf_op jit(solution)/shard_map/ppermute | solution.py:35
  23.2 28.4 %collective-permute-start.12 = (bf16[32,1024]{1,0:T(8,128)(2,1)S(1)}, bf16[32,1024]{1,0:T(8,128)(2,1)S(1)}, u32[]{:S(2)}, u32[]{:S(2)}) collective-permute-start(bf16[32,1024]{1,0:T(8,128)(2,1)S(1)} %slice.216), channel_id=1, source_target_pairs={{0,12},{4,8},{8,4},{12,0},{1,13},{5,9},{9,5},{13,1},{2,14},{6,10},... | collective-permute-start | bytes 196616 | tf_op jit(solution)/shard_map/ppermute | solution.py:35
  33.8 25.9 %collective-permute-start.3 = (f32[2,1024]{1,0:T(2,128)S(1)}, f32[2,1024]{1,0:T(2,128)S(1)}, u32[]{:S(2)}, u32[]{:S(2)}) collective-permute-start(f32[2,1024]{1,0:T(2,128)S(1)} %bitcast.187), channel_id=1, source_target_pairs={{0,16},{16,0},{1,17},{17,1},{2,18},{18,2},{3,19},{19,3},{4,20},{20... | collective-permute-start | bytes 24584 | tf_op jit(solution)/shard_map/ppermute | solution.py:30
  53.8 41.2 %all-to-all-start = ((bf16[4,384,1024]{2,1,0:T(8,128)(2,1)}), bf16[4,384,1024]{2,1,0:T(8,128)(2,1)}, u32[]{:S(2)}, u32[]{:S(2)}) async-start(bf16[4,384,1024]{2,1,0:T(8,128)(2,1)} %broadcast_in_dim.8), calls=%async_computation | async-start | bytes 6291456 | tf_op jit(solution)/shard_map/all_to_all | solution.py:48
  58.4 119.8 %all-gather.13.cloned.1.call-start = ((), (), s32[]{:S(2)}) async-start(), calls=%async_computation.6 | async-start | bytes 1474560 | tf_op jit(solution)/shard_map/all_gather | solution.py:776
  95.0 34.6 %collective-permute-start.13 = (bf16[4,384,1024]{2,1,0:T(8,128)(2,1)}, bf16[4,384,1024]{2,1,0:T(8,128)(2,1)}, u32[]{:S(2)}, u32[]{:S(2)}) collective-permute-start(bf16[4,384,1024]{2,1,0:T(8,128)(2,1)} %all-to-all-done.o2.refs_6_.refs_8_.refs_10_), channel_id=1, source_target_pairs={{0,16},{16,0},{1,17},{17,1},{2,18},{18,2},{3,19},{19,3},{4,20},{20... | collective-permute-start | bytes 9437192 | tf_op jit(solution)/shard_map/ppermute | solution.py:30
  95.6 41.8 %collective-permute-start.14 = (bf16[704,1024]{1,0:T(8,128)(2,1)}, bf16[704,1024]{1,0:T(8,128)(2,1)}, u32[]{:S(2)}, u32[]{:S(2)}) collective-permute-start(bf16[704,1024]{1,0:T(8,128)(2,1)} %bitcast.210), channel_id=1, source_target_pairs={{0,16},{16,0},{1,17},{17,1},{2,18},{18,2},{3,19},{19,3},{4,20},{20... | collective-permute-start | bytes 4325384 | tf_op jit(solution)/shard_map/ppermute | solution.py:30
  96.1 41.4 %collective-permute-start.15 = (bf16[704,1024]{1,0:T(8,128)(2,1)}, bf16[704,1024]{1,0:T(8,128)(2,1)}, u32[]{:S(2)}, u32[]{:S(2)}) collective-permute-start(bf16[704,1024]{1,0:T(8,128)(2,1)} %bitcast.200), channel_id=1, source_target_pairs={{0,16},{16,0},{1,17},{17,1},{2,18},{18,2},{3,19},{19,3},{4,20},{20... | collective-permute-start | bytes 4325384 | tf_op jit(solution)/shard_map/ppermute | solution.py:30
  96.2 43.5 %collective-permute-start.16 = (bf16[704,1024]{1,0:T(8,128)(2,1)S(1)}, bf16[704,1024]{1,0:T(8,128)(2,1)}, u32[]{:S(2)}, u32[]{:S(2)}) collective-permute-start(bf16[704,1024]{1,0:T(8,128)(2,1)S(1)} %bitcast.198), channel_id=1, source_target_pairs={{0,16},{16,0},{1,17},{17,1},{2,18},{18,2},{3,19},{19,3},{4,20},{20... | collective-permute-start | bytes 4325384 | tf_op jit(solution)/shard_map/ppermute | solution.py:30
  123.7 33.2 %collective-permute-start.31 = (bf16[288,1024]{1,0:T(8,128)(2,1)}, bf16[288,1024]{1,0:T(8,128)(2,1)}, u32[]{:S(2)}, u32[]{:S(2)}) collective-permute-start(bf16[288,1024]{1,0:T(8,128)(2,1)} %slice.175), channel_id=1, source_target_pairs={{0,8},{4,12},{8,0},{12,4},{1,9},{5,13},{9,1},{13,5},{2,10},{6,14},... | collective-permute-start | bytes 1769480 | tf_op jit(solution)/shard_map/ppermute | solution.py:35
  137.5 19.4 %collective-permute-start.29 = (bf16[32,1024]{1,0:T(8,128)(2,1)S(1)}, bf16[32,1024]{1,0:T(8,128)(2,1)S(1)}, u32[]{:S(2)}, u32[]{:S(2)}) collective-permute-start(bf16[32,1024]{1,0:T(8,128)(2,1)S(1)} %slice.174), channel_id=1, source_target_pairs={{0,8},{4,12},{8,0},{12,4},{1,9},{5,13},{9,1},{13,5},{2,10},{6,14},... | collective-permute-start | bytes 196616 | tf_op jit(solution)/shard_map/ppermute | solution.py:35
  137.6 19.3 %collective-permute-start.30 = (bf16[32,1024]{1,0:T(8,128)(2,1)S(1)}, bf16[32,1024]{1,0:T(8,128)(2,1)S(1)}, u32[]{:S(2)}, u32[]{:S(2)}) collective-permute-start(bf16[32,1024]{1,0:T(8,128)(2,1)S(1)} %slice.174), channel_id=1, source_target_pairs={{0,12},{4,8},{8,4},{12,0},{1,13},{5,9},{9,5},{13,1},{2,14},{6,10},... | collective-permute-start | bytes 196616 | tf_op jit(solution)/shard_map/ppermute | solution.py:35
  160.1 40.3 %all-to-all-start.1 = ((bf16[4,384,1024]{2,1,0:T(8,128)(2,1)}), bf16[4,384,1024]{2,1,0:T(8,128)(2,1)}, u32[]{:S(2)}, u32[]{:S(2)}) async-start(bf16[4,384,1024]{2,1,0:T(8,128)(2,1)} %broadcast_in_dim.9), calls=%async_computation.1 | async-start | bytes 6291456 | tf_op jit(solution)/shard_map/all_to_all | solution.py:48
  164.7 147.9 %all-gather.15.cloned.1.call-start = ((), (), s32[]{:S(2)}) async-start(), calls=%async_computation.7 | async-start | bytes 2621440 | tf_op jit(solution)/shard_map/all_gather | solution.py:941
  232.8 34.6 %collective-permute-start.33 = (bf16[256,1024]{1,0:T(8,128)(2,1)}, bf16[256,1024]{1,0:T(8,128)(2,1)S(1)}, u32[]{:S(2)}, u32[]{:S(2)}) collective-permute-start(bf16[256,1024]{1,0:T(8,128)(2,1)} %get-tuple-element.111.value.refs_0_), channel_id=1, source_target_pairs={{0,4},{4,0},{8,12},{12,8},{1,5},{5,1},{9,13},{13,9},{2,6},{6,2},{1... | collective-permute-start | bytes 1572872 | tf_op jit(solution)/shard_map/ppermute | solution.py:35
  234.3 44.4 %collective-permute-start.36 = (bf16[256,1024]{1,0:T(8,128)(2,1)S(1)}, bf16[256,1024]{1,0:T(8,128)(2,1)S(1)}, u32[]{:S(2)}, u32[]{:S(2)}) collective-permute-start(bf16[256,1024]{1,0:T(8,128)(2,1)S(1)} %get-tuple-element.271.value.refs_4_), channel_id=1, source_target_pairs={{0,4},{4,0},{8,12},{12,8},{1,5},{5,1},{9,13},{13,9},{2,6},{6,2},{1... | collective-permute-start | bytes 1572872 | tf_op jit(solution)/shard_map/ppermute | solution.py:35
  251.9 43.3 %collective-permute-start.42 = (bf16[3,256,768]{2,1,0:T(8,128)(2,1)}, bf16[3,256,768]{2,1,0:T(8,128)(2,1)S(1)}, u32[]{:S(2)}, u32[]{:S(2)}) collective-permute-start(bf16[3,256,768]{2,1,0:T(8,128)(2,1)} %get-tuple-element.121), channel_id=1, source_target_pairs={{0,16},{16,0},{1,17},{17,1},{2,18},{18,2},{3,19},{19,3},{4,20},{20... | collective-permute-start | bytes 3538952 | tf_op jit(solution)/shard_map/ppermute | solution.py:30
  293.7 18.9 %collective-permute-start.37 = (bf16[256,1024]{1,0:T(8,128)(2,1)}, bf16[256,1024]{1,0:T(8,128)(2,1)S(1)}, u32[]{:S(2)}, u32[]{:S(2)}) collective-permute-start(bf16[256,1024]{1,0:T(8,128)(2,1)} %get-tuple-element.118), channel_id=1, source_target_pairs={{0,4},{4,0},{8,12},{12,8},{1,5},{5,1},{9,13},{13,9},{2,6},{6,2},{1... | collective-permute-start | bytes 1572872 | tf_op jit(solution)/shard_map/ppermute | solution.py:35
  294.5 23.9 %collective-permute-start.34 = (bf16[256,1024]{1,0:T(8,128)(2,1)}, bf16[256,1024]{1,0:T(8,128)(2,1)}, u32[]{:S(2)}, u32[]{:S(2)}) collective-permute-start(bf16[256,1024]{1,0:T(8,128)(2,1)} %get-tuple-element.114), channel_id=1, source_target_pairs={{0,4},{4,0},{8,12},{12,8},{1,5},{5,1},{9,13},{13,9},{2,6},{6,2},{1... | collective-permute-start | bytes 1572872 | tf_op jit(solution)/shard_map/ppermute | solution.py:35
  307.6 64.9 %all-to-all-start.2 = ((bf16[4,3,256,768]{3,2,1,0:T(8,128)(2,1)}), bf16[4,3,256,768]{3,2,1,0:T(8,128)(2,1)}, u32[]{:S(2)}, u32[]{:S(2)}) async-start(bf16[4,3,256,768]{3,2,1,0:T(8,128)(2,1)} %feed_weights.2), calls=%async_computation.2 | async-start | bytes 9437184 | tf_op jit(solution)/shard_map/all_to_all | solution.py:853
  312.5 60.0 %all-gather.17.cloned.1.call-start = ((), (), s32[]{:S(2)}) async-start(), calls=%async_computation.8 | async-start | bytes 2621440 | tf_op jit(solution)/shard_map/all_gather | solution.py:941
  353.6 26.9 %collective-permute-start.50 = (bf16[4,2,320,256]{3,2,1,0:T(8,128)(2,1)}, bf16[4,2,320,256]{3,2,1,0:T(8,128)(2,1)}, u32[]{:S(2)}, u32[]{:S(2)}) collective-permute-start(bf16[4,2,320,256]{3,2,1,0:T(8,128)(2,1)} %get-tuple-element.138), channel_id=1, source_target_pairs={{0,16},{16,0},{1,17},{17,1},{2,18},{18,2},{3,19},{19,3},{4,20},{20... | collective-permute-start | bytes 3932168 | tf_op jit(solution)/shard_map/ppermute | solution.py:30
  354.1 28.5 %collective-permute-start.51 = (bf16[4,2,320,256]{3,2,1,0:T(8,128)(2,1)}, bf16[4,2,320,256]{3,2,1,0:T(8,128)(2,1)}, u32[]{:S(2)}, u32[]{:S(2)}) collective-permute-start(bf16[4,2,320,256]{3,2,1,0:T(8,128)(2,1)} %get-tuple-element.140), channel_id=1, source_target_pairs={{0,16},{16,0},{1,17},{17,1},{2,18},{18,2},{3,19},{19,3},{4,20},{20... | collective-permute-start | bytes 3932168 | tf_op jit(solution)/shard_map/ppermute | solution.py:30
  387.4 59.5 %all-to-all-start.3 = ((bf16[4,4,400,256]{3,2,1,0:T(8,128)(2,1)}), bf16[4,4,400,256]{3,2,1,0:T(8,128)(2,1)}, u32[]{:S(2)}, u32[]{:S(2)}) async-start(bf16[4,4,400,256]{3,2,1,0:T(8,128)(2,1)} %pad_maximum_fusion), calls=%async_computation.3 | async-start | bytes 6553600 | tf_op jit(solution)/shard_map/all_to_all | solution.py:901
  392.2 54.6 %all-gather.19.cloned.1.call-start = ((), (), s32[]{:S(2)}) async-start(), calls=%async_computation.9 | async-start | bytes 1474560 | tf_op jit(solution)/shard_map/all_gather | solution.py:776
  398.6 27.5 %collective-permute-start.48 = (bf16[256,1024]{1,0:T(8,128)(2,1)S(1)}, bf16[256,1024]{1,0:T(8,128)(2,1)S(1)}, u32[]{:S(2)}, u32[]{:S(2)}) collective-permute-start(bf16[256,1024]{1,0:T(8,128)(2,1)S(1)} %get-tuple-element.212.value.refs_4_), channel_id=1, source_target_pairs={{0,4},{4,0},{8,12},{12,8},{1,5},{5,1},{9,13},{13,9},{2,6},{6,2},{1... | collective-permute-start | bytes 1572872 | tf_op jit(solution)/shard_map/ppermute | solution.py:35
  403.9 123.2 %all-gather.21.cloned.1.call-start = ((), (), s32[]{:S(2)}) async-start(), calls=%async_computation.10 | async-start | bytes 2621440 | tf_op jit(solution)/shard_map/all_gather | solution.py:941
  404.0 32.5 %collective-permute-start.54 = (bf16[256,1024]{1,0:T(8,128)(2,1)S(1)}, bf16[256,1024]{1,0:T(8,128)(2,1)}, u32[]{:S(2)}, u32[]{:S(2)}) collective-permute-start(bf16[256,1024]{1,0:T(8,128)(2,1)S(1)} %get-tuple-element.142.value.refs_0_), channel_id=1, source_target_pairs={{0,16},{16,0},{1,17},{17,1},{2,18},{18,2},{3,19},{19,3},{4,20},{20... | collective-permute-start | bytes 1572872 | tf_op jit(solution)/shard_map/ppermute | solution.py:30
  405.6 31.4 %collective-permute-start.55 = (bf16[256,1024]{1,0:T(8,128)(2,1)S(1)}, bf16[256,1024]{1,0:T(8,128)(2,1)}, u32[]{:S(2)}, u32[]{:S(2)}) collective-permute-start(bf16[256,1024]{1,0:T(8,128)(2,1)S(1)} %copy-done.8), channel_id=1, source_target_pairs={{0,16},{16,0},{1,17},{17,1},{2,18},{18,2},{3,19},{19,3},{4,20},{20... | collective-permute-start | bytes 1572872 | tf_op jit(solution)/shard_map/ppermute | solution.py:30
  410.2 31.4 %collective-permute-start.53 = (bf16[3,256,768]{2,1,0:T(8,128)(2,1)}, bf16[3,256,768]{2,1,0:T(8,128)(2,1)}, u32[]{:S(2)}, u32[]{:S(2)}) collective-permute-start(bf16[3,256,768]{2,1,0:T(8,128)(2,1)} %reduce_sum.182), channel_id=1, source_target_pairs={{0,24},{4,28},{8,16},{12,20},{1,25},{5,29},{9,17},{13,21},{2,26},{... | collective-permute-start | bytes 3538952 | tf_op jit(solution)/shard_map/ppermute | solution.py:905
  421.3 26.3 %collective-permute-start.58 = (bf16[3,256,768]{2,1,0:T(8,128)(2,1)}, bf16[3,256,768]{2,1,0:T(8,128)(2,1)}, u32[]{:S(2)}, u32[]{:S(2)}) collective-permute-start(bf16[3,256,768]{2,1,0:T(8,128)(2,1)} %get-tuple-element.145), channel_id=1, source_target_pairs={{0,16},{16,0},{1,17},{17,1},{2,18},{18,2},{3,19},{19,3},{4,20},{20... | collective-permute-start | bytes 3538952 | tf_op jit(solution)/shard_map/ppermute | solution.py:30
  441.5 23.5 %collective-permute-start.49 = (bf16[256,1024]{1,0:T(8,128)(2,1)}, bf16[256,1024]{1,0:T(8,128)(2,1)}, u32[]{:S(2)}, u32[]{:S(2)}) collective-permute-start(bf16[256,1024]{1,0:T(8,128)(2,1)} %get-tuple-element.136), channel_id=1, source_target_pairs={{0,4},{4,0},{8,12},{12,8},{1,5},{5,1},{9,13},{13,9},{2,6},{6,2},{1... | collective-permute-start | bytes 1572872 | tf_op jit(solution)/shard_map/ppermute | solution.py:35
  446.8 22.3 %collective-permute-start.63 = (bf16[4,576,256]{2,1,0:T(8,128)(2,1)}, bf16[4,576,256]{2,1,0:T(8,128)(2,1)}, u32[]{:S(2)}, u32[]{:S(2)}) collective-permute-start(bf16[4,576,256]{2,1,0:T(8,128)(2,1)} %bitcast.253), channel_id=1, source_target_pairs={{0,16},{16,0},{1,17},{17,1},{2,18},{18,2},{3,19},{19,3},{4,20},{20... | collective-permute-start | bytes 3538952 | tf_op jit(solution)/shard_map/ppermute | solution.py:30
  459.6 63.0 %all-to-all-start.4 = ((bf16[4,3,256,768]{3,2,1,0:T(8,128)(2,1)}), bf16[4,3,256,768]{3,2,1,0:T(8,128)(2,1)}, u32[]{:S(2)}, u32[]{:S(2)}) async-start(bf16[4,3,256,768]{3,2,1,0:T(8,128)(2,1)} %feed_weights.3), calls=%async_computation.4 | async-start | bytes 9437184 | tf_op jit(solution)/shard_map/all_to_all | solution.py:853
  464.8 136.8 %all-gather.23.cloned.1.call-start = ((), (), s32[]{:S(2)}) async-start(), calls=%async_computation.11 | async-start | bytes 2621440 | tf_op jit(solution)/shard_map/all_gather | solution.py:941
  484.4 20.7 %collective-permute-start.64 = (bf16[2,256,256]{2,1,0:T(8,128)(2,1)}, bf16[2,256,256]{2,1,0:T(8,128)(2,1)}, u32[]{:S(2)}, u32[]{:S(2)}) collective-permute-start(bf16[2,256,256]{2,1,0:T(8,128)(2,1)} %dynamic-slice_bitcast_fusion.3), channel_id=1, source_target_pairs={{0,16},{16,0},{1,17},{17,1},{2,18},{18,2},{3,19},{19,3},{4,20},{20... | collective-permute-start | bytes 786440 | tf_op jit(solution)/shard_map/ppermute | solution.py:30
  487.8 23.6 %collective-permute-start.68 = (bf16[2,400,256]{2,1,0:T(8,128)(2,1)}, bf16[2,400,256]{2,1,0:T(8,128)(2,1)S(1)}, u32[]{:S(2)}, u32[]{:S(2)}) collective-permute-start(bf16[2,400,256]{2,1,0:T(8,128)(2,1)} %slice.185), channel_id=1, source_target_pairs={{0,4},{4,0},{8,12},{12,8},{1,5},{5,1},{9,13},{13,9},{2,6},{6,2},{1... | collective-permute-start | bytes 1228808 | tf_op jit(solution)/shard_map/ppermute | solution.py:35
  504.5 32.6 %collective-permute-start.72 = (bf16[4,2,320,256]{3,2,1,0:T(8,128)(2,1)}, bf16[4,2,320,256]{3,2,1,0:T(8,128)(2,1)}, u32[]{:S(2)}, u32[]{:S(2)}) collective-permute-start(bf16[4,2,320,256]{3,2,1,0:T(8,128)(2,1)} %get-tuple-element.162), channel_id=1, source_target_pairs={{0,16},{16,0},{1,17},{17,1},{2,18},{18,2},{3,19},{19,3},{4,20},{20... | collective-permute-start | bytes 3932168 | tf_op jit(solution)/shard_map/ppermute | solution.py:30
  504.6 32.5 %collective-permute-start.73 = (bf16[4,2,320,256]{3,2,1,0:T(8,128)(2,1)}, bf16[4,2,320,256]{3,2,1,0:T(8,128)(2,1)}, u32[]{:S(2)}, u32[]{:S(2)}) collective-permute-start(bf16[4,2,320,256]{3,2,1,0:T(8,128)(2,1)} %get-tuple-element.165), channel_id=1, source_target_pairs={{0,16},{16,0},{1,17},{17,1},{2,18},{18,2},{3,19},{19,3},{4,20},{20... | collective-permute-start | bytes 3932168 | tf_op jit(solution)/shard_map/ppermute | solution.py:30
  542.9 40.8 %all-to-all-start.5 = ((bf16[4,4,400,256]{3,2,1,0:T(8,128)(2,1)}), bf16[4,4,400,256]{3,2,1,0:T(8,128)(2,1)S(1)}, u32[]{:S(2)}, u32[]{:S(2)}) async-start(bf16[4,4,400,256]{3,2,1,0:T(8,128)(2,1)} %pad_maximum_fusion.1), calls=%async_computation.5 | async-start | bytes 6553600 | tf_op jit(solution)/shard_map/all_to_all | solution.py:901
  546.7 39.8 %collective-permute-start.23 = (bf16[4,256,1024]{2,1,0:T(8,128)(2,1)}, bf16[4,256,1024]{2,1,0:T(8,128)(2,1)}, u32[]{:S(2)}, u32[]{:S(2)}) collective-permute-start(bf16[4,256,1024]{2,1,0:T(8,128)(2,1)} %bitcast.221), channel_id=1, source_target_pairs={{16,0},{17,1},{18,2},{19,3},{20,4},{21,5},{22,6},{23,7},{24,8},{25... | collective-permute-start | bytes 6291464 | tf_op jit(solution)/shard_map/ppermute | solution.py:944
  550.7 35.9 %collective-permute-start.35 = (bf16[4,256,1024]{2,1,0:T(8,128)(2,1)}, bf16[4,256,1024]{2,1,0:T(8,128)(2,1)}, u32[]{:S(2)}, u32[]{:S(2)}) collective-permute-start(bf16[4,256,1024]{2,1,0:T(8,128)(2,1)} %bitcast.223), channel_id=1, source_target_pairs={{0,16},{1,17},{2,18},{3,19},{4,20},{5,21},{6,22},{7,23},{8,24},{9,... | collective-permute-start | bytes 6291464 | tf_op jit(solution)/shard_map/ppermute | solution.py:944
  551.9 60.1 %collective-permute-start.78 = (bf16[3,256,768]{2,1,0:T(8,128)(2,1)}, bf16[3,256,768]{2,1,0:T(8,128)(2,1)}, u32[]{:S(2)}, u32[]{:S(2)}) collective-permute-start(bf16[3,256,768]{2,1,0:T(8,128)(2,1)} %reduce_sum.184), channel_id=1, source_target_pairs={{16,8},{20,12},{24,0},{28,4},{17,9},{21,13},{25,1},{29,5},{18,10},... | collective-permute-start | bytes 3538952 | tf_op jit(solution)/shard_map/ppermute | solution.py:905
  586.4 25.5 %collective-permute-start.75 = (bf16[2,400,256]{2,1,0:T(8,128)(2,1)S(1)}, bf16[2,400,256]{2,1,0:T(8,128)(2,1)S(1)}, u32[]{:S(2)}, u32[]{:S(2)}) collective-permute-start(bf16[2,400,256]{2,1,0:T(8,128)(2,1)S(1)} %slice.197), channel_id=1, source_target_pairs={{0,4},{4,0},{8,12},{12,8},{1,5},{5,1},{9,13},{13,9},{2,6},{6,2},{1... | collective-permute-start | bytes 1228808 | tf_op jit(solution)/shard_map/ppermute | solution.py:35
  591.4 39.7 %collective-permute-start.71 = (bf16[4,256,1024]{2,1,0:T(8,128)(2,1)}, bf16[4,256,1024]{2,1,0:T(8,128)(2,1)}, u32[]{:S(2)}, u32[]{:S(2)}) collective-permute-start(bf16[4,256,1024]{2,1,0:T(8,128)(2,1)} %bitcast.67.second), channel_id=1, source_target_pairs={{0,16},{1,17},{2,18},{3,19},{4,20},{5,21},{6,22},{7,23},{8,24},{9,... | collective-permute-start | bytes 6291464 | tf_op jit(solution)/shard_map/ppermute | solution.py:944
  601.6 29.5 %collective-permute-start.70 = (bf16[4,256,1024]{2,1,0:T(8,128)(2,1)}, bf16[4,256,1024]{2,1,0:T(8,128)(2,1)}, u32[]{:S(2)}, u32[]{:S(2)}) collective-permute-start(bf16[4,256,1024]{2,1,0:T(8,128)(2,1)} %bitcast.225), channel_id=1, source_target_pairs={{16,0},{17,1},{18,2},{19,3},{20,4},{21,5},{22,6},{23,7},{24,8},{25... | collective-permute-start | bytes 6291464 | tf_op jit(solution)/shard_map/ppermute | solution.py:944
  (93 other events, 890.4 us)
Sparse Core Ops, SparseCore 0:
  126.3 26.3 all-gather.12
  213.3 60.1 all-gather.14
  322.0 48.9 all-gather.16
  404.0 42.7 all-gather.18
  448.8 45.7 all-gather.20
  537.2 64.3 all-gather.22

commit v5 on v4

--- a/solution.py
+++ b/solution.py
@@ -757,8 +757,8 @@
     head_piece, out_piece, feed_piece = piece_rows(head_rows), piece_rows(out_rows), piece_rows(feed_rows)
     out_far = [z_swap(main_pieces[0][:out_piece], step) for step in range(1, planes)]
     feed_far = z_swap(main_pieces[0][out_piece:], planes // 2)
-    out_there = core_swap(tie(out_here, feed_far))
-    feed_there = [core_swap(tie(v, feed_far)) for v in feed_here]
+    out_there = core_swap(out_here)
+    feed_there = [core_swap(v) for v in feed_here]
     latents_w = [jnp.where(core == layer, lat_here, lat_there) for layer in range(layers)]
     gains_all = [jnp.where(core == layer, gain_here, gain_there) for layer in range(layers)]
 
@@ -914,7 +914,7 @@
         return grad_x, pack_parts, finish_feed, finish_pack
 
     lat0 = first_latents()
-    first_out, messages = first_attention(feed_far, lat0)
+    first_out, messages = first_attention(feed_far, lat0, out_there, *feed_there)
     main0 = gather(out_far + [feed_far], (), messages)
     outs0 = (out_here, out_there) + main0 + (0, out_piece)
     at = (planes - 1) * out_piece

time: 649 us -> 638 us (0.983)
  waiting for transfers between devices: 209 us -> 191 us
  starting transfers between devices: 118 us -> 128 us
    ppermute x31, waiting for transfers between devices: 141 us -> 125 us  [z_swap(): return lax.ppermute(value, 'tensor', [(i, i ^ step) for i in range(count)])]
    ppermute x31, starting transfers between devices: 34.5 us -> 44.6 us  [z_swap(): return lax.ppermute(value, 'tensor', [(i, i ^ step) for i in range(count)])]
  transfers between devices with their start and end apart: 91 -> 91, of which waited for: 35 -> 33; matrix products, arithmetic and copies ran while one was open for 15% -> 14% of each run, Pallas kernels for 29% -> 30%
where the time goes in v5:
time: 638 us; the launch traced here: 630 us
  Pallas kernels  193 us (30%)
  waiting for transfers between devices  191 us (30%)
  starting transfers between devices  128 us (20%)
  other arithmetic  57.1 us (9%)
  local copies, waits for them, and re-layouts  31.6 us (5%)
  between operations  15.9 us (2%)
  matrix products  14.3 us (2%)
    pallas_call x19, Pallas kernels, kernel_call(): pl.pallas_call(kernel, grid_spec=pltpu.PrefetchScalarGridSpec(num_scalar_...  193 us
    ppermute x31, waiting for transfers between devices, z_swap(): return lax.ppermute(value, 'tensor', [(i, i ^ step) for i in range(count)])  125 us
    ppermute x31, starting transfers between devices, z_swap(): return lax.ppermute(value, 'tensor', [(i, i ^ step) for i in range(count)])  44.6 us
    all_to_all x2, waiting for transfers between devices, backward(): lax.all_to_all(jnp.concatenate([pack_total, small_total], axis=2), 'dp',...  27.3 us
    ppermute x38, starting transfers between devices, core_swap(): return lax.ppermute(value, 'section', [(0, 1), (1, 0)])  26.6 us
  transfers between devices with their start and end apart: 91, of which 33 were waited for; matrix products, arithmetic and copies ran while one was open for 14% of the time, Pallas kernels for 30%

profile of v5, /device:TPU:1, one launch (start us, length us, event | category | flops | bytes accessed | tf_op | source)
XLA Modules:
  0.0 630.1 jit_solution(13257000015417992879)
XLA Ops:
  23.9 7.8 %collective-permute-done.13 = bf16[32,1024]{1,0:T(8,128)(2,1)S(1)} collective-permute-done((bf16[32,1024]{1,0:T(8,128)(2,1)S(1)}, bf16[32,1024]{1,0:T(8,128)(2,1)S(1)}, u32[]{:S(2)}, u32[]{:S(2)}) %collective-permute-start.13) | collective-permute-done | bytes 65568 | tf_op jit(solution)/shard_map/ppermute | solution.py:35
  33.7 14.5 %collective-permute-done.14 = bf16[32,1024]{1,0:T(8,128)(2,1)S(1)} collective-permute-done((bf16[32,1024]{1,0:T(8,128)(2,1)S(1)}, bf16[32,1024]{1,0:T(8,128)(2,1)S(1)}, u32[]{:S(2)}, u32[]{:S(2)}) %collective-permute-start.14) | collective-permute-done | bytes 65568 | tf_op jit(solution)/shard_map/ppermute | solution.py:35
  52.2 4.8 all-to-all-start
  65.9 12.3 %attend_first.1 = bf16[4,272,256]{2,1,0:T(8,128)(2,1)S(1)} custom-call(s32[4]{0:T(128)S(1)} %pad_add_fusion.info, bf16[2048,1024]{1,0:T(8,128)(2,1)} %x.11, bf16[1024,512]{1,0:T(8,128)(2,1)} %bitcast.7.lat_here, bf16[1024,512]{1,0:T(8,128)(2,1)} %collective-permute-done.lat_there, bf16[1536,256]{1,0:T(8,128)(2,1)S(1)} %pad_maximum_fusion.2.heads_here.h0, ...), custom_call_target="tpu_custom_call" | custom-call | flops 4563402752 | bytes 8437760 | tf_op jit(solution)/shard_map/attend_first/pallas_call | solution.py:83
  94.2 5.2 collective-permute-done.18
  113.8 14.8 %collective-permute-start.28 = (bf16[32,1024]{1,0:T(8,128)(2,1)S(1)}, bf16[32,1024]{1,0:T(8,128)(2,1)S(1)}, u32[]{:S(2)}, u32[]{:S(2)}) collective-permute-start(bf16[32,1024]{1,0:T(8,128)(2,1)S(1)} %slice.174), channel_id=1, source_target_pairs={{0,4},{4,0},{8,12},{12,8},{1,5},{5,1},{9,13},{13,9},{2,6},{6,2},{1... | collective-permute-start | bytes 196616 | tf_op jit(solution)/shard_map/ppermute | solution.py:35
  131.4 6.2 attend_out.1
  137.6 6.5 %feed.4 = (f32[256,1024]{1,0:T(8,128)S(1)}, bf16[2,2,256,704]{3,2,1,0:T(8,128)(2,1)}) custom-call(s32[6]{0:T(128)S(1)} %stack.115.info, bf16[256,1024]{1,0:T(8,128)(2,1)S(1)} %get-tuple-element.134.value.refs_0_, bf16[704,1024]{1,0:T(8,128)(2,1)} %bitcast.13.refs_0_, bf16[704,1024]{1,0:T(8,128)(2,1)} %bitcast.15.refs_1_, bf16[704,1024]{1,0:T(8,128)(2,1)} %bitcast.189, ...), custom_call_target="tpu_custom_call" | custom-call | flops 2214592512 | bytes 30539776 | tf_op jit(solution)/shard_map/feed/pallas_call | solution.py:83
  146.3 4.7 all-to-all-start.1
  151.4 11.6 %collective-permute-done.17.value.refs_1_ = bf16[256,1024]{1,0:T(8,128)(2,1)S(1)} collective-permute-done((bf16[256,1024]{1,0:T(8,128)(2,1)S(1)}, bf16[256,1024]{1,0:T(8,128)(2,1)S(1)}, u32[]{:S(2)}, u32[]{:S(2)}) %collective-permute-start.17) | collective-permute-done | bytes 524320 | tf_op jit(solution)/shard_map/ppermute | solution.py:35
  163.0 6.6 %feed.5 = (bf16[256,1024]{1,0:T(8,128)(2,1)S(1)}, bf16[2,2,256,704]{3,2,1,0:T(8,128)(2,1)}) custom-call(s32[6]{0:T(128)S(1)} %stack.115.info, bf16[256,1024]{1,0:T(8,128)(2,1)S(1)} %collective-permute-done.17.value.refs_1_, bf16[704,1024]{1,0:T(8,128)(2,1)} %bitcast.13.refs_0_, bf16[704,1024]{1,0:T(8,128)(2,1)} %bitcast.15.refs_1_, ...), custom_call_target="tpu_custom_call" | custom-call | flops 2214592512 | bytes 30015488 | tf_op jit(solution)/shard_map/feed/pallas_call | solution.py:83
  170.6 10.2 %collective-permute-done.22 = bf16[256,1024]{1,0:T(8,128)(2,1)S(1)} collective-permute-done((bf16[256,1024]{1,0:T(8,128)(2,1)S(1)}, bf16[256,1024]{1,0:T(8,128)(2,1)S(1)}, u32[]{:S(2)}, u32[]{:S(2)}) %collective-permute-start.22) | collective-permute-done | bytes 524320 | tf_op jit(solution)/shard_map/ppermute | solution.py:35
  192.6 4.9 collective-permute-done.25.lat2
  200.4 17.7 %attend.1 = (bf16[4,256,256]{2,1,0:T(8,128)(2,1)S(1)}, f32[4,4,256]{2,1,0:T(4,128)S(1)}, bf16[2,1024,256]{2,1,0:T(8,128)(2,1)}, f32[256,1024]{1,0:T(8,128)}, bf16[256,1024]{1,0:T(8,128)(2,1)}) custom-call(s32[6]{0:T(128)S(1)} %stack.115.info, bf16[256,1024]{1,0:T(8,128)(2,1)} %copy-done.17, bf16[256,1024]{1,0:T(8,128)(2,1)} %copy-done.2, ...), custom_call_target="tpu_custom_call" | custom-call | flops 6442450944 | bytes 16535552 | tf_op jit(solution)/shard_map/attend/pallas_call | solution.py:83
  221.4 6.6 %feed.6 = (f32[256,1024]{1,0:T(8,128)S(1)}, bf16[2,2,256,704]{3,2,1,0:T(8,128)(2,1)}) custom-call(s32[6]{0:T(128)S(1)} %stack.115.info, bf16[256,1024]{1,0:T(8,128)(2,1)S(1)} %copy-done.11, bf16[704,1024]{1,0:T(8,128)(2,1)} %bitcast.13.refs_0_, bf16[704,1024]{1,0:T(8,128)(2,1)} %bitcast.15.refs_1_, bf16[704,1024]{1,0:T(8,128)(2,1)} %bitcast.191, ...), custom_call_target="tpu_custom_call" | custom-call | flops 2214592512 | bytes 30539776 | tf_op jit(solution)/shard_map/feed/pallas_call | solution.py:83
  228.0 10.0 %feed_back.4 = (f32[256,1024]{1,0:T(8,128)S(1)}, bf16[3,256,768]{2,1,0:T(8,128)(2,1)}, bf16[3,256,768]{2,1,0:T(8,128)(2,1)}) custom-call(s32[6]{0:T(128)S(1)} %stack.115.info, bf16[256,1024]{1,0:T(8,128)(2,1)S(1)} %get-tuple-element.263.value.refs_4_, bf16[2,2,256,704]{3,2,1,0:T(8,128)(2,1)} %get-tuple-element.107.saved, bf16[704,1024]{1,0:T(8,128)(2,1)} %bitcast.13.refs_0_, ...), custom_call_target="tpu_custom_call" | custom-call | flops 2214592512 | bytes 32899072 | tf_op jit(solution)/shard_map/feed_back/pallas_call | solution.py:83
  239.0 15.3 %collective-permute-done.33.value.refs_1_ = bf16[256,1024]{1,0:T(8,128)(2,1)S(1)} collective-permute-done((bf16[256,1024]{1,0:T(8,128)(2,1)}, bf16[256,1024]{1,0:T(8,128)(2,1)S(1)}, u32[]{:S(2)}, u32[]{:S(2)}) %collective-permute-start.33) | collective-permute-done | bytes 524320 | tf_op jit(solution)/shard_map/ppermute | solution.py:35
  254.3 6.7 %feed.7 = (bf16[256,1024]{1,0:T(8,128)(2,1)}, bf16[2,2,256,704]{3,2,1,0:T(8,128)(2,1)}) custom-call(s32[6]{0:T(128)S(1)} %stack.115.info, bf16[256,1024]{1,0:T(8,128)(2,1)S(1)} %collective-permute-done.33.value.refs_1_, bf16[704,1024]{1,0:T(8,128)(2,1)} %bitcast.13.refs_0_, bf16[704,1024]{1,0:T(8,128)(2,1)} %bitcast.15.refs_1_, bf16[704,1024]{1,0:T(8,128)(2,1)} %bitcast.193, ...), custom_call_target="tpu_custom_call" | custom-call | flops 2214592512 | bytes 30015488 | tf_op jit(solution)/shard_map/feed/pallas_call | solution.py:83
  261.0 4.5 collective-permute-done.36.value.refs_5_
  265.5 10.4 %feed_back.5 = (bf16[256,1024]{1,0:T(8,128)(2,1)}, bf16[3,256,768]{2,1,0:T(8,128)(2,1)}, bf16[3,256,768]{2,1,0:T(8,128)(2,1)}) custom-call(s32[6]{0:T(128)S(1)} %stack.115.info, bf16[256,1024]{1,0:T(8,128)(2,1)S(1)} %collective-permute-done.36.value.refs_5_, bf16[2,2,256,704]{3,2,1,0:T(8,128)(2,1)} %get-tuple-element.109.saved, ...), custom_call_target="tpu_custom_call" | custom-call | flops 2214592512 | bytes 32374784 | tf_op jit(solution)/shard_map/feed_back/pallas_call | solution.py:83
  283.5 10.8 %feed_weights.2 = bf16[4,3,256,768]{3,2,1,0:T(8,128)(2,1)} custom-call(s32[6]{0:T(128)S(1)} %stack.115.info, bf16[256,1024]{1,0:T(8,128)(2,1)S(1)} %copy-done.12, bf16[256,1024]{1,0:T(8,128)(2,1)S(1)} %collective-permute-done.33.value.refs_1_, bf16[256,1024]{1,0:T(8,128)(2,1)S(1)} %collective-permute-done.38.refs_2_, bf16[256,1024]{1,0:T(8,128)(2,1)} %copy-done.48, ...), custom_call_target="tpu_custom_call" | custom-call | flops 4429185024 | bytes 13631488 | tf_op jit(solution)/shard_map/feed_weights/pallas_call | solution.py:83
  294.3 4.9 all-to-all-start.2
  309.6 14.7 %attend_back.4 = (f32[256,1024]{1,0:T(8,128)}, bf16[1024,256]{1,0:T(8,128)(2,1)S(1)}, bf16[4,2,320,256]{3,2,1,0:T(8,128)(2,1)}, bf16[4,2,320,256]{3,2,1,0:T(8,128)(2,1)}) custom-call(s32[6]{0:T(128)S(1)} %stack.115.info, bf16[256,1024]{1,0:T(8,128)(2,1)S(1)} %copy-done.10, bf16[256,1024]{1,0:T(8,128)(2,1)S(1)} %copy-done.3, ...), custom_call_target="tpu_custom_call" | custom-call | flops 8858370048 | bytes 18104320 | tf_op jit(solution)/shard_map/attend_back/pallas_call | solution.py:83
  325.6 14.5 %attend_back.5 = (f32[256,1024]{1,0:T(8,128)}, bf16[1024,256]{1,0:T(8,128)(2,1)S(1)}, bf16[4,2,320,256]{3,2,1,0:T(8,128)(2,1)}, bf16[4,2,320,256]{3,2,1,0:T(8,128)(2,1)}) custom-call(s32[6]{0:T(128)S(1)} %stack.115.info, bf16[256,1024]{1,0:T(8,128)(2,1)S(1)} %copy-done.10, bf16[256,1024]{1,0:T(8,128)(2,1)S(1)} %copy-done.3, ...), custom_call_target="tpu_custom_call" | custom-call | flops 8858370048 | bytes 18104320 | tf_op jit(solution)/shard_map/attend_back/pallas_call | solution.py:83
  342.6 12.5 %collective-permute-done.45 = bf16[256,256]{1,0:T(8,128)(2,1)S(1)} collective-permute-done((bf16[256,256]{1,0:T(8,128)(2,1)S(1)}, bf16[256,256]{1,0:T(8,128)(2,1)S(1)}, u32[]{:S(2)}, u32[]{:S(2)}) %collective-permute-start.45) | collective-permute-done | bytes 131104 | tf_op jit(solution)/shard_map/ppermute | solution.py:35
  373.7 4.8 all-to-all-start.3
  385.2 4.3 collective-permute-done.62
  392.0 4.4 reduce_sum.182
  397.8 9.7 %feed_back.6 = (f32[256,1024]{1,0:T(8,128)S(1)}, bf16[3,256,768]{2,1,0:T(8,128)(2,1)}, bf16[3,256,768]{2,1,0:T(8,128)(2,1)}) custom-call(s32[6]{0:T(128)S(1)} %stack.115.info, bf16[256,1024]{1,0:T(8,128)(2,1)S(1)} %get-tuple-element.204.value.refs_4_, bf16[2,2,256,704]{3,2,1,0:T(8,128)(2,1)} %get-tuple-element.125.saved, bf16[704,1024]{1,0:T(8,128)(2,1)} %bitcast.13.refs_0_, ...), custom_call_target="tpu_custom_call" | custom-call | flops 2214592512 | bytes 32899072 | tf_op jit(solution)/shard_map/feed_back/pallas_call | solution.py:83
  407.5 4.8 collective-permute-start.58
  412.3 10.3 %feed_back.7 = (bf16[256,1024]{1,0:T(8,128)(2,1)}, bf16[3,256,768]{2,1,0:T(8,128)(2,1)}, bf16[3,256,768]{2,1,0:T(8,128)(2,1)}) custom-call(s32[6]{0:T(128)S(1)} %stack.115.info, bf16[256,1024]{1,0:T(8,128)(2,1)S(1)} %collective-permute-done.48.value.refs_5_, bf16[2,2,256,704]{3,2,1,0:T(8,128)(2,1)} %get-tuple-element.127.saved, ...), custom_call_target="tpu_custom_call" | custom-call | flops 2214592512 | bytes 32374784 | tf_op jit(solution)/shard_map/feed_back/pallas_call | solution.py:83
  423.5 4.4 collective-permute-done.53
  427.8 5.4 all-gather.19.cloned.1.call-done
  435.1 11.0 %feed_weights.3 = bf16[4,3,256,768]{3,2,1,0:T(8,128)(2,1)} custom-call(s32[6]{0:T(128)S(1)} %stack.115.info, bf16[256,1024]{1,0:T(8,128)(2,1)S(1)} %get-tuple-element.134.value.refs_0_, bf16[256,1024]{1,0:T(8,128)(2,1)S(1)} %copy-done.9, bf16[256,1024]{1,0:T(8,128)(2,1)} %collective-permute-done.54.refs_2_, ...), custom_call_target="tpu_custom_call" | custom-call | flops 4429185024 | bytes 13631488 | tf_op jit(solution)/shard_map/feed_weights/pallas_call | solution.py:83
  446.0 5.1 all-to-all-start.4
  455.4 14.5 %attend_back.6 = (f32[256,1024]{1,0:T(8,128)}, bf16[1024,256]{1,0:T(8,128)(2,1)S(1)}, bf16[4,2,320,256]{3,2,1,0:T(8,128)(2,1)}, bf16[4,2,320,256]{3,2,1,0:T(8,128)(2,1)}) custom-call(s32[6]{0:T(128)S(1)} %stack.115.info, bf16[256,1024]{1,0:T(8,128)(2,1)S(1)} %get-tuple-element.148.grad_branch, bf16[256,1024]{1,0:T(8,128)(2,1)S(1)} %fusion.18.normed, ...), custom_call_target="tpu_custom_call" | custom-call | flops 8858370048 | bytes 18104320 | tf_op jit(solution)/shard_map/attend_back/pallas_call | solution.py:83
  475.3 14.6 %attend_back.7 = (f32[256,1024]{1,0:T(8,128)}, bf16[1024,256]{1,0:T(8,128)(2,1)S(1)}, bf16[4,2,320,256]{3,2,1,0:T(8,128)(2,1)}, bf16[4,2,320,256]{3,2,1,0:T(8,128)(2,1)}) custom-call(s32[6]{0:T(128)S(1)} %stack.115.info, bf16[256,1024]{1,0:T(8,128)(2,1)S(1)} %get-tuple-element.148.grad_branch, bf16[256,1024]{1,0:T(8,128)(2,1)S(1)} %fusion.18.normed, ...), custom_call_target="tpu_custom_call" | custom-call | flops 8858370048 | bytes 18104320 | tf_op jit(solution)/shard_map/attend_back/pallas_call | solution.py:83
  500.5 8.5 %collective-permute-done.69 = bf16[400,256]{1,0:T(8,128)(2,1)S(1)} collective-permute-done((bf16[400,256]{1,0:T(8,128)(2,1)S(1)}, bf16[400,256]{1,0:T(8,128)(2,1)S(1)}, u32[]{:S(2)}, u32[]{:S(2)}) %collective-permute-start.69) | collective-permute-done | bytes 204832 | tf_op jit(solution)/shard_map/ppermute | solution.py:35
  509.0 4.4 reduce_sum.184
  529.2 4.8 all-to-all-start.5
  539.3 4.5 collective-permute-start.78
  543.8 27.3 %all-to-all-done.5 = bf16[4,4,400,256]{3,2,1,0:T(8,128)(2,1)} async-done(((bf16[4,4,400,256]{3,2,1,0:T(8,128)(2,1)}), bf16[4,4,400,256]{3,2,1,0:T(8,128)(2,1)}, u32[]{:S(2)}, u32[]{:S(2)}) %all-to-all-start.5) | async-done | bytes 3276832 | tf_op jit(solution)/shard_map/all_to_all | solution.py:901
  573.9 4.8 rows.2
  580.0 7.6 %all-gather.23.cloned.1.call-done = bf16[1024,1024]{1,0:T(8,128)(2,1)} async-done(((bf16[256,1024]{1,0:T(8,128)(2,1)}), bf16[1024,1024]{1,0:T(8,128)(2,1)}) %all-gather.23.cloned.1.call-update) | async-done | bytes 2097168 | tf_op jit(solution)/shard_map/all_gather | solution.py:941
  587.6 4.2 collective-permute-start.70
  591.7 6.5 %collective-permute-done.75 = bf16[2,400,256]{2,1,0:T(8,128)(2,1)S(1)} collective-permute-done((bf16[2,400,256]{2,1,0:T(8,128)(2,1)S(1)}, bf16[2,400,256]{2,1,0:T(8,128)(2,1)S(1)}, u32[]{:S(2)}, u32[]{:S(2)}) %collective-permute-start.75) | collective-permute-done | bytes 409632 | tf_op jit(solution)/shard_map/ppermute | solution.py:35
  601.2 9.2 %collective-permute-done.76 = bf16[400,256]{1,0:T(8,128)(2,1)S(1)} collective-permute-done((bf16[400,256]{1,0:T(8,128)(2,1)S(1)}, bf16[400,256]{1,0:T(8,128)(2,1)S(1)}, u32[]{:S(2)}, u32[]{:S(2)}) %collective-permute-start.76) | collective-permute-done | bytes 204832 | tf_op jit(solution)/shard_map/ppermute | solution.py:35
  618.2 4.8 rows.3
  (394 shorter events, 195.5 us)
Async XLA Ops:
  10.7 48.4 %collective-permute-start = (bf16[1024,512]{1,0:T(8,128)(2,1)}, bf16[1024,512]{1,0:T(8,128)(2,1)}, u32[]{:S(2)}, u32[]{:S(2)}) collective-permute-start(bf16[1024,512]{1,0:T(8,128)(2,1)} %bitcast.7.lat_here), channel_id=1, source_target_pairs={{0,16},{16,0},{1,17},{17,1},{2,18},{18,2},{3,19},{19,3},{4,20},{20... | collective-permute-start | bytes 3145736 | tf_op jit(solution)/shard_map/ppermute | solution.py:30
  14.4 35.1 %collective-permute-start.2 = (bf16[288,1024]{1,0:T(8,128)(2,1)S(1)}, bf16[288,1024]{1,0:T(8,128)(2,1)S(1)}, u32[]{:S(2)}, u32[]{:S(2)}) collective-permute-start(bf16[288,1024]{1,0:T(8,128)(2,1)S(1)} %slice.207), channel_id=1, source_target_pairs={{0,8},{4,12},{8,0},{12,4},{1,9},{5,13},{9,1},{13,5},{2,10},{6,14},... | collective-permute-start | bytes 1769480 | tf_op jit(solution)/shard_map/ppermute | solution.py:35
  21.2 27.0 %collective-permute-start.14 = (bf16[32,1024]{1,0:T(8,128)(2,1)S(1)}, bf16[32,1024]{1,0:T(8,128)(2,1)S(1)}, u32[]{:S(2)}, u32[]{:S(2)}) collective-permute-start(bf16[32,1024]{1,0:T(8,128)(2,1)S(1)} %slice.216), channel_id=1, source_target_pairs={{0,8},{4,12},{8,0},{12,4},{1,9},{5,13},{9,1},{13,5},{2,10},{6,14},... | collective-permute-start | bytes 196616 | tf_op jit(solution)/shard_map/ppermute | solution.py:35
  21.3 28.2 %collective-permute-start.15 = (bf16[32,1024]{1,0:T(8,128)(2,1)S(1)}, bf16[32,1024]{1,0:T(8,128)(2,1)S(1)}, u32[]{:S(2)}, u32[]{:S(2)}) collective-permute-start(bf16[32,1024]{1,0:T(8,128)(2,1)S(1)} %slice.216), channel_id=1, source_target_pairs={{0,12},{4,8},{8,4},{12,0},{1,13},{5,9},{9,5},{13,1},{2,14},{6,10},... | collective-permute-start | bytes 196616 | tf_op jit(solution)/shard_map/ppermute | solution.py:35
  31.7 32.5 %collective-permute-start.5 = (bf16[704,1024]{1,0:T(8,128)(2,1)}, bf16[704,1024]{1,0:T(8,128)(2,1)}, u32[]{:S(2)}, u32[]{:S(2)}) collective-permute-start(bf16[704,1024]{1,0:T(8,128)(2,1)} %bitcast.13.refs_0_), channel_id=1, source_target_pairs={{0,16},{16,0},{1,17},{17,1},{2,18},{18,2},{3,19},{19,3},{4,20},{20... | collective-permute-start | bytes 4325384 | tf_op jit(solution)/shard_map/ppermute | solution.py:30
  48.2 16.1 %collective-permute-start.6 = (bf16[704,1024]{1,0:T(8,128)(2,1)}, bf16[704,1024]{1,0:T(8,128)(2,1)}, u32[]{:S(2)}, u32[]{:S(2)}) collective-permute-start(bf16[704,1024]{1,0:T(8,128)(2,1)} %bitcast.15.refs_1_), channel_id=1, source_target_pairs={{0,16},{16,0},{1,17},{17,1},{2,18},{18,2},{3,19},{19,3},{4,20},{20... | collective-permute-start | bytes 4325384 | tf_op jit(solution)/shard_map/ppermute | solution.py:30
  52.2 41.2 %all-to-all-start = ((bf16[4,384,1024]{2,1,0:T(8,128)(2,1)}), bf16[4,384,1024]{2,1,0:T(8,128)(2,1)}, u32[]{:S(2)}, u32[]{:S(2)}) async-start(bf16[4,384,1024]{2,1,0:T(8,128)(2,1)} %broadcast_in_dim.8), calls=%async_computation | async-start | bytes 6291456 | tf_op jit(solution)/shard_map/all_to_all | solution.py:48
  57.0 106.1 %all-gather.13.cloned.1.call-start = ((), (), s32[]{:S(2)}) async-start(), calls=%async_computation.6 | async-start | bytes 1474560 | tf_op jit(solution)/shard_map/all_gather | solution.py:776
  93.3 38.1 %collective-permute-start.16 = (bf16[4,384,1024]{2,1,0:T(8,128)(2,1)}, bf16[4,384,1024]{2,1,0:T(8,128)(2,1)}, u32[]{:S(2)}, u32[]{:S(2)}) collective-permute-start(bf16[4,384,1024]{2,1,0:T(8,128)(2,1)} %all-to-all-done.o2.refs_6_.refs_8_.refs_10_), channel_id=1, source_target_pairs={{0,16},{16,0},{1,17},{17,1},{2,18},{18,2},{3,19},{19,3},{4,20},{20... | collective-permute-start | bytes 9437192 | tf_op jit(solution)/shard_map/ppermute | solution.py:30
  104.4 39.8 %collective-permute-start.31 = (bf16[288,1024]{1,0:T(8,128)(2,1)}, bf16[288,1024]{1,0:T(8,128)(2,1)S(1)}, u32[]{:S(2)}, u32[]{:S(2)}) collective-permute-start(bf16[288,1024]{1,0:T(8,128)(2,1)} %slice.175), channel_id=1, source_target_pairs={{0,8},{4,12},{8,0},{12,4},{1,9},{5,13},{9,1},{13,5},{2,10},{6,14},... | collective-permute-start | bytes 1769480 | tf_op jit(solution)/shard_map/ppermute | solution.py:35
  113.8 30.3 %collective-permute-start.28 = (bf16[32,1024]{1,0:T(8,128)(2,1)S(1)}, bf16[32,1024]{1,0:T(8,128)(2,1)S(1)}, u32[]{:S(2)}, u32[]{:S(2)}) collective-permute-start(bf16[32,1024]{1,0:T(8,128)(2,1)S(1)} %slice.174), channel_id=1, source_target_pairs={{0,4},{4,0},{8,12},{12,8},{1,5},{5,1},{9,13},{13,9},{2,6},{6,2},{1... | collective-permute-start | bytes 196616 | tf_op jit(solution)/shard_map/ppermute | solution.py:35
  128.6 15.6 %collective-permute-start.29 = (bf16[32,1024]{1,0:T(8,128)(2,1)S(1)}, bf16[32,1024]{1,0:T(8,128)(2,1)S(1)}, u32[]{:S(2)}, u32[]{:S(2)}) collective-permute-start(bf16[32,1024]{1,0:T(8,128)(2,1)S(1)} %slice.174), channel_id=1, source_target_pairs={{0,8},{4,12},{8,0},{12,4},{1,9},{5,13},{9,1},{13,5},{2,10},{6,14},... | collective-permute-start | bytes 196616 | tf_op jit(solution)/shard_map/ppermute | solution.py:35
  146.3 40.3 %all-to-all-start.1 = ((bf16[4,384,1024]{2,1,0:T(8,128)(2,1)}), bf16[4,384,1024]{2,1,0:T(8,128)(2,1)}, u32[]{:S(2)}, u32[]{:S(2)}) async-start(bf16[4,384,1024]{2,1,0:T(8,128)(2,1)} %broadcast_in_dim.9), calls=%async_computation.1 | async-start | bytes 6291456 | tf_op jit(solution)/shard_map/all_to_all | solution.py:48
  151.0 148.3 %all-gather.15.cloned.1.call-start = ((), (), s32[]{:S(2)}) async-start(), calls=%async_computation.7 | async-start | bytes 2621440 | tf_op jit(solution)/shard_map/all_gather | solution.py:941
  218.9 35.4 %collective-permute-start.33 = (bf16[256,1024]{1,0:T(8,128)(2,1)}, bf16[256,1024]{1,0:T(8,128)(2,1)S(1)}, u32[]{:S(2)}, u32[]{:S(2)}) collective-permute-start(bf16[256,1024]{1,0:T(8,128)(2,1)} %get-tuple-element.103.value.refs_0_), channel_id=1, source_target_pairs={{0,4},{4,0},{8,12},{12,8},{1,5},{5,1},{9,13},{13,9},{2,6},{6,2},{1... | collective-permute-start | bytes 1572872 | tf_op jit(solution)/shard_map/ppermute | solution.py:35
  219.9 45.6 %collective-permute-start.36 = (bf16[256,1024]{1,0:T(8,128)(2,1)S(1)}, bf16[256,1024]{1,0:T(8,128)(2,1)S(1)}, u32[]{:S(2)}, u32[]{:S(2)}) collective-permute-start(bf16[256,1024]{1,0:T(8,128)(2,1)S(1)} %get-tuple-element.263.value.refs_4_), channel_id=1, source_target_pairs={{0,4},{4,0},{8,12},{12,8},{1,5},{5,1},{9,13},{13,9},{2,6},{6,2},{1... | collective-permute-start | bytes 1572872 | tf_op jit(solution)/shard_map/ppermute | solution.py:35
  238.0 43.9 %collective-permute-start.42 = (bf16[3,256,768]{2,1,0:T(8,128)(2,1)}, bf16[3,256,768]{2,1,0:T(8,128)(2,1)S(1)}, u32[]{:S(2)}, u32[]{:S(2)}) collective-permute-start(bf16[3,256,768]{2,1,0:T(8,128)(2,1)} %get-tuple-element.113), channel_id=1, source_target_pairs={{0,16},{16,0},{1,17},{17,1},{2,18},{18,2},{3,19},{19,3},{4,20},{20... | collective-permute-start | bytes 3538952 | tf_op jit(solution)/shard_map/ppermute | solution.py:30
  280.4 18.9 %collective-permute-start.37 = (bf16[256,1024]{1,0:T(8,128)(2,1)}, bf16[256,1024]{1,0:T(8,128)(2,1)S(1)}, u32[]{:S(2)}, u32[]{:S(2)}) collective-permute-start(bf16[256,1024]{1,0:T(8,128)(2,1)} %get-tuple-element.110), channel_id=1, source_target_pairs={{0,4},{4,0},{8,12},{12,8},{1,5},{5,1},{9,13},{13,9},{2,6},{6,2},{1... | collective-permute-start | bytes 1572872 | tf_op jit(solution)/shard_map/ppermute | solution.py:35
  281.2 23.9 %collective-permute-start.34 = (bf16[256,1024]{1,0:T(8,128)(2,1)}, bf16[256,1024]{1,0:T(8,128)(2,1)}, u32[]{:S(2)}, u32[]{:S(2)}) collective-permute-start(bf16[256,1024]{1,0:T(8,128)(2,1)} %get-tuple-element.106), channel_id=1, source_target_pairs={{0,4},{4,0},{8,12},{12,8},{1,5},{5,1},{9,13},{13,9},{2,6},{6,2},{1... | collective-permute-start | bytes 1572872 | tf_op jit(solution)/shard_map/ppermute | solution.py:35
  294.3 65.0 %all-to-all-start.2 = ((bf16[4,3,256,768]{3,2,1,0:T(8,128)(2,1)}), bf16[4,3,256,768]{3,2,1,0:T(8,128)(2,1)}, u32[]{:S(2)}, u32[]{:S(2)}) async-start(bf16[4,3,256,768]{3,2,1,0:T(8,128)(2,1)} %feed_weights.2), calls=%async_computation.2 | async-start | bytes 9437184 | tf_op jit(solution)/shard_map/all_to_all | solution.py:853
  299.2 60.0 %all-gather.17.cloned.1.call-start = ((), (), s32[]{:S(2)}) async-start(), calls=%async_computation.8 | async-start | bytes 2621440 | tf_op jit(solution)/shard_map/all_gather | solution.py:941
  324.4 16.5 %collective-permute-start.44 = (bf16[2,256,256]{2,1,0:T(8,128)(2,1)S(1)}, bf16[2,256,256]{2,1,0:T(8,128)(2,1)S(1)}, u32[]{:S(2)}, u32[]{:S(2)}) collective-permute-start(bf16[2,256,256]{2,1,0:T(8,128)(2,1)S(1)} %dynamic-slice_bitcast_fusion.5), channel_id=1, source_target_pairs={{0,16},{16,0},{1,17},{17,1},{2,18},{18,2},{3,19},{19,3},{4,20},{20... | collective-permute-start | bytes 786440 | tf_op jit(solution)/shard_map/ppermute | solution.py:30
  340.2 27.7 %collective-permute-start.50 = (bf16[4,2,320,256]{3,2,1,0:T(8,128)(2,1)}, bf16[4,2,320,256]{3,2,1,0:T(8,128)(2,1)}, u32[]{:S(2)}, u32[]{:S(2)}) collective-permute-start(bf16[4,2,320,256]{3,2,1,0:T(8,128)(2,1)} %get-tuple-element.130), channel_id=1, source_target_pairs={{0,16},{16,0},{1,17},{17,1},{2,18},{18,2},{3,19},{19,3},{4,20},{20... | collective-permute-start | bytes 3932168 | tf_op jit(solution)/shard_map/ppermute | solution.py:30
  340.7 29.3 %collective-permute-start.51 = (bf16[4,2,320,256]{3,2,1,0:T(8,128)(2,1)}, bf16[4,2,320,256]{3,2,1,0:T(8,128)(2,1)}, u32[]{:S(2)}, u32[]{:S(2)}) collective-permute-start(bf16[4,2,320,256]{3,2,1,0:T(8,128)(2,1)} %get-tuple-element.132), channel_id=1, source_target_pairs={{0,16},{16,0},{1,17},{17,1},{2,18},{18,2},{3,19},{19,3},{4,20},{20... | collective-permute-start | bytes 3932168 | tf_op jit(solution)/shard_map/ppermute | solution.py:30
  341.8 17.4 %collective-permute-start.47 = (bf16[256,256]{1,0:T(8,128)(2,1)S(1)}, bf16[256,256]{1,0:T(8,128)(2,1)S(1)}, u32[]{:S(2)}, u32[]{:S(2)}) collective-permute-start(bf16[256,256]{1,0:T(8,128)(2,1)S(1)} %dynamic-slice_bitcast_fusion.8), channel_id=1, source_target_pairs={{0,4},{4,0},{8,12},{12,8},{1,5},{5,1},{9,13},{13,9},{2,6},{6,2},{1... | collective-permute-start | bytes 393224 | tf_op jit(solution)/shard_map/ppermute | solution.py:35
  373.7 59.5 %all-to-all-start.3 = ((bf16[4,4,400,256]{3,2,1,0:T(8,128)(2,1)}), bf16[4,4,400,256]{3,2,1,0:T(8,128)(2,1)}, u32[]{:S(2)}, u32[]{:S(2)}) async-start(bf16[4,4,400,256]{3,2,1,0:T(8,128)(2,1)} %pad_maximum_fusion), calls=%async_computation.3 | async-start | bytes 6553600 | tf_op jit(solution)/shard_map/all_to_all | solution.py:901
  378.6 54.7 %all-gather.19.cloned.1.call-start = ((), (), s32[]{:S(2)}) async-start(), calls=%async_computation.9 | async-start | bytes 1474560 | tf_op jit(solution)/shard_map/all_gather | solution.py:776
  384.9 27.3 %collective-permute-start.48 = (bf16[256,1024]{1,0:T(8,128)(2,1)S(1)}, bf16[256,1024]{1,0:T(8,128)(2,1)S(1)}, u32[]{:S(2)}, u32[]{:S(2)}) collective-permute-start(bf16[256,1024]{1,0:T(8,128)(2,1)S(1)} %get-tuple-element.204.value.refs_4_), channel_id=1, source_target_pairs={{0,4},{4,0},{8,12},{12,8},{1,5},{5,1},{9,13},{13,9},{2,6},{6,2},{1... | collective-permute-start | bytes 1572872 | tf_op jit(solution)/shard_map/ppermute | solution.py:35
  390.3 123.1 %all-gather.21.cloned.1.call-start = ((), (), s32[]{:S(2)}) async-start(), calls=%async_computation.10 | async-start | bytes 2621440 | tf_op jit(solution)/shard_map/all_gather | solution.py:941
  390.4 32.3 %collective-permute-start.54 = (bf16[256,1024]{1,0:T(8,128)(2,1)S(1)}, bf16[256,1024]{1,0:T(8,128)(2,1)}, u32[]{:S(2)}, u32[]{:S(2)}) collective-permute-start(bf16[256,1024]{1,0:T(8,128)(2,1)S(1)} %get-tuple-element.134.value.refs_0_), channel_id=1, source_target_pairs={{0,16},{16,0},{1,17},{17,1},{2,18},{18,2},{3,19},{19,3},{4,20},{20... | collective-permute-start | bytes 1572872 | tf_op jit(solution)/shard_map/ppermute | solution.py:30
  391.9 31.2 %collective-permute-start.55 = (bf16[256,1024]{1,0:T(8,128)(2,1)S(1)}, bf16[256,1024]{1,0:T(8,128)(2,1)}, u32[]{:S(2)}, u32[]{:S(2)}) collective-permute-start(bf16[256,1024]{1,0:T(8,128)(2,1)S(1)} %copy-done.8), channel_id=1, source_target_pairs={{0,16},{16,0},{1,17},{17,1},{2,18},{18,2},{3,19},{19,3},{4,20},{20... | collective-permute-start | bytes 1572872 | tf_op jit(solution)/shard_map/ppermute | solution.py:30
  396.5 31.4 %collective-permute-start.53 = (bf16[3,256,768]{2,1,0:T(8,128)(2,1)}, bf16[3,256,768]{2,1,0:T(8,128)(2,1)}, u32[]{:S(2)}, u32[]{:S(2)}) collective-permute-start(bf16[3,256,768]{2,1,0:T(8,128)(2,1)} %reduce_sum.182), channel_id=1, source_target_pairs={{0,24},{4,28},{8,16},{12,20},{1,25},{5,29},{9,17},{13,21},{2,26},{... | collective-permute-start | bytes 3538952 | tf_op jit(solution)/shard_map/ppermute | solution.py:905
  407.5 26.5 %collective-permute-start.58 = (bf16[3,256,768]{2,1,0:T(8,128)(2,1)}, bf16[3,256,768]{2,1,0:T(8,128)(2,1)}, u32[]{:S(2)}, u32[]{:S(2)}) collective-permute-start(bf16[3,256,768]{2,1,0:T(8,128)(2,1)} %get-tuple-element.137), channel_id=1, source_target_pairs={{0,16},{16,0},{1,17},{17,1},{2,18},{18,2},{3,19},{19,3},{4,20},{20... | collective-permute-start | bytes 3538952 | tf_op jit(solution)/shard_map/ppermute | solution.py:30
  427.8 23.5 %collective-permute-start.49 = (bf16[256,1024]{1,0:T(8,128)(2,1)}, bf16[256,1024]{1,0:T(8,128)(2,1)}, u32[]{:S(2)}, u32[]{:S(2)}) collective-permute-start(bf16[256,1024]{1,0:T(8,128)(2,1)} %get-tuple-element.128), channel_id=1, source_target_pairs={{0,4},{4,0},{8,12},{12,8},{1,5},{5,1},{9,13},{13,9},{2,6},{6,2},{1... | collective-permute-start | bytes 1572872 | tf_op jit(solution)/shard_map/ppermute | solution.py:35
  433.3 22.2 %collective-permute-start.63 = (bf16[4,576,256]{2,1,0:T(8,128)(2,1)}, bf16[4,576,256]{2,1,0:T(8,128)(2,1)}, u32[]{:S(2)}, u32[]{:S(2)}) collective-permute-start(bf16[4,576,256]{2,1,0:T(8,128)(2,1)} %bitcast.226), channel_id=1, source_target_pairs={{0,16},{16,0},{1,17},{17,1},{2,18},{18,2},{3,19},{19,3},{4,20},{20... | collective-permute-start | bytes 3538952 | tf_op jit(solution)/shard_map/ppermute | solution.py:30
  446.0 63.0 %all-to-all-start.4 = ((bf16[4,3,256,768]{3,2,1,0:T(8,128)(2,1)}), bf16[4,3,256,768]{3,2,1,0:T(8,128)(2,1)}, u32[]{:S(2)}, u32[]{:S(2)}) async-start(bf16[4,3,256,768]{3,2,1,0:T(8,128)(2,1)} %feed_weights.3), calls=%async_computation.4 | async-start | bytes 9437184 | tf_op jit(solution)/shard_map/all_to_all | solution.py:853
  451.1 136.4 %all-gather.23.cloned.1.call-start = ((), (), s32[]{:S(2)}) async-start(), calls=%async_computation.11 | async-start | bytes 2621440 | tf_op jit(solution)/shard_map/all_gather | solution.py:941
  470.7 20.7 %collective-permute-start.64 = (bf16[2,256,256]{2,1,0:T(8,128)(2,1)}, bf16[2,256,256]{2,1,0:T(8,128)(2,1)}, u32[]{:S(2)}, u32[]{:S(2)}) collective-permute-start(bf16[2,256,256]{2,1,0:T(8,128)(2,1)} %dynamic-slice_bitcast_fusion.3), channel_id=1, source_target_pairs={{0,16},{16,0},{1,17},{17,1},{2,18},{18,2},{3,19},{19,3},{4,20},{20... | collective-permute-start | bytes 786440 | tf_op jit(solution)/shard_map/ppermute | solution.py:30
  474.1 23.6 %collective-permute-start.68 = (bf16[2,400,256]{2,1,0:T(8,128)(2,1)}, bf16[2,400,256]{2,1,0:T(8,128)(2,1)S(1)}, u32[]{:S(2)}, u32[]{:S(2)}) collective-permute-start(bf16[2,400,256]{2,1,0:T(8,128)(2,1)} %slice.185), channel_id=1, source_target_pairs={{0,4},{4,0},{8,12},{12,8},{1,5},{5,1},{9,13},{13,9},{2,6},{6,2},{1... | collective-permute-start | bytes 1228808 | tf_op jit(solution)/shard_map/ppermute | solution.py:35
  490.8 32.6 %collective-permute-start.72 = (bf16[4,2,320,256]{3,2,1,0:T(8,128)(2,1)}, bf16[4,2,320,256]{3,2,1,0:T(8,128)(2,1)}, u32[]{:S(2)}, u32[]{:S(2)}) collective-permute-start(bf16[4,2,320,256]{3,2,1,0:T(8,128)(2,1)} %get-tuple-element.154), channel_id=1, source_target_pairs={{0,16},{16,0},{1,17},{17,1},{2,18},{18,2},{3,19},{19,3},{4,20},{20... | collective-permute-start | bytes 3932168 | tf_op jit(solution)/shard_map/ppermute | solution.py:30
  490.9 32.5 %collective-permute-start.73 = (bf16[4,2,320,256]{3,2,1,0:T(8,128)(2,1)}, bf16[4,2,320,256]{3,2,1,0:T(8,128)(2,1)}, u32[]{:S(2)}, u32[]{:S(2)}) collective-permute-start(bf16[4,2,320,256]{3,2,1,0:T(8,128)(2,1)} %get-tuple-element.157), channel_id=1, source_target_pairs={{0,16},{16,0},{1,17},{17,1},{2,18},{18,2},{3,19},{19,3},{4,20},{20... | collective-permute-start | bytes 3932168 | tf_op jit(solution)/shard_map/ppermute | solution.py:30
  529.2 41.9 %all-to-all-start.5 = ((bf16[4,4,400,256]{3,2,1,0:T(8,128)(2,1)}), bf16[4,4,400,256]{3,2,1,0:T(8,128)(2,1)}, u32[]{:S(2)}, u32[]{:S(2)}) async-start(bf16[4,4,400,256]{3,2,1,0:T(8,128)(2,1)} %pad_maximum_fusion.1), calls=%async_computation.5 | async-start | bytes 6553600 | tf_op jit(solution)/shard_map/all_to_all | solution.py:901
  534.1 39.7 %collective-permute-start.23 = (bf16[4,256,1024]{2,1,0:T(8,128)(2,1)}, bf16[4,256,1024]{2,1,0:T(8,128)(2,1)}, u32[]{:S(2)}, u32[]{:S(2)}) collective-permute-start(bf16[4,256,1024]{2,1,0:T(8,128)(2,1)} %bitcast.201), channel_id=1, source_target_pairs={{16,0},{17,1},{18,2},{19,3},{20,4},{21,5},{22,6},{23,7},{24,8},{25... | collective-permute-start | bytes 6291464 | tf_op jit(solution)/shard_map/ppermute | solution.py:944
  538.0 35.8 %collective-permute-start.35 = (bf16[4,256,1024]{2,1,0:T(8,128)(2,1)}, bf16[4,256,1024]{2,1,0:T(8,128)(2,1)}, u32[]{:S(2)}, u32[]{:S(2)}) collective-permute-start(bf16[4,256,1024]{2,1,0:T(8,128)(2,1)} %bitcast.203), channel_id=1, source_target_pairs={{0,16},{1,17},{2,18},{3,19},{4,20},{5,21},{6,22},{7,23},{8,24},{9,... | collective-permute-start | bytes 6291464 | tf_op jit(solution)/shard_map/ppermute | solution.py:944
  539.3 59.3 %collective-permute-start.78 = (bf16[3,256,768]{2,1,0:T(8,128)(2,1)S(1)}, bf16[3,256,768]{2,1,0:T(8,128)(2,1)}, u32[]{:S(2)}, u32[]{:S(2)}) collective-permute-start(bf16[3,256,768]{2,1,0:T(8,128)(2,1)S(1)} %copy-done.27), channel_id=1, source_target_pairs={{16,8},{20,12},{24,0},{28,4},{17,9},{21,13},{25,1},{29,5},{18,10},... | collective-permute-start | bytes 3538952 | tf_op jit(solution)/shard_map/ppermute | solution.py:905
  573.8 24.5 %collective-permute-start.75 = (bf16[2,400,256]{2,1,0:T(8,128)(2,1)S(1)}, bf16[2,400,256]{2,1,0:T(8,128)(2,1)S(1)}, u32[]{:S(2)}, u32[]{:S(2)}) collective-permute-start(bf16[2,400,256]{2,1,0:T(8,128)(2,1)S(1)} %slice.197), channel_id=1, source_target_pairs={{0,4},{4,0},{8,12},{12,8},{1,5},{5,1},{9,13},{13,9},{2,6},{6,2},{1... | collective-permute-start | bytes 1228808 | tf_op jit(solution)/shard_map/ppermute | solution.py:35
  578.7 39.5 %collective-permute-start.71 = (bf16[4,256,1024]{2,1,0:T(8,128)(2,1)}, bf16[4,256,1024]{2,1,0:T(8,128)(2,1)}, u32[]{:S(2)}, u32[]{:S(2)}) collective-permute-start(bf16[4,256,1024]{2,1,0:T(8,128)(2,1)} %bitcast.67.second), channel_id=1, source_target_pairs={{0,16},{1,17},{2,18},{3,19},{4,20},{5,21},{6,22},{7,23},{8,24},{9,... | collective-permute-start | bytes 6291464 | tf_op jit(solution)/shard_map/ppermute | solution.py:944
  587.6 30.7 %collective-permute-start.70 = (bf16[4,256,1024]{2,1,0:T(8,128)(2,1)}, bf16[4,256,1024]{2,1,0:T(8,128)(2,1)}, u32[]{:S(2)}, u32[]{:S(2)}) collective-permute-start(bf16[4,256,1024]{2,1,0:T(8,128)(2,1)} %bitcast.205), channel_id=1, source_target_pairs={{16,0},{17,1},{18,2},{19,3},{20,4},{21,5},{22,6},{23,7},{24,8},{25... | collective-permute-start | bytes 6291464 | tf_op jit(solution)/shard_map/ppermute | solution.py:944
  (92 other events, 812.7 us)
Sparse Core Ops, SparseCore 0:
  111.5 42.2 all-gather.12
  199.4 61.8 all-gather.14
  308.7 48.9 all-gather.16
  390.4 42.7 all-gather.18
  435.2 45.6 all-gather.20
  523.5 63.9 all-gather.22

commit v6 on v5

--- a/solution.py
+++ b/solution.py
@@ -872,8 +872,7 @@
             )
             lat_parts.append(total)
         if layer == 0:
-            feed_sums = jnp.sum(feed_parts.astype(f32), axis=0).astype(bf16)
-            lat_parts[1] = tie(lat_parts[1], feed_sums, *hooks[2]())
+            lat_parts[1] = tie(lat_parts[1], feed_parts, *hooks[2]())
         else:
             lat_parts[1] = tie(lat_parts[1], feed_parts, *hooks[2]())
         lat_own = by_group(jnp.stack(lat_parts[::-1]))
@@ -892,8 +891,7 @@
         small_send = lax.dynamic_slice_in_dim(small, (1 - core) * half, half, 2)
         small_parts = (small_keep, core_swap(small_send))
 
-        if layer == 1:
-            feed_sums = jnp.sum(tie(feed_parts, grad_x).astype(f32), axis=0).astype(bf16)
+        feed_sums = jnp.sum(tie(feed_parts, grad_x).astype(f32), axis=0).astype(bf16)
         if layer == 0:
             pack_parts_here = [(a, tie(b, grad_x)) for a, b in pack_parts_here]
         pack_total = jnp.concatenate([a + b for a, b in pack_parts_here[::-1]], axis=1)

time: 638 us -> 633 us (level)
  no operation moved by 1% of the time
where the time goes in v6:
time: 633 us; the launch traced here: 625 us
  Pallas kernels  193 us (30%)
  waiting for transfers between devices  185 us (29%)
  starting transfers between devices  130 us (21%)
  other arithmetic  56 us (9%)
  local copies, waits for them, and re-layouts  31.6 us (5%)
  between operations  15.9 us (3%)
  matrix products  14.2 us (2%)
    pallas_call x19, Pallas kernels, kernel_call(): pl.pallas_call(kernel, grid_spec=pltpu.PrefetchScalarGridSpec(num_scalar_...  193 us
    ppermute x31, waiting for transfers between devices, z_swap(): return lax.ppermute(value, 'tensor', [(i, i ^ step) for i in range(count)])  123 us
    ppermute x31, starting transfers between devices, z_swap(): return lax.ppermute(value, 'tensor', [(i, i ^ step) for i in range(count)])  45.7 us
    ppermute x38, starting transfers between devices, core_swap(): return lax.ppermute(value, 'section', [(0, 1), (1, 0)])  27.4 us
    all_to_all x2, waiting for transfers between devices, backward(): lax.all_to_all(jnp.concatenate([pack_total, small_total], axis=2), 'dp',...  24.1 us
  transfers between devices with their start and end apart: 91, of which 33 were waited for; matrix products, arithmetic and copies ran while one was open for 14% of the time, Pallas kernels for 30%

profile of v6, /device:TPU:1, one launch (start us, length us, event | category | flops | bytes accessed | tf_op | source)
XLA Modules:
  0.0 624.6 jit_solution(11413067189939865810)
XLA Ops:
  23.9 7.8 %collective-permute-done.13 = bf16[32,1024]{1,0:T(8,128)(2,1)S(1)} collective-permute-done((bf16[32,1024]{1,0:T(8,128)(2,1)S(1)}, bf16[32,1024]{1,0:T(8,128)(2,1)S(1)}, u32[]{:S(2)}, u32[]{:S(2)}) %collective-permute-start.13) | collective-permute-done | bytes 65568 | tf_op jit(solution)/shard_map/ppermute | solution.py:35
  33.7 14.5 %collective-permute-done.14 = bf16[32,1024]{1,0:T(8,128)(2,1)S(1)} collective-permute-done((bf16[32,1024]{1,0:T(8,128)(2,1)S(1)}, bf16[32,1024]{1,0:T(8,128)(2,1)S(1)}, u32[]{:S(2)}, u32[]{:S(2)}) %collective-permute-start.14) | collective-permute-done | bytes 65568 | tf_op jit(solution)/shard_map/ppermute | solution.py:35
  52.2 4.8 all-to-all-start
  65.9 12.3 %attend_first.1 = bf16[4,272,256]{2,1,0:T(8,128)(2,1)S(1)} custom-call(s32[4]{0:T(128)S(1)} %pad_add_fusion.info, bf16[2048,1024]{1,0:T(8,128)(2,1)} %x.11, bf16[1024,512]{1,0:T(8,128)(2,1)} %bitcast.7.lat_here, bf16[1024,512]{1,0:T(8,128)(2,1)} %collective-permute-done.lat_there, bf16[1536,256]{1,0:T(8,128)(2,1)S(1)} %pad_maximum_fusion.2.heads_here.h0, ...), custom_call_target="tpu_custom_call" | custom-call | flops 4563402752 | bytes 8437760 | tf_op jit(solution)/shard_map/attend_first/pallas_call | solution.py:83
  94.2 5.2 collective-permute-done.18
  113.8 14.8 %collective-permute-start.28 = (bf16[32,1024]{1,0:T(8,128)(2,1)S(1)}, bf16[32,1024]{1,0:T(8,128)(2,1)S(1)}, u32[]{:S(2)}, u32[]{:S(2)}) collective-permute-start(bf16[32,1024]{1,0:T(8,128)(2,1)S(1)} %slice.174), channel_id=1, source_target_pairs={{0,4},{4,0},{8,12},{12,8},{1,5},{5,1},{9,13},{13,9},{2,6},{6,2},{1... | collective-permute-start | bytes 196616 | tf_op jit(solution)/shard_map/ppermute | solution.py:35
  131.4 6.2 attend_out.1
  137.6 6.5 %feed.4 = (f32[256,1024]{1,0:T(8,128)S(1)}, bf16[2,2,256,704]{3,2,1,0:T(8,128)(2,1)}) custom-call(s32[6]{0:T(128)S(1)} %stack.115.info, bf16[256,1024]{1,0:T(8,128)(2,1)S(1)} %get-tuple-element.135.value.refs_0_, bf16[704,1024]{1,0:T(8,128)(2,1)} %bitcast.13.refs_0_, bf16[704,1024]{1,0:T(8,128)(2,1)} %bitcast.15.refs_1_, bf16[704,1024]{1,0:T(8,128)(2,1)} %bitcast.189, ...), custom_call_target="tpu_custom_call" | custom-call | flops 2214592512 | bytes 30539776 | tf_op jit(solution)/shard_map/feed/pallas_call | solution.py:83
  146.3 4.7 all-to-all-start.1
  151.4 11.6 %collective-permute-done.17.value.refs_1_ = bf16[256,1024]{1,0:T(8,128)(2,1)S(1)} collective-permute-done((bf16[256,1024]{1,0:T(8,128)(2,1)S(1)}, bf16[256,1024]{1,0:T(8,128)(2,1)S(1)}, u32[]{:S(2)}, u32[]{:S(2)}) %collective-permute-start.17) | collective-permute-done | bytes 524320 | tf_op jit(solution)/shard_map/ppermute | solution.py:35
  163.0 6.6 %feed.5 = (bf16[256,1024]{1,0:T(8,128)(2,1)S(1)}, bf16[2,2,256,704]{3,2,1,0:T(8,128)(2,1)}) custom-call(s32[6]{0:T(128)S(1)} %stack.115.info, bf16[256,1024]{1,0:T(8,128)(2,1)S(1)} %collective-permute-done.17.value.refs_1_, bf16[704,1024]{1,0:T(8,128)(2,1)} %bitcast.13.refs_0_, bf16[704,1024]{1,0:T(8,128)(2,1)} %bitcast.15.refs_1_, ...), custom_call_target="tpu_custom_call" | custom-call | flops 2214592512 | bytes 30015488 | tf_op jit(solution)/shard_map/feed/pallas_call | solution.py:83
  170.6 10.2 %collective-permute-done.22 = bf16[256,1024]{1,0:T(8,128)(2,1)S(1)} collective-permute-done((bf16[256,1024]{1,0:T(8,128)(2,1)S(1)}, bf16[256,1024]{1,0:T(8,128)(2,1)S(1)}, u32[]{:S(2)}, u32[]{:S(2)}) %collective-permute-start.22) | collective-permute-done | bytes 524320 | tf_op jit(solution)/shard_map/ppermute | solution.py:35
  192.7 4.9 collective-permute-done.25.lat2
  200.4 17.7 %attend.1 = (bf16[4,256,256]{2,1,0:T(8,128)(2,1)S(1)}, f32[4,4,256]{2,1,0:T(4,128)S(1)}, bf16[2,1024,256]{2,1,0:T(8,128)(2,1)}, f32[256,1024]{1,0:T(8,128)}, bf16[256,1024]{1,0:T(8,128)(2,1)}) custom-call(s32[6]{0:T(128)S(1)} %stack.115.info, bf16[256,1024]{1,0:T(8,128)(2,1)} %copy-done.17, bf16[256,1024]{1,0:T(8,128)(2,1)} %copy-done.2, ...), custom_call_target="tpu_custom_call" | custom-call | flops 6442450944 | bytes 16535552 | tf_op jit(solution)/shard_map/attend/pallas_call | solution.py:83
  221.4 6.6 %feed.6 = (f32[256,1024]{1,0:T(8,128)S(1)}, bf16[2,2,256,704]{3,2,1,0:T(8,128)(2,1)}) custom-call(s32[6]{0:T(128)S(1)} %stack.115.info, bf16[256,1024]{1,0:T(8,128)(2,1)S(1)} %copy-done.11, bf16[704,1024]{1,0:T(8,128)(2,1)} %bitcast.13.refs_0_, bf16[704,1024]{1,0:T(8,128)(2,1)} %bitcast.15.refs_1_, bf16[704,1024]{1,0:T(8,128)(2,1)} %bitcast.191, ...), custom_call_target="tpu_custom_call" | custom-call | flops 2214592512 | bytes 30539776 | tf_op jit(solution)/shard_map/feed/pallas_call | solution.py:83
  228.0 10.0 %feed_back.4 = (f32[256,1024]{1,0:T(8,128)S(1)}, bf16[3,256,768]{2,1,0:T(8,128)(2,1)}, bf16[3,256,768]{2,1,0:T(8,128)(2,1)}) custom-call(s32[6]{0:T(128)S(1)} %stack.115.info, bf16[256,1024]{1,0:T(8,128)(2,1)S(1)} %get-tuple-element.265.value.refs_4_, bf16[2,2,256,704]{3,2,1,0:T(8,128)(2,1)} %get-tuple-element.108.saved, bf16[704,1024]{1,0:T(8,128)(2,1)} %bitcast.13.refs_0_, ...), custom_call_target="tpu_custom_call" | custom-call | flops 2214592512 | bytes 32899072 | tf_op jit(solution)/shard_map/feed_back/pallas_call | solution.py:83
  239.0 15.4 %collective-permute-done.33.value.refs_1_ = bf16[256,1024]{1,0:T(8,128)(2,1)S(1)} collective-permute-done((bf16[256,1024]{1,0:T(8,128)(2,1)}, bf16[256,1024]{1,0:T(8,128)(2,1)S(1)}, u32[]{:S(2)}, u32[]{:S(2)}) %collective-permute-start.33) | collective-permute-done | bytes 524320 | tf_op jit(solution)/shard_map/ppermute | solution.py:35
  254.3 6.7 %feed.7 = (bf16[256,1024]{1,0:T(8,128)(2,1)}, bf16[2,2,256,704]{3,2,1,0:T(8,128)(2,1)}) custom-call(s32[6]{0:T(128)S(1)} %stack.115.info, bf16[256,1024]{1,0:T(8,128)(2,1)S(1)} %collective-permute-done.33.value.refs_1_, bf16[704,1024]{1,0:T(8,128)(2,1)} %bitcast.13.refs_0_, bf16[704,1024]{1,0:T(8,128)(2,1)} %bitcast.15.refs_1_, bf16[704,1024]{1,0:T(8,128)(2,1)} %bitcast.193, ...), custom_call_target="tpu_custom_call" | custom-call | flops 2214592512 | bytes 30015488 | tf_op jit(solution)/shard_map/feed/pallas_call | solution.py:83
  261.0 4.5 collective-permute-done.36.value.refs_5_
  265.6 10.4 %feed_back.5 = (bf16[256,1024]{1,0:T(8,128)(2,1)}, bf16[3,256,768]{2,1,0:T(8,128)(2,1)}, bf16[3,256,768]{2,1,0:T(8,128)(2,1)}) custom-call(s32[6]{0:T(128)S(1)} %stack.115.info, bf16[256,1024]{1,0:T(8,128)(2,1)S(1)} %collective-permute-done.36.value.refs_5_, bf16[2,2,256,704]{3,2,1,0:T(8,128)(2,1)} %get-tuple-element.110.saved, ...), custom_call_target="tpu_custom_call" | custom-call | flops 2214592512 | bytes 32374784 | tf_op jit(solution)/shard_map/feed_back/pallas_call | solution.py:83
  283.5 10.7 %feed_weights.2 = bf16[4,3,256,768]{3,2,1,0:T(8,128)(2,1)} custom-call(s32[6]{0:T(128)S(1)} %stack.115.info, bf16[256,1024]{1,0:T(8,128)(2,1)S(1)} %copy-done.12, bf16[256,1024]{1,0:T(8,128)(2,1)S(1)} %collective-permute-done.33.value.refs_1_, bf16[256,1024]{1,0:T(8,128)(2,1)S(1)} %collective-permute-done.38.refs_2_, bf16[256,1024]{1,0:T(8,128)(2,1)} %copy-done.47, ...), custom_call_target="tpu_custom_call" | custom-call | flops 4429185024 | bytes 13631488 | tf_op jit(solution)/shard_map/feed_weights/pallas_call | solution.py:83
  294.2 4.9 all-to-all-start.2
  309.6 14.7 %attend_back.4 = (f32[256,1024]{1,0:T(8,128)}, bf16[1024,256]{1,0:T(8,128)(2,1)S(1)}, bf16[4,2,320,256]{3,2,1,0:T(8,128)(2,1)}, bf16[4,2,320,256]{3,2,1,0:T(8,128)(2,1)}) custom-call(s32[6]{0:T(128)S(1)} %stack.115.info, bf16[256,1024]{1,0:T(8,128)(2,1)S(1)} %copy-done.10, bf16[256,1024]{1,0:T(8,128)(2,1)S(1)} %copy-done.3, ...), custom_call_target="tpu_custom_call" | custom-call | flops 8858370048 | bytes 18104320 | tf_op jit(solution)/shard_map/attend_back/pallas_call | solution.py:83
  325.6 14.5 %attend_back.5 = (f32[256,1024]{1,0:T(8,128)}, bf16[1024,256]{1,0:T(8,128)(2,1)S(1)}, bf16[4,2,320,256]{3,2,1,0:T(8,128)(2,1)}, bf16[4,2,320,256]{3,2,1,0:T(8,128)(2,1)}) custom-call(s32[6]{0:T(128)S(1)} %stack.115.info, bf16[256,1024]{1,0:T(8,128)(2,1)S(1)} %copy-done.10, bf16[256,1024]{1,0:T(8,128)(2,1)S(1)} %copy-done.3, ...), custom_call_target="tpu_custom_call" | custom-call | flops 8858370048 | bytes 18104320 | tf_op jit(solution)/shard_map/attend_back/pallas_call | solution.py:83
  342.6 12.5 %collective-permute-done.45 = bf16[256,256]{1,0:T(8,128)(2,1)S(1)} collective-permute-done((bf16[256,256]{1,0:T(8,128)(2,1)S(1)}, bf16[256,256]{1,0:T(8,128)(2,1)S(1)}, u32[]{:S(2)}, u32[]{:S(2)}) %collective-permute-start.45) | collective-permute-done | bytes 131104 | tf_op jit(solution)/shard_map/ppermute | solution.py:35
  360.6 4.1 fusion.33
  373.7 4.8 all-to-all-start.3
  385.3 4.3 collective-permute-done.62
  392.1 4.5 reduce_sum.182
  397.8 9.8 %feed_back.6 = (f32[256,1024]{1,0:T(8,128)S(1)}, bf16[3,256,768]{2,1,0:T(8,128)(2,1)}, bf16[3,256,768]{2,1,0:T(8,128)(2,1)}) custom-call(s32[6]{0:T(128)S(1)} %stack.115.info, bf16[256,1024]{1,0:T(8,128)(2,1)S(1)} %get-tuple-element.206.value.refs_4_, bf16[2,2,256,704]{3,2,1,0:T(8,128)(2,1)} %get-tuple-element.126.saved, bf16[704,1024]{1,0:T(8,128)(2,1)} %bitcast.13.refs_0_, ...), custom_call_target="tpu_custom_call" | custom-call | flops 2214592512 | bytes 32899072 | tf_op jit(solution)/shard_map/feed_back/pallas_call | solution.py:83
  407.6 4.8 collective-permute-start.58
  412.4 10.3 %feed_back.7 = (bf16[256,1024]{1,0:T(8,128)(2,1)}, bf16[3,256,768]{2,1,0:T(8,128)(2,1)}, bf16[3,256,768]{2,1,0:T(8,128)(2,1)}) custom-call(s32[6]{0:T(128)S(1)} %stack.115.info, bf16[256,1024]{1,0:T(8,128)(2,1)S(1)} %collective-permute-done.48.value.refs_5_, bf16[2,2,256,704]{3,2,1,0:T(8,128)(2,1)} %get-tuple-element.128.saved, ...), custom_call_target="tpu_custom_call" | custom-call | flops 2214592512 | bytes 32374784 | tf_op jit(solution)/shard_map/feed_back/pallas_call | solution.py:83
  423.6 4.3 collective-permute-done.53
  427.9 5.3 all-gather.19.cloned.1.call-done
  435.0 11.0 %feed_weights.3 = bf16[4,3,256,768]{3,2,1,0:T(8,128)(2,1)} custom-call(s32[6]{0:T(128)S(1)} %stack.115.info, bf16[256,1024]{1,0:T(8,128)(2,1)S(1)} %get-tuple-element.135.value.refs_0_, bf16[256,1024]{1,0:T(8,128)(2,1)S(1)} %copy-done.9, bf16[256,1024]{1,0:T(8,128)(2,1)} %collective-permute-done.54.refs_2_, ...), custom_call_target="tpu_custom_call" | custom-call | flops 4429185024 | bytes 13631488 | tf_op jit(solution)/shard_map/feed_weights/pallas_call | solution.py:83
  446.0 5.1 all-to-all-start.4
  455.4 14.5 %attend_back.6 = (f32[256,1024]{1,0:T(8,128)}, bf16[1024,256]{1,0:T(8,128)(2,1)S(1)}, bf16[4,2,320,256]{3,2,1,0:T(8,128)(2,1)}, bf16[4,2,320,256]{3,2,1,0:T(8,128)(2,1)}) custom-call(s32[6]{0:T(128)S(1)} %stack.115.info, bf16[256,1024]{1,0:T(8,128)(2,1)S(1)} %get-tuple-element.149.grad_branch, bf16[256,1024]{1,0:T(8,128)(2,1)S(1)} %fusion.18.normed, ...), custom_call_target="tpu_custom_call" | custom-call | flops 8858370048 | bytes 18104320 | tf_op jit(solution)/shard_map/attend_back/pallas_call | solution.py:83
  475.2 14.7 %attend_back.7 = (f32[256,1024]{1,0:T(8,128)}, bf16[1024,256]{1,0:T(8,128)(2,1)S(1)}, bf16[4,2,320,256]{3,2,1,0:T(8,128)(2,1)}, bf16[4,2,320,256]{3,2,1,0:T(8,128)(2,1)}) custom-call(s32[6]{0:T(128)S(1)} %stack.115.info, bf16[256,1024]{1,0:T(8,128)(2,1)S(1)} %get-tuple-element.149.grad_branch, bf16[256,1024]{1,0:T(8,128)(2,1)S(1)} %fusion.18.normed, ...), custom_call_target="tpu_custom_call" | custom-call | flops 8858370048 | bytes 18104320 | tf_op jit(solution)/shard_map/attend_back/pallas_call | solution.py:83
  500.4 8.5 %collective-permute-done.69 = bf16[400,256]{1,0:T(8,128)(2,1)S(1)} collective-permute-done((bf16[400,256]{1,0:T(8,128)(2,1)S(1)}, bf16[400,256]{1,0:T(8,128)(2,1)S(1)}, u32[]{:S(2)}, u32[]{:S(2)}) %collective-permute-start.69) | collective-permute-done | bytes 204832 | tf_op jit(solution)/shard_map/ppermute | solution.py:35
  524.7 4.7 all-to-all-start.5
  537.9 4.5 collective-permute-start.78
  542.5 24.1 %all-to-all-done.5 = bf16[4,4,400,256]{3,2,1,0:T(8,128)(2,1)} async-done(((bf16[4,4,400,256]{3,2,1,0:T(8,128)(2,1)}), bf16[4,4,400,256]{3,2,1,0:T(8,128)(2,1)}, u32[]{:S(2)}, u32[]{:S(2)}) %all-to-all-start.5) | async-done | bytes 3276832 | tf_op jit(solution)/shard_map/all_to_all | solution.py:899
  569.2 4.8 rows.2
  575.4 6.8 %all-gather.23.cloned.1.call-done = bf16[1024,1024]{1,0:T(8,128)(2,1)} async-done(((bf16[256,1024]{1,0:T(8,128)(2,1)}), bf16[1024,1024]{1,0:T(8,128)(2,1)}) %all-gather.23.cloned.1.call-update) | async-done | bytes 2097168 | tf_op jit(solution)/shard_map/all_gather | solution.py:939
  582.2 4.2 collective-permute-start.70
  586.3 6.1 collective-permute-done.75
  596.4 7.6 %collective-permute-done.76 = bf16[400,256]{1,0:T(8,128)(2,1)S(1)} collective-permute-done((bf16[400,256]{1,0:T(8,128)(2,1)S(1)}, bf16[400,256]{1,0:T(8,128)(2,1)S(1)}, u32[]{:S(2)}, u32[]{:S(2)}) %collective-permute-start.76) | collective-permute-done | bytes 204832 | tf_op jit(solution)/shard_map/ppermute | solution.py:35
  612.7 4.8 rows.3
  (392 shorter events, 196.7 us)
Async XLA Ops:
  10.7 48.4 %collective-permute-start = (bf16[1024,512]{1,0:T(8,128)(2,1)}, bf16[1024,512]{1,0:T(8,128)(2,1)}, u32[]{:S(2)}, u32[]{:S(2)}) collective-permute-start(bf16[1024,512]{1,0:T(8,128)(2,1)} %bitcast.7.lat_here), channel_id=1, source_target_pairs={{0,16},{16,0},{1,17},{17,1},{2,18},{18,2},{3,19},{19,3},{4,20},{20... | collective-permute-start | bytes 3145736 | tf_op jit(solution)/shard_map/ppermute | solution.py:30
  14.4 35.1 %collective-permute-start.2 = (bf16[288,1024]{1,0:T(8,128)(2,1)S(1)}, bf16[288,1024]{1,0:T(8,128)(2,1)S(1)}, u32[]{:S(2)}, u32[]{:S(2)}) collective-permute-start(bf16[288,1024]{1,0:T(8,128)(2,1)S(1)} %slice.207), channel_id=1, source_target_pairs={{0,8},{4,12},{8,0},{12,4},{1,9},{5,13},{9,1},{13,5},{2,10},{6,14},... | collective-permute-start | bytes 1769480 | tf_op jit(solution)/shard_map/ppermute | solution.py:35
  21.2 27.0 %collective-permute-start.14 = (bf16[32,1024]{1,0:T(8,128)(2,1)S(1)}, bf16[32,1024]{1,0:T(8,128)(2,1)S(1)}, u32[]{:S(2)}, u32[]{:S(2)}) collective-permute-start(bf16[32,1024]{1,0:T(8,128)(2,1)S(1)} %slice.216), channel_id=1, source_target_pairs={{0,8},{4,12},{8,0},{12,4},{1,9},{5,13},{9,1},{13,5},{2,10},{6,14},... | collective-permute-start | bytes 196616 | tf_op jit(solution)/shard_map/ppermute | solution.py:35
  21.3 28.2 %collective-permute-start.15 = (bf16[32,1024]{1,0:T(8,128)(2,1)S(1)}, bf16[32,1024]{1,0:T(8,128)(2,1)S(1)}, u32[]{:S(2)}, u32[]{:S(2)}) collective-permute-start(bf16[32,1024]{1,0:T(8,128)(2,1)S(1)} %slice.216), channel_id=1, source_target_pairs={{0,12},{4,8},{8,4},{12,0},{1,13},{5,9},{9,5},{13,1},{2,14},{6,10},... | collective-permute-start | bytes 196616 | tf_op jit(solution)/shard_map/ppermute | solution.py:35
  31.7 32.5 %collective-permute-start.5 = (bf16[704,1024]{1,0:T(8,128)(2,1)}, bf16[704,1024]{1,0:T(8,128)(2,1)}, u32[]{:S(2)}, u32[]{:S(2)}) collective-permute-start(bf16[704,1024]{1,0:T(8,128)(2,1)} %bitcast.13.refs_0_), channel_id=1, source_target_pairs={{0,16},{16,0},{1,17},{17,1},{2,18},{18,2},{3,19},{19,3},{4,20},{20... | collective-permute-start | bytes 4325384 | tf_op jit(solution)/shard_map/ppermute | solution.py:30
  48.2 16.1 %collective-permute-start.6 = (bf16[704,1024]{1,0:T(8,128)(2,1)}, bf16[704,1024]{1,0:T(8,128)(2,1)}, u32[]{:S(2)}, u32[]{:S(2)}) collective-permute-start(bf16[704,1024]{1,0:T(8,128)(2,1)} %bitcast.15.refs_1_), channel_id=1, source_target_pairs={{0,16},{16,0},{1,17},{17,1},{2,18},{18,2},{3,19},{19,3},{4,20},{20... | collective-permute-start | bytes 4325384 | tf_op jit(solution)/shard_map/ppermute | solution.py:30
  52.2 41.2 %all-to-all-start = ((bf16[4,384,1024]{2,1,0:T(8,128)(2,1)}), bf16[4,384,1024]{2,1,0:T(8,128)(2,1)}, u32[]{:S(2)}, u32[]{:S(2)}) async-start(bf16[4,384,1024]{2,1,0:T(8,128)(2,1)} %broadcast_in_dim.8), calls=%async_computation | async-start | bytes 6291456 | tf_op jit(solution)/shard_map/all_to_all | solution.py:48
  57.0 106.0 %all-gather.13.cloned.1.call-start = ((), (), s32[]{:S(2)}) async-start(), calls=%async_computation.6 | async-start | bytes 1474560 | tf_op jit(solution)/shard_map/all_gather | solution.py:776
  93.3 38.1 %collective-permute-start.16 = (bf16[4,384,1024]{2,1,0:T(8,128)(2,1)}, bf16[4,384,1024]{2,1,0:T(8,128)(2,1)}, u32[]{:S(2)}, u32[]{:S(2)}) collective-permute-start(bf16[4,384,1024]{2,1,0:T(8,128)(2,1)} %all-to-all-done.o2.refs_6_.refs_8_.refs_10_), channel_id=1, source_target_pairs={{0,16},{16,0},{1,17},{17,1},{2,18},{18,2},{3,19},{19,3},{4,20},{20... | collective-permute-start | bytes 9437192 | tf_op jit(solution)/shard_map/ppermute | solution.py:30
  104.4 39.8 %collective-permute-start.31 = (bf16[288,1024]{1,0:T(8,128)(2,1)}, bf16[288,1024]{1,0:T(8,128)(2,1)S(1)}, u32[]{:S(2)}, u32[]{:S(2)}) collective-permute-start(bf16[288,1024]{1,0:T(8,128)(2,1)} %slice.175), channel_id=1, source_target_pairs={{0,8},{4,12},{8,0},{12,4},{1,9},{5,13},{9,1},{13,5},{2,10},{6,14},... | collective-permute-start | bytes 1769480 | tf_op jit(solution)/shard_map/ppermute | solution.py:35
  113.8 30.3 %collective-permute-start.28 = (bf16[32,1024]{1,0:T(8,128)(2,1)S(1)}, bf16[32,1024]{1,0:T(8,128)(2,1)S(1)}, u32[]{:S(2)}, u32[]{:S(2)}) collective-permute-start(bf16[32,1024]{1,0:T(8,128)(2,1)S(1)} %slice.174), channel_id=1, source_target_pairs={{0,4},{4,0},{8,12},{12,8},{1,5},{5,1},{9,13},{13,9},{2,6},{6,2},{1... | collective-permute-start | bytes 196616 | tf_op jit(solution)/shard_map/ppermute | solution.py:35
  128.6 15.5 %collective-permute-start.29 = (bf16[32,1024]{1,0:T(8,128)(2,1)S(1)}, bf16[32,1024]{1,0:T(8,128)(2,1)S(1)}, u32[]{:S(2)}, u32[]{:S(2)}) collective-permute-start(bf16[32,1024]{1,0:T(8,128)(2,1)S(1)} %slice.174), channel_id=1, source_target_pairs={{0,8},{4,12},{8,0},{12,4},{1,9},{5,13},{9,1},{13,5},{2,10},{6,14},... | collective-permute-start | bytes 196616 | tf_op jit(solution)/shard_map/ppermute | solution.py:35
  146.3 40.3 %all-to-all-start.1 = ((bf16[4,384,1024]{2,1,0:T(8,128)(2,1)}), bf16[4,384,1024]{2,1,0:T(8,128)(2,1)}, u32[]{:S(2)}, u32[]{:S(2)}) async-start(bf16[4,384,1024]{2,1,0:T(8,128)(2,1)} %broadcast_in_dim.9), calls=%async_computation.1 | async-start | bytes 6291456 | tf_op jit(solution)/shard_map/all_to_all | solution.py:48
  151.0 148.2 %all-gather.15.cloned.1.call-start = ((), (), s32[]{:S(2)}) async-start(), calls=%async_computation.7 | async-start | bytes 2621440 | tf_op jit(solution)/shard_map/all_gather | solution.py:939
  218.9 35.4 %collective-permute-start.33 = (bf16[256,1024]{1,0:T(8,128)(2,1)}, bf16[256,1024]{1,0:T(8,128)(2,1)S(1)}, u32[]{:S(2)}, u32[]{:S(2)}) collective-permute-start(bf16[256,1024]{1,0:T(8,128)(2,1)} %get-tuple-element.104.value.refs_0_), channel_id=1, source_target_pairs={{0,4},{4,0},{8,12},{12,8},{1,5},{5,1},{9,13},{13,9},{2,6},{6,2},{1... | collective-permute-start | bytes 1572872 | tf_op jit(solution)/shard_map/ppermute | solution.py:35
  220.0 45.6 %collective-permute-start.36 = (bf16[256,1024]{1,0:T(8,128)(2,1)S(1)}, bf16[256,1024]{1,0:T(8,128)(2,1)S(1)}, u32[]{:S(2)}, u32[]{:S(2)}) collective-permute-start(bf16[256,1024]{1,0:T(8,128)(2,1)S(1)} %get-tuple-element.265.value.refs_4_), channel_id=1, source_target_pairs={{0,4},{4,0},{8,12},{12,8},{1,5},{5,1},{9,13},{13,9},{2,6},{6,2},{1... | collective-permute-start | bytes 1572872 | tf_op jit(solution)/shard_map/ppermute | solution.py:35
  238.0 43.9 %collective-permute-start.42 = (bf16[3,256,768]{2,1,0:T(8,128)(2,1)}, bf16[3,256,768]{2,1,0:T(8,128)(2,1)S(1)}, u32[]{:S(2)}, u32[]{:S(2)}) collective-permute-start(bf16[3,256,768]{2,1,0:T(8,128)(2,1)} %get-tuple-element.114), channel_id=1, source_target_pairs={{0,16},{16,0},{1,17},{17,1},{2,18},{18,2},{3,19},{19,3},{4,20},{20... | collective-permute-start | bytes 3538952 | tf_op jit(solution)/shard_map/ppermute | solution.py:30
  280.4 18.9 %collective-permute-start.37 = (bf16[256,1024]{1,0:T(8,128)(2,1)}, bf16[256,1024]{1,0:T(8,128)(2,1)S(1)}, u32[]{:S(2)}, u32[]{:S(2)}) collective-permute-start(bf16[256,1024]{1,0:T(8,128)(2,1)} %get-tuple-element.111), channel_id=1, source_target_pairs={{0,4},{4,0},{8,12},{12,8},{1,5},{5,1},{9,13},{13,9},{2,6},{6,2},{1... | collective-permute-start | bytes 1572872 | tf_op jit(solution)/shard_map/ppermute | solution.py:35
  281.2 23.9 %collective-permute-start.34 = (bf16[256,1024]{1,0:T(8,128)(2,1)}, bf16[256,1024]{1,0:T(8,128)(2,1)}, u32[]{:S(2)}, u32[]{:S(2)}) collective-permute-start(bf16[256,1024]{1,0:T(8,128)(2,1)} %get-tuple-element.107), channel_id=1, source_target_pairs={{0,4},{4,0},{8,12},{12,8},{1,5},{5,1},{9,13},{13,9},{2,6},{6,2},{1... | collective-permute-start | bytes 1572872 | tf_op jit(solution)/shard_map/ppermute | solution.py:35
  294.2 65.0 %all-to-all-start.2 = ((bf16[4,3,256,768]{3,2,1,0:T(8,128)(2,1)}), bf16[4,3,256,768]{3,2,1,0:T(8,128)(2,1)}, u32[]{:S(2)}, u32[]{:S(2)}) async-start(bf16[4,3,256,768]{3,2,1,0:T(8,128)(2,1)} %feed_weights.2), calls=%async_computation.2 | async-start | bytes 9437184 | tf_op jit(solution)/shard_map/all_to_all | solution.py:853
  299.2 60.0 %all-gather.17.cloned.1.call-start = ((), (), s32[]{:S(2)}) async-start(), calls=%async_computation.8 | async-start | bytes 2621440 | tf_op jit(solution)/shard_map/all_gather | solution.py:939
  324.4 16.5 %collective-permute-start.44 = (bf16[2,256,256]{2,1,0:T(8,128)(2,1)S(1)}, bf16[2,256,256]{2,1,0:T(8,128)(2,1)S(1)}, u32[]{:S(2)}, u32[]{:S(2)}) collective-permute-start(bf16[2,256,256]{2,1,0:T(8,128)(2,1)S(1)} %dynamic-slice_bitcast_fusion.5), channel_id=1, source_target_pairs={{0,16},{16,0},{1,17},{17,1},{2,18},{18,2},{3,19},{19,3},{4,20},{20... | collective-permute-start | bytes 786440 | tf_op jit(solution)/shard_map/ppermute | solution.py:30
  340.2 27.7 %collective-permute-start.50 = (bf16[4,2,320,256]{3,2,1,0:T(8,128)(2,1)}, bf16[4,2,320,256]{3,2,1,0:T(8,128)(2,1)}, u32[]{:S(2)}, u32[]{:S(2)}) collective-permute-start(bf16[4,2,320,256]{3,2,1,0:T(8,128)(2,1)} %get-tuple-element.131), channel_id=1, source_target_pairs={{0,16},{16,0},{1,17},{17,1},{2,18},{18,2},{3,19},{19,3},{4,20},{20... | collective-permute-start | bytes 3932168 | tf_op jit(solution)/shard_map/ppermute | solution.py:30
  340.7 29.3 %collective-permute-start.51 = (bf16[4,2,320,256]{3,2,1,0:T(8,128)(2,1)}, bf16[4,2,320,256]{3,2,1,0:T(8,128)(2,1)}, u32[]{:S(2)}, u32[]{:S(2)}) collective-permute-start(bf16[4,2,320,256]{3,2,1,0:T(8,128)(2,1)} %get-tuple-element.133), channel_id=1, source_target_pairs={{0,16},{16,0},{1,17},{17,1},{2,18},{18,2},{3,19},{19,3},{4,20},{20... | collective-permute-start | bytes 3932168 | tf_op jit(solution)/shard_map/ppermute | solution.py:30
  341.8 17.4 %collective-permute-start.47 = (bf16[256,256]{1,0:T(8,128)(2,1)S(1)}, bf16[256,256]{1,0:T(8,128)(2,1)S(1)}, u32[]{:S(2)}, u32[]{:S(2)}) collective-permute-start(bf16[256,256]{1,0:T(8,128)(2,1)S(1)} %dynamic-slice_bitcast_fusion.8), channel_id=1, source_target_pairs={{0,4},{4,0},{8,12},{12,8},{1,5},{5,1},{9,13},{13,9},{2,6},{6,2},{1... | collective-permute-start | bytes 393224 | tf_op jit(solution)/shard_map/ppermute | solution.py:35
  373.7 59.5 %all-to-all-start.3 = ((bf16[4,4,400,256]{3,2,1,0:T(8,128)(2,1)}), bf16[4,4,400,256]{3,2,1,0:T(8,128)(2,1)}, u32[]{:S(2)}, u32[]{:S(2)}) async-start(bf16[4,4,400,256]{3,2,1,0:T(8,128)(2,1)} %pad_maximum_fusion), calls=%async_computation.3 | async-start | bytes 6553600 | tf_op jit(solution)/shard_map/all_to_all | solution.py:899
  378.6 54.6 %all-gather.19.cloned.1.call-start = ((), (), s32[]{:S(2)}) async-start(), calls=%async_computation.9 | async-start | bytes 1474560 | tf_op jit(solution)/shard_map/all_gather | solution.py:776
  384.9 27.4 %collective-permute-start.48 = (bf16[256,1024]{1,0:T(8,128)(2,1)S(1)}, bf16[256,1024]{1,0:T(8,128)(2,1)S(1)}, u32[]{:S(2)}, u32[]{:S(2)}) collective-permute-start(bf16[256,1024]{1,0:T(8,128)(2,1)S(1)} %get-tuple-element.206.value.refs_4_), channel_id=1, source_target_pairs={{0,4},{4,0},{8,12},{12,8},{1,5},{5,1},{9,13},{13,9},{2,6},{6,2},{1... | collective-permute-start | bytes 1572872 | tf_op jit(solution)/shard_map/ppermute | solution.py:35
  390.3 118.6 %all-gather.21.cloned.1.call-start = ((), (), s32[]{:S(2)}) async-start(), calls=%async_computation.10 | async-start | bytes 2621440 | tf_op jit(solution)/shard_map/all_gather | solution.py:939
  390.4 32.4 %collective-permute-start.54 = (bf16[256,1024]{1,0:T(8,128)(2,1)S(1)}, bf16[256,1024]{1,0:T(8,128)(2,1)}, u32[]{:S(2)}, u32[]{:S(2)}) collective-permute-start(bf16[256,1024]{1,0:T(8,128)(2,1)S(1)} %get-tuple-element.135.value.refs_0_), channel_id=1, source_target_pairs={{0,16},{16,0},{1,17},{17,1},{2,18},{18,2},{3,19},{19,3},{4,20},{20... | collective-permute-start | bytes 1572872 | tf_op jit(solution)/shard_map/ppermute | solution.py:30
  392.0 31.3 %collective-permute-start.55 = (bf16[256,1024]{1,0:T(8,128)(2,1)S(1)}, bf16[256,1024]{1,0:T(8,128)(2,1)}, u32[]{:S(2)}, u32[]{:S(2)}) collective-permute-start(bf16[256,1024]{1,0:T(8,128)(2,1)S(1)} %copy-done.8), channel_id=1, source_target_pairs={{0,16},{16,0},{1,17},{17,1},{2,18},{18,2},{3,19},{19,3},{4,20},{20... | collective-permute-start | bytes 1572872 | tf_op jit(solution)/shard_map/ppermute | solution.py:30
  396.5 31.4 %collective-permute-start.53 = (bf16[3,256,768]{2,1,0:T(8,128)(2,1)}, bf16[3,256,768]{2,1,0:T(8,128)(2,1)}, u32[]{:S(2)}, u32[]{:S(2)}) collective-permute-start(bf16[3,256,768]{2,1,0:T(8,128)(2,1)} %reduce_sum.182), channel_id=1, source_target_pairs={{0,24},{4,28},{8,16},{12,20},{1,25},{5,29},{9,17},{13,21},{2,26},{... | collective-permute-start | bytes 3538952 | tf_op jit(solution)/shard_map/ppermute | solution.py:903
  407.6 26.4 %collective-permute-start.58 = (bf16[3,256,768]{2,1,0:T(8,128)(2,1)}, bf16[3,256,768]{2,1,0:T(8,128)(2,1)}, u32[]{:S(2)}, u32[]{:S(2)}) collective-permute-start(bf16[3,256,768]{2,1,0:T(8,128)(2,1)} %get-tuple-element.138), channel_id=1, source_target_pairs={{0,16},{16,0},{1,17},{17,1},{2,18},{18,2},{3,19},{19,3},{4,20},{20... | collective-permute-start | bytes 3538952 | tf_op jit(solution)/shard_map/ppermute | solution.py:30
  427.9 23.5 %collective-permute-start.49 = (bf16[256,1024]{1,0:T(8,128)(2,1)}, bf16[256,1024]{1,0:T(8,128)(2,1)}, u32[]{:S(2)}, u32[]{:S(2)}) collective-permute-start(bf16[256,1024]{1,0:T(8,128)(2,1)} %get-tuple-element.129), channel_id=1, source_target_pairs={{0,4},{4,0},{8,12},{12,8},{1,5},{5,1},{9,13},{13,9},{2,6},{6,2},{1... | collective-permute-start | bytes 1572872 | tf_op jit(solution)/shard_map/ppermute | solution.py:35
  433.2 22.2 %collective-permute-start.63 = (bf16[4,576,256]{2,1,0:T(8,128)(2,1)}, bf16[4,576,256]{2,1,0:T(8,128)(2,1)}, u32[]{:S(2)}, u32[]{:S(2)}) collective-permute-start(bf16[4,576,256]{2,1,0:T(8,128)(2,1)} %bitcast.222), channel_id=1, source_target_pairs={{0,16},{16,0},{1,17},{17,1},{2,18},{18,2},{3,19},{19,3},{4,20},{20... | collective-permute-start | bytes 3538952 | tf_op jit(solution)/shard_map/ppermute | solution.py:30
  446.0 63.0 %all-to-all-start.4 = ((bf16[4,3,256,768]{3,2,1,0:T(8,128)(2,1)}), bf16[4,3,256,768]{3,2,1,0:T(8,128)(2,1)}, u32[]{:S(2)}, u32[]{:S(2)}) async-start(bf16[4,3,256,768]{3,2,1,0:T(8,128)(2,1)} %feed_weights.3), calls=%async_computation.4 | async-start | bytes 9437184 | tf_op jit(solution)/shard_map/all_to_all | solution.py:853
  451.1 131.1 %all-gather.23.cloned.1.call-start = ((), (), s32[]{:S(2)}) async-start(), calls=%async_computation.11 | async-start | bytes 2621440 | tf_op jit(solution)/shard_map/all_gather | solution.py:939
  470.7 20.7 %collective-permute-start.64 = (bf16[2,256,256]{2,1,0:T(8,128)(2,1)}, bf16[2,256,256]{2,1,0:T(8,128)(2,1)}, u32[]{:S(2)}, u32[]{:S(2)}) collective-permute-start(bf16[2,256,256]{2,1,0:T(8,128)(2,1)} %dynamic-slice_bitcast_fusion.3), channel_id=1, source_target_pairs={{0,16},{16,0},{1,17},{17,1},{2,18},{18,2},{3,19},{19,3},{4,20},{20... | collective-permute-start | bytes 786440 | tf_op jit(solution)/shard_map/ppermute | solution.py:30
  474.0 23.6 %collective-permute-start.68 = (bf16[2,400,256]{2,1,0:T(8,128)(2,1)}, bf16[2,400,256]{2,1,0:T(8,128)(2,1)S(1)}, u32[]{:S(2)}, u32[]{:S(2)}) collective-permute-start(bf16[2,400,256]{2,1,0:T(8,128)(2,1)} %slice.185), channel_id=1, source_target_pairs={{0,4},{4,0},{8,12},{12,8},{1,5},{5,1},{9,13},{13,9},{2,6},{6,2},{1... | collective-permute-start | bytes 1228808 | tf_op jit(solution)/shard_map/ppermute | solution.py:35
  490.8 28.1 %collective-permute-start.72 = (bf16[4,2,320,256]{3,2,1,0:T(8,128)(2,1)}, bf16[4,2,320,256]{3,2,1,0:T(8,128)(2,1)}, u32[]{:S(2)}, u32[]{:S(2)}) collective-permute-start(bf16[4,2,320,256]{3,2,1,0:T(8,128)(2,1)} %get-tuple-element.155), channel_id=1, source_target_pairs={{0,16},{16,0},{1,17},{17,1},{2,18},{18,2},{3,19},{19,3},{4,20},{20... | collective-permute-start | bytes 3932168 | tf_op jit(solution)/shard_map/ppermute | solution.py:30
  490.8 28.1 %collective-permute-start.73 = (bf16[4,2,320,256]{3,2,1,0:T(8,128)(2,1)}, bf16[4,2,320,256]{3,2,1,0:T(8,128)(2,1)}, u32[]{:S(2)}, u32[]{:S(2)}) collective-permute-start(bf16[4,2,320,256]{3,2,1,0:T(8,128)(2,1)} %get-tuple-element.158), channel_id=1, source_target_pairs={{0,16},{16,0},{1,17},{17,1},{2,18},{18,2},{3,19},{19,3},{4,20},{20... | collective-permute-start | bytes 3932168 | tf_op jit(solution)/shard_map/ppermute | solution.py:30
  524.7 41.8 %all-to-all-start.5 = ((bf16[4,4,400,256]{3,2,1,0:T(8,128)(2,1)}), bf16[4,4,400,256]{3,2,1,0:T(8,128)(2,1)}, u32[]{:S(2)}, u32[]{:S(2)}) async-start(bf16[4,4,400,256]{3,2,1,0:T(8,128)(2,1)} %pad_maximum_fusion.1), calls=%async_computation.5 | async-start | bytes 6553600 | tf_op jit(solution)/shard_map/all_to_all | solution.py:899
  529.5 39.8 %collective-permute-start.23 = (bf16[4,256,1024]{2,1,0:T(8,128)(2,1)}, bf16[4,256,1024]{2,1,0:T(8,128)(2,1)}, u32[]{:S(2)}, u32[]{:S(2)}) collective-permute-start(bf16[4,256,1024]{2,1,0:T(8,128)(2,1)} %bitcast.30.first), channel_id=1, source_target_pairs={{16,0},{17,1},{18,2},{19,3},{20,4},{21,5},{22,6},{23,7},{24,8},{25... | collective-permute-start | bytes 6291464 | tf_op jit(solution)/shard_map/ppermute | solution.py:942
  533.3 35.9 %collective-permute-start.35 = (bf16[4,256,1024]{2,1,0:T(8,128)(2,1)}, bf16[4,256,1024]{2,1,0:T(8,128)(2,1)}, u32[]{:S(2)}, u32[]{:S(2)}) collective-permute-start(bf16[4,256,1024]{2,1,0:T(8,128)(2,1)} %bitcast.32.second), channel_id=1, source_target_pairs={{0,16},{1,17},{2,18},{3,19},{4,20},{5,21},{6,22},{7,23},{8,24},{9,... | collective-permute-start | bytes 6291464 | tf_op jit(solution)/shard_map/ppermute | solution.py:942
  537.9 55.8 %collective-permute-start.78 = (bf16[3,256,768]{2,1,0:T(8,128)(2,1)S(1)}, bf16[3,256,768]{2,1,0:T(8,128)(2,1)}, u32[]{:S(2)}, u32[]{:S(2)}) collective-permute-start(bf16[3,256,768]{2,1,0:T(8,128)(2,1)S(1)} %reduce_sum.189), channel_id=1, source_target_pairs={{16,8},{20,12},{24,0},{28,4},{17,9},{21,13},{25,1},{29,5},{18,10},... | collective-permute-start | bytes 3538952 | tf_op jit(solution)/shard_map/ppermute | solution.py:903
  569.1 23.3 %collective-permute-start.75 = (bf16[2,400,256]{2,1,0:T(8,128)(2,1)S(1)}, bf16[2,400,256]{2,1,0:T(8,128)(2,1)S(1)}, u32[]{:S(2)}, u32[]{:S(2)}) collective-permute-start(bf16[2,400,256]{2,1,0:T(8,128)(2,1)S(1)} %slice.197), channel_id=1, source_target_pairs={{0,4},{4,0},{8,12},{12,8},{1,5},{5,1},{9,13},{13,9},{2,6},{6,2},{1... | collective-permute-start | bytes 1228808 | tf_op jit(solution)/shard_map/ppermute | solution.py:35
  574.1 38.6 %collective-permute-start.71 = (bf16[4,256,1024]{2,1,0:T(8,128)(2,1)}, bf16[4,256,1024]{2,1,0:T(8,128)(2,1)}, u32[]{:S(2)}, u32[]{:S(2)}) collective-permute-start(bf16[4,256,1024]{2,1,0:T(8,128)(2,1)} %bitcast.67.second), channel_id=1, source_target_pairs={{0,16},{1,17},{2,18},{3,19},{4,20},{5,21},{6,22},{7,23},{8,24},{9,... | collective-permute-start | bytes 6291464 | tf_op jit(solution)/shard_map/ppermute | solution.py:942
  582.2 30.5 %collective-permute-start.70 = (bf16[4,256,1024]{2,1,0:T(8,128)(2,1)}, bf16[4,256,1024]{2,1,0:T(8,128)(2,1)}, u32[]{:S(2)}, u32[]{:S(2)}) collective-permute-start(bf16[4,256,1024]{2,1,0:T(8,128)(2,1)} %bitcast.201), channel_id=1, source_target_pairs={{16,0},{17,1},{18,2},{19,3},{20,4},{21,5},{22,6},{23,7},{24,8},{25... | collective-permute-start | bytes 6291464 | tf_op jit(solution)/shard_map/ppermute | solution.py:942
  (91 other events, 802.4 us)
Sparse Core Ops, SparseCore 0:
  111.5 42.3 all-gather.12
  199.4 61.8 all-gather.14
  308.7 48.9 all-gather.16
  390.5 42.6 all-gather.18
  435.2 45.6 all-gather.20
  519.0 63.1 all-gather.22
